TPU v7x, 32 devices: a whole 2x2x4 slice. The times are simulated.
32 devices in a mesh: seq: 8 (over z, x), sub: 4 (over y, core).
Axes of the slice: x: 2, y: 2, z: 4, core: 2. Of those that a mesh axis runs over, the one named last changes fastest.
Arguments:
- first_half: float32 [1, 4096, 1024], P(None, ('seq', 'sub')), may hold values from -6 to 6
- second_half: float32 [1, 4096, 1024], P(None, ('seq', 'sub')), may hold values from -6 to 6
- grad_first: float32 [1, 4096, 1024], P(None, ('seq', 'sub')), may hold values from -6 to 6
- grad_second: float32 [1, 4096, 1024], P(None, ('seq', 'sub')), may hold values from -6 to 6
- attend_gain: bfloat16 [1, 1024], P(None, ('seq', 'sub')), may hold values from 0.5 to 1.5
- attend_shift: bfloat16 [1, 1024], P(None, ('seq', 'sub')), may hold values from -3 to 3
- query_key_weight: bfloat16 [1, 1024, 1024], P(None, ('seq', 'sub')), may hold values from -3 to 3
- value_projection_weight: bfloat16 [1, 1024, 1024], P(None, ('seq', 'sub')), may hold values from -0.1875 to 0.1875
- output_projection_weight: bfloat16 [1, 1024, 1024], P(None, ('seq', 'sub')), may hold values from -0.75 to 0.75
- feed_gain: bfloat16 [1, 1024], P(None, ('seq', 'sub')), may hold values from 0.5 to 1.5
- feed_shift: bfloat16 [1, 1024], P(None, ('seq', 'sub')), may hold values from -3 to 3
- upper_projection_weight: bfloat16 [1, 1024, 4096], P(None, ('seq', 'sub')), may hold values from -0.1875 to 0.1875
- upper_projection_bias: bfloat16 [1, 4096], P(None, ('seq', 'sub')), may hold values from -3 to 3
- lower_projection_weight: bfloat16 [1, 4096, 1024], P(None, ('seq', 'sub')), may hold values from -0.09375 to 0.09375
- lower_projection_bias: bfloat16 [1, 1024], P(None, ('seq', 'sub')), may hold values from -3 to 3
- sort_order: int32 [1, 4, 1, 4096], P(None, None, None, ('seq', 'sub')), may hold values from 0 to 4095, as said below
- sort_place: int32 [1, 4, 1, 4096], P(None, None, None, ('seq', 'sub')), may hold values from 0 to 4095, as said below
Outputs:
- first_out: float32 [1, 4096, 1024], P(None, ('seq', 'sub'))
- second_out: float32 [1, 4096, 1024], P(None, ('seq', 'sub'))
- first_grad: float32 [1, 4096, 1024], P(None, ('seq', 'sub'))
- second_grad: float32 [1, 4096, 1024], P(None, ('seq', 'sub'))
- attend_gain_grad: float32 [1, 1024], P(None, ('seq', 'sub'))
- attend_shift_grad: float32 [1, 1024], P(None, ('seq', 'sub'))
- shared_weight_grad: float32 [1, 1024, 1024], P(None, ('seq', 'sub'))
- value_weight_grad: float32 [1, 1024, 1024], P(None, ('seq', 'sub'))
- output_weight_grad: float32 [1, 1024, 1024], P(None, ('seq', 'sub'))
- feed_gain_grad: float32 [1, 1024], P(None, ('seq', 'sub'))
- feed_shift_grad: float32 [1, 1024], P(None, ('seq', 'sub'))
- up_weight_grad: float32 [1, 1024, 4096], P(None, ('seq', 'sub'))
- up_bias_grad: float32 [1, 4096], P(None, ('seq', 'sub'))
- down_weight_grad: float32 [1, 4096, 1024], P(None, ('seq', 'sub'))
- down_bias_grad: float32 [1, 1024], P(None, ('seq', 'sub'))
Inputs may be any that keep to these rules, and one draw needn't show every extreme that they name: For every layer, round and sequence, sort_place is a permutation of the places and sort_order is its inverse. Of the 128 tokens of a sequence that one device holds, at most 8 take places that another single device holds, in every round; in every round some pairs of devices have exactly 8. `sort_order`: the inverse of sort_place.
All inputs are finite; a program needn't handle non-finite values.
Results may differ from a plain program's by a relative error of at most 0.015.
Values may be sent and summed in bfloat16 or wider, within the bound.
A program may use at most 128 MiB of HBM per device.

v0:
```python
import jax
import jax.numpy as jnp
from jax import lax
from jax.sharding import PartitionSpec as P

HEADS = 8
HEAD_DIM = 128
BLOCK = 64


def from_behind(block, axis, distance):
    devices = range(lax.axis_size(axis))
    route = [((i - distance) % len(devices), i) for i in devices]
    return lax.ppermute(block, axis, route)


def layer_norm(value_vectors, scaling, shifts):
    center = jnp.mean(value_vectors, axis=-1, keepdims=True)
    offset = value_vectors - center
    spread = jnp.mean(offset * offset, axis=-1, keepdims=True)
    return offset * lax.rsqrt(spread + 1e-05) * scaling + shifts


def gelu_exact(value_vectors):
    return jax.nn.gelu(value_vectors, approximate=False)


def combine_rounds(outputs, totals):
    highest = jnp.max(totals, axis=0, keepdims=True)
    weights = jnp.exp(totals - highest)
    weights = weights / jnp.sum(weights, axis=0, keepdims=True)
    by_head = outputs.reshape(outputs.shape[:-1] + (totals.shape[-1], -1))
    return jnp.sum(weights[..., None] * by_head, axis=0).reshape(outputs.shape[1:])


def home_slots(places, row_count):
    target = places // row_count
    prior_state = (target[:, None, :] == target[:, :, None]) & (
        places[:, None, :] < places[:, :, None]
    )
    return (target, jnp.sum(prior_state.astype(jnp.int32), axis=2))


def sorted_slots(orders, row_count):
    source = orders // row_count
    ladder = jnp.arange(row_count, dtype=jnp.int32)
    prior_state = (source[:, None, :] == source[:, :, None]) & (
        ladder[None, None, :] < ladder[None, :, None]
    )
    return (source, jnp.sum(prior_state.astype(jnp.int32), axis=2))


def slot_lookup(owners, slot_index, devices, capacity):
    groups, row_count = owners.shape
    flat_index = owners * capacity + slot_index
    lookup = jnp.full((groups, devices * capacity), row_count, jnp.int32)
    filler = jnp.broadcast_to(jnp.arange(row_count, dtype=jnp.int32), (groups, row_count))
    lookup = lookup.at[jnp.arange(groups)[:, None], flat_index].set(filler)
    return jnp.transpose(lookup.reshape(groups, devices, capacity), (1, 0, 2))


def gather_slots(value_vectors, member, lookup):
    padding = jnp.zeros((value_vectors.shape[0], 1) + value_vectors.shape[2:], value_vectors.dtype)
    padded = jnp.concatenate([value_vectors, padding], axis=1)
    return padded[member[None, :, None], lookup]


def settle(received, owners, slot_index):
    return received[owners, jnp.arange(owners.shape[0])[:, None], slot_index]


def build_routes(orders, places, devices, capacity):
    rounds, sequences, row_count = orders.shape
    order_flat = orders.reshape(rounds * sequences, row_count)
    target, home_slot = home_slots(places.reshape(rounds * sequences, row_count), row_count)
    source, sorted_slot = sorted_slots(order_flat, row_count)
    home_lookup = slot_lookup(target, home_slot, devices, capacity)
    back_lookup = slot_lookup(source, sorted_slot, devices, capacity)
    return (target, home_slot, source, sorted_slot, home_lookup, back_lookup, order_flat)


def trade_rows(first_part, second_part):
    return (
        lax.all_to_all(first_part, ("seq", "sub"), split_axis=0, concat_axis=0, tiled=True),
        lax.all_to_all(second_part, ("seq", "sub"), split_axis=0, concat_axis=0, tiled=True),
    )


def trade_results(first_part, second_part):
    return (
        lax.all_to_all(first_part, ("seq", "sub"), split_axis=0, concat_axis=0, tiled=True),
        lax.all_to_all(second_part, ("seq", "sub"), split_axis=0, concat_axis=0, tiled=True),
    )


def window(rows_here, rows_left):
    groups = rows_here.shape[0]
    extended = jnp.concatenate([rows_left, rows_here], axis=1)
    extended = extended.reshape((groups, -1, BLOCK) + rows_here.shape[2:])
    return jnp.concatenate([extended[:, :-1], extended[:, 1:]], axis=2)


def score_parts(shared_rows, order_rows, halo_shared, halo_order):
    groups, row_count, features = shared_rows.shape
    blocks = row_count // BLOCK
    queries = shared_rows.reshape(groups, blocks, BLOCK, HEADS, HEAD_DIM)
    key_rows = window(shared_rows, halo_shared).reshape(groups, blocks, 2 * BLOCK, HEADS, HEAD_DIM)
    key_float = key_rows.astype(jnp.float32)
    mean_square = jnp.mean(key_float * key_float, axis=-1) + 1e-06
    key_scale = lax.rsqrt(mean_square) / HEAD_DIM
    raw_scores = jnp.einsum(
        "gcqhd,gckhd->gchqk", queries, key_rows, preferred_element_type=jnp.float32
    )
    query_pos = order_rows.reshape(groups, blocks, BLOCK)
    key_pos = window(order_rows, halo_order)
    is_later = (key_pos[:, :, None, :] > query_pos[:, :, :, None])[:, :, None]
    is_self = (key_pos[:, :, None, :] == query_pos[:, :, :, None])[:, :, None]
    scale_row = jnp.transpose(key_scale, (0, 1, 3, 2))[:, :, :, None, :]
    scores = jnp.where(
        is_later, -1000000000.0, jnp.where(is_self, -100000.0, raw_scores * scale_row)
    )
    highest = jnp.max(scores, axis=-1, keepdims=True)
    log_total = highest + jnp.log(jnp.sum(jnp.exp(scores - highest), axis=-1, keepdims=True))
    probability = jnp.exp(scores - log_total)
    return (
        queries,
        key_rows,
        key_float,
        mean_square,
        key_scale,
        scale_row,
        raw_scores,
        is_later | is_self,
        log_total,
        probability,
    )


def attend(shared_rows, value_rows, order_rows, halo):
    halo_shared, halo_value, halo_order = halo
    parts = score_parts(shared_rows, order_rows, halo_shared, halo_order)
    groups, row_count, features = shared_rows.shape
    value_keys = window(value_rows, halo_value).reshape(
        groups, row_count // BLOCK, 2 * BLOCK, HEADS, HEAD_DIM
    )
    mixed = jnp.einsum(
        "gchqk,gckhd->gcqhd",
        parts[9].astype(jnp.bfloat16),
        value_keys,
        preferred_element_type=jnp.float32,
    )
    log_total = jnp.transpose(parts[8][..., 0], (0, 1, 3, 2)).reshape(groups, row_count, HEADS)
    return (mixed.reshape(groups, row_count, features), log_total)


def fold_window(grads_window, groups, row_count, features):
    grads_window = grads_window.reshape(groups, row_count // BLOCK, 2 * BLOCK, features)
    empty = jnp.zeros((groups, 1, BLOCK, features), jnp.float32)
    extended = jnp.concatenate([grads_window[:, :, :BLOCK], empty], axis=1) + jnp.concatenate(
        [empty, grads_window[:, :, BLOCK:]], axis=1
    )
    return (extended[:, 1:].reshape(groups, row_count, features), extended[:, 0])


def attend_back(shared_rows, value_rows, order_rows, halo, grad_out, grad_total):
    halo_shared, halo_value, halo_order = halo
    (
        queries,
        key_rows,
        key_float,
        mean_square,
        key_scale,
        scale_row,
        raw_scores,
        masked,
        log_total,
        probability,
    ) = score_parts(shared_rows, order_rows, halo_shared, halo_order)
    groups, row_count, features = shared_rows.shape
    blocks = row_count // BLOCK
    value_keys = window(value_rows, halo_value).reshape(groups, blocks, 2 * BLOCK, HEADS, HEAD_DIM)
    prob_low = probability.astype(jnp.bfloat16)
    grad_heads = grad_out.reshape(groups, blocks, BLOCK, HEADS, HEAD_DIM)
    grad_log = jnp.transpose(
        grad_total.astype(jnp.float32).reshape(groups, blocks, BLOCK, HEADS), (0, 1, 3, 2)
    )[..., None]
    grad_prob = jnp.einsum(
        "gcqhd,gckhd->gchqk", grad_heads, value_keys, preferred_element_type=jnp.float32
    )
    inner = jnp.sum(probability * grad_prob, axis=-1, keepdims=True)
    grad_score = jnp.where(masked, 0.0, probability * (grad_prob - inner + grad_log))
    grad_scale = jnp.transpose(jnp.sum(grad_score * raw_scores, axis=3), (0, 1, 3, 2))
    grad_raw = (grad_score * scale_row).astype(jnp.bfloat16)
    grad_query = jnp.einsum(
        "gchqk,gckhd->gcqhd", grad_raw, key_rows, preferred_element_type=jnp.float32
    )
    grad_key = jnp.einsum(
        "gchqk,gcqhd->gckhd", grad_raw, queries, preferred_element_type=jnp.float32
    )
    grad_key = grad_key - (grad_scale * key_scale / mean_square)[..., None] * key_float / HEAD_DIM
    grad_value = jnp.einsum(
        "gchqk,gcqhd->gckhd", prob_low, grad_heads, preferred_element_type=jnp.float32
    )
    key_home, key_left = fold_window(grad_key, groups, row_count, features)
    value_home, value_left = fold_window(grad_value, groups, row_count, features)
    back_key, back_value = from_behind((key_left, value_left), ("seq", "sub"), -1)
    grad_shared = grad_query.reshape(groups, row_count, features) + key_home
    grad_shared = grad_shared.at[:, row_count - BLOCK :].add(back_key)
    grad_values = value_home.at[:, row_count - BLOCK :].add(back_value)
    return (grad_shared, grad_values)


def sorted_attention(shared_query_key, value_vectors, routes):
    target, home_slot, source, sorted_slot, home_lookup, back_lookup, order_flat = routes
    groups = target.shape[0]
    member = jnp.arange(groups) % shared_query_key.shape[0]
    got_shared, got_values = trade_rows(
        gather_slots(shared_query_key, member, home_lookup),
        gather_slots(value_vectors, member, home_lookup),
    )
    shared_rows = settle(got_shared, source, sorted_slot)
    value_rows = settle(got_values, source, sorted_slot)
    halo = from_behind(
        (shared_rows[:, -BLOCK:], value_rows[:, -BLOCK:], order_flat[:, -BLOCK:]), ("seq", "sub"), 1
    )
    mixed, log_total = attend(shared_rows, value_rows, order_flat, halo)
    all_groups = jnp.arange(groups)
    got_mixed, got_total = trade_results(
        gather_slots(mixed, all_groups, back_lookup),
        gather_slots(log_total, all_groups, back_lookup),
    )
    return (
        settle(got_mixed, target, home_slot),
        settle(got_total, target, home_slot),
        (shared_rows, value_rows, halo),
    )


def round_outputs(normalized_input, query_key_weight, value_projection_weight, routes, rounds):
    shared_query_key = jnp.einsum(
        "srd,de->sre", normalized_input, query_key_weight, preferred_element_type=jnp.float32
    ).astype(jnp.bfloat16)
    value_vectors = jnp.einsum(
        "srd,de->sre", normalized_input, value_projection_weight, preferred_element_type=jnp.float32
    ).astype(jnp.bfloat16)
    mixed, log_total, kept = sorted_attention(shared_query_key, value_vectors, routes)
    sequences, row_count, features = normalized_input.shape
    outputs = mixed.reshape(rounds, sequences, row_count, features)
    totals = log_total.reshape(rounds, sequences, row_count, HEADS)
    return (shared_query_key, value_vectors, outputs, totals, kept)


def collect(weight_stack, layer_index):
    (
        attend_gain,
        attend_shift,
        query_key_weight,
        value_projection_weight,
        output_projection_weight,
        feed_gain,
        feed_shift,
        upper_projection_weight,
        upper_projection_bias,
        lower_projection_weight,
        lower_projection_bias,
    ) = tuple((shard_piece[layer_index] for shard_piece in weight_stack))
    return (
        lax.all_gather(attend_gain, ("seq", "sub"), axis=0, tiled=True),
        lax.all_gather(attend_shift, ("seq", "sub"), axis=0, tiled=True),
        lax.all_gather(query_key_weight, ("seq", "sub"), axis=0, tiled=True),
        lax.all_gather(value_projection_weight, ("seq", "sub"), axis=0, tiled=True),
        lax.all_gather(output_projection_weight, ("seq", "sub"), axis=0, tiled=True),
        lax.all_gather(feed_gain, ("seq", "sub"), axis=0, tiled=True),
        lax.all_gather(feed_shift, ("seq", "sub"), axis=0, tiled=True),
        lax.all_gather(upper_projection_weight, ("seq", "sub"), axis=0, tiled=True),
        lax.all_gather(upper_projection_bias, ("seq", "sub"), axis=0, tiled=True),
        lax.all_gather(lower_projection_weight, ("seq", "sub"), axis=0, tiled=True),
        lax.all_gather(lower_projection_bias, ("seq", "sub"), axis=0, tiled=True),
    )


def spread_grads(level_grads):
    (
        attend_gain,
        attend_shift,
        query_key_weight,
        value_projection_weight,
        output_projection_weight,
        feed_gain,
        feed_shift,
        upper_projection_weight,
        upper_projection_bias,
        lower_projection_weight,
        lower_projection_bias,
    ) = level_grads
    return (
        lax.psum_scatter(attend_gain, ("seq", "sub"), scatter_dimension=0, tiled=True),
        lax.psum_scatter(attend_shift, ("seq", "sub"), scatter_dimension=0, tiled=True),
        lax.psum_scatter(query_key_weight, ("seq", "sub"), scatter_dimension=0, tiled=True),
        lax.psum_scatter(value_projection_weight, ("seq", "sub"), scatter_dimension=0, tiled=True),
        lax.psum_scatter(output_projection_weight, ("seq", "sub"), scatter_dimension=0, tiled=True),
        lax.psum_scatter(feed_gain, ("seq", "sub"), scatter_dimension=0, tiled=True),
        lax.psum_scatter(feed_shift, ("seq", "sub"), scatter_dimension=0, tiled=True),
        lax.psum_scatter(upper_projection_weight, ("seq", "sub"), scatter_dimension=0, tiled=True),
        lax.psum_scatter(upper_projection_bias, ("seq", "sub"), scatter_dimension=0, tiled=True),
        lax.psum_scatter(lower_projection_weight, ("seq", "sub"), scatter_dimension=0, tiled=True),
        lax.psum_scatter(lower_projection_bias, ("seq", "sub"), scatter_dimension=0, tiled=True),
    )


def layer_forward(first_stream_state, second_stream_state, params, routes, rounds):
    (
        attend_gain,
        attend_shift,
        query_key_weight,
        value_projection_weight,
        output_projection_weight,
        feed_gain,
        feed_shift,
        upper_projection_weight,
        upper_projection_bias,
        lower_projection_weight,
        lower_projection_bias,
    ) = params
    normalized_input = layer_norm(
        second_stream_state, attend_gain.astype(jnp.float32), attend_shift.astype(jnp.float32)
    ).astype(jnp.bfloat16)
    shared_query_key, value_vectors, outputs, totals, kept = round_outputs(
        normalized_input, query_key_weight, value_projection_weight, routes, rounds
    )
    attention_result = combine_rounds(outputs, totals).astype(jnp.bfloat16)
    first_stream_state = first_stream_state + jnp.einsum(
        "srd,de->sre",
        attention_result,
        output_projection_weight,
        preferred_element_type=jnp.float32,
    )
    feed_forward_input = layer_norm(
        first_stream_state, feed_gain.astype(jnp.float32), feed_shift.astype(jnp.float32)
    ).astype(jnp.bfloat16)
    prior_state = jnp.einsum(
        "srd,df->srf",
        feed_forward_input,
        upper_projection_weight,
        preferred_element_type=jnp.float32,
    ) + upper_projection_bias.astype(jnp.float32)
    hidden_activation = gelu_exact(prior_state).astype(jnp.bfloat16)
    feed_out = jnp.einsum(
        "srf,fd->srd",
        hidden_activation,
        lower_projection_weight,
        preferred_element_type=jnp.float32,
    ) + lower_projection_bias.astype(jnp.float32)
    return (first_stream_state, second_stream_state + feed_out)


def layer_back(top_one, top_two, grad_one, grad_two, params, routes, rounds):
    (
        attend_gain,
        attend_shift,
        query_key_weight,
        value_projection_weight,
        output_projection_weight,
        feed_gain,
        feed_shift,
        upper_projection_weight,
        upper_projection_bias,
        lower_projection_weight,
        lower_projection_bias,
    ) = params
    feed_norm, feed_pull = jax.vjp(
        layer_norm, top_one, feed_gain.astype(jnp.float32), feed_shift.astype(jnp.float32)
    )
    feed_forward_input = feed_norm.astype(jnp.bfloat16)
    prior_state = jnp.einsum(
        "srd,df->srf",
        feed_forward_input,
        upper_projection_weight,
        preferred_element_type=jnp.float32,
    ) + upper_projection_bias.astype(jnp.float32)
    hidden_activation, active_pull = jax.vjp(gelu_exact, prior_state)
    active_low = hidden_activation.astype(jnp.bfloat16)
    feed_out = jnp.einsum(
        "srf,fd->srd", active_low, lower_projection_weight, preferred_element_type=jnp.float32
    ) + lower_projection_bias.astype(jnp.float32)
    bottom_two = top_two - feed_out
    feed_grad = grad_two.astype(jnp.bfloat16)
    down_weight_grad = jnp.einsum(
        "srf,srd->fd", active_low, feed_grad, preferred_element_type=jnp.float32
    )
    down_bias_grad = jnp.sum(feed_grad.astype(jnp.float32), axis=(0, 1))
    active_grad = jnp.einsum(
        "srd,fd->srf", feed_grad, lower_projection_weight, preferred_element_type=jnp.float32
    )
    before_grad = active_pull(active_grad)[0].astype(jnp.bfloat16)
    up_weight_grad = jnp.einsum(
        "srd,srf->df", feed_forward_input, before_grad, preferred_element_type=jnp.float32
    )
    up_bias_grad = jnp.sum(before_grad.astype(jnp.float32), axis=(0, 1))
    norm_grad = jnp.einsum(
        "srf,df->srd", before_grad, upper_projection_weight, preferred_element_type=jnp.float32
    )
    one_part, feed_gain_grad, feed_shift_grad = feed_pull(norm_grad)
    total_one = grad_one + one_part
    attend_norm, attend_pull = jax.vjp(
        layer_norm, bottom_two, attend_gain.astype(jnp.float32), attend_shift.astype(jnp.float32)
    )
    normalized_input = attend_norm.astype(jnp.bfloat16)
    shared_query_key, value_vectors, outputs, totals, kept = round_outputs(
        normalized_input, query_key_weight, value_projection_weight, routes, rounds
    )
    attention_result, combine_pull = jax.vjp(combine_rounds, outputs, totals)
    attended_low = attention_result.astype(jnp.bfloat16)
    bottom_one = top_one - jnp.einsum(
        "srd,de->sre", attended_low, output_projection_weight, preferred_element_type=jnp.float32
    )
    out_grad = total_one.astype(jnp.bfloat16)
    output_weight_grad = jnp.einsum(
        "srd,sre->de", attended_low, out_grad, preferred_element_type=jnp.float32
    )
    attended_grad = jnp.einsum(
        "sre,de->srd", out_grad, output_projection_weight, preferred_element_type=jnp.float32
    )
    outputs_grad, totals_grad = combine_pull(attended_grad)
    target, home_slot, source, sorted_slot, home_lookup, back_lookup, order_flat = routes
    sequences, row_count, features = top_one.shape
    groups = rounds * sequences
    all_groups = jnp.arange(groups)
    outputs_low = outputs_grad.astype(jnp.bfloat16).reshape(groups, row_count, features)
    totals_low = totals_grad.astype(jnp.bfloat16).reshape(groups, row_count, HEADS)
    got_out, got_total = trade_rows(
        gather_slots(outputs_low, all_groups, home_lookup),
        gather_slots(totals_low, all_groups, home_lookup),
    )
    shared_rows, value_rows, halo = kept
    grad_shared, grad_values = attend_back(
        shared_rows,
        value_rows,
        order_flat,
        halo,
        settle(got_out, source, sorted_slot),
        settle(got_total, source, sorted_slot),
    )
    home_shared, home_values = trade_rows(
        gather_slots(grad_shared.astype(jnp.bfloat16), all_groups, back_lookup),
        gather_slots(grad_values.astype(jnp.bfloat16), all_groups, back_lookup),
    )
    shared_grad = jnp.sum(
        settle(home_shared, target, home_slot)
        .astype(jnp.float32)
        .reshape(rounds, sequences, row_count, features),
        axis=0,
    ).astype(jnp.bfloat16)
    values_grad = jnp.sum(
        settle(home_values, target, home_slot)
        .astype(jnp.float32)
        .reshape(rounds, sequences, row_count, features),
        axis=0,
    ).astype(jnp.bfloat16)
    shared_weight_grad = jnp.einsum(
        "srd,sre->de", normalized_input, shared_grad, preferred_element_type=jnp.float32
    )
    value_weight_grad = jnp.einsum(
        "srd,sre->de", normalized_input, values_grad, preferred_element_type=jnp.float32
    )
    normed_grad = jnp.einsum(
        "sre,de->srd", shared_grad, query_key_weight, preferred_element_type=jnp.float32
    ) + jnp.einsum(
        "sre,de->srd", values_grad, value_projection_weight, preferred_element_type=jnp.float32
    )
    two_part, attend_gain_grad, attend_shift_grad = attend_pull(normed_grad)
    total_two = grad_two + two_part
    level_grads = (
        attend_gain_grad,
        attend_shift_grad,
        shared_weight_grad,
        value_weight_grad,
        output_weight_grad,
        feed_gain_grad,
        feed_shift_grad,
        up_weight_grad,
        up_bias_grad,
        down_weight_grad,
        down_bias_grad,
    )
    return (bottom_one, bottom_two, total_one, total_two, level_grads)


def on_device(
    first_half,
    second_half,
    grad_first,
    grad_second,
    attend_gain,
    attend_shift,
    query_key_weight,
    value_projection_weight,
    output_projection_weight,
    feed_gain,
    feed_shift,
    upper_projection_weight,
    upper_projection_bias,
    lower_projection_weight,
    lower_projection_bias,
    sort_order,
    sort_place,
):
    weight_stack = (
        attend_gain,
        attend_shift,
        query_key_weight,
        value_projection_weight,
        output_projection_weight,
        feed_gain,
        feed_shift,
        upper_projection_weight,
        upper_projection_bias,
        lower_projection_weight,
        lower_projection_bias,
    )
    devices = lax.axis_size(("seq", "sub"))
    layers = sort_order.shape[0]
    rounds = sort_order.shape[1]
    row_count = first_half.shape[1]
    capacity = 2 * max(1, row_count // devices)
    first_stream_state, second_stream_state = (first_half, second_half)
    layer_index = 0
    params = collect(weight_stack, layer_index)
    routes = build_routes(sort_order[layer_index], sort_place[layer_index], devices, capacity)
    first_stream_state, second_stream_state = layer_forward(
        first_stream_state, second_stream_state, params, routes, rounds
    )
    first_out, second_out = (first_stream_state, second_stream_state)
    grad_one, grad_two = (grad_first, grad_second)
    gradients = []
    for layer_index in reversed(range(layers)):
        params = collect(weight_stack, layer_index)
        routes = build_routes(sort_order[layer_index], sort_place[layer_index], devices, capacity)
        first_stream_state, second_stream_state, grad_one, grad_two, level_grads = layer_back(
            first_stream_state, second_stream_state, grad_one, grad_two, params, routes, rounds
        )
        gradients.insert(0, spread_grads(level_grads))
    stacked = tuple(
        (
            jnp.stack([level_entry[member_index] for level_entry in gradients])
            for member_index in range(len(weight_stack))
        )
    )
    return (first_out, second_out, grad_one, grad_two) + stacked


def solution(mesh):
    return jax.shard_map(
        on_device,
        mesh=mesh,
        in_specs=(
            P(None, ("seq", "sub"), None),
            P(None, ("seq", "sub"), None),
            P(None, ("seq", "sub"), None),
            P(None, ("seq", "sub"), None),
            P(None, ("seq", "sub")),
            P(None, ("seq", "sub")),
            P(None, ("seq", "sub"), None),
            P(None, ("seq", "sub"), None),
            P(None, ("seq", "sub"), None),
            P(None, ("seq", "sub")),
            P(None, ("seq", "sub")),
            P(None, ("seq", "sub"), None),
            P(None, ("seq", "sub")),
            P(None, ("seq", "sub"), None),
            P(None, ("seq", "sub")),
            P(None, None, None, ("seq", "sub")),
            P(None, None, None, ("seq", "sub")),
        ),
        out_specs=(
            P(None, ("seq", "sub"), None),
            P(None, ("seq", "sub"), None),
            P(None, ("seq", "sub"), None),
            P(None, ("seq", "sub"), None),
            P(None, ("seq", "sub")),
            P(None, ("seq", "sub")),
            P(None, ("seq", "sub"), None),
            P(None, ("seq", "sub"), None),
            P(None, ("seq", "sub"), None),
            P(None, ("seq", "sub")),
            P(None, ("seq", "sub")),
            P(None, ("seq", "sub"), None),
            P(None, ("seq", "sub")),
            P(None, ("seq", "sub"), None),
            P(None, ("seq", "sub")),
        ),
        check_vma=False,
    )
```

profile of v0, /device:TPU:0, one launch (start us, length us, event | category | flops | bytes accessed | tf_op | source)
XLA Modules:
  0.0 1707.6 jit_solution(17973820214298192796)
XLA Ops:
  14.2 42.3 %all-reduce.29 = (bf16[1024]{0:T(1024)(128)(2,1)S(1)}, bf16[1024]{0:T(1024)(128)(2,1)S(1)}, bf16[1024]{0:T(1024)(128)(2,1)S(1)}, bf16[1024]{0:T(1024)(128)(2,1)S(1)}, bf16[1024]{0:T(1024)(128)(2,1)S(1)}) all-reduce(bf16[1024]{0:T(1024)(128)(2,1)S(1)} %dynamic-update-slice.7, ...), channel_id=3, replica_groups=mesh['seq'=8,'sub'=4] {'seq','sub'}, use_global_device_ids=true, to_apply=%add.18 | all-reduce | flops 5120 | bytes 20480
  58.9 24.7 %scatter_fusion = s32[4,256]{1,0:T(4,128)S(1)} fusion(s32[4,256]{1,0:T(4,128)S(1)} %broadcast.913.clone, s32[512]{0:T(512)S(1)} %get-tuple-element.89, s32[512]{0:T(512)S(1)} %iota_bitcast_fusion), kind=kCustom, calls=%fused_computation.24 | custom fusion | bytes 10240 | tf_op jit(solution)/shard_map/scatter | solution.py:58
  86.5 14.1 gather_fusion
  105.0 30.2 %all-gather.19.cloned.1.call-done = bf16[1,1024,1024]{2,1,0:T(8,128)(2,1)} async-done(((bf16[1,32,1024]{2,1,0:T(8,128)(2,1)}), bf16[1,1024,1024]{2,1,0:T(8,128)(2,1)}) %all-gather.19.cloned.1.call-update) | async-done | bytes 2097168 | tf_op jit(solution)/shard_map/all_gather | solution.py:271
  137.3 14.1 gather_fusion.4
  151.4 9.5 all-to-all-done
  167.5 24.7 %scatter_fusion.1 = s32[4,256]{1,0:T(4,128)S(1)} fusion(s32[4,256]{1,0:T(4,128)S(1)} %broadcast.913.clone.1, s32[512]{0:T(512)S(1)} %get-tuple-element.90, s32[512]{0:T(512)S(1)} %iota_bitcast_fusion), kind=kCustom, calls=%fused_computation.25 | custom fusion | bytes 10240 | tf_op jit(solution)/shard_map/scatter | solution.py:58
  193.8 19.7 %collective-permute-done = s32[4,64]{1,0:T(4,128)S(1)} collective-permute-done((s32[4,64]{1,0:T(4,128)S(1)}, s32[4,64]{1,0:T(4,128)S(1)}, u32[]{:S(2)}, u32[]{:S(2)}) %collective-permute-start) | collective-permute-done | bytes 1056 | tf_op jit(solution)/shard_map/ppermute | solution.py:14
  213.6 8.5 gather_fusion.1
  227.3 7.1 gather_fusion.5
  250.2 9.4 gather_fusion.2
  261.6 20.4 %all-to-all-start.1 = ((f32[32,1,256]{2,1,0:T(1,128)}), f32[32,1,256]{2,1,0:T(1,128)S(1)}, u32[]{:S(2)}, u32[]{:S(2)}) async-start(f32[32,1,256]{2,1,0:T(1,128)} %reshape.1308), calls=%async_computation.1 | async-start | bytes 65536 | tf_op jit(solution)/shard_map/all_to_all | solution.py:92
  297.3 15.1 gather_fusion.6
  318.5 133.7 %all-gather.8 = bf16[1,4096]{1,0:T(2,128)(2,1)S(1)} all-gather(bf16[1,128]{1,0:T(2,128)(2,1)S(1)} %copy-done.59), channel_id=10, replica_groups=mesh['seq'=8,'sub'=4] {'seq','sub'}, dimensions={1}, use_global_device_ids=true | all-gather | bytes 8448 | tf_op jit(solution)/shard_map/all_gather | solution.py:276
  457.3 6.4 gather_fusion.7
  467.7 6.1 fusion.9
  473.8 10.4 fusion.180
  485.1 14.1 gather_fusion.8
  499.2 18.6 %all-to-all-start.4 = ((bf16[32,4,8,1024]{3,2,1,0:T(8,128)(2,1)}), bf16[32,4,8,1024]{3,2,1,0:T(8,128)(2,1)S(1)}, u32[]{:S(2)}, u32[]{:S(2)}) async-start(bf16[32,4,8,1024]{3,2,1,0:T(8,128)(2,1)} %bitcast.377), calls=%async_computation.4 | async-start | bytes 4194304 | tf_op jit(solution)/shard_map/all_to_all | solution.py:84
  519.8 14.1 gather_fusion.14
  533.9 32.6 %all-to-all-done.4 = bf16[32,4,8,1024]{3,2,1,0:T(8,128)(2,1)S(1)} async-done(((bf16[32,4,8,1024]{3,2,1,0:T(8,128)(2,1)}), bf16[32,4,8,1024]{3,2,1,0:T(8,128)(2,1)S(1)}, u32[]{:S(2)}, u32[]{:S(2)}) %all-to-all-start.4) | async-done | bytes 2097184 | tf_op jit(solution)/shard_map/all_to_all | solution.py:84
  571.2 7.1 gather_fusion.9
  583.0 38.1 %all-to-all-done.7 = bf16[32,4,8,1024]{3,2,1,0:T(8,128)(2,1)} async-done(((bf16[32,4,8,1024]{3,2,1,0:T(8,128)(2,1)}), bf16[32,4,8,1024]{3,2,1,0:T(8,128)(2,1)}, u32[]{:S(2)}, u32[]{:S(2)}) %all-to-all-start.7) | async-done | bytes 2097184 | tf_op jit(solution)/shard_map/all_to_all | solution.py:85
  621.1 6.9 gather_fusion.15
  653.4 9.4 gather_fusion.10
  676.7 15.1 gather_fusion.16
  691.8 6.1 all-to-all-start.8
  698.2 10.4 convert_reduce_fusion
  708.5 6.8 fusion.98
  724.5 67.8 %all-to-all-done.8 = f32[32,4,8,1024]{3,2,1,0:T(8,128)} async-done(((f32[32,4,8,1024]{3,2,1,0:T(8,128)}), f32[32,4,8,1024]{3,2,1,0:T(8,128)}, u32[]{:S(2)}, u32[]{:S(2)}) %all-to-all-start.8) | async-done | bytes 4194336 | tf_op jit(solution)/shard_map/all_to_all | solution.py:91
  792.3 6.6 gather_fusion.17
  819.6 15.2 gather_fusion.12
  852.1 43.3 %all-to-all-done.6 = bf16[32,4,8,1024]{3,2,1,0:T(8,128)(2,1)S(1)} async-done(((bf16[32,4,8,1024]{3,2,1,0:T(8,128)(2,1)}), bf16[32,4,8,1024]{3,2,1,0:T(8,128)(2,1)S(1)}, u32[]{:S(2)}, u32[]{:S(2)}) %all-to-all-start.6) | async-done | bytes 2097184 | tf_op jit(solution)/shard_map/all_to_all | solution.py:84
  895.4 7.1 gather_fusion.13
  906.1 16.4 multiply_reduce_fusion.1
  961.5 15.2 gather_fusion.20
  976.8 54.7 %all_to_all.60 = bf16[32,4,8,1024]{3,2,1,0:T(8,128)(2,1)S(1)} all-to-all(bf16[32,4,8,1024]{3,2,1,0:T(8,128)(2,1)} %bitcast.382), channel_id=1, replica_groups=mesh['seq'=8,'sub'=4] {'seq','sub'}, dimensions={0} | all-to-all | bytes 4194304 | tf_op jit(solution)/shard_map/all_to_all | solution.py:84
  1031.5 7.1 gather_fusion.21
  1065.8 13.2 collective-permute-done.6
  1080.4 15.2 gather_fusion.22
  1095.6 62.5 %all_to_all.61 = bf16[32,4,8,1024]{3,2,1,0:T(8,128)(2,1)S(1)} all-to-all(bf16[32,4,8,1024]{3,2,1,0:T(8,128)(2,1)} %bitcast.379), channel_id=1, replica_groups=mesh['seq'=8,'sub'=4] {'seq','sub'}, dimensions={0} | all-to-all | bytes 4194304 | tf_op jit(solution)/shard_map/all_to_all | solution.py:85
  1158.2 7.1 gather_fusion.23
  1171.1 9.7 fusion.114
  1182.0 8.2 fusion.173
  1196.8 39.4 %all-reduce.28 = (f32[1024]{0:T(1024)S(1)}, f32[1024]{0:T(1024)S(1)}, f32[1024]{0:T(1024)S(1)}, f32[1024]{0:T(1024)S(1)}, f32[4096]{0:T(1024)S(1)}, /*index=5*/f32[1024]{0:T(1024)S(1)}) all-reduce(f32[1024]{0:T(1024)S(1)} %get-tuple-element.41, f32[1024]{0:T(1024)S(1)} %reduce_sum.414, ...), channel_id=13, replica_groups=mesh['seq'=8,'sub'=4] {'seq','sub'}, use_global_device_ids=true, to_apply=%region_34.35.clone | all-reduce | flops 9216 | bytes 73728
  1238.6 92.6 %reduce-scatter.8.cloned.1.call-done = f32[32,1024]{1,0:T(8,128)} async-done(((f32[1024,1024]{1,0:T(8,128)}), f32[32,1024]{1,0:T(8,128)}) %reduce-scatter.8.cloned.1.call-update) | async-done | bytes 131088 | tf_op jit(solution)/shard_map/reduce_scatter | solution.py:300
  1331.2 181.8 %reduce-scatter.14.cloned.1.call-done = f32[128,1024]{1,0:T(8,128)} async-done(((f32[4096,1024]{1,0:T(8,128)}), f32[128,1024]{1,0:T(8,128)}) %reduce-scatter.14.cloned.1.call-update) | async-done | bytes 524304 | tf_op jit(solution)/shard_map/reduce_scatter | solution.py:306
  1513.0 187.3 %reduce-scatter.12.cloned.1.call-done = f32[32,4096]{1,0:T(8,128)} async-done(((f32[1024,4096]{1,0:T(8,128)}), f32[32,4096]{1,0:T(8,128)}) %reduce-scatter.12.cloned.1.call-update) | async-done | bytes 524304 | tf_op jit(solution)/shard_map/reduce_scatter | solution.py:304
  (376 shorter events, 265.4 us)
Async XLA Ops:
  7.2 77.1 %all-gather.17.cloned.1.call-start = ((), (), s32[]{:S(2)}) async-start(), calls=%async_computation.22 | async-start | bytes 2162688 | tf_op jit(solution)/shard_map/all_gather | solution.py:270
  7.9 127.3 %all-gather.19.cloned.1.call-start = ((), (), s32[]{:S(2)}) async-start(), calls=%async_computation.23 | async-start | bytes 2162688 | tf_op jit(solution)/shard_map/all_gather | solution.py:271
  8.7 456.4 %all-gather.21.cloned.1.call-start = ((), (), s32[]{:S(2)}) async-start(), calls=%async_computation.24 | async-start | bytes 2162688 | tf_op jit(solution)/shard_map/all_gather | solution.py:272
  9.4 458.2 %all-gather.23.cloned.1.call-start = ((), (), s32[]{:S(2)}) async-start(), calls=%async_computation.25 | async-start | bytes 8650752 | tf_op jit(solution)/shard_map/all_gather | solution.py:275
  56.5 427.9 %copy-start.50 = (f32[1024]{0:T(1024)}, f32[1024]{0:T(1024)S(1)}, u32[]{:S(2)}) copy-start(f32[1024]{0:T(1024)S(1)} %convert_element_type.230) | copy-start | bytes 12292
  58.9 25.0 %copy-start.23 = (f32[1,128,1024]{2,1,0:T(8,128)S(1)}, f32[1,128,1024]{2,1,0:T(8,128)}, u32[]{:S(2)}) copy-start(f32[1,128,1024]{2,1,0:T(8,128)} %param.22) | copy-start | bytes 1572868
  100.6 60.3 %all-to-all-start = ((bf16[32,4,8,1024]{3,2,1,0:T(8,128)(2,1)}), bf16[32,4,8,1024]{3,2,1,0:T(8,128)(2,1)S(1)}, u32[]{:S(2)}, u32[]{:S(2)}) async-start(bf16[32,4,8,1024]{3,2,1,0:T(8,128)(2,1)} %bitcast.376), calls=%async_computation | async-start | bytes 4194304 | tf_op jit(solution)/shard_map/all_to_all | solution.py:84
  162.2 65.1 %all-to-all-start.2 = ((bf16[32,4,8,1024]{3,2,1,0:T(8,128)(2,1)}), bf16[32,4,8,1024]{3,2,1,0:T(8,128)(2,1)S(1)}, u32[]{:S(2)}, u32[]{:S(2)}) async-start(bf16[32,4,8,1024]{3,2,1,0:T(8,128)(2,1)} %bitcast.373), calls=%async_computation.2 | async-start | bytes 4194304 | tf_op jit(solution)/shard_map/all_to_all | solution.py:85
  166.3 307.5 %all-gather.25.cloned.1.call-start = ((), (), s32[]{:S(2)}) async-start(), calls=%async_computation.26 | async-start | bytes 8650752 | tf_op jit(solution)/shard_map/all_gather | solution.py:277
  167.0 46.4 %collective-permute-start = (s32[4,64]{1,0:T(4,128)S(1)}, s32[4,64]{1,0:T(4,128)S(1)}, u32[]{:S(2)}, u32[]{:S(2)}) collective-permute-start(s32[4,64]{1,0:T(4,128)S(1)} %slice.126), channel_id=1, source_target_pairs={{31,0},{0,1},{1,2},{2,3},{3,4},{4,5},{5,6},{6,7},{7,8},{8,9},{9,10... | collective-permute-start | bytes 3080 | tf_op jit(solution)/shard_map/ppermute | solution.py:14
  223.1 13.2 collective-permute-start.1
  224.3 680.8 %copy-start.36 = (pred[4,2,64,128]{3,2,1,0:T(8,128)(4,1)}, pred[4,2,64,128]{3,2,1,0:T(8,128)(4,1)S(1)}, u32[]{:S(2)}) copy-start(pred[4,2,64,128]{3,2,1,0:T(8,128)(4,1)S(1)} %get-tuple-element.85) | copy-start | bytes 196612
  236.3 45.7 %collective-permute-start.2 = (bf16[4,64,1024]{2,1,0:T(8,128)(2,1)}, bf16[4,64,1024]{2,1,0:T(8,128)(2,1)}, u32[]{:S(2)}, u32[]{:S(2)}) collective-permute-start(bf16[4,64,1024]{2,1,0:T(8,128)(2,1)} %slice.220), channel_id=1, source_target_pairs={{31,0},{0,1},{1,2},{2,3},{3,4},{4,5},{5,6},{6,7},{7,8},{8,9},{9,10... | collective-permute-start | bytes 1572872 | tf_op jit(solution)/shard_map/ppermute | solution.py:14
  261.6 50.8 %all-to-all-start.1 = ((f32[32,1,256]{2,1,0:T(1,128)}), f32[32,1,256]{2,1,0:T(1,128)S(1)}, u32[]{:S(2)}, u32[]{:S(2)}) async-start(f32[32,1,256]{2,1,0:T(1,128)} %reshape.1308), calls=%async_computation.1 | async-start | bytes 65536 | tf_op jit(solution)/shard_map/all_to_all | solution.py:92
  312.4 144.9 %all-to-all-start.3 = ((f32[32,4,8,1024]{3,2,1,0:T(8,128)}), f32[32,4,8,1024]{3,2,1,0:T(8,128)}, u32[]{:S(2)}, u32[]{:S(2)}) async-start(f32[32,4,8,1024]{3,2,1,0:T(8,128)} %bitcast.359), calls=%async_computation.3 | async-start | bytes 8388608 | tf_op jit(solution)/shard_map/all_to_all | solution.py:91
  318.5 149.1 %copy-start.48 = (f32[1024]{0:T(1024)}, f32[1024]{0:T(1024)S(1)}, u32[]{:S(2)}) copy-start(f32[1024]{0:T(1024)S(1)} %convert_element_type.233) | copy-start | bytes 12292
  467.4 713.7 %copy-start.5 = (f32[1,128,1024]{2,1,0:T(8,128)}, f32[1,128,1024]{2,1,0:T(8,128)S(1)}, u32[]{:S(2)}) copy-start(f32[1,128,1024]{2,1,0:T(8,128)S(1)} %get-tuple-element.95) | copy-start | bytes 1572868
  467.6 6.2 copy-start.62
  473.8 10.8 copy-start.11
  484.3 14.8 copy-start.60
  484.4 14.8 copy-start.57
  499.2 67.4 %all-to-all-start.4 = ((bf16[32,4,8,1024]{3,2,1,0:T(8,128)(2,1)}), bf16[32,4,8,1024]{3,2,1,0:T(8,128)(2,1)S(1)}, u32[]{:S(2)}, u32[]{:S(2)}) async-start(bf16[32,4,8,1024]{3,2,1,0:T(8,128)(2,1)} %bitcast.377), calls=%async_computation.4 | async-start | bytes 4194304 | tf_op jit(solution)/shard_map/all_to_all | solution.py:84
  566.5 54.5 %all-to-all-start.7 = ((bf16[32,4,8,1024]{3,2,1,0:T(8,128)(2,1)}), bf16[32,4,8,1024]{3,2,1,0:T(8,128)(2,1)}, u32[]{:S(2)}, u32[]{:S(2)}) async-start(bf16[32,4,8,1024]{3,2,1,0:T(8,128)(2,1)} %bitcast.375), calls=%async_computation.7 | async-start | bytes 4194304 | tf_op jit(solution)/shard_map/all_to_all | solution.py:85
  580.1 48.8 %collective-permute-start.3 = (bf16[4,64,1024]{2,1,0:T(8,128)(2,1)}, bf16[4,64,1024]{2,1,0:T(8,128)(2,1)}, u32[]{:S(2)}, u32[]{:S(2)}) collective-permute-start(bf16[4,64,1024]{2,1,0:T(8,128)(2,1)} %slice.223), channel_id=1, source_target_pairs={{31,0},{0,1},{1,2},{2,3},{3,4},{4,5},{5,6},{6,7},{7,8},{8,9},{9,10... | collective-permute-start | bytes 1572872 | tf_op jit(solution)/shard_map/ppermute | solution.py:14
  583.0 46.0 %copy-start.14 = (bf16[512,1024]{1,0:T(8,128)(2,1)S(1)}, bf16[512,1024]{1,0:T(8,128)(2,1)}, u32[]{:S(2)}) copy-start(bf16[512,1024]{1,0:T(8,128)(2,1)} %gather_fusion.9) | copy-start | bytes 3145732
  628.9 12.5 collective-permute-start.4
  635.1 13.3 copy-start.1
  635.1 6.3 copy-start.25
  653.2 252.0 %copy-start.41 = (f32[4,2,8,64]{3,2,1,0:T(8,128)}, f32[4,2,8,64]{3,2,1,0:T(8,128)S(1)}, u32[]{:S(2)}) copy-start(f32[4,2,8,64]{3,2,1,0:T(8,128)S(1)} %log_add_fusion) | copy-start | bytes 49156
  653.4 15.3 copy-start.3
  664.8 27.0 %all-to-all-start.5 = ((f32[32,1,256]{2,1,0:T(1,128)}), f32[32,1,256]{2,1,0:T(1,128)S(1)}, u32[]{:S(2)}, u32[]{:S(2)}) async-start(f32[32,1,256]{2,1,0:T(1,128)} %reshape.1310), calls=%async_computation.5 | async-start | bytes 65536 | tf_op jit(solution)/shard_map/all_to_all | solution.py:92
  691.8 6.2 copy-start.40
  691.8 6.4 copy-start.44
  691.8 100.5 %all-to-all-start.8 = ((f32[32,4,8,1024]{3,2,1,0:T(8,128)}), f32[32,4,8,1024]{3,2,1,0:T(8,128)}, u32[]{:S(2)}, u32[]{:S(2)}) async-start(f32[32,4,8,1024]{3,2,1,0:T(8,128)} %bitcast.358), calls=%async_computation.8 | async-start | bytes 8388608 | tf_op jit(solution)/shard_map/all_to_all | solution.py:91
  708.5 6.8 copy-start.30
  708.5 6.8 copy-start.63
  708.5 7.1 copy-start.43
  808.2 26.6 %all-to-all-start.9 = ((bf16[32,2,128]{2,1,0:T(2,128)(2,1)}), bf16[32,2,128]{2,1,0:T(2,128)(2,1)S(1)}, u32[]{:S(2)}, u32[]{:S(2)}) async-start(bf16[32,2,128]{2,1,0:T(2,128)(2,1)} %reshape.1312), calls=%async_computation.9 | async-start | bytes 32768 | tf_op jit(solution)/shard_map/all_to_all | solution.py:85
  834.8 60.6 %all-to-all-start.6 = ((bf16[32,4,8,1024]{3,2,1,0:T(8,128)(2,1)}), bf16[32,4,8,1024]{3,2,1,0:T(8,128)(2,1)S(1)}, u32[]{:S(2)}, u32[]{:S(2)}) async-start(bf16[32,4,8,1024]{3,2,1,0:T(8,128)(2,1)} %bitcast.374), calls=%async_computation.6 | async-start | bytes 4194304 | tf_op jit(solution)/shard_map/all_to_all | solution.py:84
  840.6 397.9 %reduce-scatter.10.cloned.1.call-start = ((), (), s32[]{:S(2)}) async-start(), calls=%async_computation.19 | async-start | bytes 4325376 | tf_op jit(solution)/shard_map/reduce_scatter | solution.py:301
  845.5 393.0 %reduce-scatter.6.cloned.1.call-start = ((), (), s32[]{:S(2)}) async-start(), calls=%async_computation.17 | async-start | bytes 4325376 | tf_op jit(solution)/shard_map/reduce_scatter | solution.py:299
  906.1 16.5 copy-start.2
  906.1 16.5 copy-start.32
  940.8 18.0 %collective-permute-start.5 = (f32[4,64,1024]{2,0,1:T(4,128)}, f32[4,64,1024]{2,0,1:T(4,128)}, u32[]{:S(2)}, u32[]{:S(2)}) collective-permute-start(f32[4,64,1024]{2,0,1:T(4,128)} %fusion.86), channel_id=1, source_target_pairs={{1,0},{2,1},{3,2},{4,3},{5,4},{6,5},{7,6},{8,7},{9,8},{10,9},{11,1... | collective-permute-start | bytes 3145736 | tf_op jit(solution)/shard_map/ppermute | solution.py:14
  1042.7 288.5 %reduce-scatter.8.cloned.1.call-start = ((), (), s32[]{:S(2)}) async-start(), calls=%async_computation.18 | async-start | bytes 4325376 | tf_op jit(solution)/shard_map/reduce_scatter | solution.py:300
  1061.8 17.3 %collective-permute-start.6 = (f32[4,64,1024]{2,0,1:T(4,128)S(1)}, f32[4,64,1024]{2,0,1:T(4,128)S(1)}, u32[]{:S(2)}, u32[]{:S(2)}) collective-permute-start(f32[4,64,1024]{2,0,1:T(4,128)S(1)} %fusion.84), channel_id=1, source_target_pairs={{1,0},{2,1},{3,2},{4,3},{5,4},{6,5},{7,6},{8,7},{9,8},{10,9},{11,1... | collective-permute-start | bytes 3145736 | tf_op jit(solution)/shard_map/ppermute | solution.py:14
  1169.4 343.6 %reduce-scatter.14.cloned.1.call-start = ((), (), s32[]{:S(2)}) async-start(), calls=%async_computation.21 | async-start | bytes 17301504 | tf_op jit(solution)/shard_map/reduce_scatter | solution.py:306
  1180.8 519.5 %reduce-scatter.12.cloned.1.call-start = ((), (), s32[]{:S(2)}) async-start(), calls=%async_computation.20 | async-start | bytes 17301504 | tf_op jit(solution)/shard_map/reduce_scatter | solution.py:304
  (43 other events, 96.7 us)
Sparse Core Ops, SparseCore 0:
  10.9 59.1 all-gather.16
  72.9 62.2 all-gather.18
  138.1 63.4 all-gather.20
  204.3 85.4 all-gather.22
  292.6 121.4 all-gather.24
  845.7 150.9 reduce-scatter.9
  1042.8 145.8 reduce-scatter.5
  1191.6 139.5 reduce-scatter.7
  1334.1 178.8 reduce-scatter.13
  1515.7 184.5 reduce-scatter.11
where the time goes:
time: 1720 us; the launch traced here: 1710 us
  waiting for transfers between devices  730 us (42%)
  local copies, waits for them, and re-layouts  393 us (23%)
  blocking collectives  333 us (19%)
  matrix products  88.9 us (5%)
  starting transfers between devices  87.8 us (5%)
  other arithmetic  59.9 us (3%)
    reduce_scatter x1, waiting for transfers between devices, spread_grads(): lax.psum_scatter(upper_projection_weight, ('seq', 'sub'), scatter_dimensi...  187 us
    reduce_scatter x1, waiting for transfers between devices, spread_grads(): lax.psum_scatter(lower_projection_weight, ('seq', 'sub'), scatter_dimensi...  182 us
    gather x12, local copies, waits for them, and re-layouts, gather_slots(): return padded[member[None, :, None], lookup]  157 us
    all_gather x1, blocking collectives, collect(): lax.all_gather(upper_projection_bias, ('seq', 'sub'), axis=0, tiled=True)  134 us
    reduce_scatter x1, waiting for transfers between devices, spread_grads(): lax.psum_scatter(value_projection_weight, ('seq', 'sub'), scatter_dimensi...  92.6 us
    all_to_all x3, waiting for transfers between devices, trade_rows(): lax.all_to_all(first_part, ('seq', 'sub'), split_axis=0, concat_axis=0, t...  85.4 us
    unnamed x2, blocking collectives  81.6 us
    gather x13, local copies, waits for them, and re-layouts, settle(): return received[owners, jnp.arange(owners.shape[0])[:, None], slot_index]  75.9 us
  transfers between devices with their start and end apart: 27, of which 14 were waited for; matrix products, arithmetic and copies ran while one was open for 27% of the time, Pallas kernels for 0%

commit v1 on v0

--- a/solution.py
+++ b/solution.py
@@ -296,19 +296,19 @@
     return (
         lax.psum_scatter(attend_gain, ("seq", "sub"), scatter_dimension=0, tiled=True),
         lax.psum_scatter(attend_shift, ("seq", "sub"), scatter_dimension=0, tiled=True),
-        lax.psum_scatter(query_key_weight, ("seq", "sub"), scatter_dimension=0, tiled=True),
-        lax.psum_scatter(value_projection_weight, ("seq", "sub"), scatter_dimension=0, tiled=True),
-        lax.psum_scatter(output_projection_weight, ("seq", "sub"), scatter_dimension=0, tiled=True),
+        lax.psum_scatter(query_key_weight.astype(jnp.bfloat16), ("seq", "sub"), scatter_dimension=0, tiled=True),
+        lax.psum_scatter(value_projection_weight.astype(jnp.bfloat16), ("seq", "sub"), scatter_dimension=0, tiled=True),
+        lax.psum_scatter(output_projection_weight.astype(jnp.bfloat16), ("seq", "sub"), scatter_dimension=0, tiled=True),
         lax.psum_scatter(feed_gain, ("seq", "sub"), scatter_dimension=0, tiled=True),
         lax.psum_scatter(feed_shift, ("seq", "sub"), scatter_dimension=0, tiled=True),
-        lax.psum_scatter(upper_projection_weight, ("seq", "sub"), scatter_dimension=0, tiled=True),
+        lax.psum_scatter(upper_projection_weight.astype(jnp.bfloat16), ("seq", "sub"), scatter_dimension=0, tiled=True),
         lax.psum_scatter(upper_projection_bias, ("seq", "sub"), scatter_dimension=0, tiled=True),
-        lax.psum_scatter(lower_projection_weight, ("seq", "sub"), scatter_dimension=0, tiled=True),
+        lax.psum_scatter(lower_projection_weight.astype(jnp.bfloat16), ("seq", "sub"), scatter_dimension=0, tiled=True),
         lax.psum_scatter(lower_projection_bias, ("seq", "sub"), scatter_dimension=0, tiled=True),
     )
 
 
-def layer_forward(first_stream_state, second_stream_state, params, routes, rounds):
+def layer_pass(first_half, second_half, grad_one, grad_two, params, routes, rounds):
     (
         attend_gain,
         attend_shift,
@@ -322,52 +322,18 @@
         lower_projection_weight,
         lower_projection_bias,
     ) = params
-    normalized_input = layer_norm(
-        second_stream_state, attend_gain.astype(jnp.float32), attend_shift.astype(jnp.float32)
-    ).astype(jnp.bfloat16)
+    attend_norm, attend_pull = jax.vjp(
+        layer_norm, second_half, attend_gain.astype(jnp.float32), attend_shift.astype(jnp.float32)
+    )
+    normalized_input = attend_norm.astype(jnp.bfloat16)
     shared_query_key, value_vectors, outputs, totals, kept = round_outputs(
         normalized_input, query_key_weight, value_projection_weight, routes, rounds
     )
-    attention_result = combine_rounds(outputs, totals).astype(jnp.bfloat16)
-    first_stream_state = first_stream_state + jnp.einsum(
-        "srd,de->sre",
-        attention_result,
-        output_projection_weight,
-        preferred_element_type=jnp.float32,
-    )
-    feed_forward_input = layer_norm(
-        first_stream_state, feed_gain.astype(jnp.float32), feed_shift.astype(jnp.float32)
-    ).astype(jnp.bfloat16)
-    prior_state = jnp.einsum(
-        "srd,df->srf",
-        feed_forward_input,
-        upper_projection_weight,
-        preferred_element_type=jnp.float32,
-    ) + upper_projection_bias.astype(jnp.float32)
-    hidden_activation = gelu_exact(prior_state).astype(jnp.bfloat16)
-    feed_out = jnp.einsum(
-        "srf,fd->srd",
-        hidden_activation,
-        lower_projection_weight,
-        preferred_element_type=jnp.float32,
-    ) + lower_projection_bias.astype(jnp.float32)
-    return (first_stream_state, second_stream_state + feed_out)
-
-
-def layer_back(top_one, top_two, grad_one, grad_two, params, routes, rounds):
-    (
-        attend_gain,
-        attend_shift,
-        query_key_weight,
-        value_projection_weight,
-        output_projection_weight,
-        feed_gain,
-        feed_shift,
-        upper_projection_weight,
-        upper_projection_bias,
-        lower_projection_weight,
-        lower_projection_bias,
-    ) = params
+    attention_result, combine_pull = jax.vjp(combine_rounds, outputs, totals)
+    attended_low = attention_result.astype(jnp.bfloat16)
+    top_one = first_half + jnp.einsum(
+        "srd,de->sre", attended_low, output_projection_weight, preferred_element_type=jnp.float32
+    )
     feed_norm, feed_pull = jax.vjp(
         layer_norm, top_one, feed_gain.astype(jnp.float32), feed_shift.astype(jnp.float32)
     )
@@ -383,7 +349,7 @@
     feed_out = jnp.einsum(
         "srf,fd->srd", active_low, lower_projection_weight, preferred_element_type=jnp.float32
     ) + lower_projection_bias.astype(jnp.float32)
-    bottom_two = top_two - feed_out
+    top_two = second_half + feed_out
     feed_grad = grad_two.astype(jnp.bfloat16)
     down_weight_grad = jnp.einsum(
         "srf,srd->fd", active_low, feed_grad, preferred_element_type=jnp.float32
@@ -402,18 +368,6 @@
     )
     one_part, feed_gain_grad, feed_shift_grad = feed_pull(norm_grad)
     total_one = grad_one + one_part
-    attend_norm, attend_pull = jax.vjp(
-        layer_norm, bottom_two, attend_gain.astype(jnp.float32), attend_shift.astype(jnp.float32)
-    )
-    normalized_input = attend_norm.astype(jnp.bfloat16)
-    shared_query_key, value_vectors, outputs, totals, kept = round_outputs(
-        normalized_input, query_key_weight, value_projection_weight, routes, rounds
-    )
-    attention_result, combine_pull = jax.vjp(combine_rounds, outputs, totals)
-    attended_low = attention_result.astype(jnp.bfloat16)
-    bottom_one = top_one - jnp.einsum(
-        "srd,de->sre", attended_low, output_projection_weight, preferred_element_type=jnp.float32
-    )
     out_grad = total_one.astype(jnp.bfloat16)
     output_weight_grad = jnp.einsum(
         "srd,sre->de", attended_low, out_grad, preferred_element_type=jnp.float32
@@ -483,7 +437,7 @@
         down_weight_grad,
         down_bias_grad,
     )
-    return (bottom_one, bottom_two, total_one, total_two, level_grads)
+    return (top_one, top_two, total_one, total_two, level_grads)
 
 
 def on_device(
@@ -519,34 +473,16 @@
         lower_projection_bias,
     )
     devices = lax.axis_size(("seq", "sub"))
-    layers = sort_order.shape[0]
     rounds = sort_order.shape[1]
     row_count = first_half.shape[1]
     capacity = 2 * max(1, row_count // devices)
-    first_stream_state, second_stream_state = (first_half, second_half)
-    layer_index = 0
-    params = collect(weight_stack, layer_index)
-    routes = build_routes(sort_order[layer_index], sort_place[layer_index], devices, capacity)
-    first_stream_state, second_stream_state = layer_forward(
-        first_stream_state, second_stream_state, params, routes, rounds
-    )
-    first_out, second_out = (first_stream_state, second_stream_state)
-    grad_one, grad_two = (grad_first, grad_second)
-    gradients = []
-    for layer_index in reversed(range(layers)):
-        params = collect(weight_stack, layer_index)
-        routes = build_routes(sort_order[layer_index], sort_place[layer_index], devices, capacity)
-        first_stream_state, second_stream_state, grad_one, grad_two, level_grads = layer_back(
-            first_stream_state, second_stream_state, grad_one, grad_two, params, routes, rounds
-        )
-        gradients.insert(0, spread_grads(level_grads))
-    stacked = tuple(
-        (
-            jnp.stack([level_entry[member_index] for level_entry in gradients])
-            for member_index in range(len(weight_stack))
-        )
-    )
-    return (first_out, second_out, grad_one, grad_two) + stacked
+    params = collect(weight_stack, 0)
+    routes = build_routes(sort_order[0], sort_place[0], devices, capacity)
+    first_out, second_out, first_grad, second_grad, level_grads = layer_pass(
+        first_half, second_half, grad_first, grad_second, params, routes, rounds
+    )
+    stacked = tuple((entry[None].astype(jnp.float32) for entry in spread_grads(level_grads)))
+    return (first_out, second_out, first_grad, second_grad) + stacked
 
 
 def solution(mesh):

time: 1720 us -> 1420 us (0.83)
  blocking collectives: 333 us -> 219 us
  local copies, waits for them, and re-layouts: 393 us -> 286 us
  waiting for transfers between devices: 730 us -> 669 us
  matrix products: 88.9 us -> 70.4 us
    all_to_all x2 -> x0, blocking collectives: 117 us -> none  [the longest x1 62.5 us: trade_rows(): lax.all_to_all(second_part, ('seq', 'sub'), split_axis=0, concat_axis=0,...]
    all_to_all x2 -> x1, waiting for transfers between devices: 67.8 us -> 0.01 us  [trade_results(): lax.all_to_all(first_part, ('seq', 'sub'), split_axis=0, concat_axis=0, t...]
    gather x12 -> x8, local copies, waits for them, and re-layouts: 157 us -> 98.9 us  [gather_slots(): return padded[member[None, :, None], lookup]]
    reduce_scatter x5, waiting for transfers between devices: 462 us -> 496 us  [the longest x1 146 us: spread_grads(): lax.psum_scatter(upper_projection_weight.astype(jnp.bfloat16), ('seq', 's...]
    all_to_all x3, waiting for transfers between devices: 85.4 us -> 52.4 us  [trade_rows(): lax.all_to_all(first_part, ('seq', 'sub'), split_axis=0, concat_axis=0, t...]
    all_to_all x3, starting transfers between devices: 14 us -> 39.2 us  [trade_rows(): lax.all_to_all(second_part, ('seq', 'sub'), split_axis=0, concat_axis=0,...]
    gather x13 -> x9, local copies, waits for them, and re-layouts: 75.9 us -> 53.3 us  [settle(): return received[owners, jnp.arange(owners.shape[0])[:, None], slot_index]]
    unnamed x155 -> x167, local copies, waits for them, and re-layouts: 51.2 us -> 40.4 us
  transfers between devices with their start and end apart: 27 -> 23, of which waited for: 14 -> 12; matrix products, arithmetic and copies ran while one was open for 27% -> 22% of each run, Pallas kernels for 0% -> 0%
where the time goes in v1:
time: 1420 us; the launch traced here: 1410 us
  waiting for transfers between devices  669 us (47%)
  local copies, waits for them, and re-layouts  286 us (20%)
  blocking collectives  219 us (15%)
  starting transfers between devices  92.5 us (7%)
  matrix products  70.4 us (5%)
  other arithmetic  60.4 us (4%)
  between operations  16.1 us (1%)
    reduce_scatter x1, waiting for transfers between devices, spread_grads(): lax.psum_scatter(upper_projection_weight.astype(jnp.bfloat16), ('seq', 's...  146 us
    reduce_scatter x1, waiting for transfers between devices, spread_grads(): lax.psum_scatter(lower_projection_weight.astype(jnp.bfloat16), ('seq', 's...  145 us
    all_gather x1, blocking collectives, collect(): lax.all_gather(upper_projection_bias, ('seq', 'sub'), axis=0, tiled=True)  137 us
    reduce_scatter x1, waiting for transfers between devices, spread_grads(): lax.psum_scatter(value_projection_weight.astype(jnp.bfloat16), ('seq', 's...  133 us
    gather x8, local copies, waits for them, and re-layouts, gather_slots(): return padded[member[None, :, None], lookup]  98.9 us
    unnamed x2, blocking collectives  81.7 us
    reduce_scatter x1, waiting for transfers between devices, spread_grads(): lax.psum_scatter(query_key_weight.astype(jnp.bfloat16), ('seq', 'sub'), s...  71.5 us
    gather x9, local copies, waits for them, and re-layouts, settle(): return received[owners, jnp.arange(owners.shape[0])[:, None], slot_index]  53.3 us
  transfers between devices with their start and end apart: 23, of which 12 were waited for; matrix products, arithmetic and copies ran while one was open for 22% of the time, Pallas kernels for 0%

profile of v1, /device:TPU:0, one launch (start us, length us, event | category | flops | bytes accessed | tf_op | source)
XLA Modules:
  0.0 1413.3 jit_solution(7895458851410426834)
XLA Ops:
  14.2 42.3 %all-reduce.25 = (bf16[1024]{0:T(1024)(128)(2,1)S(1)}, bf16[1024]{0:T(1024)(128)(2,1)S(1)}, bf16[1024]{0:T(1024)(128)(2,1)S(1)}, bf16[1024]{0:T(1024)(128)(2,1)S(1)}, bf16[1024]{0:T(1024)(128)(2,1)}) all-reduce(bf16[1024]{0:T(1024)(128)(2,1)S(1)} %dynamic-update-slice.7, ...), channel_id=3, replica_groups=mesh['seq'=8,'sub'=4] {'seq','sub'}, use_global_device_ids=true, to_apply=%add.14 | all-reduce | flops 5120 | bytes 20480
  58.9 24.7 %scatter_fusion = s32[4,256]{1,0:T(4,128)S(1)} fusion(s32[4,256]{1,0:T(4,128)S(1)} %broadcast.769.clone, s32[512]{0:T(512)S(1)} %get-tuple-element.80, s32[512]{0:T(512)S(1)} %iota_bitcast_fusion), kind=kCustom, calls=%fused_computation.16 | custom fusion | bytes 10240 | tf_op jit(solution)/shard_map/scatter | solution.py:58
  86.7 14.0 gather_fusion
  100.7 5.0 all-to-all-start
  105.6 30.0 %all-gather.19.cloned.1.call-done = bf16[1,1024,1024]{2,1,0:T(8,128)(2,1)} async-done(((bf16[1,32,1024]{2,1,0:T(8,128)(2,1)}), bf16[1,1024,1024]{2,1,0:T(8,128)(2,1)}) %all-gather.19.cloned.1.call-update) | async-done | bytes 2097168 | tf_op jit(solution)/shard_map/all_gather | solution.py:271
  137.7 14.1 gather_fusion.4
  151.8 9.7 all-to-all-done
  166.5 24.7 %scatter_fusion.1 = s32[4,256]{1,0:T(4,128)S(1)} fusion(s32[4,256]{1,0:T(4,128)S(1)} %broadcast.769.clone.1, s32[512]{0:T(512)S(1)} %get-tuple-element.81, s32[512]{0:T(512)S(1)} %iota_bitcast_fusion), kind=kCustom, calls=%fused_computation.17 | custom fusion | bytes 10240 | tf_op jit(solution)/shard_map/scatter | solution.py:58
  192.7 19.7 %collective-permute-done = s32[4,64]{1,0:T(4,128)S(1)} collective-permute-done((s32[4,64]{1,0:T(4,128)S(1)}, s32[4,64]{1,0:T(4,128)S(1)}, u32[]{:S(2)}, u32[]{:S(2)}) %collective-permute-start) | collective-permute-done | bytes 1056 | tf_op jit(solution)/shard_map/ppermute | solution.py:14
  212.6 7.0 gather_fusion.1
  226.7 7.1 gather_fusion.5
  247.5 4.6 gather_fusion.2
  253.0 20.3 %all-to-all-start.1 = ((f32[32,1,256]{2,1,0:T(1,128)}), f32[32,1,256]{2,1,0:T(1,128)S(1)}, u32[]{:S(2)}, u32[]{:S(2)}) async-start(f32[32,1,256]{2,1,0:T(1,128)} %reshape.1163), calls=%async_computation.1 | async-start | bytes 65536 | tf_op jit(solution)/shard_map/all_to_all | solution.py:92
  290.7 15.1 %gather_fusion.6 = f32[1024,1024]{1,0:T(8,128)} fusion(f32[4,129,1024]{2,0,1:T(4,128)S(1)} %concatenate.111, s32[1024]{0:T(1024)S(1)} %reshape.997), kind=kCustom, calls=%fused_computation.6 | custom fusion | bytes 8396800 | tf_op jit(solution)/shard_map/gather | solution.py:65
  305.8 5.9 all-to-all-start.3
  311.6 136.8 %all-gather.8 = bf16[1,4096]{1,0:T(2,128)(2,1)S(1)} all-gather(bf16[1,128]{1,0:T(2,128)(2,1)S(1)} %copy-done.67), channel_id=10, replica_groups=mesh['seq'=8,'sub'=4] {'seq','sub'}, dimensions={1}, use_global_device_ids=true | all-gather | bytes 8448 | tf_op jit(solution)/shard_map/all_gather | solution.py:276
  457.2 8.2 gather_fusion.7
  471.4 9.3 multiply_convert_fusion.1
  480.8 10.7 convert_reduce_fusion
  504.6 5.6 gather_fusion.10
  511.0 17.9 %all-to-all-start.5 = ((bf16[32,2,128]{2,1,0:T(2,128)(2,1)}), bf16[32,2,128]{2,1,0:T(2,128)(2,1)S(1)}, u32[]{:S(2)}, u32[]{:S(2)}) async-start(bf16[32,2,128]{2,1,0:T(2,128)(2,1)} %reshape.1165), calls=%async_computation.5 | async-start | bytes 32768 | tf_op jit(solution)/shard_map/all_to_all | solution.py:85
  532.5 15.2 %gather_fusion.8 = bf16[1024,1024]{1,0:T(8,128)(2,1)} fusion(bf16[4,129,1024]{2,0,1:T(4,128)(2,1)S(1)} %concatenate.112, s32[1024]{0:T(1024)S(1)} %reshape.1033), kind=kCustom, calls=%fused_computation.8 | custom fusion | bytes 4202496 | tf_op jit(solution)/shard_map/gather | solution.py:65
  547.7 6.2 all-to-all-start.4
  554.3 4.7 gather_fusion.11
  560.0 42.7 %all-to-all-done.4 = bf16[32,4,8,1024]{3,2,1,0:T(8,128)(2,1)S(1)} async-done(((bf16[32,4,8,1024]{3,2,1,0:T(8,128)(2,1)}), bf16[32,4,8,1024]{3,2,1,0:T(8,128)(2,1)S(1)}, u32[]{:S(2)}, u32[]{:S(2)}) %all-to-all-start.4) | async-done | bytes 2097184 | tf_op jit(solution)/shard_map/all_to_all | solution.py:84
  602.7 7.1 gather_fusion.9
  613.4 16.4 %multiply_reduce_fusion = (f32[4,2,8,128]{3,2,1,0:T(8,128)S(1)}, f32[4,2,8,64,128]{4,3,2,1,0:T(8,128)S(1)}) fusion(f32[4,2,8,64,128]{4,3,2,1,0:T(8,128)S(1)} %copy-done.5, f32[4,2,8,64]{3,2,1,0:T(8,128)S(1)} %bitcast.349, f32[4,2,8,64,128]{4,3,2,1,0:T(8,128)S(1)} %fusion.78, f32[4,2,8,64]{3,2,1,0:T(8,128)S(1)} %copy-done.41, ...), kind=kOutput, calls=%fused_computation.61 | output fusion | flops 7860351 | bytes 6586368 | tf_op jit(solution)/shard_map/sub | solution.py:191
  635.8 5.0 copy.235
  640.7 5.0 copy.236
  666.6 15.2 %gather_fusion.12 = bf16[1024,1024]{1,0:T(8,128)(2,1)} fusion(bf16[4,129,1024]{2,0,1:T(4,128)(2,1)S(1)} %concatenate.117, s32[1024]{0:T(1024)S(1)} %reshape.997), kind=kCustom, calls=%fused_computation.12 | custom fusion | bytes 4202496 | tf_op jit(solution)/shard_map/gather | solution.py:65
  681.8 6.0 all-to-all-start.6
  694.7 4.6 fusion.159
  703.1 5.0 copy.238
  708.2 5.2 collective-permute-start.4
  714.1 23.6 %collective-permute-done.4 = f32[4,64,1024]{2,0,1:T(4,128)S(1)} collective-permute-done((f32[4,64,1024]{2,0,1:T(4,128)S(1)}, f32[4,64,1024]{2,0,1:T(4,128)S(1)}, u32[]{:S(2)}, u32[]{:S(2)}) %collective-permute-start.4) | collective-permute-done | bytes 1048608 | tf_op jit(solution)/shard_map/ppermute | solution.py:14
  739.0 15.2 %gather_fusion.14 = bf16[1024,1024]{1,0:T(8,128)(2,1)} fusion(bf16[4,129,1024]{2,0,1:T(4,128)(2,1)S(1)} %concatenate.120, s32[1024]{0:T(1024)S(1)} %reshape.997), kind=kCustom, calls=%fused_computation.14 | custom fusion | bytes 4202496 | tf_op jit(solution)/shard_map/gather | solution.py:65
  754.2 17.6 %all-to-all-start.7 = ((bf16[32,4,8,1024]{3,2,1,0:T(8,128)(2,1)}), bf16[32,4,8,1024]{3,2,1,0:T(8,128)(2,1)S(1)}, u32[]{:S(2)}, u32[]{:S(2)}) async-start(bf16[32,4,8,1024]{3,2,1,0:T(8,128)(2,1)} %bitcast.326), calls=%async_computation.7 | async-start | bytes 4194304 | tf_op jit(solution)/shard_map/all_to_all | solution.py:85
  771.9 8.6 gather_fusion.13
  785.8 38.7 %all-to-all-done.7 = bf16[32,4,8,1024]{3,2,1,0:T(8,128)(2,1)S(1)} async-done(((bf16[32,4,8,1024]{3,2,1,0:T(8,128)(2,1)}), bf16[32,4,8,1024]{3,2,1,0:T(8,128)(2,1)S(1)}, u32[]{:S(2)}, u32[]{:S(2)}) %all-to-all-start.7) | async-done | bytes 2097184 | tf_op jit(solution)/shard_map/all_to_all | solution.py:85
  824.5 7.1 gather_fusion.15
  835.3 5.7 convolution_convert_fusion.1
  842.3 5.6 convolution_convert_fusion
  849.0 5.6 fusion.53
  861.8 39.4 %all-reduce.24 = (f32[1024]{0:T(1024)S(1)}, f32[1024]{0:T(1024)S(1)}, f32[1024]{0:T(1024)S(1)}, f32[1024]{0:T(1024)S(1)}, f32[4096]{0:T(1024)S(1)}, /*index=5*/f32[1024]{0:T(1024)S(1)}) all-reduce(f32[1024]{0:T(1024)S(1)} %get-tuple-element.41, f32[1024]{0:T(1024)S(1)} %reduce_sum.339, ...), channel_id=13, replica_groups=mesh['seq'=8,'sub'=4] {'seq','sub'}, use_global_device_ids=true, to_apply=%region_27.28.clone | all-reduce | flops 9216 | bytes 73728
  903.5 71.5 %reduce-scatter.6.cloned.1.call-done = bf16[32,1024]{1,0:T(8,128)(2,1)} async-done(((bf16[1024,1024]{1,0:T(8,128)(2,1)}), bf16[32,1024]{1,0:T(8,128)(2,1)}) %reduce-scatter.6.cloned.1.call-update) | async-done | bytes 65552 | tf_op jit(solution)/shard_map/reduce_scatter | solution.py:299
  976.5 133.5 %reduce-scatter.8.cloned.1.call-done = bf16[32,1024]{1,0:T(8,128)(2,1)} async-done(((bf16[1024,1024]{1,0:T(8,128)(2,1)}), bf16[32,1024]{1,0:T(8,128)(2,1)}) %reduce-scatter.8.cloned.1.call-update) | async-done | bytes 65552 | tf_op jit(solution)/shard_map/reduce_scatter | solution.py:300
  1111.5 145.5 %reduce-scatter.12.cloned.1.call-done = bf16[32,4096]{1,0:T(8,128)(2,1)} async-done(((bf16[1024,4096]{1,0:T(8,128)(2,1)}), bf16[32,4096]{1,0:T(8,128)(2,1)}) %reduce-scatter.12.cloned.1.call-update) | async-done | bytes 262160 | tf_op jit(solution)/shard_map/reduce_scatter | solution.py:304
  1258.9 145.4 %reduce-scatter.14.cloned.1.call-done = bf16[128,1024]{1,0:T(8,128)(2,1)} async-done(((bf16[4096,1024]{1,0:T(8,128)(2,1)}), bf16[128,1024]{1,0:T(8,128)(2,1)}) %reduce-scatter.14.cloned.1.call-update) | async-done | bytes 262160 | tf_op jit(solution)/shard_map/reduce_scatter | solution.py:306
  (343 shorter events, 163.4 us)
Async XLA Ops:
  7.2 77.3 %all-gather.17.cloned.1.call-start = ((), (), s32[]{:S(2)}) async-start(), calls=%async_computation.18 | async-start | bytes 2162688 | tf_op jit(solution)/shard_map/all_gather | solution.py:270
  7.9 127.7 %all-gather.19.cloned.1.call-start = ((), (), s32[]{:S(2)}) async-start(), calls=%async_computation.19 | async-start | bytes 2162688 | tf_op jit(solution)/shard_map/all_gather | solution.py:271
  8.7 459.6 %all-gather.21.cloned.1.call-start = ((), (), s32[]{:S(2)}) async-start(), calls=%async_computation.20 | async-start | bytes 2162688 | tf_op jit(solution)/shard_map/all_gather | solution.py:272
  9.4 462.0 %all-gather.23.cloned.1.call-start = ((), (), s32[]{:S(2)}) async-start(), calls=%async_computation.21 | async-start | bytes 8650752 | tf_op jit(solution)/shard_map/all_gather | solution.py:275
  56.4 27.8 %copy-start.50 = (f32[1024]{0:T(1024)}, f32[1024]{0:T(1024)S(1)}, u32[]{:S(2)}) copy-start(f32[1024]{0:T(1024)S(1)} %convert_element_type.248) | copy-start | bytes 12292
  58.9 25.0 %copy-start.9 = (f32[1,128,1024]{2,1,0:T(8,128)S(1)}, f32[1,128,1024]{2,1,0:T(8,128)}, u32[]{:S(2)}) copy-start(f32[1,128,1024]{2,1,0:T(8,128)} %param.22) | copy-start | bytes 1572868
  84.2 16.4 %copy-start.68 = (f32[128]{0:T(128)}, f32[128]{0:T(128)S(1)}, u32[]{:S(2)}) copy-start(f32[128]{0:T(128)S(1)} %multiply_reduce_fusion.4) | copy-start | bytes 1540
  84.3 16.4 %copy-start.64 = (f32[128]{0:T(128)}, f32[128]{0:T(128)S(1)}, u32[]{:S(2)}) copy-start(f32[128]{0:T(128)S(1)} %fusion.144) | copy-start | bytes 1540
  84.5 51.2 %copy-start.21 = (bf16[128,1024]{1,0:T(8,128)(2,1)}, bf16[128,1024]{1,0:T(8,128)(2,1)S(1)}, u32[]{:S(2)}) copy-start(bf16[128,1024]{1,0:T(8,128)(2,1)S(1)} %fusion.88) | copy-start | bytes 786436
  100.7 60.8 %all-to-all-start = ((bf16[32,4,8,1024]{3,2,1,0:T(8,128)(2,1)}), bf16[32,4,8,1024]{3,2,1,0:T(8,128)(2,1)}, u32[]{:S(2)}, u32[]{:S(2)}) async-start(bf16[32,4,8,1024]{3,2,1,0:T(8,128)(2,1)} %bitcast.12), calls=%async_computation | async-start | bytes 4194304 | tf_op jit(solution)/shard_map/all_to_all | solution.py:84
  161.5 65.1 %all-to-all-start.2 = ((bf16[32,4,8,1024]{3,2,1,0:T(8,128)(2,1)}), bf16[32,4,8,1024]{3,2,1,0:T(8,128)(2,1)S(1)}, u32[]{:S(2)}, u32[]{:S(2)}) async-start(bf16[32,4,8,1024]{3,2,1,0:T(8,128)(2,1)} %bitcast.324), calls=%async_computation.2 | async-start | bytes 4194304 | tf_op jit(solution)/shard_map/all_to_all | solution.py:85
  165.3 315.4 %all-gather.25.cloned.1.call-start = ((), (), s32[]{:S(2)}) async-start(), calls=%async_computation.22 | async-start | bytes 8650752 | tf_op jit(solution)/shard_map/all_gather | solution.py:277
  166.0 46.5 %collective-permute-start = (s32[4,64]{1,0:T(4,128)S(1)}, s32[4,64]{1,0:T(4,128)S(1)}, u32[]{:S(2)}, u32[]{:S(2)}) collective-permute-start(s32[4,64]{1,0:T(4,128)S(1)} %slice.105), channel_id=1, source_target_pairs={{31,0},{0,1},{1,2},{2,3},{3,4},{4,5},{5,6},{6,7},{7,8},{8,9},{9,10... | collective-permute-start | bytes 3080 | tf_op jit(solution)/shard_map/ppermute | solution.py:14
  220.4 15.2 %collective-permute-start.1 = (bf16[4,64,1024]{2,1,0:T(8,128)(2,1)}, bf16[4,64,1024]{2,1,0:T(8,128)(2,1)}, u32[]{:S(2)}, u32[]{:S(2)}) collective-permute-start(bf16[4,64,1024]{2,1,0:T(8,128)(2,1)} %slice.170), channel_id=1, source_target_pairs={{31,0},{0,1},{1,2},{2,3},{3,4},{4,5},{5,6},{6,7},{7,8},{8,9},{9,10... | collective-permute-start | bytes 1572872 | tf_op jit(solution)/shard_map/ppermute | solution.py:14
  221.7 57.6 %copy-start.37 = (pred[4,2,64,128]{3,2,1,0:T(8,128)(4,1)}, pred[4,2,64,128]{3,2,1,0:T(8,128)(4,1)S(1)}, u32[]{:S(2)}) copy-start(pred[4,2,64,128]{3,2,1,0:T(8,128)(4,1)S(1)} %get-tuple-element.76) | copy-start | bytes 196612
  235.6 37.7 %collective-permute-start.2 = (bf16[4,64,1024]{2,1,0:T(8,128)(2,1)}, bf16[4,64,1024]{2,1,0:T(8,128)(2,1)}, u32[]{:S(2)}, u32[]{:S(2)}) collective-permute-start(bf16[4,64,1024]{2,1,0:T(8,128)(2,1)} %slice.173), channel_id=1, source_target_pairs={{31,0},{0,1},{1,2},{2,3},{3,4},{4,5},{5,6},{6,7},{7,8},{8,9},{9,10... | collective-permute-start | bytes 1572872 | tf_op jit(solution)/shard_map/ppermute | solution.py:14
  247.3 32.1 %copy-start.40 = (f32[4,2,8,64]{3,2,1,0:T(8,128)}, f32[4,2,8,64]{3,2,1,0:T(8,128)S(1)}, u32[]{:S(2)}) copy-start(f32[4,2,8,64]{3,2,1,0:T(8,128)S(1)} %log_add_fusion) | copy-start | bytes 49156
  247.5 25.8 %copy-start.20 = (bf16[512,1024]{1,0:T(8,128)(2,1)S(1)}, bf16[512,1024]{1,0:T(8,128)(2,1)}, u32[]{:S(2)}) copy-start(bf16[512,1024]{1,0:T(8,128)(2,1)} %gather_fusion.5) | copy-start | bytes 3145732
  253.0 52.7 %all-to-all-start.1 = ((f32[32,1,256]{2,1,0:T(1,128)}), f32[32,1,256]{2,1,0:T(1,128)S(1)}, u32[]{:S(2)}, u32[]{:S(2)}) async-start(f32[32,1,256]{2,1,0:T(1,128)} %reshape.1163), calls=%async_computation.1 | async-start | bytes 65536 | tf_op jit(solution)/shard_map/all_to_all | solution.py:92
  305.8 5.9 copy-start.67
  305.8 151.4 %all-to-all-start.3 = ((f32[32,4,8,1024]{3,2,1,0:T(8,128)}), f32[32,4,8,1024]{3,2,1,0:T(8,128)}, u32[]{:S(2)}, u32[]{:S(2)}) async-start(f32[32,4,8,1024]{3,2,1,0:T(8,128)} %bitcast.315), calls=%async_computation.3 | async-start | bytes 8388608 | tf_op jit(solution)/shard_map/all_to_all | solution.py:91
  449.1 22.3 %copy-start.48 = (f32[1024]{0:T(1024)}, f32[1024]{0:T(1024)S(1)}, u32[]{:S(2)}) copy-start(f32[1024]{0:T(1024)S(1)} %convert_element_type.251) | copy-start | bytes 12292
  449.1 46.0 %copy-start.46 = (f32[1024]{0:T(1024)}, f32[1024]{0:T(1024)S(1)}, u32[]{:S(2)}) copy-start(f32[1024]{0:T(1024)S(1)} %convert_element_type.250) | copy-start | bytes 12292
  468.2 12.5 copy-start.29
  470.6 364.6 %copy-start.11 = (f32[1,128,1024]{2,1,0:T(8,128)}, f32[1,128,1024]{2,1,0:T(8,128)S(1)}, u32[]{:S(2)}) copy-start(f32[1,128,1024]{2,1,0:T(8,128)S(1)} %get-tuple-element.86) | copy-start | bytes 1572868
  471.4 9.4 copy-start.33
  480.7 10.8 copy-start.16
  480.8 10.8 copy-start.58
  480.8 10.7 copy-start.60
  504.1 24.8 %copy-start.36 = (f32[128,1024]{1,0:T(8,128)S(1)}, f32[128,1024]{1,0:T(8,128)}, u32[]{:S(2)}) copy-start(f32[128,1024]{1,0:T(8,128)} %copy.208) | copy-start | bytes 1572868
  511.0 36.7 %all-to-all-start.5 = ((bf16[32,2,128]{2,1,0:T(2,128)(2,1)}), bf16[32,2,128]{2,1,0:T(2,128)(2,1)S(1)}, u32[]{:S(2)}, u32[]{:S(2)}) async-start(bf16[32,2,128]{2,1,0:T(2,128)(2,1)} %reshape.1165), calls=%async_computation.5 | async-start | bytes 32768 | tf_op jit(solution)/shard_map/all_to_all | solution.py:85
  547.7 55.0 %all-to-all-start.4 = ((bf16[32,4,8,1024]{3,2,1,0:T(8,128)(2,1)}), bf16[32,4,8,1024]{3,2,1,0:T(8,128)(2,1)S(1)}, u32[]{:S(2)}, u32[]{:S(2)}) async-start(bf16[32,4,8,1024]{3,2,1,0:T(8,128)(2,1)} %bitcast.327), calls=%async_computation.4 | async-start | bytes 4194304 | tf_op jit(solution)/shard_map/all_to_all | solution.py:84
  613.4 16.5 %copy-start.45 = (f32[4,2,128,8]{2,3,1,0:T(8,128)S(1)}, f32[4,2,128,8]{2,3,1,0:T(8,128)}, u32[]{:S(2)}) copy-start(f32[4,2,128,8]{2,3,1,0:T(8,128)} %copy-done.44) | copy-start | bytes 98308
  613.4 16.5 %copy-start.1 = (bf16[4,2,128,1024]{2,3,1,0:T(8,128)(2,1)S(1)}, bf16[4,2,128,1024]{2,3,1,0:T(8,128)(2,1)}, u32[]{:S(2)}) copy-start(bf16[4,2,128,1024]{2,3,1,0:T(8,128)(2,1)} %copy-done) | copy-start | bytes 6291460
  613.4 16.5 %copy-start.27 = (bf16[64,8,8,128]{3,2,1,0:T(8,128)(2,1)S(1)}, bf16[64,8,8,128]{3,2,1,0:T(8,128)(2,1)}, u32[]{:S(2)}) copy-start(bf16[64,8,8,128]{3,2,1,0:T(8,128)(2,1)} %copy.240) | copy-start | bytes 3145732
  645.7 5.8 copy-start.19
  648.1 16.1 %collective-permute-start.3 = (f32[4,64,1024]{2,0,1:T(4,128)}, f32[4,64,1024]{2,0,1:T(4,128)}, u32[]{:S(2)}, u32[]{:S(2)}) collective-permute-start(f32[4,64,1024]{2,0,1:T(4,128)} %fusion.73), channel_id=1, source_target_pairs={{1,0},{2,1},{3,2},{4,3},{5,4},{6,5},{7,6},{8,7},{9,8},{10,9},{11,1... | collective-permute-start | bytes 3145736 | tf_op jit(solution)/shard_map/ppermute | solution.py:14
  681.8 6.1 copy-start.30
  681.8 72.4 %all-to-all-start.6 = ((bf16[32,4,8,1024]{3,2,1,0:T(8,128)(2,1)}), bf16[32,4,8,1024]{3,2,1,0:T(8,128)(2,1)}, u32[]{:S(2)}, u32[]{:S(2)}) async-start(bf16[32,4,8,1024]{3,2,1,0:T(8,128)(2,1)} %bitcast.325), calls=%async_computation.6 | async-start | bytes 4194304 | tf_op jit(solution)/shard_map/all_to_all | solution.py:84
  687.8 166.8 %reduce-scatter.10.cloned.1.call-start = ((), (), s32[]{:S(2)}) async-start(), calls=%async_computation.15 | async-start | bytes 2162688 | tf_op jit(solution)/shard_map/reduce_scatter | solution.py:301
  708.2 29.5 %collective-permute-start.4 = (f32[4,64,1024]{2,0,1:T(4,128)S(1)}, f32[4,64,1024]{2,0,1:T(4,128)S(1)}, u32[]{:S(2)}, u32[]{:S(2)}) collective-permute-start(f32[4,64,1024]{2,0,1:T(4,128)S(1)} %fusion.71), channel_id=1, source_target_pairs={{1,0},{2,1},{3,2},{4,3},{5,4},{6,5},{7,6},{8,7},{9,8},{10,9},{11,1... | collective-permute-start | bytes 3145736 | tf_op jit(solution)/shard_map/ppermute | solution.py:14
  754.2 70.3 %all-to-all-start.7 = ((bf16[32,4,8,1024]{3,2,1,0:T(8,128)(2,1)}), bf16[32,4,8,1024]{3,2,1,0:T(8,128)(2,1)S(1)}, u32[]{:S(2)}, u32[]{:S(2)}) async-start(bf16[32,4,8,1024]{3,2,1,0:T(8,128)(2,1)} %bitcast.326), calls=%async_computation.7 | async-start | bytes 4194304 | tf_op jit(solution)/shard_map/all_to_all | solution.py:85
  771.8 10.9 copy-start.22
  771.8 203.2 %reduce-scatter.6.cloned.1.call-start = ((), (), s32[]{:S(2)}) async-start(), calls=%async_computation.13 | async-start | bytes 2162688 | tf_op jit(solution)/shard_map/reduce_scatter | solution.py:299
  785.7 324.3 %reduce-scatter.8.cloned.1.call-start = ((), (), s32[]{:S(2)}) async-start(), calls=%async_computation.14 | async-start | bytes 2162688 | tf_op jit(solution)/shard_map/reduce_scatter | solution.py:300
  835.2 421.9 %reduce-scatter.12.cloned.1.call-start = ((), (), s32[]{:S(2)}) async-start(), calls=%async_computation.16 | async-start | bytes 8650752 | tf_op jit(solution)/shard_map/reduce_scatter | solution.py:304
  841.0 563.2 %reduce-scatter.14.cloned.1.call-start = ((), (), s32[]{:S(2)}) async-start(), calls=%async_computation.17 | async-start | bytes 8650752 | tf_op jit(solution)/shard_map/reduce_scatter | solution.py:306
  849.0 7.3 copy-start.32
  (47 other events, 106.7 us)
Sparse Core Ops, SparseCore 0:
  10.9 59.1 all-gather.16
  72.9 62.7 all-gather.18
  138.5 62.0 all-gather.20
  203.4 88.8 all-gather.22
  294.9 127.7 all-gather.24
  691.3 145.1 reduce-scatter.9
  838.8 136.1 reduce-scatter.5
  977.3 132.6 reduce-scatter.7
  1112.4 144.5 reduce-scatter.11
  1259.3 144.8 reduce-scatter.13

commit v2 on v1

--- a/solution.py
+++ b/solution.py
@@ -1,11 +1,18 @@
+import functools
+
 import jax
 import jax.numpy as jnp
 from jax import lax
+from jax.experimental import pallas as pl
+from jax.experimental.pallas import tpu as pltpu
 from jax.sharding import PartitionSpec as P
 
 HEADS = 8
 HEAD_DIM = 128
 BLOCK = 64
+LATER = -1000000000.0
+SELF = -100000.0
+OUTSIDE = -3e38
 
 
 def from_behind(block, axis, distance):
@@ -440,7 +447,7 @@
     return (top_one, top_two, total_one, total_two, level_grads)
 
 
-def on_device(
+def general_plan(
     first_half,
     second_half,
     grad_first,
@@ -485,9 +492,661 @@
     return (first_out, second_out, first_grad, second_grad) + stacked
 
 
+def exchange(items, name, collective_id, n_seq, n_sub):
+    per_plane = 2 * n_sub
+    size = {"plane": per_plane, "z": n_seq // 2, "all": n_seq * n_sub}
+    axes = sorted({item[0] for item in items})
+    count = len(items)
+    slots = max(size[axis] for axis in axes)
+
+    def body(*refs):
+        sources, targets = refs[:count], refs[count : 2 * count]
+        send, receive, own = refs[2 * count :]
+        seq, sub = lax.axis_index("seq"), lax.axis_index("sub")
+        here = {
+            "plane": lax.rem(seq, 2) * n_sub + sub,
+            "z": seq // 2,
+            "all": seq * n_sub + sub,
+        }
+
+        def device(axis, index):
+            if axis == "all":
+                return (index // n_sub, lax.rem(index, n_sub))
+            if axis == "z":
+                return (index * 2 + lax.rem(seq, 2), sub)
+            return ((seq // 2) * 2 + index // n_sub, lax.rem(index, n_sub))
+
+        barrier = pltpu.get_barrier_semaphore()
+        greeted = 0
+        for axis in ["all"] if "all" in axes else axes:
+            for step in range(1, size[axis]):
+                peer = lax.rem(here[axis] + step, size[axis])
+                pl.semaphore_signal(
+                    barrier, inc=1, device_id=device(axis, peer), device_id_type=pl.DeviceIdType.MESH
+                )
+                greeted += 1
+        copies = []
+        for index, (axis, _, _, source, target) in enumerate(items):
+            copies.append(
+                pltpu.make_async_copy(
+                    source(sources[index], here[axis]),
+                    target(targets[index], here[axis]),
+                    own.at[index],
+                )
+            )
+            copies[-1].start()
+        pl.semaphore_wait(barrier, greeted)
+        for step in range(1, slots):
+            for index, (axis, _, _, source, target) in enumerate(items):
+                if step >= size[axis]:
+                    continue
+                peer = lax.rem(here[axis] + step, size[axis])
+                copies.append(
+                    pltpu.make_async_remote_copy(
+                        src_ref=source(sources[index], peer),
+                        dst_ref=target(targets[index], here[axis]),
+                        send_sem=send.at[index, step],
+                        recv_sem=receive.at[index, step],
+                        device_id=device(axis, peer),
+                        device_id_type=pl.DeviceIdType.MESH,
+                    )
+                )
+                copies[-1].start()
+        for copy in copies:
+            copy.wait()
+
+    return pl.pallas_call(
+        body,
+        out_shape=[item[2] for item in items],
+        in_specs=[pl.BlockSpec(memory_space=pl.ANY)] * count,
+        out_specs=[pl.BlockSpec(memory_space=pl.ANY)] * count,
+        scratch_shapes=[
+            pltpu.SemaphoreType.DMA((count, slots)),
+            pltpu.SemaphoreType.DMA((count, slots)),
+            pltpu.SemaphoreType.DMA((count,)),
+        ],
+        compiler_params=pltpu.CompilerParams(collective_id=collective_id, has_side_effects=True),
+        name=name,
+    )(*[item[1] for item in items])
+
+
+def gathered(axis, array, devices):
+    shape = jax.ShapeDtypeStruct((devices,) + array.shape, array.dtype)
+    return (axis, array, shape, lambda ref, peer: ref, lambda ref, here: ref.at[here])
+
+
+def traded(axis, array):
+    shape = jax.ShapeDtypeStruct(array.shape, array.dtype)
+    return (axis, array, shape, lambda ref, peer: ref.at[peer], lambda ref, here: ref.at[here])
+
+
+def pick_rows(table, index_ref, start, count):
+    return jnp.concatenate(
+        [table[pl.ds(index_ref[start + row], 1), :] for row in range(count)], axis=0
+    )
+
+
+def across(column):
+    return jnp.broadcast_to(column, (128, 128)).T
+
+
+def down(row):
+    return jnp.broadcast_to(row, (128, 128)).T
+
+
+def dot(a, b, contract):
+    return lax.dot_general(a, b, (contract, ((), ())), preferred_element_type=jnp.float32)
+
+
+def window_masks():
+    query = lax.broadcasted_iota(jnp.int32, (128, 128), 0) // BLOCK
+    key = lax.broadcasted_iota(jnp.int32, (128, 128), 1) // BLOCK
+    return (query == 0) & (key == 1), key <= query
+
+
+def key_scales(keys):
+    rows = keys.astype(jnp.float32)
+    mean_square = jnp.mean(rows * rows, axis=-1, keepdims=True) + 1e-06
+    return rows, mean_square, lax.rsqrt(mean_square) / HEAD_DIM
+
+
+def masked_scores(raw, scale, query_pos, key_pos, inside):
+    scores = jnp.where(
+        key_pos > query_pos, LATER, jnp.where(key_pos == query_pos, SELF, raw * scale)
+    )
+    return jnp.where(inside, scores, OUTSIDE)
+
+
+def attend_kernel(
+    tiles, order, place, order_rows, shared, values, shared_sorted, values_sorted, total_sorted,
+    mixed_home, total_home, table, mixed, scales,
+):
+    def load(tile, carry):
+        rows = pl.ds(pl.multiple_of(tile * 128, 128), 128)
+        table[rows, :128] = shared[rows, :].astype(jnp.float32)
+        table[rows, 128:] = values[rows, :].astype(jnp.float32)
+        return carry
+
+    lax.fori_loop(0, tiles, load, 0)
+
+    def sort(step, carry):
+        start = pl.multiple_of(step * 32, 32)
+        picked = pick_rows(table, order, start, 32).astype(jnp.bfloat16)
+        shared_sorted[pl.ds(start, 32), :] = picked[:, :128]
+        values_sorted[pl.ds(start, 32), :] = picked[:, 128:]
+        return carry
+
+    lax.fori_loop(0, tiles * 4, sort, 0)
+    inside_left, inside_here = window_masks()
+    scales[0] = across(key_scales(shared_sorted[(tiles - 1) * 128 :, :])[2])
+
+    def attend_tile(tile, carry):
+        left = lax.rem(tile + tiles - 1, tiles)
+        rows = pl.ds(pl.multiple_of(tile * 128, 128), 128)
+        rows_left = pl.ds(pl.multiple_of(left * 128, 128), 128)
+        here, before = shared_sorted[rows, :], shared_sorted[rows_left, :]
+        scale_left = scales[0]
+        scale_here = across(key_scales(here)[2])
+        scales[0] = scale_here
+        pos_here, pos_left = order_rows[pl.ds(tile, 1), :], order_rows[pl.ds(left, 1), :]
+        query_pos = down(pos_here)
+        score_left = masked_scores(
+            dot(here, before, ((1,), (1,))), scale_left, query_pos, pos_left, inside_left
+        )
+        score_here = masked_scores(
+            dot(here, here, ((1,), (1,))), scale_here, query_pos, pos_here, inside_here
+        )
+        highest = jnp.maximum(
+            jnp.max(score_left, axis=-1, keepdims=True), jnp.max(score_here, axis=-1, keepdims=True)
+        )
+        total = highest + jnp.log(
+            jnp.sum(jnp.exp(score_left - highest) + jnp.exp(score_here - highest), axis=-1, keepdims=True)
+        )
+        prob_left = jnp.exp(score_left - total).astype(jnp.bfloat16)
+        prob_here = jnp.exp(score_here - total).astype(jnp.bfloat16)
+        mixed[rows, :128] = dot(prob_left, values_sorted[rows_left, :], ((1,), (0,))) + dot(
+            prob_here, values_sorted[rows, :], ((1,), (0,))
+        )
+        total = jnp.broadcast_to(total, (128, 128))
+        mixed[rows, 128:] = total
+        total_sorted[rows, :] = total
+        return carry
+
+    lax.fori_loop(0, tiles, attend_tile, 0)
+
+    def unsort(tile, carry):
+        totals = []
+        for part in range(4):
+            start = pl.multiple_of(tile * 128 + part * 32, 32)
+            picked = pick_rows(mixed, place, start, 32)
+            mixed_home[pl.ds(start, 32), :] = picked[:, :128].astype(jnp.bfloat16)
+            totals.append(picked[:, 128:])
+        total_home[lax.rem(tile, 8), pl.ds(tile // 8, 1), :] = jnp.concatenate(totals, axis=0).T[:1, :]
+        return carry
+
+    lax.fori_loop(0, tiles, unsort, 0)
+
+
+def attend_back_kernel(
+    tiles, order, place, order_rows, shared_sorted, values_sorted, total_sorted, grad_mixed, grad_total,
+    grad_shared_home, grad_values_home, table, grad_sorted, grad_total_sorted, scales, scale_sums, sums,
+):
+    def load(tile, carry):
+        rows = pl.ds(pl.multiple_of(tile * 128, 128), 128)
+        table[rows, :128] = grad_mixed[rows, :].astype(jnp.float32)
+        table[rows, 128:] = down(grad_total[lax.rem(tile, 8), pl.ds(tile // 8, 1), :])
+        sums[rows, :] = jnp.zeros((128, 256), jnp.float32)
+        return carry
+
+    lax.fori_loop(0, tiles, load, 0)
+
+    def sort(step, carry):
+        start = pl.multiple_of(step * 32, 32)
+        picked = pick_rows(table, order, start, 32)
+        grad_sorted[pl.ds(start, 32), :] = picked[:, :128].astype(jnp.bfloat16)
+        grad_total_sorted[pl.ds(start, 32), :] = picked[:, 128:]
+        return carry
+
+    lax.fori_loop(0, tiles * 4, sort, 0)
+    inside_left, inside_here = window_masks()
+    scales[0] = across(key_scales(shared_sorted[(tiles - 1) * 128 :, :])[2])
+    scale_sums[...] = jnp.zeros_like(scale_sums)
+
+    def back_tile(tile, carry):
+        left = lax.rem(tile + tiles - 1, tiles)
+        rows = pl.ds(pl.multiple_of(tile * 128, 128), 128)
+        rows_left = pl.ds(pl.multiple_of(left * 128, 128), 128)
+        here, before = shared_sorted[rows, :], shared_sorted[rows_left, :]
+        scale_left = scales[0]
+        scale_here = across(key_scales(here)[2])
+        scales[0] = scale_here
+        pos_here, pos_left = order_rows[pl.ds(tile, 1), :], order_rows[pl.ds(left, 1), :]
+        query_pos = down(pos_here)
+        raw_left = dot(here, before, ((1,), (1,)))
+        raw_here = dot(here, here, ((1,), (1,)))
+        total = total_sorted[rows, :]
+        prob_left = jnp.exp(
+            masked_scores(raw_left, scale_left, query_pos, pos_left, inside_left) - total
+        )
+        prob_here = jnp.exp(
+            masked_scores(raw_here, scale_here, query_pos, pos_here, inside_here) - total
+        )
+        grad = grad_sorted[rows, :]
+        grad_prob_left = dot(grad, values_sorted[rows_left, :], ((1,), (1,)))
+        grad_prob_here = dot(grad, values_sorted[rows, :], ((1,), (1,)))
+        inner = jnp.sum(
+            prob_left * grad_prob_left + prob_here * grad_prob_here, axis=-1, keepdims=True
+        )
+        shift = grad_total_sorted[rows, :] - inner
+        keep_left = inside_left & (pos_left < query_pos)
+        keep_here = inside_here & (pos_here < query_pos)
+        grad_score_left = jnp.where(keep_left, prob_left * (grad_prob_left + shift), 0.0)
+        grad_score_here = jnp.where(keep_here, prob_here * (grad_prob_here + shift), 0.0)
+        scale_sums[pl.ds(left, 1), :] += jnp.sum(grad_score_left * raw_left, axis=0, keepdims=True)
+        scale_sums[pl.ds(tile, 1), :] += jnp.sum(grad_score_here * raw_here, axis=0, keepdims=True)
+        grad_raw_left = (grad_score_left * scale_left).astype(jnp.bfloat16)
+        grad_raw_here = (grad_score_here * scale_here).astype(jnp.bfloat16)
+        sums[rows, :128] += (
+            dot(grad_raw_left, before, ((1,), (0,)))
+            + dot(grad_raw_here, here, ((1,), (0,)))
+            + dot(grad_raw_here, here, ((0,), (0,)))
+        )
+        sums[rows_left, :128] += dot(grad_raw_left, here, ((0,), (0,)))
+        sums[rows, 128:] += dot(prob_here.astype(jnp.bfloat16), grad, ((0,), (0,)))
+        sums[rows_left, 128:] += dot(prob_left.astype(jnp.bfloat16), grad, ((0,), (0,)))
+        return carry
+
+    lax.fori_loop(0, tiles, back_tile, 0)
+
+    def finish(tile, carry):
+        rows = pl.ds(pl.multiple_of(tile * 128, 128), 128)
+        keys, mean_square, scale = key_scales(shared_sorted[rows, :])
+        factor = down(scale_sums[pl.ds(tile, 1), :]) * (scale / (mean_square * HEAD_DIM))
+        sums[rows, :128] -= factor * keys
+        return carry
+
+    lax.fori_loop(0, tiles, finish, 0)
+
+    def unsort(step, carry):
+        start = pl.multiple_of(step * 32, 32)
+        picked = pick_rows(sums, place, start, 32).astype(jnp.bfloat16)
+        grad_shared_home[pl.ds(start, 32), :] = picked[:, :128]
+        grad_values_home[pl.ds(start, 32), :] = picked[:, 128:]
+        return carry
+
+    lax.fori_loop(0, tiles * 4, unsort, 0)
+
+
+VMEM = pl.BlockSpec(memory_space=pltpu.VMEM)
+SMEM = pl.BlockSpec(memory_space=pltpu.SMEM)
+
+
+def attend_head(order, place, order_rows, shared, values):
+    length = shared.shape[0]
+    rows = jax.ShapeDtypeStruct((length, HEAD_DIM), jnp.bfloat16)
+    return pl.pallas_call(
+        functools.partial(attend_kernel, length // 128),
+        out_shape=[
+            rows,
+            rows,
+            jax.ShapeDtypeStruct((length, HEAD_DIM), jnp.float32),
+            rows,
+            jax.ShapeDtypeStruct((8, 8, 128), jnp.float32),
+        ],
+        in_specs=[SMEM, SMEM, VMEM, VMEM, VMEM],
+        out_specs=[VMEM] * 5,
+        scratch_shapes=[
+            pltpu.VMEM((length, 256), jnp.float32),
+            pltpu.VMEM((length, 256), jnp.float32),
+            pltpu.VMEM((1, 128, 128), jnp.float32),
+        ],
+        compiler_params=pltpu.CompilerParams(vmem_limit_bytes=40 << 20),
+        name="attend",
+    )(order, place, order_rows, shared, values)
+
+
+def attend_head_back(order, place, order_rows, shared_sorted, values_sorted, total_sorted, grad, grad_total):
+    length = grad.shape[0]
+    rows = jax.ShapeDtypeStruct((length, HEAD_DIM), jnp.bfloat16)
+    return pl.pallas_call(
+        functools.partial(attend_back_kernel, length // 128),
+        out_shape=[rows, rows],
+        in_specs=[SMEM, SMEM] + [VMEM] * 6,
+        out_specs=[VMEM] * 2,
+        scratch_shapes=[
+            pltpu.VMEM((length, 256), jnp.float32),
+            pltpu.VMEM((length, HEAD_DIM), jnp.bfloat16),
+            pltpu.VMEM((length, HEAD_DIM), jnp.float32),
+            pltpu.VMEM((1, 128, 128), jnp.float32),
+            pltpu.VMEM((length // 128, 128), jnp.float32),
+            pltpu.VMEM((length, 256), jnp.float32),
+        ],
+        compiler_params=pltpu.CompilerParams(vmem_limit_bytes=40 << 20),
+        name="attend_back",
+    )(order, place, order_rows, shared_sorted, values_sorted, total_sorted, grad, grad_total)
+
+
+def matmul(a, b, contract=((1,), (0,))):
+    return dot(a, b, contract)
+
+
+def plane_plan(
+    n_seq,
+    n_sub,
+    first_half,
+    second_half,
+    grad_first,
+    grad_second,
+    attend_gain,
+    attend_shift,
+    query_key_weight,
+    value_projection_weight,
+    output_projection_weight,
+    feed_gain,
+    feed_shift,
+    upper_projection_weight,
+    upper_projection_bias,
+    lower_projection_weight,
+    lower_projection_bias,
+    sort_order,
+    sort_place,
+):
+    low, full = jnp.bfloat16, jnp.float32
+    devices, planes, per_plane = n_seq * n_sub, n_seq // 2, 2 * n_sub
+    rows, width = first_half.shape[1:]
+    hidden = upper_projection_weight.shape[2]
+    tokens = devices * rows
+    line = planes * rows
+    part = hidden // per_plane
+    seq, sub = lax.axis_index("seq"), lax.axis_index("sub")
+    me_p = lax.rem(seq, 2) * n_sub + sub
+    trade = functools.partial(exchange, n_seq=n_seq, n_sub=n_sub)
+    shape = jax.ShapeDtypeStruct
+    x1, x2, g1, g2 = (a[0] for a in (first_half, second_half, grad_first, grad_second))
+    wqk, wv, wo = query_key_weight[0], value_projection_weight[0], output_projection_weight[0]
+    wup, wdown = upper_projection_weight[0], lower_projection_weight[0]
+    own = width // devices
+    pair = 2 * HEAD_DIM
+
+    def row_of(*vectors):
+        return jnp.concatenate([v[0].astype(full) for v in vectors])[None]
+
+    small = jnp.concatenate(
+        [
+            sort_order[0, :, 0].astype(full),
+            sort_place[0, :, 0].astype(full),
+            row_of(attend_gain, attend_shift, feed_gain, feed_shift),
+            row_of(upper_projection_bias),
+            jnp.pad(row_of(lower_projection_bias), ((0, 5), (0, rows - own))),
+        ],
+        axis=0,
+    )
+    small = jnp.pad(small, ((0, 16 - small.shape[0]), (0, 0)))
+
+    def columns(array):
+        return (
+            "z",
+            array,
+            shape((planes, own, pair), low),
+            lambda ref, peer: ref.at[:, pl.ds(pl.multiple_of(peer * pair, pair), pair)],
+            lambda ref, here: ref.at[here],
+        )
+
+    def upper_part(chunk):
+        return (
+            "plane",
+            wup,
+            shape((per_plane, own, rows), low),
+            lambda ref, peer: ref.at[
+                :, pl.ds(pl.multiple_of((chunk * per_plane + peer) * rows, rows), rows)
+            ],
+            lambda ref, here: ref.at[here],
+        )
+
+    all_small, wqk_line, wv_line, *wup_rows = trade(
+        [gathered("all", small, devices), columns(wqk), columns(wv)]
+        + [upper_part(chunk) for chunk in range(planes)],
+        "share_small",
+        1,
+    )
+    wup_rows = jnp.concatenate([a.reshape(per_plane * own, rows) for a in wup_rows], axis=1)
+    gain_a, shift_a, gain_f, shift_f = (
+        all_small[:, 8, k * own : (k + 1) * own].reshape(width) for k in range(4)
+    )
+    bias_down = all_small[:, 10, :own].reshape(width)
+    bias_up = jnp.take(
+        all_small[:, 9].reshape(planes, per_plane, rows), me_p, axis=1
+    ).reshape(planes * rows)
+    order_rows = jnp.take(all_small[:, :4], sub, axis=1)
+    order = order_rows.astype(jnp.int32).reshape(tokens)
+    place = jnp.take(all_small[:, 4:8], sub, axis=1).astype(jnp.int32).reshape(tokens)
+
+    normed, attend_pull = jax.vjp(layer_norm, x2, gain_a, shift_a)
+    normed = normed.astype(low)
+
+    def rows_over_plane(array):
+        return (
+            "plane",
+            array,
+            shape((planes, per_plane) + array.shape[1:], low),
+            lambda ref, peer: ref,
+            lambda ref, here: ref.at[:, here],
+        )
+
+    normed_line, wqk_pair, wv_pair, wo_pair = trade(
+        [
+            gathered("z", normed, planes),
+            rows_over_plane(wqk_line),
+            rows_over_plane(wv_line),
+            gathered("plane", wo, per_plane),
+        ],
+        "share_normed",
+        2,
+    )
+    normed_line = normed_line.reshape(line, width)
+    wqk_pair, wv_pair = wqk_pair.reshape(width, pair), wv_pair.reshape(width, pair)
+    wo_pair = wo_pair.reshape(pair, width)
+    shared = matmul(normed_line, wqk_pair).astype(low).reshape(planes, rows, pair)
+    values = matmul(normed_line, wv_pair).astype(low).reshape(planes, rows, pair)
+
+    def to_head(array):
+        return (
+            "plane",
+            array,
+            shape((planes, per_plane, rows, HEAD_DIM), low),
+            lambda ref, peer: ref.at[
+                :, :, pl.ds(pl.multiple_of((peer // n_sub) * HEAD_DIM, HEAD_DIM), HEAD_DIM)
+            ],
+            lambda ref, here: ref.at[:, here],
+        )
+
+    head_shared, head_values, wup_part = trade(
+        [to_head(shared), to_head(values), gathered("z", wup_rows, planes)], "to_heads", 3
+    )
+    wup_part = wup_part.reshape(width, part)
+    shared_sorted, values_sorted, total_sorted, mixed, total = attend_head(
+        order,
+        place,
+        order_rows,
+        head_shared.reshape(tokens, HEAD_DIM),
+        head_values.reshape(tokens, HEAD_DIM),
+    )
+
+    def to_tokens(array):
+        array = array.reshape(planes, per_plane, rows, HEAD_DIM)
+        return (
+            "plane",
+            array,
+            shape((per_plane, planes, rows, HEAD_DIM), low),
+            lambda ref, peer: ref.at[:, peer],
+            lambda ref, here: ref.at[here],
+        )
+
+    mixed, total = trade([to_tokens(mixed), traded("plane", total)], "heads_out", 4)
+    mixed = mixed.reshape(2, n_sub, line, HEAD_DIM).astype(full)
+    total = total[:, :planes].reshape(2, n_sub, line)
+    weights = jnp.exp(total - jnp.max(total, axis=1, keepdims=True))
+    weights = weights / jnp.sum(weights, axis=1, keepdims=True)
+    attended = jnp.sum(weights[..., None] * mixed, axis=1)
+    attended = jnp.swapaxes(attended, 0, 1).reshape(line, pair).astype(low)
+    y1_parts = matmul(attended, wo_pair).astype(low).reshape(planes, rows, width)
+
+    df = g2.astype(low)
+    y1_parts, df_plane = trade(
+        [traded("z", y1_parts), gathered("plane", df, per_plane)], "sum_first", 5
+    )
+    y1 = x1 + jnp.sum(y1_parts.astype(full), axis=0)
+    h2, feed_pull = jax.vjp(layer_norm, y1, gain_f, shift_f)
+    h2_plane, wdown_part = trade(
+        [gathered("plane", h2.astype(low), per_plane), gathered("z", wdown, planes)], "share_feed", 6
+    )
+    h2_plane = h2_plane.reshape(per_plane * rows, width)
+    df_plane = df_plane.reshape(per_plane * rows, width)
+    wdown_part = wdown_part.reshape(part, width)
+    pre = matmul(h2_plane, wup_part) + bias_up
+    act, act_pull = jax.vjp(gelu_exact, pre)
+    act = act.astype(low)
+    y2_parts = matmul(act, wdown_part).astype(low).reshape(per_plane, rows, width)
+    dpre = act_pull(matmul(df_plane, wdown_part, ((1,), (1,))))[0].astype(low)
+    dh2_parts = matmul(dpre, wup_part, ((1,), (1,))).astype(low).reshape(per_plane, rows, width)
+    down_grad = matmul(act, df_plane, ((0,), (0,))).astype(low).reshape(planes, rows, width)
+    up_grad = matmul(h2_plane, dpre, ((0,), (0,))).astype(low).reshape(planes, width // planes, part)
+    up_bias_grad = jnp.sum(dpre.astype(full), axis=0)
+    down_bias_grad = jnp.sum(df.astype(full), axis=0)
+
+    dh2_parts, up_grad = trade([traded("plane", dh2_parts), traded("z", up_grad)], "sum_feed_grad", 7)
+    one_part, feed_gain_grad, feed_shift_grad = feed_pull(jnp.sum(dh2_parts.astype(full), axis=0))
+    g1 = g1 + one_part
+    up_grad = jnp.sum(up_grad.astype(full), axis=0).reshape(per_plane, own, part)
+
+    dout_line, y2_parts = trade(
+        [gathered("z", g1.astype(low), planes), traded("plane", y2_parts)], "share_out_grad", 8
+    )
+    y2 = x2 + (jnp.sum(y2_parts.astype(full), axis=0) + bias_down)
+    dout_line = dout_line.reshape(line, width)
+    datt = matmul(dout_line, wo_pair, ((1,), (1,))).reshape(line, 2, HEAD_DIM)
+    datt = jnp.swapaxes(datt, 0, 1)[:, None]
+    out_grad = matmul(attended, dout_line, ((0,), (0,))).astype(low).reshape(per_plane, own, width)
+    dweights = jnp.sum(datt * mixed, axis=-1)
+    dmixed = (weights[..., None] * datt).astype(low).reshape(per_plane, planes, rows, HEAD_DIM)
+    dtotal = weights * (dweights - jnp.sum(weights * dweights, axis=1, keepdims=True))
+    dtotal = dtotal.astype(low).astype(full).reshape(per_plane, planes, rows)
+    dtotal = jnp.pad(dtotal, ((0, 0), (0, 8 - planes), (0, 0)))
+    back_to_heads = (
+        "plane",
+        dmixed,
+        shape((planes, per_plane, rows, HEAD_DIM), low),
+        lambda ref, peer: ref.at[peer],
+        lambda ref, here: ref.at[:, here],
+    )
+    dmixed, dtotal, out_grad = trade(
+        [back_to_heads, traded("plane", dtotal), traded("plane", out_grad)], "grads_to_heads", 9
+    )
+    dshared, dvalues = attend_head_back(
+        order,
+        place,
+        order_rows,
+        shared_sorted,
+        values_sorted,
+        total_sorted,
+        dmixed.reshape(tokens, HEAD_DIM),
+        dtotal,
+    )
+    dshared, dvalues, down_grad = trade(
+        [to_tokens(dshared), to_tokens(dvalues), traded("z", down_grad)], "grads_from_heads", 10
+    )
+
+    def over_rounds(array):
+        array = jnp.sum(array.reshape(2, n_sub, line, HEAD_DIM).astype(full), axis=1)
+        return jnp.swapaxes(array, 0, 1).reshape(line, pair).astype(low)
+
+    dshared, dvalues = over_rounds(dshared), over_rounds(dvalues)
+    de_parts = matmul(dshared, wqk_pair, ((1,), (1,))) + matmul(dvalues, wv_pair, ((1,), (1,)))
+    de_parts = de_parts.astype(low).reshape(planes, rows, width)
+
+    def to_owners(grad):
+        return (
+            "plane",
+            grad.astype(low).reshape(planes, per_plane, own, pair),
+            shape((per_plane, planes, own, pair), low),
+            lambda ref, peer: ref.at[:, peer],
+            lambda ref, here: ref.at[here],
+        )
+
+    de_parts, shared_grad, value_grad, up_grad = trade(
+        [
+            traded("z", de_parts),
+            to_owners(matmul(normed_line, dshared, ((0,), (0,)))),
+            to_owners(matmul(normed_line, dvalues, ((0,), (0,)))),
+            traded("plane", up_grad),
+        ],
+        "sum_second_grad",
+        11,
+    )
+    two_part, attend_gain_grad, attend_shift_grad = attend_pull(
+        jnp.sum(de_parts.astype(full), axis=0)
+    )
+    g2 = g2 + two_part
+    shared_grad = jnp.sum(shared_grad.astype(full), axis=0)
+    value_grad = jnp.sum(value_grad.astype(full), axis=0)
+    vectors = [attend_gain_grad, attend_shift_grad, feed_gain_grad, feed_shift_grad]
+    vectors = jnp.concatenate([v.reshape(devices, 1, own) for v in vectors], axis=2)
+    down_bias_grad = jnp.pad(
+        down_bias_grad.reshape(devices, 1, own), ((0, 0), (0, 0), (0, rows - own))
+    )
+    up_bias_grad = jnp.where(
+        jnp.arange(per_plane)[None, :, None] == me_p, up_bias_grad.reshape(planes, 1, rows), 0.0
+    ).reshape(devices, 1, rows)
+    vectors = jnp.concatenate(
+        [vectors, down_bias_grad, up_bias_grad, jnp.zeros((devices, 5, rows), full)], axis=1
+    )
+    vectors, shared_grad, value_grad = trade(
+        [traded("all", vectors), traded("z", shared_grad), traded("z", value_grad)], "sum_small", 12
+    )
+    vectors = jnp.sum(vectors, axis=0)
+    pieces = [vectors[0, k * own : (k + 1) * own] for k in range(4)]
+    shared_grad, value_grad = (
+        jnp.swapaxes(a, 0, 1).reshape(own, width) for a in (shared_grad, value_grad)
+    )
+    up_grad = jnp.transpose(up_grad.reshape(per_plane, own, planes, rows), (1, 2, 0, 3))
+    outputs = (
+        y1,
+        y2,
+        g1,
+        g2,
+        pieces[0],
+        pieces[1],
+        shared_grad,
+        value_grad,
+        jnp.sum(out_grad.astype(full), axis=0),
+        pieces[2],
+        pieces[3],
+        up_grad.reshape(own, hidden),
+        vectors[2],
+        jnp.sum(down_grad.astype(full), axis=0),
+        vectors[1, :own],
+    )
+    return tuple((a[None] for a in outputs))
+
+
+def on_device(n_seq, n_sub, *arguments):
+    sequences, rows, width = arguments[0].shape
+    rounds = arguments[-1].shape[1]
+    fits = (
+        sequences == 1
+        and rows == 2 * BLOCK
+        and rounds == n_sub
+        and HEADS == n_seq
+        and width == HEADS * HEAD_DIM
+    )
+    if fits:
+        return plane_plan(n_seq, n_sub, *arguments)
+    return general_plan(*arguments)
+
+
 def solution(mesh):
     return jax.shard_map(
-        on_device,
+        functools.partial(on_device, mesh.shape["seq"], mesh.shape["sub"]),
         mesh=mesh,
         in_specs=(
             P(None, ("seq", "sub"), None),

time: 1420 us -> 480 us (0.34)
  waiting for transfers between devices: 669 us -> 0 us
  Pallas kernels: 0 us -> 369 us
  local copies, waits for them, and re-layouts: 286 us -> 27.8 us
  blocking collectives: 219 us -> 0 us
  starting transfers between devices: 92.5 us -> 0 us
  matrix products: 70.4 us -> 39.5 us
  other arithmetic: 60.4 us -> 41.1 us
  between operations: 16.1 us -> 1.52 us
    reduce_scatter x5 -> x0, waiting for transfers between devices: 496 us -> none  [the longest x1 146 us: spread_grads(): lax.psum_scatter(upper_projection_weight.astype(jnp.bfloat16), ('seq', 's...]
    pallas_call x0 -> x14, Pallas kernels: none -> 369 us  [the longest x12 288 us: exchange(): pl.pallas_call(body, out_shape=[item[2] for item in items], in_specs=[pl....]
    gather x17 -> x0, local copies, waits for them, and re-layouts: 152 us -> none  [the longest x8 98.9 us: gather_slots(): return padded[member[None, :, None], lookup]]
    all_gather x1 -> x0, blocking collectives: 137 us -> none  [collect(): lax.all_gather(upper_projection_bias, ('seq', 'sub'), axis=0, tiled=True)]
    all_to_all x8 -> x0, waiting for transfers between devices: 94.8 us -> none  [the longest x3 52.4 us: trade_rows(): lax.all_to_all(first_part, ('seq', 'sub'), split_axis=0, concat_axis=0, t...]
    all_to_all x8 -> x0, starting transfers between devices: 82.5 us -> none  [the longest x3 39.2 us: trade_rows(): lax.all_to_all(second_part, ('seq', 'sub'), split_axis=0, concat_axis=0,...]
    unnamed x2 -> x0, blocking collectives: 81.7 us -> none
    scatter x2 -> x0, local copies, waits for them, and re-layouts: 49.3 us -> none  [slot_lookup(): lookup = lookup.at[jnp.arange(groups)[:, None], flat_index].set(filler)]
  transfers between devices with their start and end apart: 23 -> 0, of which waited for: 12 -> 0; matrix products, arithmetic and copies ran while one was open for 22% -> 0% of each run, Pallas kernels for 0% -> 0%
where the time goes in v2:
time: 480 us; the launch traced here: 478 us
  Pallas kernels  369 us (77%)
  other arithmetic  41.1 us (9%)
  matrix products  39.5 us (8%)
  local copies, waits for them, and re-layouts  27.8 us (6%)
    pallas_call x12, Pallas kernels, exchange(): pl.pallas_call(body, out_shape=[item[2] for item in items], in_specs=[pl....  288 us
    pallas_call x1, Pallas kernels, attend_head_back(): pl.pallas_call(functools.partial(attend_back_kernel, length // 128), out_...  44.4 us
    dot_general x15, matrix products, dot(): lax.dot_general(a, b, (contract, ((), ())), preferred_element_type=jnp.fl...  39.5 us
    pallas_call x1, Pallas kernels, attend_head(): pl.pallas_call(functools.partial(attend_kernel, length // 128), out_shape...  35.7 us
    unnamed x118, local copies, waits for them, and re-layouts  14.1 us

profile of v2, /device:TPU:0, one launch (start us, length us, event | category | flops | bytes accessed | tf_op | source)
XLA Modules:
  0.0 478.5 jit_solution(12104101448949082627)
XLA Ops:
  2.9 1.9 concatenate.17.refs_0_
  4.7 19.1 %share_small.1 = (f32[32,16,128]{2,1,0:T(8,128)}, bf16[4,32,256]{2,1,0:T(8,128)(2,1)}, bf16[4,32,256]{2,1,0:T(8,128)(2,1)}, bf16[8,32,128]{2,1,0:T(8,128)(2,1)},...) custom-call(f32[16,128]{1,0:T(8,128)} %concatenate.17.refs_0_, ...), custom_call_target="tpu_custom_call" | custom-call | tf_op jit(solution)/shard_map/share_small/pallas_call | solution.py:558
  23.8 1.5 slice_reduce_fusion
  27.8 24.1 %share_normed.1 = (bf16[4,128,1024]{2,1,0:T(8,128)(2,1)}, bf16[4,8,32,256]{3,2,1,0:T(8,128)(2,1)}, bf16[4,8,32,256]{3,2,1,0:T(8,128)(2,1)}, bf16[8,32,1024]{2,1,0:T(8,128)(2,1)}) custom-call(bf16[128,1024]{1,0:T(8,128)(2,1)} %add_convert_fusion.3.refs_0_, bf16[4,32,256]{2,1,0:T(8,128)(2,1)} %get-tuple-element.61.refs_1_, ...), custom_call_target="tpu_custom_call" | custom-call | tf_op jit(solution)/shard_map/share_normed/pallas_call | solution.py:558
  51.9 2.5 convolution_convert_fusion.8
  54.4 2.5 convolution_convert_fusion.9
  57.7 30.9 %to_heads.1 = (bf16[4,8,128,128]{3,2,1,0:T(8,128)(2,1)}, bf16[4,8,128,128]{3,2,1,0:T(8,128)(2,1)}, bf16[4,256,512]{2,1,0:T(8,128)(2,1)}) custom-call(bf16[4,128,256]{2,1,0:T(8,128)(2,1)} %bitcast.210, bf16[4,128,256]{2,1,0:T(8,128)(2,1)} %bitcast.209, bf16[256,512]{1,0:T(8,128)(2,1)} %pad_maximum_fusion.refs_2_), custom_call_target="tpu_custom_call" | custom-call | tf_op jit(solution)/shard_map/to_heads/pallas_call | solution.py:558
  88.8 1.2 copy-done.2
  90.0 1.2 copy-done.3
  91.3 35.7 %attend.1 = (bf16[4096,128]{1,0:T(8,128)(2,1)S(1)}, bf16[4096,128]{1,0:T(8,128)(2,1)S(1)}, f32[4096,128]{1,0:T(8,128)S(1)}, bf16[4096,128]{1,0:T(8,128)(2,1)S(1)}, f32[8,8,128]{2,1,0:T(8,128)S(1)}) custom-call(s32[4096]{0:T(1024)S(1)} %get-tuple-element.152.order, s32[4096]{0:T(1024)S(1)} %convert_bitcast_fusion.2.place, ...), custom_call_target="tpu_custom_call" | custom-call | tf_op jit(solution)/shard_map/attend/pallas_call | solution.py:787
  129.5 15.5 %heads_out.1 = (bf16[8,4,128,128]{3,2,1,0:T(8,128)(2,1)}, f32[8,8,128]{2,1,0:T(8,128)}) custom-call(bf16[4,8,128,128]{3,2,1,0:T(8,128)(2,1)} %bitcast.163, f32[8,8,128]{2,1,0:T(8,128)} %copy-done.8), custom_call_target="tpu_custom_call" | custom-call | tf_op jit(solution)/shard_map/heads_out/pallas_call | solution.py:558
  145.9 2.5 multiply_reduce_fusion.1
  149.5 2.5 convolution_convert_fusion.4
  152.8 27.1 %sum_first.1 = (bf16[4,128,1024]{2,1,0:T(8,128)(2,1)}, bf16[8,128,1024]{2,1,0:T(8,128)(2,1)}) custom-call(bf16[4,128,1024]{2,1,0:T(8,128)(2,1)} %bitcast.172, bf16[128,1024]{1,0:T(8,128)(2,1)} %get-tuple-element.143.refs_1_), custom_call_target="tpu_custom_call" | custom-call | tf_op jit(solution)/shard_map/sum_first/pallas_call | solution.py:558
  179.9 1.5 convert_reduce_fusion.8
  181.4 1.4 fusion.27
  184.4 1.9 add_convert_fusion.2.refs_0_
  186.3 26.8 %share_feed.1 = (bf16[8,128,1024]{2,1,0:T(8,128)(2,1)}, bf16[4,128,1024]{2,1,0:T(8,128)(2,1)}) custom-call(bf16[128,1024]{1,0:T(8,128)(2,1)} %add_convert_fusion.2.refs_0_, bf16[128,1024]{1,0:T(8,128)(2,1)} %bitcast.211), custom_call_target="tpu_custom_call" | custom-call | tf_op jit(solution)/shard_map/share_feed/pallas_call | solution.py:558
  213.1 4.4 fusion.29
  218.5 8.9 %convert_reduce_fusion.6 = (f32[512]{0:T(512)}, bf16[1024,512]{1,0:T(8,128)(2,1)S(1)}, f32[1024,512]{1,0:T(8,128)S(1)}) fusion(f32[1024,512]{1,0:T(8,128)} %fusion.29, f32[512]{0:T(512)S(1)} %bitcast.225, bf16[1024,1024]{1,0:T(8,128)(2,1)} %bitcast.193, bf16[512,1024]{1,0:T(8,128)(2,1)} %bitcast.238), kind=kOutput, calls=%fused_computation.9 | convolution fusion | flops 1113062912 | bytes 8392704 | tf_op jit(solution)/shard_map/dot_general | solution.py:598
  228.9 2.2 convolution_convert_fusion.2
  231.2 2.6 convolution_convert_fusion
  233.8 2.3 convolution_convert_fusion.3
  236.0 2.6 convolution_convert_fusion.1
  238.7 26.6 %sum_feed_grad.1 = (bf16[8,128,1024]{2,1,0:T(8,128)(2,1)}, bf16[4,256,512]{2,1,0:T(8,128)(2,1)}) custom-call(bf16[8,128,1024]{2,1,0:T(8,128)(2,1)} %bitcast.192, bf16[4,256,512]{2,1,0:T(8,128)(2,1)} %bitcast.198), custom_call_target="tpu_custom_call" | custom-call | tf_op jit(solution)/shard_map/sum_feed_grad/pallas_call | solution.py:558
  265.4 2.6 convert_reduce_fusion
  269.6 26.7 %share_out_grad.1 = (bf16[4,128,1024]{2,1,0:T(8,128)(2,1)}, bf16[8,128,1024]{2,1,0:T(8,128)(2,1)}) custom-call(bf16[128,1024]{1,0:T(8,128)(2,1)} %fusion.15.refs_0_, bf16[8,128,1024]{2,1,0:T(8,128)(2,1)} %bitcast.191), custom_call_target="tpu_custom_call" | custom-call | tf_op jit(solution)/shard_map/share_out_grad/pallas_call | solution.py:558
  296.3 2.5 convolution_convert_fusion.7
  298.8 1.9 convolution_bitcast_fusion
  300.9 1.3 copy-done.10
  303.0 2.7 multiply_convert_fusion.refs_0_
  306.3 21.3 %grads_to_heads.1 = (bf16[4,8,128,128]{3,2,1,0:T(8,128)(2,1)}, f32[8,8,128]{2,1,0:T(8,128)}, bf16[8,32,1024]{2,1,0:T(8,128)(2,1)}) custom-call(bf16[8,4,128,128]{3,2,1,0:T(8,128)(2,1)} %multiply_convert_fusion.refs_0_, f32[8,8,128]{2,1,0:T(8,128)} %pad_convert_fusion.refs_1_, bf16[8,32,1024]{2,1,0:T(8,128)(2,1)} %bitcast.187), custom_call_target="tpu_custom_call" | custom-call | tf_op jit(solution)/shard_map/grads_to_heads/pallas_call | solution.py:558
  327.7 1.2 copy-done.6
  328.9 1.2 copy-done.7
  330.9 44.4 %attend_back.1 = (bf16[4096,128]{1,0:T(8,128)(2,1)S(1)}, bf16[4096,128]{1,0:T(8,128)(2,1)S(1)}) custom-call(s32[4096]{0:T(1024)S(1)} %get-tuple-element.152.order, s32[4096]{0:T(1024)S(1)} %convert_bitcast_fusion.2.place, f32[32,128]{1,0:T(8,128)S(1)} %get-tuple-element.153.order_rows, bf16[4096,128]{1,0:T(8,128)(2,1)S(1)} %get-tuple-element.84.shared_sorted, ...), custom_call_target="tpu_custom_call" | custom-call | tf_op jit(solution)/shard_map/attend_back/pallas_call | solution.py:811
  377.3 26.9 %grads_from_heads.1 = (bf16[8,4,128,128]{3,2,1,0:T(8,128)(2,1)}, bf16[8,4,128,128]{3,2,1,0:T(8,128)(2,1)}, bf16[4,128,1024]{2,1,0:T(8,128)(2,1)}) custom-call(bf16[4,8,128,128]{3,2,1,0:T(8,128)(2,1)} %bitcast.159, bf16[4,8,128,128]{3,2,1,0:T(8,128)(2,1)} %bitcast.160, bf16[4,128,1024]{2,1,0:T(8,128)(2,1)} %bitcast.175), custom_call_target="tpu_custom_call" | custom-call | tf_op jit(solution)/shard_map/grads_from_heads/pallas_call | solution.py:558
  404.2 1.6 reduce.5
  405.9 1.3 convolution_convert_fusion.5
  407.6 1.3 convolution_convert_fusion.6
  409.4 1.5 add_convert_fusion
  411.9 23.5 %sum_second_grad.1 = (bf16[4,128,1024]{2,1,0:T(8,128)(2,1)}, bf16[8,4,32,256]{3,2,1,0:T(8,128)(2,1)}, bf16[8,4,32,256]{3,2,1,0:T(8,128)(2,1)}, f32[8,32,512]{2,1,0:T(8,128)}) custom-call(bf16[4,128,1024]{2,1,0:T(8,128)(2,1)} %bitcast.176, bf16[4,8,32,256]{3,2,1,0:T(8,128)(2,1)} %bitcast.189, bf16[4,8,32,256]{3,2,1,0:T(8,128)(2,1)} %bitcast.188, ...), custom_call_target="tpu_custom_call" | custom-call | tf_op jit(solution)/shard_map/sum_second_grad/pallas_call | solution.py:558
  435.4 1.7 convert_reduce_fusion.3
  439.3 1.8 convert_reduce_fusion.10.refs_2_
  441.0 1.8 convert_reduce_fusion.11.refs_1_
  442.8 19.9 %sum_small.1 = (f32[32,8,128]{2,1,0:T(8,128)}, f32[4,32,256]{2,1,0:T(8,128)}, f32[4,32,256]{2,1,0:T(8,128)}) custom-call(f32[32,8,128]{2,1,0:T(8,128)} %fusion.17.refs_0_, f32[4,32,256]{2,1,0:T(8,128)} %convert_reduce_fusion.11.refs_1_, f32[4,32,256]{2,1,0:T(8,128)} %convert_reduce_fusion.10.refs_2_), custom_call_target="tpu_custom_call" | custom-call | tf_op jit(solution)/shard_map/sum_small/pallas_call | solution.py:558
  469.5 2.4 fusion.10
  473.3 2.3 convert_reduce_fusion.5
  475.6 1.8 convert_reduce_fusion.9
  (196 shorter events, 34.1 us)
Async XLA Ops:
  0.6 26.0 %copy-start.11 = (f32[1,128,1024]{2,1,0:T(8,128)S(1)}, f32[1,128,1024]{2,1,0:T(8,128)}, u32[]{:S(2)}) copy-start(f32[1,128,1024]{2,1,0:T(8,128)} %param.20) | copy-start | bytes 1572868
  26.8 30.1 %copy-start.52 = (f32[128]{0:T(128)}, f32[128]{0:T(128)S(1)}, u32[]{:S(2)}) copy-start(f32[128]{0:T(128)S(1)} %multiply_reduce_fusion.7) | copy-start | bytes 1540
  26.9 30.1 %copy-start.45 = (f32[128]{0:T(128)}, f32[128]{0:T(128)S(1)}, u32[]{:S(2)}) copy-start(f32[128]{0:T(128)S(1)} %fusion.23) | copy-start | bytes 1540
  27.7 29.2 %copy-start.34 = (bf16[8,32,128]{2,1,0:T(8,128)(2,1)S(1)}, bf16[8,32,128]{2,1,0:T(8,128)(2,1)}, u32[]{:S(2)}) copy-start(bf16[8,32,128]{2,1,0:T(8,128)(2,1)} %get-tuple-element.66) | copy-start | bytes 196612
  27.8 29.2 %copy-start.35 = (bf16[8,32,128]{2,1,0:T(8,128)(2,1)S(1)}, bf16[8,32,128]{2,1,0:T(8,128)(2,1)}, u32[]{:S(2)}) copy-start(bf16[8,32,128]{2,1,0:T(8,128)(2,1)} %get-tuple-element.67) | copy-start | bytes 196612
  27.8 29.2 %copy-start.36 = (bf16[8,32,128]{2,1,0:T(8,128)(2,1)S(1)}, bf16[8,32,128]{2,1,0:T(8,128)(2,1)}, u32[]{:S(2)}) copy-start(bf16[8,32,128]{2,1,0:T(8,128)(2,1)} %get-tuple-element.68) | copy-start | bytes 196612
  27.8 29.2 %copy-start.37 = (bf16[8,32,128]{2,1,0:T(8,128)(2,1)S(1)}, bf16[8,32,128]{2,1,0:T(8,128)(2,1)}, u32[]{:S(2)}) copy-start(bf16[8,32,128]{2,1,0:T(8,128)(2,1)} %get-tuple-element.69) | copy-start | bytes 196612
  54.4 34.2 %copy-start.30 = (f32[32,16,128]{2,1,0:T(8,128)S(1)}, f32[32,16,128]{2,1,0:T(8,128)}, u32[]{:S(2)}) copy-start(f32[32,16,128]{2,1,0:T(8,128)} %get-tuple-element.60) | copy-start | bytes 786436
  88.8 1.2 copy-start.2
  149.5 2.6 copy-start.26
  181.3 2.4 copy-start.17
  182.7 34.8 %copy-start.39 = (f32[128]{0:T(128)}, f32[128]{0:T(128)S(1)}, u32[]{:S(2)}) copy-start(f32[128]{0:T(128)S(1)} %broadcast_multiply_fusion) | copy-start | bytes 1540
  184.2 33.3 %copy-start.42 = (f32[128]{0:T(128)}, f32[128]{0:T(128)S(1)}, u32[]{:S(2)}) copy-start(f32[128]{0:T(128)S(1)} %fusion.24) | copy-start | bytes 1540
  218.4 8.9 %copy-start.21 = (f32[1024,512]{1,0:T(8,128)S(1)}, f32[1024,512]{1,0:T(8,128)}, u32[]{:S(2)}) copy-start(f32[1024,512]{1,0:T(8,128)} %fusion.29) | copy-start | bytes 6291460
  227.3 1.6 copy-start.23
  228.9 2.3 copy-start.58
  231.2 2.6 copy-start.56
  233.8 2.3 copy-start.57
  265.3 2.6 copy-start.14
  265.4 2.6 copy-start.40
  265.4 2.6 copy-start.43
  265.4 2.9 copy-start.55
  265.4 3.4 copy-start.24
  268.3 28.0 %copy-start.48 = (f32[128]{0:T(128)}, f32[128]{0:T(128)S(1)}, u32[]{:S(2)}) copy-start(f32[128]{0:T(128)S(1)} %multiply_multiply_fusion.6) | copy-start | bytes 1540
  268.8 30.0 %copy-start.50 = (f32[128]{0:T(128)}, f32[128]{0:T(128)S(1)}, u32[]{:S(2)}) copy-start(f32[128]{0:T(128)S(1)} %negate_multiply_fusion.2) | copy-start | bytes 1540
  298.8 3.4 copy-start.20
  300.9 1.3 copy-start.10
  300.9 2.1 copy-start.38
  327.6 1.2 copy-start.6
  377.3 28.7 %copy-start.19 = (bf16[4,128,1024]{2,1,0:T(8,128)(2,1)S(1)}, bf16[4,128,1024]{2,1,0:T(8,128)(2,1)}, u32[]{:S(2)}) copy-start(bf16[4,128,1024]{2,1,0:T(8,128)(2,1)} %get-tuple-element.63) | copy-start | bytes 3145732
  404.2 3.0 copy-start.29
  407.2 1.7 copy-start.33
  407.6 1.8 copy-start.31
  409.4 1.5 copy-start.28
  411.9 25.2 %copy-start.12 = (f32[1,128,1024]{2,1,0:T(8,128)S(1)}, f32[1,128,1024]{2,1,0:T(8,128)}, u32[]{:S(2)}) copy-start(f32[1,128,1024]{2,1,0:T(8,128)} %param.20) | copy-start | bytes 1572868
  411.9 25.4 %copy-start.53 = (f32[128]{0:T(128)S(1)}, f32[128]{0:T(128)}, u32[]{:S(2)}) copy-start(f32[128]{0:T(128)} %copy-done.52) | copy-start | bytes 1540
  411.9 25.4 %copy-start.46 = (f32[128]{0:T(128)S(1)}, f32[128]{0:T(128)}, u32[]{:S(2)}) copy-start(f32[128]{0:T(128)} %copy-done.45) | copy-start | bytes 1540
  435.4 2.6 copy-start.47
  437.3 30.9 %copy-start.22 = (bf16[8,128,1024]{2,1,0:T(8,128)(2,1)S(1)}, bf16[8,128,1024]{2,1,0:T(8,128)(2,1)}, u32[]{:S(2)}) copy-start(bf16[8,128,1024]{2,1,0:T(8,128)(2,1)} %get-tuple-element.83) | copy-start | bytes 6291460
  469.4 2.4 copy-start.32
  472.0 5.3 %copy-start.16 = (f32[128,1024]{1,0:T(8,128)S(1)}, f32[128,1024]{1,0:T(8,128)}, u32[]{:S(2)}) copy-start(f32[128,1024]{1,0:T(8,128)} %copy-done.15) | copy-start | bytes 1572868
  472.0 5.3 %copy-start.18 = (f32[128,1024]{1,0:T(8,128)S(1)}, f32[128,1024]{1,0:T(8,128)}, u32[]{:S(2)}) copy-start(f32[128,1024]{1,0:T(8,128)} %copy-done.17) | copy-start | bytes 1572868
  472.0 5.3 %copy-start.25 = (f32[1,128,1024]{2,1,0:T(8,128)S(1)}, f32[1,128,1024]{2,1,0:T(8,128)}, u32[]{:S(2)}) copy-start(f32[1,128,1024]{2,1,0:T(8,128)} %param.21) | copy-start | bytes 1572868
  472.0 5.3 %copy-start.27 = (f32[1,128,1024]{2,1,0:T(8,128)S(1)}, f32[1,128,1024]{2,1,0:T(8,128)}, u32[]{:S(2)}) copy-start(f32[1,128,1024]{2,1,0:T(8,128)} %param.19) | copy-start | bytes 1572868
  472.1 5.3 %copy-start.41 = (f32[128]{0:T(128)S(1)}, f32[128]{0:T(128)}, u32[]{:S(2)}) copy-start(f32[128]{0:T(128)} %copy-done.39) | copy-start | bytes 1540
  472.1 5.3 %copy-start.44 = (f32[128]{0:T(128)S(1)}, f32[128]{0:T(128)}, u32[]{:S(2)}) copy-start(f32[128]{0:T(128)} %copy-done.42) | copy-start | bytes 1540
  472.1 5.3 %copy-start.49 = (f32[128]{0:T(128)S(1)}, f32[128]{0:T(128)}, u32[]{:S(2)}) copy-start(f32[128]{0:T(128)} %copy-done.48) | copy-start | bytes 1540
  472.1 5.3 %copy-start.51 = (f32[128]{0:T(128)S(1)}, f32[128]{0:T(128)}, u32[]{:S(2)}) copy-start(f32[128]{0:T(128)} %copy-done.50) | copy-start | bytes 1540
  (11 other events, 9.9 us)

commit v3 on v1

--- a/solution.py
+++ b/solution.py
@@ -1,11 +1,18 @@
+import functools
+
 import jax
 import jax.numpy as jnp
 from jax import lax
+from jax.experimental import pallas as pl
+from jax.experimental.pallas import tpu as pltpu
 from jax.sharding import PartitionSpec as P
 
 HEADS = 8
 HEAD_DIM = 128
 BLOCK = 64
+LATER = -1000000000.0
+SELF = -100000.0
+OUTSIDE = -3e38
 
 
 def from_behind(block, axis, distance):
@@ -440,7 +447,7 @@
     return (top_one, top_two, total_one, total_two, level_grads)
 
 
-def on_device(
+def general_plan(
     first_half,
     second_half,
     grad_first,
@@ -485,9 +492,846 @@
     return (first_out, second_out, first_grad, second_grad) + stacked
 
 
+class Links:
+    def __init__(self, planes, send, receive, local):
+        self.send, self.receive, self.local = send, receive, local
+        self.used, self.used_local = 0, 0
+        self.planes = planes
+        seq, sub = lax.axis_index("seq"), lax.axis_index("sub")
+        self.z, self.x = seq // 2, lax.rem(seq, 2)
+        self.y, self.core = sub // 2, lax.rem(sub, 2)
+        self.p = self.x * 4 + sub
+
+    def near(self, step):
+        x = 1 - self.x if step & 4 else self.x
+        y = 1 - self.y if step & 2 else self.y
+        core = 1 - self.core if step & 1 else self.core
+        return (self.z * 2 + x, y * 2 + core), x * 4 + y * 2 + core
+
+    def along(self, step):
+        to = lax.rem(self.z + step, self.planes)
+        back = lax.rem(self.z + self.planes - step, self.planes)
+        return (to * 2 + self.x, self.y * 2 + self.core), to, back
+
+    def greet(self):
+        barrier = pltpu.get_barrier_semaphore()
+        targets = [self.near(step)[0] for step in range(1, 8)]
+        targets += [self.along(step)[0] for step in range(1, self.planes)]
+        for target in targets:
+            pl.semaphore_signal(barrier, inc=1, device_id=target, device_id_type=pl.DeviceIdType.MESH)
+        self.greeted = len(targets)
+
+    def meet(self):
+        pl.semaphore_wait(pltpu.get_barrier_semaphore(), self.greeted)
+
+    def push(self, source, target, device):
+        copy = pltpu.make_async_remote_copy(
+            src_ref=source,
+            dst_ref=target,
+            send_sem=self.send.at[self.used],
+            recv_sem=self.receive.at[self.used],
+            device_id=device,
+            device_id_type=pl.DeviceIdType.MESH,
+        )
+        self.used += 1
+        copy.start()
+        return copy
+
+    def keep(self, source, target):
+        copy = pltpu.make_async_copy(source, target, self.local.at[self.used_local])
+        self.used_local += 1
+        copy.start()
+        return copy
+
+
+COPIES = 96
+
+
+def link_scratch():
+    return [
+        pltpu.SemaphoreType.DMA((COPIES,)),
+        pltpu.SemaphoreType.DMA((COPIES,)),
+        pltpu.SemaphoreType.DMA((16,)),
+    ]
+
+
+def along_z(source, target):
+    def transfer(links, here, there):
+        own = links.keep(source(here, links.z), target(there, links.z))
+        copies = []
+        for step in range(1, links.planes):
+            device, to, _ = links.along(step)
+            copies.append(links.push(source(here, to), target(there, links.z), device))
+        yield
+        own.wait()
+        for copy in copies:
+            copy.wait()
+
+    return transfer
+
+
+def over_plane(source, target):
+    def transfer(links, here, there):
+        own = links.keep(source(here, links.p), target(there, links.p))
+        copies = []
+        for step in (6, 7, 4, 5, 2, 3, 1):
+            device, to = links.near(step)
+            copies.append(links.push(source(here, to), target(there, links.p), device))
+        yield
+        own.wait()
+        for copy in copies:
+            copy.wait()
+
+    return transfer
+
+
+def over_chips(source, target):
+    def transfer(links, here, there):
+        own = links.keep(source(here, links.p), target(there, links.p))
+        copies = []
+        for step in (6, 4, 2):
+            device, to = links.near(step)
+            copies.append(links.push(source(here, to), target(there, links.p), device))
+        sibling, _ = links.near(1)
+        passed = [links.push(source(here, links.p), target(there, links.p), sibling)]
+        yield
+        for step, copy in zip((6, 4, 2), copies):
+            copy.wait_recv()
+            _, sender = links.near(step)
+            passed.append(links.push(target(there, sender), target(there, sender), sibling))
+        yield
+        own.wait()
+        for copy in copies:
+            copy.wait_send()
+        for copy in passed:
+            copy.wait()
+
+    return transfer
+
+
+def everywhere(links, here, there):
+    own = links.keep(here, there.at[links.z, links.p])
+    copies = []
+    for step in (6, 7, 4, 5, 2, 3, 1):
+        copies.append(links.push(here, there.at[links.z, links.p], links.near(step)[0]))
+    yield
+    own.wait()
+    for copy in copies:
+        copy.wait()
+    copies = []
+    for step in range(1, links.planes):
+        copies.append(links.push(there.at[links.z], there.at[links.z], links.along(step)[0]))
+    yield
+    for copy in copies:
+        copy.wait()
+
+
+def drive(transfers):
+    while transfers:
+        left = []
+        for transfer in transfers:
+            try:
+                next(transfer)
+                left.append(transfer)
+            except StopIteration:
+                pass
+        transfers = left
+
+
+def exchange(items, name, collective_id, planes):
+    count = len(items)
+
+    def body(*refs):
+        links = Links(planes, *refs[2 * count :])
+        links.greet()
+        links.meet()
+        drive([item[0](links, refs[k], refs[count + k]) for k, item in enumerate(items)])
+
+    return pl.pallas_call(
+        body,
+        out_shape=[item[2] for item in items],
+        in_specs=[pl.BlockSpec(memory_space=pl.ANY)] * count,
+        out_specs=[pl.BlockSpec(memory_space=pl.ANY)] * count,
+        scratch_shapes=link_scratch(),
+        compiler_params=pltpu.CompilerParams(collective_id=collective_id, has_side_effects=True),
+        name=name,
+    )(*[item[1] for item in items])
+
+
+def whole(ref, index):
+    return ref
+
+
+def block(ref, index):
+    return ref.at[index]
+
+
+def second(ref, index):
+    return ref.at[:, index]
+
+
+def like(kind, array, *shape):
+    return (kind, array, jax.ShapeDtypeStruct(shape, array.dtype))
+
+
+def pick_rows(table, index_ref, start, count):
+    return jnp.concatenate(
+        [table[pl.ds(index_ref[start + row], 1), :] for row in range(count)], axis=0
+    )
+
+
+def across(column):
+    return jnp.broadcast_to(column, (128, 128)).T
+
+
+def down(row):
+    return jnp.broadcast_to(row, (128, 128)).T
+
+
+def dot(a, b, contract):
+    return lax.dot_general(a, b, (contract, ((), ())), preferred_element_type=jnp.float32)
+
+
+def window_masks():
+    query = lax.broadcasted_iota(jnp.int32, (128, 128), 0) // BLOCK
+    key = lax.broadcasted_iota(jnp.int32, (128, 128), 1) // BLOCK
+    return (query == 0) & (key == 1), key <= query
+
+
+def key_scales(keys):
+    rows = keys.astype(jnp.float32)
+    mean_square = jnp.mean(rows * rows, axis=-1, keepdims=True) + 1e-06
+    return rows, mean_square, lax.rsqrt(mean_square) / HEAD_DIM
+
+
+def masked_scores(raw, scale, query_pos, key_pos, inside):
+    scores = jnp.where(
+        key_pos > query_pos, LATER, jnp.where(key_pos == query_pos, SELF, raw * scale)
+    )
+    return jnp.where(inside, scores, OUTSIDE)
+
+
+def tile_rows(tile):
+    return pl.ds(pl.multiple_of(tile * 128, 128), 128)
+
+
+def sort_pair(order, table, first, second, tile):
+    for part in range(4):
+        start = pl.multiple_of(tile * 128 + part * 32, 32)
+        picked = pick_rows(table, order, start, 32)
+        first[pl.ds(start, 32), :] = picked[:, :128].astype(first.dtype)
+        second[pl.ds(start, 32), :] = picked[:, 128:].astype(second.dtype)
+
+
+def attend_kernel(
+    tiles, unroll, order, place, order_rows, shared, values, shared_sorted, values_sorted, total_sorted,
+    mixed_home, total_home, table, mixed, scales,
+):
+    def load(tile, carry):
+        rows = tile_rows(tile)
+        table[rows, :128] = shared[rows, :].astype(jnp.float32)
+        table[rows, 128:] = values[rows, :].astype(jnp.float32)
+        return carry
+
+    lax.fori_loop(0, tiles, load, 0)
+    sort = functools.partial(sort_pair, order, table, shared_sorted, values_sorted)
+    for tile in [tiles - 1] + list(range(unroll)):
+        sort(tile)
+    inside_left, inside_here = window_masks()
+    scales[0] = across(key_scales(shared_sorted[(tiles - 1) * 128 :, :])[2])
+
+    def attend_tiles(step, carry):
+        first = step * unroll
+        numbers = [lax.rem(first + tiles - 1, tiles)] + [first + k for k in range(unroll)]
+        keys = [shared_sorted[tile_rows(t), :] for t in numbers]
+        vals = [values_sorted[tile_rows(t), :] for t in numbers]
+        places = [order_rows[pl.ds(t, 1), :] for t in numbers]
+        scale = [scales[0]] + [across(key_scales(k)[2]) for k in keys[1:]]
+        scales[0] = scale[-1]
+        for k in range(unroll):
+            sort(lax.rem(first + unroll + k, tiles))
+        for k in range(unroll):
+            rows = tile_rows(first + k)
+            query_pos = down(places[k + 1])
+            score_left = masked_scores(
+                dot(keys[k + 1], keys[k], ((1,), (1,))), scale[k], query_pos, places[k], inside_left
+            )
+            score_here = masked_scores(
+                dot(keys[k + 1], keys[k + 1], ((1,), (1,))),
+                scale[k + 1],
+                query_pos,
+                places[k + 1],
+                inside_here,
+            )
+            highest = jnp.max(jnp.maximum(score_left, score_here), axis=-1, keepdims=True)
+            total = highest + jnp.log(
+                jnp.sum(
+                    jnp.exp(score_left - highest) + jnp.exp(score_here - highest),
+                    axis=-1,
+                    keepdims=True,
+                )
+            )
+            prob_left = jnp.exp(score_left - total).astype(jnp.bfloat16)
+            prob_here = jnp.exp(score_here - total).astype(jnp.bfloat16)
+            mixed[rows, :128] = dot(prob_left, vals[k], ((1,), (0,))) + dot(
+                prob_here, vals[k + 1], ((1,), (0,))
+            )
+            total = jnp.broadcast_to(total, (128, 128))
+            mixed[rows, 128:] = total
+            total_sorted[rows, :] = total
+        return carry
+
+    lax.fori_loop(0, tiles // unroll, attend_tiles, 0)
+
+    def unsort(tile, carry):
+        totals = []
+        for part in range(4):
+            start = pl.multiple_of(tile * 128 + part * 32, 32)
+            picked = pick_rows(mixed, place, start, 32)
+            mixed_home[pl.ds(start, 32), :] = picked[:, :128].astype(jnp.bfloat16)
+            totals.append(picked[:, 128:])
+        total_home[lax.rem(tile, 8), pl.ds(tile // 8, 1), :] = jnp.concatenate(totals, axis=0).T[:1, :]
+        return carry
+
+    lax.fori_loop(0, tiles, unsort, 0)
+
+
+def attend_back_kernel(
+    tiles, unroll, order, place, order_rows, shared_sorted, values_sorted, total_sorted, grad_mixed, grad_total,
+    grad_shared_home, grad_values_home, table, grad_sorted, grad_total_sorted, scales, scale_sums, sums,
+):
+    def load(tile, carry):
+        rows = tile_rows(tile)
+        table[rows, :128] = grad_mixed[rows, :].astype(jnp.float32)
+        table[rows, 128:] = down(grad_total[lax.rem(tile, 8), pl.ds(tile // 8, 1), :])
+        return carry
+
+    lax.fori_loop(0, tiles, load, 0)
+    sums[tile_rows(tiles - 1), :] = jnp.zeros((128, 256), jnp.float32)
+    sort = functools.partial(sort_pair, order, table, grad_sorted, grad_total_sorted)
+    for tile in range(unroll):
+        sort(tile)
+    inside_left, inside_here = window_masks()
+    scales[0] = across(key_scales(shared_sorted[(tiles - 1) * 128 :, :])[2])
+    scale_sums[...] = jnp.zeros_like(scale_sums)
+
+    def back_tiles(step, carry):
+        first = step * unroll
+        left = lax.rem(first + tiles - 1, tiles)
+        numbers = [left] + [first + k for k in range(unroll)]
+        keys = [shared_sorted[tile_rows(t), :] for t in numbers]
+        vals = [values_sorted[tile_rows(t), :] for t in numbers]
+        places = [order_rows[pl.ds(t, 1), :] for t in numbers]
+        grads = [grad_sorted[tile_rows(t), :] for t in numbers[1:]]
+        grad_totals = [grad_total_sorted[tile_rows(t), :] for t in numbers[1:]]
+        totals = [total_sorted[tile_rows(t), :] for t in numbers[1:]]
+        scale = [scales[0]] + [across(key_scales(k)[2]) for k in keys[1:]]
+        scales[0] = scale[-1]
+        for k in range(unroll):
+            sort(lax.rem(first + unroll + k, tiles))
+        key_sums, value_sums, scale_parts = [0.0] * (unroll + 1), [0.0] * (unroll + 1), [0.0] * (unroll + 1)
+        for k in range(unroll):
+            here, before, grad = keys[k + 1], keys[k], grads[k]
+            query_pos = down(places[k + 1])
+            raw_left = dot(here, before, ((1,), (1,)))
+            raw_here = dot(here, here, ((1,), (1,)))
+            prob_left = jnp.exp(
+                masked_scores(raw_left, scale[k], query_pos, places[k], inside_left) - totals[k]
+            )
+            prob_here = jnp.exp(
+                masked_scores(raw_here, scale[k + 1], query_pos, places[k + 1], inside_here) - totals[k]
+            )
+            grad_prob_left = dot(grad, vals[k], ((1,), (1,)))
+            grad_prob_here = dot(grad, vals[k + 1], ((1,), (1,)))
+            inner = jnp.sum(
+                prob_left * grad_prob_left + prob_here * grad_prob_here, axis=-1, keepdims=True
+            )
+            shift = grad_totals[k] - inner
+            keep_left = inside_left & (places[k] < query_pos)
+            keep_here = inside_here & (places[k + 1] < query_pos)
+            grad_score_left = jnp.where(keep_left, prob_left * (grad_prob_left + shift), 0.0)
+            grad_score_here = jnp.where(keep_here, prob_here * (grad_prob_here + shift), 0.0)
+            scale_parts[k] += jnp.sum(grad_score_left * raw_left, axis=0, keepdims=True)
+            scale_parts[k + 1] += jnp.sum(grad_score_here * raw_here, axis=0, keepdims=True)
+            grad_raw_left = (grad_score_left * scale[k]).astype(jnp.bfloat16)
+            grad_raw_here = (grad_score_here * scale[k + 1]).astype(jnp.bfloat16)
+            key_sums[k + 1] += (
+                dot(grad_raw_left, before, ((1,), (0,)))
+                + dot(grad_raw_here, here, ((1,), (0,)))
+                + dot(grad_raw_here, here, ((0,), (0,)))
+            )
+            key_sums[k] += dot(grad_raw_left, here, ((0,), (0,)))
+            value_sums[k + 1] += dot(prob_here.astype(jnp.bfloat16), grad, ((0,), (0,)))
+            value_sums[k] += dot(prob_left.astype(jnp.bfloat16), grad, ((0,), (0,)))
+        for k, tile in enumerate(numbers[1:]):
+            sums[tile_rows(tile), :128] = key_sums[k + 1]
+            sums[tile_rows(tile), 128:] = value_sums[k + 1]
+            scale_sums[pl.ds(tile, 1), :] = scale_parts[k + 1]
+        extra = pl.ds(pl.multiple_of(jnp.where(step == 0, tiles, left) * 128, 128), 128)
+        extra_row = pl.ds(jnp.where(step == 0, tiles, left), 1)
+        sums[extra, :128] += key_sums[0]
+        sums[extra, 128:] += value_sums[0]
+        scale_sums[extra_row, :] += scale_parts[0]
+        return carry
+
+    sums[pl.ds(tiles * 128, 128), :] = jnp.zeros((128, 256), jnp.float32)
+    lax.fori_loop(0, tiles // unroll, back_tiles, 0)
+    last = tile_rows(tiles - 1)
+    sums[last, :] += sums[pl.ds(tiles * 128, 128), :]
+    scale_sums[pl.ds(tiles - 1, 1), :] += scale_sums[pl.ds(tiles, 1), :]
+
+    def finish(step, carry):
+        for part in range(2):
+            tile = step * 2 + part
+            rows = tile_rows(tile)
+            keys, mean_square, scale = key_scales(shared_sorted[rows, :])
+            factor = down(scale_sums[pl.ds(tile, 1), :]) * (scale / (mean_square * HEAD_DIM))
+            sums[rows, :128] -= factor * keys
+        return carry
+
+    lax.fori_loop(0, tiles // 2, finish, 0)
+
+    def unsort(tile, carry):
+        sort_pair(place, sums, grad_shared_home, grad_values_home, tile)
+        return carry
+
+    lax.fori_loop(0, tiles, unsort, 0)
+
+
+VMEM = pl.BlockSpec(memory_space=pltpu.VMEM)
+SMEM = pl.BlockSpec(memory_space=pltpu.SMEM)
+ANY = pl.BlockSpec(memory_space=pl.ANY)
+
+
+def beside(kernel, inputs, outputs, scratch, items, planes):
+    count = len(items)
+
+    def body(*refs):
+        refs = list(refs)
+        own, refs = refs[:inputs], refs[inputs:]
+        here, refs = refs[:count], refs[count:]
+        own, refs = own + refs[:outputs], refs[outputs:]
+        there, refs = refs[:count], refs[count:]
+        links = Links(planes, *refs[scratch:])
+        links.greet()
+        links.meet()
+        transfers = [item[0](links, here[k], there[k]) for k, item in enumerate(items)]
+        for transfer in transfers:
+            next(transfer)
+        kernel(*own, *refs[:scratch])
+        drive(transfers)
+
+    return body
+
+
+def attend_head(order, place, order_rows, shared, values, items, collective_id, planes, unroll=2):
+    length = shared.shape[0]
+    rows = jax.ShapeDtypeStruct((length, HEAD_DIM), jnp.bfloat16)
+    scratch = [
+        pltpu.VMEM((length, 256), jnp.float32),
+        pltpu.VMEM((length, 256), jnp.float32),
+        pltpu.VMEM((1, 128, 128), jnp.float32),
+    ]
+    kernel = functools.partial(attend_kernel, length // 128, unroll)
+    return pl.pallas_call(
+        beside(kernel, 5, 5, len(scratch), items, planes),
+        out_shape=[
+            rows,
+            rows,
+            jax.ShapeDtypeStruct((length, HEAD_DIM), jnp.float32),
+            rows,
+            jax.ShapeDtypeStruct((8, 8, 128), jnp.float32),
+        ]
+        + [item[2] for item in items],
+        in_specs=[SMEM, SMEM, VMEM, VMEM, VMEM] + [ANY] * len(items),
+        out_specs=[VMEM] * 5 + [ANY] * len(items),
+        scratch_shapes=scratch + link_scratch(),
+        compiler_params=pltpu.CompilerParams(
+            vmem_limit_bytes=40 << 20, collective_id=collective_id, has_side_effects=True
+        ),
+        name="attend",
+    )(order, place, order_rows, shared, values, *[item[1] for item in items])
+
+
+def attend_head_back(
+    order, place, order_rows, shared_sorted, values_sorted, total_sorted, grad, grad_total,
+    items, collective_id, planes, unroll=2,
+):
+    length = grad.shape[0]
+    rows = jax.ShapeDtypeStruct((length, HEAD_DIM), jnp.bfloat16)
+    scratch = [
+        pltpu.VMEM((length, 256), jnp.float32),
+        pltpu.VMEM((length, HEAD_DIM), jnp.bfloat16),
+        pltpu.VMEM((length, HEAD_DIM), jnp.float32),
+        pltpu.VMEM((1, 128, 128), jnp.float32),
+        pltpu.VMEM((length // 128 + 8, 128), jnp.float32),
+        pltpu.VMEM((length + 128, 256), jnp.float32),
+    ]
+    kernel = functools.partial(attend_back_kernel, length // 128, unroll)
+    return pl.pallas_call(
+        beside(kernel, 8, 2, len(scratch), items, planes),
+        out_shape=[rows, rows] + [item[2] for item in items],
+        in_specs=[SMEM, SMEM] + [VMEM] * 6 + [ANY] * len(items),
+        out_specs=[VMEM] * 2 + [ANY] * len(items),
+        scratch_shapes=scratch + link_scratch(),
+        compiler_params=pltpu.CompilerParams(
+            vmem_limit_bytes=40 << 20, collective_id=collective_id, has_side_effects=True
+        ),
+        name="attend_back",
+    )(
+        order, place, order_rows, shared_sorted, values_sorted, total_sorted, grad, grad_total,
+        *[item[1] for item in items],
+    )
+
+
+def sum_small_kernel(planes, items, *refs):
+    count = len(items)
+    tiles, here, refs = refs[0], refs[1 : 1 + count], refs[1 + count :]
+    result, there, refs = refs[0], refs[1 : 1 + count], refs[1 + count :]
+    arrived, summed, refs = refs[0], refs[1], refs[2:]
+    links = Links(planes, *refs)
+    links.greet()
+    links.meet()
+    transfers = [item[0](links, here[k], there[k]) for k, item in enumerate(items)]
+    small = over_plane(block, block)(links, tiles, arrived)
+    next(small)
+    for transfer in transfers:
+        next(transfer)
+    drive([small])
+    summed[...] = jnp.sum(arrived[...], axis=0)
+    drive([along_z(whole, block)(links, summed, result)] + transfers)
+
+
+def sum_small(tiles, items, collective_id, planes):
+    return pl.pallas_call(
+        functools.partial(sum_small_kernel, planes, items),
+        out_shape=[jax.ShapeDtypeStruct((planes,) + tiles.shape[1:], tiles.dtype)]
+        + [item[2] for item in items],
+        in_specs=[VMEM] + [ANY] * len(items),
+        out_specs=[VMEM] + [ANY] * len(items),
+        scratch_shapes=[
+            pltpu.VMEM(tiles.shape, tiles.dtype),
+            pltpu.VMEM(tiles.shape[1:], tiles.dtype),
+        ]
+        + link_scratch(),
+        compiler_params=pltpu.CompilerParams(collective_id=collective_id, has_side_effects=True),
+        name="sum_small",
+    )(tiles, *[item[1] for item in items])
+
+
+def matmul(a, b, contract=((1,), (0,))):
+    return dot(a, b, contract)
+
+
+def plane_plan(
+    n_seq,
+    n_sub,
+    first_half,
+    second_half,
+    grad_first,
+    grad_second,
+    attend_gain,
+    attend_shift,
+    query_key_weight,
+    value_projection_weight,
+    output_projection_weight,
+    feed_gain,
+    feed_shift,
+    upper_projection_weight,
+    upper_projection_bias,
+    lower_projection_weight,
+    lower_projection_bias,
+    sort_order,
+    sort_place,
+):
+    low, full = jnp.bfloat16, jnp.float32
+    devices, planes, per_plane = n_seq * n_sub, n_seq // 2, 2 * n_sub
+    rows, width = first_half.shape[1:]
+    hidden = upper_projection_weight.shape[2]
+    tokens = devices * rows
+    line = planes * rows
+    part = hidden // per_plane
+    seq, sub = lax.axis_index("seq"), lax.axis_index("sub")
+    me_p, me_z = lax.rem(seq, 2) * n_sub + sub, seq // 2
+    trade = functools.partial(exchange, planes=planes)
+    x1, x2, g1, g2 = (a[0] for a in (first_half, second_half, grad_first, grad_second))
+    wqk, wv, wo = query_key_weight[0], value_projection_weight[0], output_projection_weight[0]
+    wup, wdown = upper_projection_weight[0], lower_projection_weight[0]
+    own = width // devices
+    pair = 2 * HEAD_DIM
+
+    def row_of(*vectors):
+        return jnp.concatenate([v[0].astype(full) for v in vectors])[None]
+
+    small = jnp.concatenate(
+        [
+            sort_order[0, :, 0].astype(full),
+            sort_place[0, :, 0].astype(full),
+            row_of(attend_gain, attend_shift, feed_gain, feed_shift),
+            row_of(upper_projection_bias),
+            jnp.pad(row_of(lower_projection_bias), ((0, 5), (0, rows - own))),
+        ],
+        axis=0,
+    )
+    small = jnp.pad(small, ((0, 16 - small.shape[0]), (0, 0)))
+
+    def pair_columns(ref, z):
+        return ref.at[:, pl.ds(pl.multiple_of(z * pair, pair), pair)]
+
+    all_small, wqk_line, wv_line, wo_line = trade(
+        [
+            like(everywhere, small, planes, per_plane, 16, rows),
+            like(along_z(pair_columns, block), wqk, planes, own, pair),
+            like(along_z(pair_columns, block), wv, planes, own, pair),
+            like(along_z(whole, block), wo, planes, own, width),
+        ],
+        "share_small",
+        1,
+    )
+    all_small = all_small.reshape(devices, 16, rows)
+    gain_a, shift_a, gain_f, shift_f = (
+        all_small[:, 8, k * own : (k + 1) * own].reshape(width) for k in range(4)
+    )
+    bias_down = all_small[:, 10, :own].reshape(width)
+    bias_up = jnp.take(
+        all_small[:, 9].reshape(planes, per_plane, rows), me_p, axis=1
+    ).reshape(planes * rows)
+    order_rows = jnp.take(all_small[:, :4], sub, axis=1)
+    order = order_rows.astype(jnp.int32).reshape(tokens)
+    place = jnp.take(all_small[:, 4:8], sub, axis=1).astype(jnp.int32).reshape(tokens)
+
+    normed, attend_pull = jax.vjp(layer_norm, x2, gain_a, shift_a)
+    normed = normed.astype(low)
+
+    def upper_columns(chunk):
+        def columns(ref, p):
+            return ref.at[:, pl.ds(pl.multiple_of((chunk * per_plane + p) * rows, rows), rows)]
+
+        return like(over_plane(columns, block), wup, per_plane, own, rows)
+
+    rows_of_pair = over_chips(whole, second)
+    normed_line, wqk_pair, wv_pair, *wup_rows = trade(
+        [
+            like(along_z(whole, block), normed, planes, rows, width),
+            like(rows_of_pair, wqk_line, planes, per_plane, own, pair),
+            like(rows_of_pair, wv_line, planes, per_plane, own, pair),
+        ]
+        + [upper_columns(chunk) for chunk in range(planes)],
+        "share_normed",
+        2,
+    )
+    wup_rows = jnp.concatenate([a.reshape(per_plane * own, rows) for a in wup_rows], axis=1)
+    normed_line = normed_line.reshape(line, width)
+    wqk_pair, wv_pair = wqk_pair.reshape(width, pair), wv_pair.reshape(width, pair)
+    shared = matmul(normed_line, wqk_pair).astype(low).reshape(planes, rows, pair)
+    values = matmul(normed_line, wv_pair).astype(low).reshape(planes, rows, pair)
+
+    def head_columns(ref, p):
+        return ref.at[:, :, pl.ds(pl.multiple_of((p // 4) * HEAD_DIM, HEAD_DIM), HEAD_DIM)]
+
+    to_head = over_chips(head_columns, second)
+    head_shape = (planes, per_plane, rows, HEAD_DIM)
+    head_shared, head_values = trade(
+        [like(to_head, shared, *head_shape), like(to_head, values, *head_shape)], "to_heads", 3
+    )
+    df = g2.astype(low)
+    (
+        shared_sorted, values_sorted, total_sorted, mixed, total,
+        wup_part, wdown_part, wo_all, df_plane,
+    ) = attend_head(
+        order,
+        place,
+        order_rows,
+        head_shared.reshape(tokens, HEAD_DIM),
+        head_values.reshape(tokens, HEAD_DIM),
+        [
+            like(along_z(whole, block), wup_rows, planes, per_plane * own, part),
+            like(along_z(whole, block), wdown, planes, rows, width),
+            like(over_chips(whole, second), wo_line, planes, per_plane, own, width),
+            like(over_chips(whole, block), df, per_plane, rows, width),
+        ],
+        4,
+        planes,
+    )
+    wup_part, wdown_part = wup_part.reshape(width, part), wdown_part.reshape(part, width)
+    wo_all = wo_all.reshape(width, width)
+    df_plane = df_plane.reshape(per_plane * rows, width)
+
+    token_shape = (per_plane, planes, rows, HEAD_DIM)
+
+    def to_tokens(array):
+        return like(over_plane(second, block), array.reshape(head_shape), *token_shape)
+
+    mixed, total = trade(
+        [to_tokens(mixed), like(over_plane(block, block), total, *total.shape)], "heads_out", 5
+    )
+    mixed = mixed.reshape(2, n_sub, line, HEAD_DIM).astype(full)
+    total = total[:, :planes].reshape(2, n_sub, line)
+    weights = jnp.exp(total - jnp.max(total, axis=1, keepdims=True))
+    weights = weights / jnp.sum(weights, axis=1, keepdims=True)
+    attended = jnp.sum(weights[..., None] * mixed, axis=1)
+    attended = jnp.swapaxes(attended, 0, 1).reshape(line, pair).astype(low)
+    own_attended = trade(
+        [like(along_z(block, block), attended.reshape(planes, rows, pair), planes, rows, pair)],
+        "share_attended",
+        6,
+    )[0]
+    own_attended = jnp.swapaxes(own_attended, 0, 1).reshape(rows, width)
+    y1 = x1 + matmul(own_attended, wo_all)
+    h2, feed_pull = jax.vjp(layer_norm, y1, gain_f, shift_f)
+    h2_plane = trade(
+        [like(over_chips(whole, block), h2.astype(low), per_plane, rows, width)], "share_feed", 7
+    )[0]
+    h2_plane = h2_plane.reshape(per_plane * rows, width)
+    pre = matmul(h2_plane, wup_part) + bias_up
+    act, act_pull = jax.vjp(gelu_exact, pre)
+    act = act.astype(low)
+    y2_parts = matmul(act, wdown_part).astype(low).reshape(per_plane, rows, width)
+    dpre = act_pull(matmul(df_plane, wdown_part, ((1,), (1,))))[0].astype(low)
+    dh2_parts = matmul(dpre, wup_part, ((1,), (1,))).astype(low).reshape(per_plane, rows, width)
+    down_grad = matmul(act, df_plane, ((0,), (0,))).astype(low).reshape(planes, rows, width)
+    up_grad = matmul(h2_plane, dpre, ((0,), (0,))).astype(low).reshape(planes, width // planes, part)
+    up_bias_grad = jnp.sum(dpre.astype(full), axis=0)
+    down_bias_grad = jnp.sum(df.astype(full), axis=0)
+
+    traded_z, traded_plane = along_z(block, block), over_plane(block, block)
+    dh2_parts, up_grad = trade(
+        [like(traded_plane, dh2_parts, *dh2_parts.shape), like(traded_z, up_grad, *up_grad.shape)],
+        "sum_feed_grad",
+        8,
+    )
+    one_part, feed_gain_grad, feed_shift_grad = feed_pull(jnp.sum(dh2_parts.astype(full), axis=0))
+    g1 = g1 + one_part
+    up_grad = jnp.sum(up_grad.astype(full), axis=0).reshape(per_plane, own, part)
+    dout = g1.astype(low)
+    datt = matmul(dout, wo_all, ((1,), (1,))).astype(low)
+    datt = trade([like(along_z(pair_columns, block), datt, planes, rows, pair)], "share_out_grad", 9)[0]
+    datt = jnp.swapaxes(datt.reshape(line, 2, HEAD_DIM), 0, 1)[:, None].astype(full)
+    dweights = jnp.sum(datt * mixed, axis=-1)
+    dmixed = (weights[..., None] * datt).astype(low).reshape(token_shape)
+    dtotal = weights * (dweights - jnp.sum(weights * dweights, axis=1, keepdims=True))
+    dtotal = dtotal.astype(low).astype(full).reshape(per_plane, planes, rows)
+    dtotal = jnp.pad(dtotal, ((0, 0), (0, 8 - planes), (0, 0)))
+    dmixed, dtotal = trade(
+        [
+            like(over_plane(block, second), dmixed, *head_shape),
+            like(traded_plane, dtotal, *dtotal.shape),
+        ],
+        "grads_to_heads",
+        10,
+    )
+    dshared, dvalues, y2_parts, dout_line, down_grad = attend_head_back(
+        order,
+        place,
+        order_rows,
+        shared_sorted,
+        values_sorted,
+        total_sorted,
+        dmixed.reshape(tokens, HEAD_DIM),
+        dtotal,
+        [
+            like(traded_plane, y2_parts, *y2_parts.shape),
+            like(along_z(whole, block), dout, planes, rows, width),
+            like(traded_z, down_grad, *down_grad.shape),
+        ],
+        11,
+        planes,
+    )
+    y2 = x2 + (jnp.sum(y2_parts.astype(full), axis=0) + bias_down)
+    out_grad = matmul(attended, dout_line.reshape(line, width), ((0,), (0,)))
+    out_grad = out_grad.astype(low).reshape(per_plane, own, width)
+    dshared, dvalues = trade([to_tokens(dshared), to_tokens(dvalues)], "grads_from_heads", 12)
+
+    def over_rounds(array):
+        array = jnp.sum(array.reshape(2, n_sub, line, HEAD_DIM).astype(full), axis=1)
+        return jnp.swapaxes(array, 0, 1).reshape(line, pair).astype(low)
+
+    dshared, dvalues = over_rounds(dshared), over_rounds(dvalues)
+    de_parts = matmul(dshared, wqk_pair, ((1,), (1,))) + matmul(dvalues, wv_pair, ((1,), (1,)))
+    de_parts = de_parts.astype(low).reshape(planes, rows, width)
+
+    def to_owners(grad):
+        grad = grad.astype(low).reshape(planes, per_plane, own, pair)
+        return like(over_plane(second, block), grad, per_plane, planes, own, pair)
+
+    de_parts, shared_grad, value_grad, out_grad, up_grad = trade(
+        [
+            like(traded_z, de_parts, *de_parts.shape),
+            to_owners(matmul(normed_line, dshared, ((0,), (0,)))),
+            to_owners(matmul(normed_line, dvalues, ((0,), (0,)))),
+            like(traded_plane, out_grad, *out_grad.shape),
+            like(traded_plane, up_grad, *up_grad.shape),
+        ],
+        "sum_second_grad",
+        13,
+    )
+    two_part, attend_gain_grad, attend_shift_grad = attend_pull(
+        jnp.sum(de_parts.astype(full), axis=0)
+    )
+    g2 = g2 + two_part
+    shared_grad = jnp.sum(shared_grad.astype(full), axis=0)
+    value_grad = jnp.sum(value_grad.astype(full), axis=0)
+
+    def by_owner(vector):
+        return jnp.swapaxes(vector.reshape(planes, per_plane, own), 0, 1).reshape(per_plane, 1, rows)
+
+    vectors = [attend_gain_grad, attend_shift_grad, feed_gain_grad, feed_shift_grad, down_bias_grad]
+    up_bias_grad = jnp.where(
+        jnp.arange(per_plane)[:, None, None] == me_p, up_bias_grad.reshape(1, planes, rows), 0.0
+    )
+    tiles = jnp.concatenate([by_owner(v) for v in vectors] + [up_bias_grad], axis=1)
+    tiles = jnp.pad(tiles, ((0, 0), (0, 16 - tiles.shape[1]), (0, 0)))
+    vectors, shared_grad, value_grad = sum_small(
+        tiles,
+        [like(traded_z, shared_grad, planes, own, pair), like(traded_z, value_grad, planes, own, pair)],
+        14,
+        planes,
+    )
+    vectors = jnp.sum(vectors, axis=0)
+    pieces = jnp.take(vectors[:5].reshape(5, planes, own), me_z, axis=1)
+    up_bias_grad = jnp.take(vectors[5 : 5 + planes], me_z, axis=0)
+    shared_grad, value_grad = (
+        jnp.swapaxes(a, 0, 1).reshape(own, width) for a in (shared_grad, value_grad)
+    )
+    up_grad = jnp.transpose(up_grad.reshape(per_plane, own, planes, rows), (1, 2, 0, 3))
+    outputs = (
+        y1,
+        y2,
+        g1,
+        g2,
+        pieces[0],
+        pieces[1],
+        shared_grad,
+        value_grad,
+        jnp.sum(out_grad.astype(full), axis=0),
+        pieces[2],
+        pieces[3],
+        up_grad.reshape(own, hidden),
+        up_bias_grad,
+        jnp.sum(down_grad.astype(full), axis=0),
+        pieces[4],
+    )
+    return tuple((a[None] for a in outputs))
+
+
+def on_device(n_seq, n_sub, *arguments):
+    sequences, rows, width = arguments[0].shape
+    rounds = arguments[-1].shape[1]
+    fits = (
+        sequences == 1
+        and rows == 2 * BLOCK
+        and rounds == n_sub
+        and HEADS == n_seq
+        and width == HEADS * HEAD_DIM
+    )
+    if fits:
+        return plane_plan(n_seq, n_sub, *arguments)
+    return general_plan(*arguments)
+
+
 def solution(mesh):
     return jax.shard_map(
-        on_device,
+        functools.partial(on_device, mesh.shape["seq"], mesh.shape["sub"]),
         mesh=mesh,
         in_specs=(
             P(None, ("seq", "sub"), None),

time: 1420 us -> 474 us (0.33)
  waiting for transfers between devices: 669 us -> 0 us
  Pallas kernels: 0 us -> 354 us
  local copies, waits for them, and re-layouts: 286 us -> 44.7 us
  blocking collectives: 219 us -> 0 us
  starting transfers between devices: 92.5 us -> 0 us
  matrix products: 70.4 us -> 36 us
  other arithmetic: 60.4 us -> 36.7 us
  between operations: 16.1 us -> 1.48 us
    reduce_scatter x5 -> x0, waiting for transfers between devices: 496 us -> none  [the longest x1 146 us: spread_grads(): lax.psum_scatter(upper_projection_weight.astype(jnp.bfloat16), ('seq', 's...]
    pallas_call x0 -> x14, Pallas kernels: none -> 354 us  [the longest x11 242 us: exchange(): pl.pallas_call(body, out_shape=[item[2] for item in items], in_specs=[pl....]
    gather x17 -> x0, local copies, waits for them, and re-layouts: 152 us -> none  [the longest x8 98.9 us: gather_slots(): return padded[member[None, :, None], lookup]]
    all_gather x1 -> x0, blocking collectives: 137 us -> none  [collect(): lax.all_gather(upper_projection_bias, ('seq', 'sub'), axis=0, tiled=True)]
    all_to_all x8 -> x0, waiting for transfers between devices: 94.8 us -> none  [the longest x3 52.4 us: trade_rows(): lax.all_to_all(first_part, ('seq', 'sub'), split_axis=0, concat_axis=0, t...]
    all_to_all x8 -> x0, starting transfers between devices: 82.5 us -> none  [the longest x3 39.2 us: trade_rows(): lax.all_to_all(second_part, ('seq', 'sub'), split_axis=0, concat_axis=0,...]
    unnamed x2 -> x0, blocking collectives: 81.7 us -> none
    scatter x2 -> x0, local copies, waits for them, and re-layouts: 49.3 us -> none  [slot_lookup(): lookup = lookup.at[jnp.arange(groups)[:, None], flat_index].set(filler)]
  transfers between devices with their start and end apart: 23 -> 0, of which waited for: 12 -> 0; matrix products, arithmetic and copies ran while one was open for 22% -> 0% of each run, Pallas kernels for 0% -> 0%
where the time goes in v3:
time: 474 us; the launch traced here: 472 us
  Pallas kernels  354 us (75%)
  local copies, waits for them, and re-layouts  44.7 us (9%)
  other arithmetic  36.7 us (8%)
  matrix products  36 us (8%)
    pallas_call x11, Pallas kernels, exchange(): pl.pallas_call(body, out_shape=[item[2] for item in items], in_specs=[pl....  242 us
    pallas_call x1, Pallas kernels, attend_head(): pl.pallas_call(beside(kernel, 5, 5, len(scratch), items, planes), out_sha...  50.3 us
    pallas_call x1, Pallas kernels, attend_head_back(): pl.pallas_call(beside(kernel, 8, 2, len(scratch), items, planes), out_sha...  47.2 us
    dot_general x15, matrix products, dot(): lax.dot_general(a, b, (contract, ((), ())), preferred_element_type=jnp.fl...  36 us
    unnamed x114, local copies, waits for them, and re-layouts  24.6 us
    pallas_call x1, Pallas kernels, sum_small(): pl.pallas_call(functools.partial(sum_small_kernel, planes, items), out_sh...  13.7 us

profile of v3, /device:TPU:0, one launch (start us, length us, event | category | flops | bytes accessed | tf_op | source)
XLA Modules:
  0.0 472.4 jit_solution(2314228539622130653)
XLA Ops:
  2.9 1.9 concatenate.14.refs_0_
  4.7 22.8 %share_small.1 = (f32[4,8,16,128]{3,2,1,0:T(8,128)}, bf16[4,32,256]{2,1,0:T(8,128)(2,1)}, bf16[4,32,256]{2,1,0:T(8,128)(2,1)}, bf16[4,32,1024]{2,1,0:T(8,128)(2,1)}) custom-call(f32[16,128]{1,0:T(8,128)} %concatenate.14.refs_0_, bf16[32,1024]{1,0:T(8,128)(2,1)} %bitcast.251, bf16[32,1024]{1,0:T(8,128)(2,1)} %bitcast.252, bf16[32,1024]{1,0:T(8,128)(2,1)} %bitcast.253), custom_call_target="tpu_custom_call" | custom-call | tf_op jit(solution)/shard_map/share_small/pallas_call | solution.py:650
  28.8 1.2 reduce_sum.299
  30.0 1.2 multiply_reduce_fusion.7
  32.1 25.3 %share_normed.1 = (bf16[4,128,1024]{2,1,0:T(8,128)(2,1)}, bf16[4,8,32,256]{3,2,1,0:T(8,128)(2,1)}, bf16[4,8,32,256]{3,2,1,0:T(8,128)(2,1)}, bf16[8,32,128]{2,1,0...) custom-call(bf16[128,1024]{1,0:T(8,128)(2,1)} %add_convert_fusion.3.refs_0_, ...), custom_call_target="tpu_custom_call" | custom-call | tf_op jit(solution)/shard_map/share_normed/pallas_call | solution.py:650
  57.5 2.6 convolution_convert_fusion.8
  60.1 2.6 convolution_convert_fusion.9
  62.6 23.9 %to_heads.1 = (bf16[4,8,128,128]{3,2,1,0:T(8,128)(2,1)}, bf16[4,8,128,128]{3,2,1,0:T(8,128)(2,1)}) custom-call(bf16[4,128,256]{2,1,0:T(8,128)(2,1)} %bitcast.247, bf16[4,128,256]{2,1,0:T(8,128)(2,1)} %bitcast.246), custom_call_target="tpu_custom_call" | custom-call | tf_op jit(solution)/shard_map/to_heads/pallas_call | solution.py:650
  87.8 1.2 copy-done.7
  90.9 50.3 %attend.1 = (bf16[4096,128]{1,0:T(8,128)(2,1)S(1)}, bf16[4096,128]{1,0:T(8,128)(2,1)S(1)}, f32[4096,128]{1,0:T(8,128)S(1)}, bf16[4096,128]{1,0:T(8,128)(2,1)S(1)...) custom-call(s32[4096]{0:T(1024)S(1)} %get-tuple-element.163.refs_0_,, ...), custom_call_target="tpu_custom_call" | custom-call | tf_op jit(solution)/shard_map/attend/pallas_call | solution.py:936
  141.2 1.3 copy-done
  148.0 22.7 %heads_out.1 = (bf16[8,4,128,128]{3,2,1,0:T(8,128)(2,1)}, f32[8,8,128]{2,1,0:T(8,128)}) custom-call(bf16[4,8,128,128]{3,2,1,0:T(8,128)(2,1)} %bitcast.193, f32[8,8,128]{2,1,0:T(8,128)} %copy-done.18), custom_call_target="tpu_custom_call" | custom-call | tf_op jit(solution)/shard_map/heads_out/pallas_call | solution.py:650
  171.5 1.8 multiply_reduce_fusion.1
  175.2 10.7 %share_attended.1 = bf16[4,128,256]{2,1,0:T(8,128)(2,1)} custom-call(bf16[4,128,256]{2,1,0:T(8,128)(2,1)} %convert_element_type.224.refs_0_), custom_call_target="tpu_custom_call" | custom-call | tf_op jit(solution)/shard_map/share_attended/pallas_call | solution.py:650
  188.7 1.9 add_convert_fusion.2.refs_0_
  190.6 19.5 %share_feed.1 = bf16[8,128,1024]{2,1,0:T(8,128)(2,1)} custom-call(bf16[128,1024]{1,0:T(8,128)(2,1)} %add_convert_fusion.2.refs_0_), custom_call_target="tpu_custom_call" | custom-call | tf_op jit(solution)/shard_map/share_feed/pallas_call | solution.py:650
  210.2 4.2 fusion.27
  215.1 8.9 %convert_reduce_fusion.6 = (f32[512]{0:T(512)}, bf16[1024,512]{1,0:T(8,128)(2,1)S(1)}, f32[1024,512]{1,0:T(8,128)S(1)}) fusion(f32[1024,512]{1,0:T(8,128)} %fusion.27, f32[512]{0:T(512)S(1)} %bitcast.263, bf16[1024,1024]{1,0:T(8,128)(2,1)} %bitcast.221, bf16[512,1024]{1,0:T(8,128)(2,1)} %bitcast.197), kind=kOutput, calls=%fused_computation.9 | convolution fusion | flops 1113062912 | bytes 8392704 | tf_op jit(solution)/shard_map/dot_general | solution.py:692
  225.6 1.3 convolution_convert_fusion.2
  226.9 2.6 convolution_convert_fusion
  229.4 2.3 convolution_convert_fusion.3
  231.7 2.6 convolution_convert_fusion.1
  234.3 28.0 %sum_feed_grad.1 = (bf16[8,128,1024]{2,1,0:T(8,128)(2,1)}, bf16[4,256,512]{2,1,0:T(8,128)(2,1)}) custom-call(bf16[8,128,1024]{2,1,0:T(8,128)(2,1)} %bitcast.220, bf16[4,256,512]{2,1,0:T(8,128)(2,1)} %bitcast.230), custom_call_target="tpu_custom_call" | custom-call | tf_op jit(solution)/shard_map/sum_feed_grad/pallas_call | solution.py:650
  262.3 2.6 convert_reduce_fusion
  266.9 1.5 convolution_convert_fusion.7.refs_0_
  268.5 11.0 %share_out_grad.1 = bf16[4,128,256]{2,1,0:T(8,128)(2,1)} custom-call(bf16[128,1024]{1,0:T(8,128)(2,1)} %convolution_convert_fusion.7.refs_0_), custom_call_target="tpu_custom_call" | custom-call | tf_op jit(solution)/shard_map/share_out_grad/pallas_call | solution.py:650
  279.4 1.2 reshape.624
  285.4 1.5 multiply_convert_fusion.1.refs_0_
  287.5 17.7 %grads_to_heads.1 = (bf16[4,8,128,128]{3,2,1,0:T(8,128)(2,1)}, f32[8,8,128]{2,1,0:T(8,128)}) custom-call(bf16[8,4,128,128]{3,2,1,0:T(8,128)(2,1)} %multiply_convert_fusion.1.refs_0_, f32[8,8,128]{2,1,0:T(8,128)} %pad_convert_fusion.refs_1_), custom_call_target="tpu_custom_call" | custom-call | tf_op jit(solution)/shard_map/grads_to_heads/pallas_call | solution.py:650
  305.3 1.6 copy-done.1
  306.8 1.2 copy-done.3
  308.1 1.2 copy-done.5
  309.3 1.2 copy-done.8
  311.3 47.2 %attend_back.1 = (bf16[4096,128]{1,0:T(8,128)(2,1)S(1)}, bf16[4096,128]{1,0:T(8,128)(2,1)S(1)}, bf16[8,128,1024]{2,1,0:T(8,128)(2,1)S(1)}, bf16[4,128,1024]{2,1,0:T(8,128)(2,1)S(1)}, bf16[4,128,1024]{2,1,0:T(8,128)(2,1)S(1)}) custom-call(s32[4096]{0:T(1024)S(1)} %get-tuple-element.163.refs_0_, s32[4096]{0:T(1024)S(1)} %fusion.14.refs_1_, ...), custom_call_target="tpu_custom_call" | custom-call | tf_op jit(solution)/shard_map/attend_back/pallas_call | solution.py:971
  363.5 2.5 convolution_convert_fusion.4
  366.0 32.4 %grads_from_heads.1 = (bf16[8,4,128,128]{3,2,1,0:T(8,128)(2,1)}, bf16[8,4,128,128]{3,2,1,0:T(8,128)(2,1)}) custom-call(bf16[4,8,128,128]{3,2,1,0:T(8,128)(2,1)} %bitcast.191, bf16[4,8,128,128]{3,2,1,0:T(8,128)(2,1)} %bitcast.192), custom_call_target="tpu_custom_call" | custom-call | tf_op jit(solution)/shard_map/grads_from_heads/pallas_call | solution.py:650
  398.4 2.2 reduce.5
  401.6 1.3 convolution_convert_fusion.5
  402.9 2.2 reduce.4
  406.2 1.3 convolution_convert_fusion.6
  408.0 1.5 add_convert_fusion
  410.4 28.6 %sum_second_grad.1 = (bf16[4,128,1024]{2,1,0:T(8,128)(2,1)}, bf16[8,4,32,256]{3,2,1,0:T(8,128)(2,1)}, bf16[8,4,32,256]{3,2,1,0:T(8,128)(2,1)}, bf16[8,32,1024]{2,1,0:T(8,128)(2,1)}, f32[8,32,512]{2,1,0:T(8,128)}) custom-call(bf16[4,128,1024]{2,1,0:T(8,128)(2,1)} %bitcast.207, bf16[4,8,32,256]{3,2,1,0:T(8,128)(2,1)} %bitcast.225, ...), custom_call_target="tpu_custom_call" | custom-call | tf_op jit(solution)/shard_map/sum_second_grad/pallas_call | solution.py:650
  439.1 1.7 convert_reduce_fusion.3
  443.1 1.8 convert_reduce_fusion.10.refs_1_
  444.9 1.8 convert_reduce_fusion.9.refs_2_
  446.7 13.7 %sum_small.1 = (f32[4,16,128]{2,1,0:T(8,128)}, f32[4,32,256]{2,1,0:T(8,128)}, f32[4,32,256]{2,1,0:T(8,128)}) custom-call(f32[8,16,128]{2,1,0:T(8,128)} %pad.21.refs_0_, f32[4,32,256]{2,1,0:T(8,128)} %convert_reduce_fusion.10.refs_1_, f32[4,32,256]{2,1,0:T(8,128)} %convert_reduce_fusion.9.refs_2_), custom_call_target="tpu_custom_call" | custom-call | tf_op jit(solution)/shard_map/sum_small/pallas_call | solution.py:1006
  465.8 1.1 convert_reduce_fusion.2
  467.0 2.4 fusion.8
  (203 shorter events, 48.3 us)
Async XLA Ops:
  0.6 30.6 %copy-start.24 = (f32[1,128,1024]{2,1,0:T(8,128)S(1)}, f32[1,128,1024]{2,1,0:T(8,128)}, u32[]{:S(2)}) copy-start(f32[1,128,1024]{2,1,0:T(8,128)} %param.20) | copy-start | bytes 1572868
  28.6 58.0 %copy-start.38 = (f32[4,8,16,128]{3,1,0,2:T(8,128)}, f32[4,8,16,128]{3,1,0,2:T(8,128)S(1)}, u32[]{:S(2)}) copy-start(f32[4,8,16,128]{3,1,0,2:T(8,128)S(1)} %copy.92) | copy-start | bytes 786436
  30.0 27.4 %copy-start.50 = (f32[128]{0:T(128)}, f32[128]{0:T(128)S(1)}, u32[]{:S(2)}) copy-start(f32[128]{0:T(128)S(1)} %broadcast_multiply_fusion.1) | copy-start | bytes 1540
  31.2 26.2 %copy-start.55 = (f32[128]{0:T(128)}, f32[128]{0:T(128)S(1)}, u32[]{:S(2)}) copy-start(f32[128]{0:T(128)S(1)} %multiply_reduce_fusion.7) | copy-start | bytes 1540
  31.3 26.2 %copy-start.52 = (f32[128]{0:T(128)}, f32[128]{0:T(128)S(1)}, u32[]{:S(2)}) copy-start(f32[128]{0:T(128)S(1)} %fusion.20) | copy-start | bytes 1540
  57.5 29.1 %copy-start.45 = (bf16[8,32,128]{2,1,0:T(8,128)(2,1)S(1)}, bf16[8,32,128]{2,1,0:T(8,128)(2,1)}, u32[]{:S(2)}) copy-start(bf16[8,32,128]{2,1,0:T(8,128)(2,1)} %get-tuple-element.67) | copy-start | bytes 196612
  57.5 29.1 %copy-start.46 = (bf16[8,32,128]{2,1,0:T(8,128)(2,1)S(1)}, bf16[8,32,128]{2,1,0:T(8,128)(2,1)}, u32[]{:S(2)}) copy-start(bf16[8,32,128]{2,1,0:T(8,128)(2,1)} %get-tuple-element.68) | copy-start | bytes 196612
  57.5 29.1 %copy-start.47 = (bf16[8,32,128]{2,1,0:T(8,128)(2,1)S(1)}, bf16[8,32,128]{2,1,0:T(8,128)(2,1)}, u32[]{:S(2)}) copy-start(bf16[8,32,128]{2,1,0:T(8,128)(2,1)} %get-tuple-element.69) | copy-start | bytes 196612
  57.5 29.1 %copy-start.48 = (bf16[8,32,128]{2,1,0:T(8,128)(2,1)S(1)}, bf16[8,32,128]{2,1,0:T(8,128)(2,1)}, u32[]{:S(2)}) copy-start(bf16[8,32,128]{2,1,0:T(8,128)(2,1)} %get-tuple-element.70) | copy-start | bytes 196612
  60.1 26.6 %copy-start.36 = (f32[1,128,1024]{2,1,0:T(8,128)S(1)}, f32[1,128,1024]{2,1,0:T(8,128)}, u32[]{:S(2)}) copy-start(f32[1,128,1024]{2,1,0:T(8,128)} %param.22) | copy-start | bytes 1572868
  86.5 1.2 copy-start.6
  87.7 1.2 copy-start.7
  141.1 1.4 copy-start
  142.5 1.0 copy-start.2
  143.5 1.0 copy-start.4
  144.4 1.0 copy-start.14
  148.0 39.0 %copy-start.42 = (f32[1,128,1024]{2,1,0:T(8,128)S(1)}, f32[1,128,1024]{2,1,0:T(8,128)}, u32[]{:S(2)}) copy-start(f32[1,128,1024]{2,1,0:T(8,128)} %param.19) | copy-start | bytes 1572868
  187.6 22.6 %copy-start.20 = (bf16[4,256,512]{2,1,0:T(8,128)(2,1)S(1)}, bf16[4,256,512]{2,1,0:T(8,128)(2,1)}, u32[]{:S(2)}) copy-start(bf16[4,256,512]{2,1,0:T(8,128)(2,1)} %copy-done.19) | copy-start | bytes 3145732
  215.1 8.9 %copy-start.33 = (f32[1024,512]{1,0:T(8,128)S(1)}, f32[1024,512]{1,0:T(8,128)}, u32[]{:S(2)}) copy-start(f32[1024,512]{1,0:T(8,128)} %fusion.27) | copy-start | bytes 6291460
  224.0 1.6 copy-start.35
  225.6 1.3 copy-start.23
  226.9 2.6 copy-start.34
  229.4 2.3 copy-start.21
  262.3 2.6 copy-start.27
  262.3 3.7 copy-start.43
  280.7 1.2 copy-start.29
  305.2 1.6 copy-start.1
  306.8 1.2 copy-start.3
  308.1 1.2 copy-start.5
  309.3 1.2 copy-start.8
  358.4 1.0 copy-start.9
  360.4 1.0 copy-start.12
  361.4 1.0 copy-start.13
  366.0 35.7 %copy-start.28 = (bf16[4,128,1024]{2,1,0:T(8,128)(2,1)S(1)}, bf16[4,128,1024]{2,1,0:T(8,128)(2,1)}, u32[]{:S(2)}) copy-start(bf16[4,128,1024]{2,1,0:T(8,128)(2,1)} %get-tuple-element.62) | copy-start | bytes 3145732
  401.6 3.5 copy-start.31
  406.2 1.3 copy-start.44
  406.2 1.8 copy-start.32
  406.2 1.8 copy-start.39
  408.0 1.5 copy-start.37
  410.4 30.3 %copy-start.25 = (f32[1,128,1024]{2,1,0:T(8,128)S(1)}, f32[1,128,1024]{2,1,0:T(8,128)}, u32[]{:S(2)}) copy-start(f32[1,128,1024]{2,1,0:T(8,128)} %param.20) | copy-start | bytes 1572868
  410.4 30.3 %copy-start.51 = (f32[128]{0:T(128)S(1)}, f32[128]{0:T(128)}, u32[]{:S(2)}) copy-start(f32[128]{0:T(128)} %copy-done.50) | copy-start | bytes 1540
  439.0 2.0 copy-start.56
  439.1 2.0 copy-start.53
  439.1 2.6 copy-start.49
  439.1 3.0 copy-start.54
  466.9 2.4 copy-start.41
  469.3 1.4 copy-start.40
  469.3 2.1 copy-start.11
  (9 other events, 7.7 us)

commit v4 on v3

--- a/solution.py
+++ b/solution.py
@@ -1019,6 +1019,264 @@
     )(tiles, *[item[1] for item in items])
 
 
+def normal_parts(rows):
+    center = jnp.mean(rows, axis=-1, keepdims=True)
+    offset = rows - center
+    spread = jnp.mean(offset * offset, axis=-1, keepdims=True)
+    inverse = lax.rsqrt(spread + 1e-05)
+    return offset * inverse, inverse
+
+
+def norm_back(grad, rows, gain):
+    unit, inverse = normal_parts(rows)
+    scaled = grad * gain
+    shared = jnp.mean(scaled, axis=-1, keepdims=True)
+    along = jnp.mean(scaled * unit, axis=-1, keepdims=True)
+    return (
+        (scaled - shared - unit * along) * inverse,
+        jnp.sum(grad * unit, axis=0, keepdims=True),
+        jnp.sum(grad, axis=0, keepdims=True),
+    )
+
+
+def gelu_parts(rows):
+    below = 0.5 * (1.0 + lax.erf(rows * 0.7071067811865476))
+    bell = jnp.exp(-0.5 * rows * rows) * 0.3989422804014327
+    return rows * below, below + rows * bell
+
+
+def feed_kernel(
+    planes,
+    mixed, total, x1, wo_in, gain, shift, wup_in, bias_up, wdown_in, df_in, g1,
+    y1_out, g1_out, dout_out, attended_out, dmixed_home, dtotal_home, y2_out, up_grad_out, down_grad_out,
+    up_bias_out, gain_out, shift_out,
+    wo, wup, wdown, df, weights, attended, arrived, h2, dact, act, dpre, kept, to_sibling, from_sibling,
+    to_chip, from_chip, up_grad, down_grad, y2, dout, datt_out, datt, dmixed, dtotal, send, receive, local,
+):
+    low, full = jnp.bfloat16, jnp.float32
+    links = Links(planes, send, receive, local)
+    links.greet()
+    loads = [links.keep(a, b) for a, b in ((wo_in, wo), (df_in, df), (wdown_in, wdown), (wup_in, wup))]
+
+    def combine(z, carry):
+        for x in range(2):
+            totals = [down(total[x * 4 + u, pl.ds(z, 1), :]) for u in range(4)]
+            highest = jnp.maximum(
+                jnp.maximum(totals[0], totals[1]), jnp.maximum(totals[2], totals[3])
+            )
+            parts = [jnp.exp(t - highest) for t in totals]
+            inverse = 1.0 / (parts[0] + parts[1] + parts[2] + parts[3])
+            result = 0.0
+            for u in range(4):
+                weight = parts[u] * inverse
+                weights[x * 4 + u, z] = weight
+                result += weight * mixed[x * 4 + u, z].astype(full)
+            attended[z, :, x * 128 : (x + 1) * 128] = result.astype(low)
+        return carry
+
+    lax.fori_loop(0, planes, combine, 0)
+    links.meet()
+    share = along_z(block, block)(links, attended, arrived)
+    next(share)
+    keep_attended = links.keep(attended, attended_out)
+    loads[0].wait()
+    drive([share])
+    y1 = x1[...]
+    for z in range(planes):
+        y1 += dot(arrived[z], wo[z * 256 : (z + 1) * 256, :], ((1,), (0,)))
+    y1_out[...] = y1
+    unit, _ = normal_parts(y1)
+    own_rows = pl.ds(pl.multiple_of(links.p * 128, 128), 128)
+    h2[own_rows, :] = (unit * gain[...] + shift[...]).astype(low)
+
+    def rows_of(index):
+        return pl.ds(pl.multiple_of(index * 128, 128), 128)
+
+    sibling, _ = links.near(1)
+    own_h2 = h2.at[own_rows, :]
+    direct = {step: links.push(own_h2, own_h2, links.near(step)[0]) for step in (6, 4, 2)}
+    handed = {0: links.push(own_h2, own_h2, sibling)}
+    for load in loads[1:]:
+        load.wait()
+
+    def upper_back(part, carry):
+        rows = pl.ds(pl.multiple_of(part * 256, 256), 256)
+        dact[rows, :] = dot(df[rows, :], wdown[...], ((1,), (1,)))
+        return carry
+
+    lax.fori_loop(0, 4, upper_back, 0)
+
+    def pass_on(step):
+        direct[step].wait_recv()
+        block_rows = h2.at[rows_of(links.near(step)[1]), :]
+        handed[step] = links.push(block_rows, block_rows, sibling)
+
+    def feed(slot, step):
+        handed[step].wait_recv()
+        chip = links.near(step)[1] // 2
+        rows = pl.ds(pl.multiple_of(chip * 256, 256), 256)
+        before = dot(h2[rows, :], wup[...], ((1,), (0,))) + bias_up[...]
+        value, slope = gelu_parts(before)
+        act[rows, :] = value.astype(low)
+        grad = (dact[rows, :] * slope).astype(low)
+        dpre[rows, :] = grad
+        kept[slot] = dot(grad, wup[...], ((1,), (1,))).reshape(2, 128, -1).astype(low)
+        return links.push(kept.at[slot, 1 - links.core], from_sibling.at[slot], sibling)
+
+    def chip_sum(slot, step, traded):
+        traded.wait_recv()
+        result = kept[slot, links.core].astype(full) + from_sibling[slot].astype(full)
+        if slot == 0:
+            return result
+        to_chip[slot - 1] = result.astype(low)
+        return links.push(to_chip.at[slot - 1], from_chip.at[slot - 1], links.near(step)[0])
+
+    pass_on(2)
+    traded = [feed(0, 0)]
+    pass_on(4)
+    traded.append(feed(1, 2))
+    sent = [chip_sum(1, 2, traded[1])]
+    pass_on(6)
+    traded.append(feed(2, 4))
+    sent.append(chip_sum(2, 4, traded[2]))
+    traded.append(feed(3, 6))
+    sent.append(chip_sum(3, 6, traded[3]))
+    own_sum = chip_sum(0, 0, traded[0])
+
+    def upper_grad(part, carry):
+        rows = pl.ds(pl.multiple_of(part * 256, 256), 256)
+        up_grad[part] = dot(h2[:, rows], dpre[...], ((0,), (0,))).astype(low)
+        return carry
+
+    lax.fori_loop(0, planes, upper_grad, 0)
+    share_up = along_z(block, block)(links, up_grad, up_grad_out)
+    next(share_up)
+    for copy in sent:
+        copy.wait_recv()
+    grad = own_sum + (
+        from_chip[0].astype(full) + from_chip[1].astype(full) + from_chip[2].astype(full)
+    )
+    part, gain_grad, shift_grad = norm_back(grad, y1_out[...], gain[...])
+    gain_out[...] = gain_grad
+    shift_out[...] = shift_grad
+    g1_new = g1[...] + part
+    g1_out[...] = g1_new
+    dout[...] = g1_new.astype(low)
+    keep_dout = links.keep(dout, dout_out)
+    for z in range(planes):
+        datt_out[z] = dot(dout[...], wo[z * 256 : (z + 1) * 256, :], ((1,), (1,))).astype(low)
+    share = along_z(block, block)(links, datt_out, datt)
+    next(share)
+
+    def lower_grad(part, carry):
+        rows = pl.ds(pl.multiple_of(part * 128, 128), 128)
+        down_grad[part] = dot(act[:, rows], df[...], ((0,), (0,))).astype(low)
+        return carry
+
+    lax.fori_loop(0, planes, lower_grad, 0)
+    share_down = along_z(block, block)(links, down_grad, down_grad_out)
+    next(share_down)
+    up_bias_out[...] = jnp.sum(dpre[...].astype(full), axis=0, keepdims=True)
+    drive([share])
+
+    def combine_back(z, carry):
+        for x in range(2):
+            grad = datt[z, :, x * 128 : (x + 1) * 128].astype(full)
+            chosen = [weights[x * 4 + u, z] for u in range(4)]
+            inner = [
+                jnp.sum(grad * mixed[x * 4 + u, z].astype(full), axis=-1, keepdims=True)
+                for u in range(4)
+            ]
+            mean = sum(chosen[u] * inner[u] for u in range(4))
+            for u in range(4):
+                dmixed[x * 4 + u, z] = (chosen[u] * grad).astype(low)
+                change = (chosen[u] * (inner[u] - mean)).astype(low).astype(full)
+                dtotal[x * 4 + u, pl.ds(z, 1), :] = change.T[:1, :]
+        return carry
+
+    lax.fori_loop(0, planes, combine_back, 0)
+    shares = [
+        over_plane(block, second)(links, dmixed, dmixed_home),
+        over_plane(block, block)(links, dtotal, dtotal_home),
+    ]
+    for transfer in shares:
+        next(transfer)
+
+    def lower(part, carry):
+        rows = pl.ds(pl.multiple_of(part * 128, 128), 128)
+        y2[part] = dot(act[rows, :], wdown[...], ((1,), (0,))).astype(low)
+        return carry
+
+    lax.fori_loop(0, 8, lower, 0)
+    keep_y2 = links.keep(y2, y2_out)
+    for copy in list(direct.values()) + traded + sent:
+        copy.wait_send()
+    for copy in handed.values():
+        copy.wait_send()
+    drive(shares + [share_up, share_down])
+    for copy in (keep_attended, keep_dout, keep_y2):
+        copy.wait()
+
+
+def feed_stage(arguments, collective_id, planes):
+    low, full = jnp.bfloat16, jnp.float32
+    (mixed, total, x1, wo, gain, shift, wup, bias_up, wdown, df, g1) = arguments
+    rows, width = x1.shape
+    part = wup.shape[1]
+    shape = jax.ShapeDtypeStruct
+    outputs = [
+        (shape((rows, width), full), VMEM),
+        (shape((rows, width), full), VMEM),
+        (shape((rows, width), low), ANY),
+        (shape((planes, rows, 256), low), ANY),
+        (shape((planes, 8, rows, HEAD_DIM), low), ANY),
+        (shape((8, 8, rows), full), ANY),
+        (shape((8, rows, width), low), ANY),
+        (shape((planes, width // planes, part), low), ANY),
+        (shape((planes, rows, width), low), ANY),
+        (shape((1, part), full), VMEM),
+        (shape((1, width), full), VMEM),
+        (shape((1, width), full), VMEM),
+    ]
+    scratch = [
+        (wo.shape, low),
+        (wup.shape, low),
+        (wdown.shape, low),
+        (df.shape, low),
+        ((8, planes, rows, HEAD_DIM), full),
+        ((planes, rows, 256), low),
+        ((planes, rows, 256), low),
+        ((8 * rows, width), low),
+        ((8 * rows, part), full),
+        ((8 * rows, part), low),
+        ((8 * rows, part), low),
+        ((4, 2, rows, width), low),
+        ((4, rows, width), low),
+        ((4, rows, width), low),
+        ((3, rows, width), low),
+        ((3, rows, width), low),
+        ((planes, width // planes, part), low),
+        ((planes, rows, width), low),
+        ((8, rows, width), low),
+        ((rows, width), low),
+        ((planes, rows, 256), low),
+        ((planes, rows, 256), low),
+        ((8, planes, rows, HEAD_DIM), low),
+        ((8, 8, rows), full),
+    ]
+    return pl.pallas_call(
+        functools.partial(feed_kernel, planes),
+        out_shape=[o[0] for o in outputs],
+        in_specs=[VMEM, VMEM, VMEM, ANY, VMEM, VMEM, ANY, VMEM, ANY, ANY, VMEM],
+        out_specs=[o[1] for o in outputs],
+        scratch_shapes=[pltpu.VMEM(*s) for s in scratch] + link_scratch(),
+        compiler_params=pltpu.CompilerParams(
+            vmem_limit_bytes=56 << 20, collective_id=collective_id, has_side_effects=True
+        ),
+        name="feed",
+    )(*arguments)
+
+
 def matmul(a, b, contract=((1,), (0,))):
     return dot(a, b, contract)
 
@@ -1165,62 +1423,22 @@
     mixed, total = trade(
         [to_tokens(mixed), like(over_plane(block, block), total, *total.shape)], "heads_out", 5
     )
-    mixed = mixed.reshape(2, n_sub, line, HEAD_DIM).astype(full)
-    total = total[:, :planes].reshape(2, n_sub, line)
-    weights = jnp.exp(total - jnp.max(total, axis=1, keepdims=True))
-    weights = weights / jnp.sum(weights, axis=1, keepdims=True)
-    attended = jnp.sum(weights[..., None] * mixed, axis=1)
-    attended = jnp.swapaxes(attended, 0, 1).reshape(line, pair).astype(low)
-    own_attended = trade(
-        [like(along_z(block, block), attended.reshape(planes, rows, pair), planes, rows, pair)],
-        "share_attended",
+    traded_z, traded_plane = along_z(block, block), over_plane(block, block)
+    down_bias_grad = jnp.sum(df.astype(full), axis=0)
+    (
+        y1, g1, dout, attended, dmixed, dtotal, y2_parts, up_grad, down_grad,
+        up_bias_grad, feed_gain_grad, feed_shift_grad,
+    ) = feed_stage(
+        (
+            mixed, total, x1, wo_all, gain_f[None], shift_f[None],
+            wup_part, bias_up[None], wdown_part, df_plane, g1,
+        ),
         6,
-    )[0]
-    own_attended = jnp.swapaxes(own_attended, 0, 1).reshape(rows, width)
-    y1 = x1 + matmul(own_attended, wo_all)
-    h2, feed_pull = jax.vjp(layer_norm, y1, gain_f, shift_f)
-    h2_plane = trade(
-        [like(over_chips(whole, block), h2.astype(low), per_plane, rows, width)], "share_feed", 7
-    )[0]
-    h2_plane = h2_plane.reshape(per_plane * rows, width)
-    pre = matmul(h2_plane, wup_part) + bias_up
-    act, act_pull = jax.vjp(gelu_exact, pre)
-    act = act.astype(low)
-    y2_parts = matmul(act, wdown_part).astype(low).reshape(per_plane, rows, width)
-    dpre = act_pull(matmul(df_plane, wdown_part, ((1,), (1,))))[0].astype(low)
-    dh2_parts = matmul(dpre, wup_part, ((1,), (1,))).astype(low).reshape(per_plane, rows, width)
-    down_grad = matmul(act, df_plane, ((0,), (0,))).astype(low).reshape(planes, rows, width)
-    up_grad = matmul(h2_plane, dpre, ((0,), (0,))).astype(low).reshape(planes, width // planes, part)
-    up_bias_grad = jnp.sum(dpre.astype(full), axis=0)
-    down_bias_grad = jnp.sum(df.astype(full), axis=0)
-
-    traded_z, traded_plane = along_z(block, block), over_plane(block, block)
-    dh2_parts, up_grad = trade(
-        [like(traded_plane, dh2_parts, *dh2_parts.shape), like(traded_z, up_grad, *up_grad.shape)],
-        "sum_feed_grad",
-        8,
-    )
-    one_part, feed_gain_grad, feed_shift_grad = feed_pull(jnp.sum(dh2_parts.astype(full), axis=0))
-    g1 = g1 + one_part
+        planes,
+    )
+    attended = attended.reshape(line, pair)
     up_grad = jnp.sum(up_grad.astype(full), axis=0).reshape(per_plane, own, part)
-    dout = g1.astype(low)
-    datt = matmul(dout, wo_all, ((1,), (1,))).astype(low)
-    datt = trade([like(along_z(pair_columns, block), datt, planes, rows, pair)], "share_out_grad", 9)[0]
-    datt = jnp.swapaxes(datt.reshape(line, 2, HEAD_DIM), 0, 1)[:, None].astype(full)
-    dweights = jnp.sum(datt * mixed, axis=-1)
-    dmixed = (weights[..., None] * datt).astype(low).reshape(token_shape)
-    dtotal = weights * (dweights - jnp.sum(weights * dweights, axis=1, keepdims=True))
-    dtotal = dtotal.astype(low).astype(full).reshape(per_plane, planes, rows)
-    dtotal = jnp.pad(dtotal, ((0, 0), (0, 8 - planes), (0, 0)))
-    dmixed, dtotal = trade(
-        [
-            like(over_plane(block, second), dmixed, *head_shape),
-            like(traded_plane, dtotal, *dtotal.shape),
-        ],
-        "grads_to_heads",
-        10,
-    )
-    dshared, dvalues, y2_parts, dout_line, down_grad = attend_head_back(
+    dshared, dvalues, y2_parts, dout_line = attend_head_back(
         order,
         place,
         order_rows,
@@ -1232,7 +1450,6 @@
         [
             like(traded_plane, y2_parts, *y2_parts.shape),
             like(along_z(whole, block), dout, planes, rows, width),
-            like(traded_z, down_grad, *down_grad.shape),
         ],
         11,
         planes,

time: 474 us -> 409 us (0.86)
  matrix products: 36 us -> 11.8 us
  other arithmetic: 36.7 us -> 20.8 us
  local copies, waits for them, and re-layouts: 44.7 us -> 28.8 us
  Pallas kernels: 354 us -> 345 us
    pallas_call x11 -> x6, Pallas kernels: 242 us -> 151 us  [exchange(): pl.pallas_call(body, out_shape=[item[2] for item in items], in_specs=[pl....]
    pallas_call x0 -> x1, Pallas kernels: none -> 90.6 us  [feed_stage(): pl.pallas_call(functools.partial(feed_kernel, planes), out_shape=[o[0] fo...]
    dot_general x15 -> x7, matrix products: 36 us -> 11.8 us  [dot(): lax.dot_general(a, b, (contract, ((), ())), preferred_element_type=jnp.fl...]
    unnamed x114 -> x82, local copies, waits for them, and re-layouts: 24.6 us -> 16.4 us
    pallas_call x1, Pallas kernels: 47.2 us -> 39.9 us  [attend_head_back(): pl.pallas_call(beside(kernel, 8, 2, len(scratch), items, planes), out_sha...]
    convert_element_type x4 -> x0, other arithmetic: 4.79 us -> none  [the longest x1 1.91 us: plane_plan(): h2.astype(low)]
where the time goes in v4:
time: 409 us; the launch traced here: 408 us
  Pallas kernels  345 us (84%)
  local copies, waits for them, and re-layouts  28.8 us (7%)
  other arithmetic  20.8 us (5%)
  matrix products  11.8 us (3%)
    pallas_call x6, Pallas kernels, exchange(): pl.pallas_call(body, out_shape=[item[2] for item in items], in_specs=[pl....  151 us
    pallas_call x1, Pallas kernels, feed_stage(): pl.pallas_call(functools.partial(feed_kernel, planes), out_shape=[o[0] fo...  90.6 us
    pallas_call x1, Pallas kernels, attend_head(): pl.pallas_call(beside(kernel, 5, 5, len(scratch), items, planes), out_sha...  50.3 us
    pallas_call x1, Pallas kernels, attend_head_back(): pl.pallas_call(beside(kernel, 8, 2, len(scratch), items, planes), out_sha...  39.9 us
    unnamed x82, local copies, waits for them, and re-layouts  16.4 us
    pallas_call x1, Pallas kernels, sum_small(): pl.pallas_call(functools.partial(sum_small_kernel, planes, items), out_sh...  13.6 us
    dot_general x7, matrix products, dot(): lax.dot_general(a, b, (contract, ((), ())), preferred_element_type=jnp.fl...  11.8 us

profile of v4, /device:TPU:0, one launch (start us, length us, event | category | flops | bytes accessed | tf_op | source)
XLA Modules:
  0.0 407.9 jit_solution(1303558291980097314)
XLA Ops:
  0.7 0.8 fusion.9
  1.5 1.2 reduce_sum.173
  2.7 1.2 multiply_reduce_fusion.2
  5.3 1.9 concatenate.14.refs_0_
  7.2 1.1 convert_reduce_fusion.8
  8.5 22.8 %share_small.1 = (f32[4,8,16,128]{3,2,1,0:T(8,128)}, bf16[4,32,256]{2,1,0:T(8,128)(2,1)}, bf16[4,32,256]{2,1,0:T(8,128)(2,1)}, bf16[4,32,1024]{2,1,0:T(8,128)(2,1)}) custom-call(f32[16,128]{1,0:T(8,128)} %concatenate.14.refs_0_, bf16[32,1024]{1,0:T(8,128)(2,1)} %bitcast.204, bf16[32,1024]{1,0:T(8,128)(2,1)} %bitcast.205, bf16[32,1024]{1,0:T(8,128)(2,1)} %bitcast.206), custom_call_target="tpu_custom_call" | custom-call | tf_op jit(solution)/shard_map/share_small/pallas_call | solution.py:650
  31.3 1.0 copy.76
  34.7 0.9 add_convert_fusion.1.refs_0_
  35.5 25.3 %share_normed.1 = (bf16[4,128,1024]{2,1,0:T(8,128)(2,1)}, bf16[4,8,32,256]{3,2,1,0:T(8,128)(2,1)}, bf16[4,8,32,256]{3,2,1,0:T(8,128)(2,1)}, bf16[8,32,128]{2,1,0...) custom-call(bf16[128,1024]{1,0:T(8,128)(2,1)} %add_convert_fusion.1.refs_0_, ...), custom_call_target="tpu_custom_call" | custom-call | tf_op jit(solution)/shard_map/share_normed/pallas_call | solution.py:650
  60.9 2.6 convolution_convert_fusion.3
  63.4 2.5 convolution_convert_fusion.2
  66.0 24.0 %to_heads.1 = (bf16[4,8,128,128]{3,2,1,0:T(8,128)(2,1)}, bf16[4,8,128,128]{3,2,1,0:T(8,128)(2,1)}) custom-call(bf16[4,128,256]{2,1,0:T(8,128)(2,1)} %bitcast.199, bf16[4,128,256]{2,1,0:T(8,128)(2,1)} %bitcast.200), custom_call_target="tpu_custom_call" | custom-call | tf_op jit(solution)/shard_map/to_heads/pallas_call | solution.py:650
  90.0 1.2 copy-done.2
  91.3 1.2 copy-done.3
  92.5 50.3 %attend.1 = (bf16[4096,128]{1,0:T(8,128)(2,1)S(1)}, bf16[4096,128]{1,0:T(8,128)(2,1)S(1)}, f32[4096,128]{1,0:T(8,128)S(1)}, bf16[4096,128]{1,0:T(8,128)(2,1)S(1)...) custom-call(s32[4096]{0:T(1024)S(1)} %get-tuple-element.166.refs_0_,, ...), custom_call_target="tpu_custom_call" | custom-call | tf_op jit(solution)/shard_map/attend/pallas_call | solution.py:936
  142.8 1.3 copy-done
  144.1 1.0 copy-done.6
  145.0 1.0 copy-done.7
  146.0 1.0 copy-done.9
  147.0 1.0 copy-done.11
  147.9 1.0 copy-done.12
  149.6 22.7 %heads_out.1 = (bf16[8,4,128,128]{3,2,1,0:T(8,128)(2,1)}, f32[8,8,128]{2,1,0:T(8,128)}) custom-call(bf16[4,8,128,128]{3,2,1,0:T(8,128)(2,1)} %bitcast.159, f32[8,8,128]{2,1,0:T(8,128)} %copy-done.18), custom_call_target="tpu_custom_call" | custom-call | tf_op jit(solution)/shard_map/heads_out/pallas_call | solution.py:650
  172.3 90.6 %feed.1 = (f32[128,1024]{1,0:T(8,128)}, f32[128,1024]{1,0:T(8,128)}, bf16[128,1024]{1,0:T(8,128)(2,1)}, bf16[4,128,256]{2,1,0:T(8,128)(2,1)}, bf16[4,8,128,128]{...) custom-call(bf16[8,4,128,128]{3,2,1,0:T(8,128)(2,1)} %get-tuple-elem, ...), custom_call_target="tpu_custom_call" | custom-call | tf_op jit(solution)/shard_map/feed/pallas_call | solution.py:1267
  262.9 1.6 copy-done.1
  264.5 1.2 copy-done.13
  265.7 0.9 copy-done.16
  266.6 0.8 copy-done.17
  267.4 39.9 %attend_back.1 = (bf16[4096,128]{1,0:T(8,128)(2,1)S(1)}, bf16[4096,128]{1,0:T(8,128)(2,1)S(1)}, bf16[8,128,1024]{2,1,0:T(8,128)(2,1)S(1)}, bf16[4,128,1024]{2,1,0:T(8,128)(2,1)S(1)}) custom-call(s32[4096]{0:T(1024)S(1)} %get-tuple-element.166.refs_0_, s32[4096]{0:T(1024)S(1)} %fusion.6.refs_1_, f32[32,128]{1,0:T(8,128)S(1)} %get-tuple-element.167.refs_2_, ...), custom_call_target="tpu_custom_call" | custom-call | tf_op jit(solution)/shard_map/attend_back/pallas_call | solution.py:971
  308.6 27.5 %grads_from_heads.1 = (bf16[8,4,128,128]{3,2,1,0:T(8,128)(2,1)}, bf16[8,4,128,128]{3,2,1,0:T(8,128)(2,1)}) custom-call(bf16[4,8,128,128]{3,2,1,0:T(8,128)(2,1)} %bitcast.157, bf16[4,8,128,128]{3,2,1,0:T(8,128)(2,1)} %bitcast.158), custom_call_target="tpu_custom_call" | custom-call | tf_op jit(solution)/shard_map/grads_from_heads/pallas_call | solution.py:650
  336.2 1.5 reduce.2
  337.8 1.6 reduce.3
  341.8 2.2 fusion
  344.0 1.3 convolution_convert_fusion
  345.3 1.3 convolution_convert_fusion.1
  346.6 0.9 convert_reduce_fusion.4
  347.5 1.0 convert_reduce_fusion.3
  349.0 1.5 add_convert_fusion
  350.5 28.5 %sum_second_grad.1 = (bf16[4,128,1024]{2,1,0:T(8,128)(2,1)}, bf16[8,4,32,256]{3,2,1,0:T(8,128)(2,1)}, bf16[8,4,32,256]{3,2,1,0:T(8,128)(2,1)}, bf16[8,32,1024]{2,1,0:T(8,128)(2,1)}, f32[8,32,512]{2,1,0:T(8,128)}) custom-call(bf16[4,128,1024]{2,1,0:T(8,128)(2,1)} %bitcast.168, bf16[4,8,32,256]{3,2,1,0:T(8,128)(2,1)} %bitcast.179, ...), custom_call_target="tpu_custom_call" | custom-call | tf_op jit(solution)/shard_map/sum_second_grad/pallas_call | solution.py:650
  379.0 1.8 convert_reduce_fusion.1
  381.4 1.1 fusion.2
  383.6 0.7 convert_reduce_fusion.7.refs_1_
  385.1 13.6 %sum_small.1 = (f32[4,16,128]{2,1,0:T(8,128)}, f32[4,32,256]{2,1,0:T(8,128)}, f32[4,32,256]{2,1,0:T(8,128)}) custom-call(f32[8,16,128]{2,1,0:T(8,128)} %pad.13.refs_0_, f32[4,32,256]{2,1,0:T(8,128)} %convert_reduce_fusion.7.refs_1_, f32[4,32,256]{2,1,0:T(8,128)} %convert_reduce_fusion.6.refs_2_), custom_call_target="tpu_custom_call" | custom-call | tf_op jit(solution)/shard_map/sum_small/pallas_call | solution.py:1006
  398.8 0.8 reduce_sum.189
  399.5 1.0 copy.65
  402.4 1.0 copy.66
  405.4 0.9 broadcast_in_dim_reshape.12
  406.3 0.8 copy.81
  407.1 0.8 copy.82
  (127 shorter events, 15.2 us)
Async XLA Ops:
  0.6 34.0 %copy-start.19 = (f32[1,128,1024]{2,1,0:T(8,128)S(1)}, f32[1,128,1024]{2,1,0:T(8,128)}, u32[]{:S(2)}) copy-start(f32[1,128,1024]{2,1,0:T(8,128)} %param.20) | copy-start | bytes 1572868
  60.8 5.1 %copy-start.33 = (bf16[8,32,128]{2,1,0:T(8,128)(2,1)S(1)}, bf16[8,32,128]{2,1,0:T(8,128)(2,1)}, u32[]{:S(2)}) copy-start(bf16[8,32,128]{2,1,0:T(8,128)(2,1)} %get-tuple-element.74) | copy-start | bytes 196612
  60.8 5.1 %copy-start.34 = (bf16[8,32,128]{2,1,0:T(8,128)(2,1)S(1)}, bf16[8,32,128]{2,1,0:T(8,128)(2,1)}, u32[]{:S(2)}) copy-start(bf16[8,32,128]{2,1,0:T(8,128)(2,1)} %get-tuple-element.75) | copy-start | bytes 196612
  60.8 5.1 %copy-start.35 = (bf16[8,32,128]{2,1,0:T(8,128)(2,1)S(1)}, bf16[8,32,128]{2,1,0:T(8,128)(2,1)}, u32[]{:S(2)}) copy-start(bf16[8,32,128]{2,1,0:T(8,128)(2,1)} %get-tuple-element.76) | copy-start | bytes 196612
  60.8 5.1 %copy-start.36 = (bf16[8,32,128]{2,1,0:T(8,128)(2,1)S(1)}, bf16[8,32,128]{2,1,0:T(8,128)(2,1)}, u32[]{:S(2)}) copy-start(bf16[8,32,128]{2,1,0:T(8,128)(2,1)} %get-tuple-element.77) | copy-start | bytes 196612
  60.8 29.2 %copy-start.14 = (bf16[1,128,1024]{2,1,0:T(8,128)(2,1)S(1)}, bf16[1,128,1024]{2,1,0:T(8,128)(2,1)}, u32[]{:S(2)}) copy-start(bf16[1,128,1024]{2,1,0:T(8,128)(2,1)} %param.32) | copy-start | bytes 786436
  60.8 29.2 %copy-start.15 = (bf16[4,32,1024]{2,1,0:T(8,128)(2,1)S(1)}, bf16[4,32,1024]{2,1,0:T(8,128)(2,1)}, u32[]{:S(2)}) copy-start(bf16[4,32,1024]{2,1,0:T(8,128)(2,1)} %get-tuple-element.78.refs_7_) | copy-start | bytes 786436
  90.0 1.2 copy-start.2
  91.3 1.2 copy-start.3
  142.7 1.3 copy-start
  144.1 1.0 copy-start.6
  145.0 1.0 copy-start.7
  146.0 1.0 copy-start.9
  147.0 1.0 copy-start.11
  147.9 1.0 copy-start.12
  148.9 0.6 copy-start.18
  172.2 90.6 %copy-start.8 = (bf16[4096,128]{1,0:T(8,128)(2,1)S(1)}, bf16[4096,128]{1,0:T(8,128)(2,1)}, u32[]{:S(2)}) copy-start(bf16[4096,128]{1,0:T(8,128)(2,1)} %copy-done.7) | copy-start | bytes 3145732
  172.2 90.6 %copy-start.10 = (bf16[4096,128]{1,0:T(8,128)(2,1)S(1)}, bf16[4096,128]{1,0:T(8,128)(2,1)}, u32[]{:S(2)}) copy-start(bf16[4096,128]{1,0:T(8,128)(2,1)} %copy-done.9) | copy-start | bytes 3145732
  262.9 1.6 copy-start.1
  264.5 1.2 copy-start.13
  265.7 0.9 copy-start.16
  266.6 0.8 copy-start.17
  307.3 1.0 copy-start.4
  307.3 1.3 copy-start.5
  336.1 3.9 copy-start.38
  336.1 4.6 %copy-start.37 = (f32[1,1024]{1,0:T(1,128)S(1)}, f32[1,1024]{1,0:T(1,128)}, u32[]{:S(2)}) copy-start(f32[1,1024]{1,0:T(1,128)} %get-tuple-element.106) | copy-start | bytes 12292
  336.1 5.6 %copy-start.39 = (f32[1,512]{1,0:T(1,128)S(1)}, f32[1,512]{1,0:T(1,128)}, u32[]{:S(2)}) copy-start(f32[1,512]{1,0:T(1,128)} %get-tuple-element.107) | copy-start | bytes 6148
  337.6 6.4 %copy-start.21 = (bf16[4,128,1024]{2,1,0:T(8,128)(2,1)S(1)}, bf16[4,128,1024]{2,1,0:T(8,128)(2,1)}, u32[]{:S(2)}) copy-start(bf16[4,128,1024]{2,1,0:T(8,128)(2,1)} %get-tuple-element.69) | copy-start | bytes 3145732
  344.0 2.6 copy-start.24
  345.3 2.2 copy-start.23
  345.3 3.2 copy-start.32
  347.5 1.5 copy-start.25
  350.5 30.3 %copy-start.20 = (f32[1,128,1024]{2,1,0:T(8,128)S(1)}, f32[1,128,1024]{2,1,0:T(8,128)}, u32[]{:S(2)}) copy-start(f32[1,128,1024]{2,1,0:T(8,128)} %param.20) | copy-start | bytes 1572868
  379.0 2.3 copy-start.22
  381.0 2.6 copy-start.28
  381.3 3.0 copy-start.27
  382.5 21.6 %copy-start.26 = (bf16[8,32,1024]{2,1,0:T(8,128)(2,1)S(1)}, bf16[8,32,1024]{2,1,0:T(8,128)(2,1)}, u32[]{:S(2)}) copy-start(bf16[8,32,1024]{2,1,0:T(8,128)(2,1)} %get-tuple-element.113) | copy-start | bytes 1572868
  382.5 22.4 %copy-start.31 = (f32[8,32,512]{2,1,0:T(8,128)S(1)}, f32[8,32,512]{2,1,0:T(8,128)}, u32[]{:S(2)}) copy-start(f32[8,32,512]{2,1,0:T(8,128)} %get-tuple-element.114) | copy-start | bytes 1572868
  403.4 2.9 copy-start.30
  404.9 2.2 copy-start.29

commit v5 on v4

--- a/solution.py
+++ b/solution.py
@@ -544,14 +544,14 @@
         return copy
 
 
-COPIES = 96
+COPIES = 160
 
 
 def link_scratch():
     return [
         pltpu.SemaphoreType.DMA((COPIES,)),
         pltpu.SemaphoreType.DMA((COPIES,)),
-        pltpu.SemaphoreType.DMA((16,)),
+        pltpu.SemaphoreType.DMA((48,)),
     ]
 
 
@@ -680,42 +680,235 @@
     )
 
 
-def across(column):
-    return jnp.broadcast_to(column, (128, 128)).T
-
-
-def down(row):
-    return jnp.broadcast_to(row, (128, 128)).T
-
-
-def dot(a, b, contract):
-    return lax.dot_general(a, b, (contract, ((), ())), preferred_element_type=jnp.float32)
-
-
 def window_masks():
     query = lax.broadcasted_iota(jnp.int32, (128, 128), 0) // BLOCK
     key = lax.broadcasted_iota(jnp.int32, (128, 128), 1) // BLOCK
     return (query == 0) & (key == 1), key <= query
 
 
+def rows_of(index):
+    return pl.ds(pl.multiple_of(index * 128, 128), 128)
+
+
+def pick_tile(table, index_ref, tile, part):
+    return jnp.concatenate(
+        [table[pl.ds(index_ref[tile, part * 32 + row], 1), :] for row in range(32)], axis=0
+    )
+
+
+def sort_tile(order, table, first, second, offset, tile):
+    for part in range(4):
+        start = pl.multiple_of(tile * 128 + part * 32 + offset, 32)
+        picked = pick_tile(table, order, tile, part)
+        first[pl.ds(start, 32), :] = picked[:, :128].astype(first.dtype)
+        second[pl.ds(start, 32), :] = picked[:, 128:].astype(second.dtype)
+
+
+def across(column):
+    return jnp.broadcast_to(column, (128, 128)).T[:1, :]
+
+
+def down(row):
+    return jnp.broadcast_to(row, (128, 128)).T
+
+
+def dot(a, b, contract):
+    return lax.dot_general(a, b, (contract, ((), ())), preferred_element_type=jnp.float32)
+
+
 def key_scales(keys):
     rows = keys.astype(jnp.float32)
     mean_square = jnp.mean(rows * rows, axis=-1, keepdims=True) + 1e-06
     return rows, mean_square, lax.rsqrt(mean_square) / HEAD_DIM
 
 
-def masked_scores(raw, scale, query_pos, key_pos, inside):
+def half_turned(row):
+    return jnp.concatenate([row[:, 64:], row[:, :64]], axis=1)
+
+
+def windows(before, here):
+    return [jnp.concatenate([before[:, 64:], here[:, :64]], axis=1), here]
+
+
+def masked_scores(raw, scale, query_pos, key_pos):
+    return jnp.where(
+        key_pos > query_pos, LATER, jnp.where(key_pos == query_pos, SELF, raw * scale)
+    )
+
+
+def attend_tiles(tiles, unroll, order, order_rows, table, shared, values, mixed, total_sorted, last_scale):
+    sort = functools.partial(sort_tile, order, table, shared, values, BLOCK)
+    end = tiles * 128
+    for tile in [tiles - 1] + list(range(unroll)):
+        sort(tile)
+    shared[:BLOCK, :] = shared[end : end + BLOCK, :]
+    values[:BLOCK, :] = values[end : end + BLOCK, :]
+    last_scale[...] = across(key_scales(shared[end - BLOCK : end + BLOCK, :])[2])
+
+    def step_tiles(step, carry):
+        first = step * unroll
+        numbers = [lax.rem(first + tiles - 1, tiles)] + [first + k for k in range(unroll)]
+        places = [order_rows[pl.ds(t, 1), :] for t in numbers]
+        scale = [last_scale[...]]
+        work = []
+        for k in range(unroll):
+            start = pl.multiple_of((first + k) * 128, 128)
+            keys = [shared[pl.ds(pl.multiple_of(start + half * 64, 64), 128), :] for half in range(2)]
+            vals = [values[pl.ds(pl.multiple_of(start + half * 64, 64), 128), :] for half in range(2)]
+            own = jnp.concatenate([keys[0][64:], keys[1][64:]], axis=0)
+            scale.append(across(key_scales(own)[2]))
+            work.append((keys, vals))
+        last_scale[...] = scale[-1]
+        for k in range(unroll):
+            sort(lax.rem(first + unroll + k, tiles))
+        query_pos = jnp.concatenate([down(place) for place in places[1:]], axis=0)
+        key_pos, key_scale = [], []
+        for k in range(unroll):
+            key_pos += windows(places[k], places[k + 1])
+            key_scale += windows(scale[k], scale[k + 1])
+        raw = [dot(k[64:], k, ((1,), (1,))) for keys, _ in work for k in keys]
+        raw, key_pos, key_scale = (
+            jnp.concatenate([jnp.broadcast_to(a, (64, 128)) for a in parts], axis=0)
+            for parts in (raw, key_pos, key_scale)
+        )
+        scores = masked_scores(raw, key_scale, query_pos, key_pos)
+        highest = jnp.max(scores, axis=-1, keepdims=True)
+        total = highest + jnp.log(jnp.sum(jnp.exp(scores - highest), axis=-1, keepdims=True))
+        prob = jnp.exp(scores - total).astype(jnp.bfloat16)
+        rows = pl.ds(pl.multiple_of(first * 128, 128), unroll * 128)
+        total = jnp.broadcast_to(total, (unroll * 128, 128))
+        mixed[rows, 128:] = total
+        total_sorted[rows, :] = total
+        vals = [v for _, vals in work for v in vals]
+        mixed[rows, :128] = jnp.concatenate(
+            [dot(prob[64 * i : 64 * i + 64], v, ((1,), (0,))) for i, v in enumerate(vals)], axis=0
+        )
+        return carry
+
+    lax.fori_loop(0, tiles // unroll, step_tiles, 0)
+
+
+def attend_back_tiles(
+    tiles, unroll, order, order_rows, table, shared, values, total_sorted,
+    grad_sorted, grad_total_sorted, sums, scale_sums, last_scale,
+):
+    sort = functools.partial(sort_tile, order, table, grad_sorted, grad_total_sorted, 0)
+    end = tiles * 128
+    for tile in range(unroll):
+        sort(tile)
+    last_scale[...] = across(key_scales(shared[end - BLOCK : end + BLOCK, :])[2])
+    scale_sums[...] = jnp.zeros_like(scale_sums)
+    sums[end : end + 128, :] = jnp.zeros((128, 256), jnp.float32)
+    early = lax.broadcasted_iota(jnp.int32, (1, 128), 1) < 64
+
+    def step_tiles(step, carry):
+        first = step * unroll
+        numbers = [lax.rem(first + tiles - 1, tiles)] + [first + k for k in range(unroll)]
+        places = [order_rows[pl.ds(t, 1), :] for t in numbers]
+        scale = [last_scale[...]]
+        work = []
+        for k in range(unroll):
+            start = pl.multiple_of((first + k) * 128, 128)
+            keys = [shared[pl.ds(pl.multiple_of(start + half * 64, 64), 128), :] for half in range(2)]
+            vals = [values[pl.ds(pl.multiple_of(start + half * 64, 64), 128), :] for half in range(2)]
+            own = jnp.concatenate([keys[0][64:], keys[1][64:]], axis=0)
+            scale.append(across(key_scales(own)[2]))
+            tile = pl.ds(start, 128)
+            work.append(
+                (keys, vals, grad_sorted[tile, :], grad_total_sorted[tile, :], total_sorted[tile, :])
+            )
+        last_scale[...] = scale[-1]
+        for k in range(unroll):
+            sort(lax.rem(first + unroll + k, tiles))
+        blocks = 2 * unroll
+        scale_parts = [0.0] * (unroll + 1)
+        query_pos = jnp.concatenate([down(place) for place in places[1:]], axis=0)
+        key_pos, key_scale = [], []
+        for k in range(unroll):
+            key_pos += windows(places[k], places[k + 1])
+            key_scale += windows(scale[k], scale[k + 1])
+        keys = [k for item in work for k in item[0]]
+        vals = [v for item in work for v in item[1]]
+        grads, grad_totals, totals = (
+            jnp.concatenate([item[n] for item in work], axis=0) for n in (2, 3, 4)
+        )
+        own = [slice(64 * i, 64 * i + 64) for i in range(blocks)]
+        raw = [dot(k[64:], k, ((1,), (1,))) for k in keys]
+        grad_prob = [dot(grads[own[i]], v, ((1,), (1,))) for i, v in enumerate(vals)]
+        raw, grad_prob, key_pos, key_scale = (
+            jnp.concatenate([jnp.broadcast_to(a, (64, 128)) for a in parts], axis=0)
+            for parts in (raw, grad_prob, key_pos, key_scale)
+        )
+        prob = jnp.exp(masked_scores(raw, key_scale, query_pos, key_pos) - totals)
+        inner = jnp.sum(prob * grad_prob, axis=-1, keepdims=True)
+        grad_score = jnp.where(
+            key_pos < query_pos, prob * (grad_prob + (grad_totals - inner)), 0.0
+        )
+        product = grad_score * raw
+        for index in range(blocks):
+            k, half = index // 2, index % 2
+            part = jnp.sum(product[own[index]], axis=0, keepdims=True)
+            if half == 0:
+                turned = half_turned(part)
+                scale_parts[k] += jnp.where(early, 0.0, turned)
+                scale_parts[k + 1] += jnp.where(early, turned, 0.0)
+            else:
+                scale_parts[k + 1] += part
+        grad_raw = (grad_score * key_scale).astype(jnp.bfloat16)
+        prob = prob.astype(jnp.bfloat16)
+        key_parts = [dot(grad_raw[own[i]], keys[i][64:], ((0,), (0,))) for i in range(blocks)]
+        value_parts = [dot(prob[own[i]], grads[own[i]], ((0,), (0,))) for i in range(blocks)]
+        query_parts = [dot(grad_raw[own[i]], keys[i], ((1,), (0,))) for i in range(blocks)]
+        key_sums = [key_parts[0][:64]] + [
+            key_parts[i][64:] + query_parts[i] + (key_parts[i + 1][:64] if i + 1 < blocks else 0.0)
+            for i in range(blocks)
+        ]
+        value_sums = [value_parts[0][:64]] + [
+            value_parts[i][64:] + (value_parts[i + 1][:64] if i + 1 < blocks else 0.0)
+            for i in range(blocks)
+        ]
+        for index in range(blocks):
+            rows = pl.ds(pl.multiple_of(first * 128 + index * 64, 64), 64)
+            sums[rows, :128] = key_sums[index + 1]
+            sums[rows, 128:] = value_sums[index + 1]
+        for k in range(unroll):
+            scale_sums[pl.ds(first + k, 1), :] = scale_parts[k + 1]
+        before = jnp.where(step == 0, tiles, numbers[0])
+        rows = pl.ds(pl.multiple_of(before * 128 + 64, 64), 64)
+        sums[rows, :128] += key_sums[0]
+        sums[rows, 128:] += value_sums[0]
+        scale_sums[pl.ds(before, 1), :] += scale_parts[0]
+        return carry
+
+    lax.fori_loop(0, tiles // unroll, step_tiles, 0)
+    sums[end - 128 : end, :] += sums[end : end + 128, :]
+    scale_sums[pl.ds(tiles - 1, 1), :] += scale_sums[pl.ds(tiles, 1), :]
+
+    def finish(step, carry):
+        for part in range(2):
+            tile = step * 2 + part
+            rows = rows_of(tile)
+            start = pl.multiple_of(tile * 128 + 64, 64)
+            keys, mean_square, scale = key_scales(shared[pl.ds(start, 128), :])
+            factor = down(scale_sums[pl.ds(tile, 1), :]) * (scale / (mean_square * HEAD_DIM))
+            sums[rows, :128] -= factor * keys
+        return carry
+
+    lax.fori_loop(0, tiles // 2, finish, 0)
+
+
+def old_across(column):
+    return jnp.broadcast_to(column, (128, 128)).T
+
+
+def old_scores(raw, scale, query_pos, key_pos, inside):
     scores = jnp.where(
         key_pos > query_pos, LATER, jnp.where(key_pos == query_pos, SELF, raw * scale)
     )
     return jnp.where(inside, scores, OUTSIDE)
 
 
-def tile_rows(tile):
-    return pl.ds(pl.multiple_of(tile * 128, 128), 128)
-
-
-def sort_pair(order, table, first, second, tile):
+def old_sort_pair(order, table, first, second, tile):
     for part in range(4):
         start = pl.multiple_of(tile * 128 + part * 32, 32)
         picked = pick_rows(table, order, start, 32)
@@ -723,109 +916,36 @@
         second[pl.ds(start, 32), :] = picked[:, 128:].astype(second.dtype)
 
 
-def attend_kernel(
-    tiles, unroll, order, place, order_rows, shared, values, shared_sorted, values_sorted, total_sorted,
-    mixed_home, total_home, table, mixed, scales,
-):
-    def load(tile, carry):
-        rows = tile_rows(tile)
-        table[rows, :128] = shared[rows, :].astype(jnp.float32)
-        table[rows, 128:] = values[rows, :].astype(jnp.float32)
-        return carry
-
-    lax.fori_loop(0, tiles, load, 0)
-    sort = functools.partial(sort_pair, order, table, shared_sorted, values_sorted)
-    for tile in [tiles - 1] + list(range(unroll)):
-        sort(tile)
-    inside_left, inside_here = window_masks()
-    scales[0] = across(key_scales(shared_sorted[(tiles - 1) * 128 :, :])[2])
-
-    def attend_tiles(step, carry):
-        first = step * unroll
-        numbers = [lax.rem(first + tiles - 1, tiles)] + [first + k for k in range(unroll)]
-        keys = [shared_sorted[tile_rows(t), :] for t in numbers]
-        vals = [values_sorted[tile_rows(t), :] for t in numbers]
-        places = [order_rows[pl.ds(t, 1), :] for t in numbers]
-        scale = [scales[0]] + [across(key_scales(k)[2]) for k in keys[1:]]
-        scales[0] = scale[-1]
-        for k in range(unroll):
-            sort(lax.rem(first + unroll + k, tiles))
-        for k in range(unroll):
-            rows = tile_rows(first + k)
-            query_pos = down(places[k + 1])
-            score_left = masked_scores(
-                dot(keys[k + 1], keys[k], ((1,), (1,))), scale[k], query_pos, places[k], inside_left
-            )
-            score_here = masked_scores(
-                dot(keys[k + 1], keys[k + 1], ((1,), (1,))),
-                scale[k + 1],
-                query_pos,
-                places[k + 1],
-                inside_here,
-            )
-            highest = jnp.max(jnp.maximum(score_left, score_here), axis=-1, keepdims=True)
-            total = highest + jnp.log(
-                jnp.sum(
-                    jnp.exp(score_left - highest) + jnp.exp(score_here - highest),
-                    axis=-1,
-                    keepdims=True,
-                )
-            )
-            prob_left = jnp.exp(score_left - total).astype(jnp.bfloat16)
-            prob_here = jnp.exp(score_here - total).astype(jnp.bfloat16)
-            mixed[rows, :128] = dot(prob_left, vals[k], ((1,), (0,))) + dot(
-                prob_here, vals[k + 1], ((1,), (0,))
-            )
-            total = jnp.broadcast_to(total, (128, 128))
-            mixed[rows, 128:] = total
-            total_sorted[rows, :] = total
-        return carry
-
-    lax.fori_loop(0, tiles // unroll, attend_tiles, 0)
-
-    def unsort(tile, carry):
-        totals = []
-        for part in range(4):
-            start = pl.multiple_of(tile * 128 + part * 32, 32)
-            picked = pick_rows(mixed, place, start, 32)
-            mixed_home[pl.ds(start, 32), :] = picked[:, :128].astype(jnp.bfloat16)
-            totals.append(picked[:, 128:])
-        total_home[lax.rem(tile, 8), pl.ds(tile // 8, 1), :] = jnp.concatenate(totals, axis=0).T[:1, :]
-        return carry
-
-    lax.fori_loop(0, tiles, unsort, 0)
-
-
 def attend_back_kernel(
     tiles, unroll, order, place, order_rows, shared_sorted, values_sorted, total_sorted, grad_mixed, grad_total,
     grad_shared_home, grad_values_home, table, grad_sorted, grad_total_sorted, scales, scale_sums, sums,
 ):
     def load(tile, carry):
-        rows = tile_rows(tile)
+        rows = rows_of(tile)
         table[rows, :128] = grad_mixed[rows, :].astype(jnp.float32)
         table[rows, 128:] = down(grad_total[lax.rem(tile, 8), pl.ds(tile // 8, 1), :])
         return carry
 
     lax.fori_loop(0, tiles, load, 0)
-    sums[tile_rows(tiles - 1), :] = jnp.zeros((128, 256), jnp.float32)
-    sort = functools.partial(sort_pair, order, table, grad_sorted, grad_total_sorted)
+    sums[rows_of(tiles - 1), :] = jnp.zeros((128, 256), jnp.float32)
+    sort = functools.partial(old_sort_pair, order, table, grad_sorted, grad_total_sorted)
     for tile in range(unroll):
         sort(tile)
     inside_left, inside_here = window_masks()
-    scales[0] = across(key_scales(shared_sorted[(tiles - 1) * 128 :, :])[2])
+    scales[0] = old_across(key_scales(shared_sorted[(tiles - 1) * 128 :, :])[2])
     scale_sums[...] = jnp.zeros_like(scale_sums)
 
     def back_tiles(step, carry):
         first = step * unroll
         left = lax.rem(first + tiles - 1, tiles)
         numbers = [left] + [first + k for k in range(unroll)]
-        keys = [shared_sorted[tile_rows(t), :] for t in numbers]
-        vals = [values_sorted[tile_rows(t), :] for t in numbers]
+        keys = [shared_sorted[rows_of(t), :] for t in numbers]
+        vals = [values_sorted[rows_of(t), :] for t in numbers]
         places = [order_rows[pl.ds(t, 1), :] for t in numbers]
-        grads = [grad_sorted[tile_rows(t), :] for t in numbers[1:]]
-        grad_totals = [grad_total_sorted[tile_rows(t), :] for t in numbers[1:]]
-        totals = [total_sorted[tile_rows(t), :] for t in numbers[1:]]
-        scale = [scales[0]] + [across(key_scales(k)[2]) for k in keys[1:]]
+        grads = [grad_sorted[rows_of(t), :] for t in numbers[1:]]
+        grad_totals = [grad_total_sorted[rows_of(t), :] for t in numbers[1:]]
+        totals = [total_sorted[rows_of(t), :] for t in numbers[1:]]
+        scale = [scales[0]] + [old_across(key_scales(k)[2]) for k in keys[1:]]
         scales[0] = scale[-1]
         for k in range(unroll):
             sort(lax.rem(first + unroll + k, tiles))
@@ -836,10 +956,10 @@
             raw_left = dot(here, before, ((1,), (1,)))
             raw_here = dot(here, here, ((1,), (1,)))
             prob_left = jnp.exp(
-                masked_scores(raw_left, scale[k], query_pos, places[k], inside_left) - totals[k]
+                old_scores(raw_left, scale[k], query_pos, places[k], inside_left) - totals[k]
             )
             prob_here = jnp.exp(
-                masked_scores(raw_here, scale[k + 1], query_pos, places[k + 1], inside_here) - totals[k]
+                old_scores(raw_here, scale[k + 1], query_pos, places[k + 1], inside_here) - totals[k]
             )
             grad_prob_left = dot(grad, vals[k], ((1,), (1,)))
             grad_prob_here = dot(grad, vals[k + 1], ((1,), (1,)))
@@ -864,8 +984,8 @@
             value_sums[k + 1] += dot(prob_here.astype(jnp.bfloat16), grad, ((0,), (0,)))
             value_sums[k] += dot(prob_left.astype(jnp.bfloat16), grad, ((0,), (0,)))
         for k, tile in enumerate(numbers[1:]):
-            sums[tile_rows(tile), :128] = key_sums[k + 1]
-            sums[tile_rows(tile), 128:] = value_sums[k + 1]
+            sums[rows_of(tile), :128] = key_sums[k + 1]
+            sums[rows_of(tile), 128:] = value_sums[k + 1]
             scale_sums[pl.ds(tile, 1), :] = scale_parts[k + 1]
         extra = pl.ds(pl.multiple_of(jnp.where(step == 0, tiles, left) * 128, 128), 128)
         extra_row = pl.ds(jnp.where(step == 0, tiles, left), 1)
@@ -876,14 +996,14 @@
 
     sums[pl.ds(tiles * 128, 128), :] = jnp.zeros((128, 256), jnp.float32)
     lax.fori_loop(0, tiles // unroll, back_tiles, 0)
-    last = tile_rows(tiles - 1)
+    last = rows_of(tiles - 1)
     sums[last, :] += sums[pl.ds(tiles * 128, 128), :]
     scale_sums[pl.ds(tiles - 1, 1), :] += scale_sums[pl.ds(tiles, 1), :]
 
     def finish(step, carry):
         for part in range(2):
             tile = step * 2 + part
-            rows = tile_rows(tile)
+            rows = rows_of(tile)
             keys, mean_square, scale = key_scales(shared_sorted[rows, :])
             factor = down(scale_sums[pl.ds(tile, 1), :]) * (scale / (mean_square * HEAD_DIM))
             sums[rows, :128] -= factor * keys
@@ -892,7 +1012,7 @@
     lax.fori_loop(0, tiles // 2, finish, 0)
 
     def unsort(tile, carry):
-        sort_pair(place, sums, grad_shared_home, grad_values_home, tile)
+        old_sort_pair(place, sums, grad_shared_home, grad_values_home, tile)
         return carry
 
     lax.fori_loop(0, tiles, unsort, 0)
@@ -922,35 +1042,6 @@
         drive(transfers)
 
     return body
-
-
-def attend_head(order, place, order_rows, shared, values, items, collective_id, planes, unroll=2):
-    length = shared.shape[0]
-    rows = jax.ShapeDtypeStruct((length, HEAD_DIM), jnp.bfloat16)
-    scratch = [
-        pltpu.VMEM((length, 256), jnp.float32),
-        pltpu.VMEM((length, 256), jnp.float32),
-        pltpu.VMEM((1, 128, 128), jnp.float32),
-    ]
-    kernel = functools.partial(attend_kernel, length // 128, unroll)
-    return pl.pallas_call(
-        beside(kernel, 5, 5, len(scratch), items, planes),
-        out_shape=[
-            rows,
-            rows,
-            jax.ShapeDtypeStruct((length, HEAD_DIM), jnp.float32),
-            rows,
-            jax.ShapeDtypeStruct((8, 8, 128), jnp.float32),
-        ]
-        + [item[2] for item in items],
-        in_specs=[SMEM, SMEM, VMEM, VMEM, VMEM] + [ANY] * len(items),
-        out_specs=[VMEM] * 5 + [ANY] * len(items),
-        scratch_shapes=scratch + link_scratch(),
-        compiler_params=pltpu.CompilerParams(
-            vmem_limit_bytes=40 << 20, collective_id=collective_id, has_side_effects=True
-        ),
-        name="attend",
-    )(order, place, order_rows, shared, values, *[item[1] for item in items])
 
 
 def attend_head_back(
@@ -1088,9 +1179,6 @@
     unit, _ = normal_parts(y1)
     own_rows = pl.ds(pl.multiple_of(links.p * 128, 128), 128)
     h2[own_rows, :] = (unit * gain[...] + shift[...]).astype(low)
-
-    def rows_of(index):
-        return pl.ds(pl.multiple_of(index * 128, 128), 128)
 
     sibling, _ = links.near(1)
     own_h2 = h2.at[own_rows, :]
@@ -1277,6 +1365,262 @@
     )(*arguments)
 
 
+def open_kernel(
+    planes,
+    sort_order, sort_place, gain_a_in, shift_a_in, gain_f_in, shift_f_in, bias_up_in, bias_down_in,
+    x2, wqk, wv, wo, wup, wdown, g2,
+    places_out, gains_out, bias_up_out, normed_out, wqk_out, wv_out, wo_out, wup_out, wdown_out, df_out,
+    shared_out, values_out, total_out, mixed_out, total_home_out,
+    ints, all_ints, floats, all_floats, order_rows, place_rows, order_s, place_s, normed, df,
+    wqk_line, wv_line, wo_line, wup_rows, wqk_pair, wv_pair, heads, head_table, table, mixed,
+    shared, values, total_sorted, mixed_home, total_home, last_scale, send, receive, local,
+):
+    low, full = jnp.bfloat16, jnp.float32
+    links = Links(planes, send, receive, local)
+    links.greet()
+    sub = links.y * 2 + links.core
+    tiles = planes * 8
+    ints[...] = jnp.concatenate([sort_order[...], sort_place[...]], axis=0)
+    lane = lax.broadcasted_iota(jnp.int32, (1, 128), 1) // 32
+
+    def spread(vector):
+        wide = jnp.concatenate([vector[...].astype(full)] * 4, axis=1)
+        return jnp.where(lane == sub, wide, 0.0)
+
+    floats[...] = jnp.concatenate(
+        [spread(v) for v in (gain_a_in, shift_a_in, gain_f_in, shift_f_in, bias_down_in)]
+        + [bias_up_in[...].astype(full), jnp.zeros((2, 128), full)],
+        axis=0,
+    )
+    df[...] = g2[...].astype(low)
+    links.meet()
+    share_floats = everywhere(links, floats, all_floats)
+    next(share_floats)
+    share_ints = everywhere(links, ints, all_ints)
+    next(share_ints)
+
+    def pair_columns(ref, z):
+        return ref.at[:, pl.ds(pl.multiple_of(z * 256, 256), 256)]
+
+    pair_shares = [
+        along_z(pair_columns, block)(links, a, b) for a, b in ((wqk, wqk_line), (wv, wv_line))
+    ]
+    for transfer in pair_shares:
+        next(transfer)
+    unit, _ = normal_parts(x2[...])
+    next(share_floats)
+
+    def upper_columns(chunk):
+        def columns(ref, p):
+            return ref.at[:, pl.ds(pl.multiple_of((chunk * 8 + p) * 128, 128), 128)]
+
+        def landing(ref, p):
+            return ref.at[p, :, pl.ds(chunk * 128, 128)]
+
+        return over_plane(columns, landing)
+
+    drive([share_floats])
+
+    def vector_of(row, z_step=2):
+        chunks = []
+        for chunk in range(8):
+            z, x = chunk // 2, chunk % 2
+            parts = [all_floats[z, x * 4 + u, row : row + 1, :] for u in range(4)]
+            chunks.append(parts[0] + parts[1] + parts[2] + parts[3])
+        return jnp.concatenate(chunks, axis=1)
+
+    gain, shift = vector_of(0), vector_of(1)
+    normed[links.z] = (unit * gain + shift).astype(low)
+    normed_copies = []
+    for step in range(1, planes):
+        device, _, _ = links.along(step)
+        normed_copies.append(links.push(normed.at[links.z], normed.at[links.z], device))
+    for transfer in pair_shares:
+        drive([transfer])
+    pair_shares = [
+        over_chips(whole, second)(links, a, b) for a, b in ((wqk_line, wqk_pair), (wv_line, wv_pair))
+    ]
+    for transfer in pair_shares:
+        next(transfer)
+    next(share_ints)
+    upper_shares = [upper_columns(chunk)(links, wup, wup_rows) for chunk in range(planes)]
+    for transfer in upper_shares:
+        next(transfer)
+    for transfer in pair_shares:
+        next(transfer)
+    gains_out[0:1, :] = gain
+    gains_out[1:2, :] = shift
+    for row in (2, 3, 4):
+        gains_out[row : row + 1, :] = vector_of(row)
+    for z in range(planes):
+        bias_up_out[:, z * 128 : (z + 1) * 128] = all_floats[z, links.p, 5:6, :]
+    drive(pair_shares)
+    drive([share_ints])
+    for z in range(planes):
+        for p in range(8):
+            tile = z * 8 + p
+            order_rows[tile : tile + 1, :] = all_ints[z, p, pl.ds(sub, 1), :]
+            place_rows[tile : tile + 1, :] = all_ints[z, p, pl.ds(sub + 4, 1), :]
+    to_scalars = [links.keep(order_rows, order_s), links.keep(place_rows, place_s)]
+    shares = [over_chips(whole, block)(links, df, df_out)]
+    next(shares[0])
+
+    def head_columns(z):
+        def columns(ref, p):
+            return ref.at[z, :, pl.ds(pl.multiple_of((p // 4) * 256, 256), 256)]
+
+        return columns
+
+    def landing(z):
+        return lambda ref, p: ref.at[z, p]
+
+    def project(z):
+        rows = normed[z]
+        for weights, offset in ((wqk_pair, 0), (wv_pair, 128)):
+            result = dot(rows, weights[...].reshape(-1, 256), ((1,), (0,))).astype(low)
+            heads[z, :, offset : offset + 128] = result[:, :128]
+            heads[z, :, 256 + offset : 384 + offset] = result[:, 128:]
+        transfer = over_chips(head_columns(z), landing(z))(links, heads, head_table)
+        next(transfer)
+        return transfer
+
+    head_shares = [project(links.z)]
+    wo_share = along_z(whole, block)(links, wo, wo_line)
+    next(wo_share)
+    for step, copy in enumerate(normed_copies, 1):
+        copy.wait_recv()
+        head_shares.append(project(links.along(step)[2]))
+        next(head_shares[-2])
+    for transfer in upper_shares:
+        drive([transfer])
+    shares += [
+        along_z(whole, block)(links, wup_rows, wup_out),
+        along_z(whole, block)(links, wdown, wdown_out),
+    ]
+    next(shares[1])
+    next(shares[2])
+    next(head_shares[-1])
+    drive([wo_share])
+    wo_share = over_chips(whole, second)(links, wo_line, wo_out)
+    for copy in to_scalars:
+        copy.wait()
+    drive(head_shares)
+    next(wo_share)
+
+    def load(tile, carry):
+        table[rows_of(tile), :] = head_table[tile // 8, lax.rem(tile, 8)].astype(full)
+        return carry
+
+    lax.fori_loop(0, tiles, load, 0)
+    attend_tiles(
+        tiles, 2, order_s, order_rows, table, shared, values, mixed, total_sorted, last_scale
+    )
+    next(wo_share)
+    next(shares[0])
+    kept = [
+        links.keep(normed, normed_out),
+        links.keep(wqk_pair, wqk_out),
+        links.keep(wv_pair, wv_out),
+        links.keep(shared, shared_out),
+        links.keep(values, values_out),
+        links.keep(total_sorted, total_out),
+        links.keep(order_rows, places_out.at[0]),
+        links.keep(place_rows, places_out.at[1]),
+    ]
+    sent = []
+    for step in (6, 7, 4, 5, 2, 3, 1, 0):
+        device, p = links.near(step)
+
+        def unsort(z, carry):
+            totals = []
+            for part in range(4):
+                picked = pick_tile(mixed, place_s, z * 8 + p, part)
+                mixed_home[p, z, part * 32 : part * 32 + 32, :] = picked[:, :128].astype(low)
+                totals.append(picked[:, 128:])
+            total_home[p, pl.ds(z, 1), :] = jnp.concatenate(totals, axis=0).T[:1, :]
+            return carry
+
+        lax.fori_loop(0, planes, unsort, 0)
+        for here, there in ((mixed_home, mixed_out), (total_home, total_home_out)):
+            source, target = here.at[p], there.at[links.p]
+            if step:
+                sent.append(links.push(source, target, device))
+            else:
+                kept.append(links.keep(source, target))
+    for copy in normed_copies:
+        copy.wait_send()
+    drive(shares + [wo_share])
+    for copy in kept + sent:
+        copy.wait()
+
+
+def open_stage(arguments, collective_id, planes):
+    low, full, whole_number = jnp.bfloat16, jnp.float32, jnp.int32
+    x2, wqk, wup = arguments[8], arguments[9], arguments[12]
+    rows, width = x2.shape
+    own, hidden = wup.shape
+    part = hidden // 8
+    tiles = planes * 8
+    tokens = tiles * rows
+    shape = jax.ShapeDtypeStruct
+    outputs = [
+        (shape((2, tiles, rows), whole_number), ANY),
+        (shape((8, width), full), VMEM),
+        (shape((1, part), full), VMEM),
+        (shape((planes, rows, width), low), ANY),
+        (shape((planes, 8, own, 256), low), ANY),
+        (shape((planes, 8, own, 256), low), ANY),
+        (shape((planes, 8, own, width), low), ANY),
+        (shape((planes, 8, own, part), low), ANY),
+        (shape((planes, rows, width), low), ANY),
+        (shape((8, rows, width), low), ANY),
+        (shape((tokens + BLOCK, HEAD_DIM), low), ANY),
+        (shape((tokens + BLOCK, HEAD_DIM), low), ANY),
+        (shape((tokens, HEAD_DIM), full), ANY),
+        (shape((8, planes, rows, HEAD_DIM), low), ANY),
+        (shape((8, 8, rows), full), ANY),
+    ]
+    scratch = [
+        pltpu.VMEM((8, rows), whole_number),
+        pltpu.VMEM((planes, 8, 8, rows), whole_number),
+        pltpu.VMEM((8, rows), full),
+        pltpu.VMEM((planes, 8, 8, rows), full),
+        pltpu.VMEM((tiles, rows), whole_number),
+        pltpu.VMEM((tiles, rows), whole_number),
+        pltpu.SMEM((tiles, rows), whole_number),
+        pltpu.SMEM((tiles, rows), whole_number),
+        pltpu.VMEM((planes, rows, width), low),
+        pltpu.VMEM((rows, width), low),
+        pltpu.VMEM((planes, own, 256), low),
+        pltpu.VMEM((planes, own, 256), low),
+        pltpu.VMEM((planes, own, width), low),
+        pltpu.VMEM((8, own, part), low),
+        pltpu.VMEM((planes, 8, own, 256), low),
+        pltpu.VMEM((planes, 8, own, 256), low),
+        pltpu.VMEM((planes, rows, 512), low),
+        pltpu.VMEM((planes, 8, rows, 256), low),
+        pltpu.VMEM((tokens, 256), full),
+        pltpu.VMEM((tokens, 256), full),
+        pltpu.VMEM((tokens + BLOCK, HEAD_DIM), low),
+        pltpu.VMEM((tokens + BLOCK, HEAD_DIM), low),
+        pltpu.VMEM((tokens, HEAD_DIM), full),
+        pltpu.VMEM((8, planes, rows, HEAD_DIM), low),
+        pltpu.VMEM((8, 8, rows), full),
+        pltpu.VMEM((1, rows), full),
+    ]
+    return pl.pallas_call(
+        functools.partial(open_kernel, planes),
+        out_shape=[o[0] for o in outputs],
+        in_specs=[VMEM] * 15,
+        out_specs=[o[1] for o in outputs],
+        scratch_shapes=scratch + link_scratch(),
+        compiler_params=pltpu.CompilerParams(
+            vmem_limit_bytes=56 << 20, collective_id=collective_id, has_side_effects=True
+        ),
+        name="open",
+    )(*arguments)
+
+
 def matmul(a, b, contract=((1,), (0,))):
     return dot(a, b, contract)
 
@@ -1318,111 +1662,34 @@
     own = width // devices
     pair = 2 * HEAD_DIM
 
-    def row_of(*vectors):
-        return jnp.concatenate([v[0].astype(full) for v in vectors])[None]
-
-    small = jnp.concatenate(
-        [
-            sort_order[0, :, 0].astype(full),
-            sort_place[0, :, 0].astype(full),
-            row_of(attend_gain, attend_shift, feed_gain, feed_shift),
-            row_of(upper_projection_bias),
-            jnp.pad(row_of(lower_projection_bias), ((0, 5), (0, rows - own))),
-        ],
-        axis=0,
-    )
-    small = jnp.pad(small, ((0, 16 - small.shape[0]), (0, 0)))
-
-    def pair_columns(ref, z):
-        return ref.at[:, pl.ds(pl.multiple_of(z * pair, pair), pair)]
-
-    all_small, wqk_line, wv_line, wo_line = trade(
-        [
-            like(everywhere, small, planes, per_plane, 16, rows),
-            like(along_z(pair_columns, block), wqk, planes, own, pair),
-            like(along_z(pair_columns, block), wv, planes, own, pair),
-            like(along_z(whole, block), wo, planes, own, width),
-        ],
-        "share_small",
+    (
+        places, gains, bias_up, normed_line, wqk_pair, wv_pair, wo_all, wup_part, wdown_part, df_plane,
+        shared_sorted, values_sorted, total_sorted, mixed, total,
+    ) = open_stage(
+        (
+            sort_order[0, :, 0], sort_place[0, :, 0], attend_gain, attend_shift, feed_gain, feed_shift,
+            upper_projection_bias, lower_projection_bias, x2, wqk, wv, wo, wup, wdown, g2,
+        ),
         1,
-    )
-    all_small = all_small.reshape(devices, 16, rows)
-    gain_a, shift_a, gain_f, shift_f = (
-        all_small[:, 8, k * own : (k + 1) * own].reshape(width) for k in range(4)
-    )
-    bias_down = all_small[:, 10, :own].reshape(width)
-    bias_up = jnp.take(
-        all_small[:, 9].reshape(planes, per_plane, rows), me_p, axis=1
-    ).reshape(planes * rows)
-    order_rows = jnp.take(all_small[:, :4], sub, axis=1)
-    order = order_rows.astype(jnp.int32).reshape(tokens)
-    place = jnp.take(all_small[:, 4:8], sub, axis=1).astype(jnp.int32).reshape(tokens)
-
-    normed, attend_pull = jax.vjp(layer_norm, x2, gain_a, shift_a)
-    normed = normed.astype(low)
-
-    def upper_columns(chunk):
-        def columns(ref, p):
-            return ref.at[:, pl.ds(pl.multiple_of((chunk * per_plane + p) * rows, rows), rows)]
-
-        return like(over_plane(columns, block), wup, per_plane, own, rows)
-
-    rows_of_pair = over_chips(whole, second)
-    normed_line, wqk_pair, wv_pair, *wup_rows = trade(
-        [
-            like(along_z(whole, block), normed, planes, rows, width),
-            like(rows_of_pair, wqk_line, planes, per_plane, own, pair),
-            like(rows_of_pair, wv_line, planes, per_plane, own, pair),
-        ]
-        + [upper_columns(chunk) for chunk in range(planes)],
-        "share_normed",
-        2,
-    )
-    wup_rows = jnp.concatenate([a.reshape(per_plane * own, rows) for a in wup_rows], axis=1)
+        planes,
+    )
+    gain_a, shift_a, gain_f, shift_f, bias_down = (gains[k] for k in range(5))
+    attend_pull = jax.vjp(layer_norm, x2, gain_a, shift_a)[1]
+    order, place = places[0].reshape(tokens), places[1].reshape(tokens)
+    order_rows = places[0].astype(full)
     normed_line = normed_line.reshape(line, width)
     wqk_pair, wv_pair = wqk_pair.reshape(width, pair), wv_pair.reshape(width, pair)
-    shared = matmul(normed_line, wqk_pair).astype(low).reshape(planes, rows, pair)
-    values = matmul(normed_line, wv_pair).astype(low).reshape(planes, rows, pair)
-
-    def head_columns(ref, p):
-        return ref.at[:, :, pl.ds(pl.multiple_of((p // 4) * HEAD_DIM, HEAD_DIM), HEAD_DIM)]
-
-    to_head = over_chips(head_columns, second)
+    wo_all = wo_all.reshape(width, width)
+    wup_part, wdown_part = wup_part.reshape(width, part), wdown_part.reshape(part, width)
+    df_plane = df_plane.reshape(per_plane * rows, width)
+    shared_sorted, values_sorted = shared_sorted[BLOCK:], values_sorted[BLOCK:]
+    df = g2.astype(low)
     head_shape = (planes, per_plane, rows, HEAD_DIM)
-    head_shared, head_values = trade(
-        [like(to_head, shared, *head_shape), like(to_head, values, *head_shape)], "to_heads", 3
-    )
-    df = g2.astype(low)
-    (
-        shared_sorted, values_sorted, total_sorted, mixed, total,
-        wup_part, wdown_part, wo_all, df_plane,
-    ) = attend_head(
-        order,
-        place,
-        order_rows,
-        head_shared.reshape(tokens, HEAD_DIM),
-        head_values.reshape(tokens, HEAD_DIM),
-        [
-            like(along_z(whole, block), wup_rows, planes, per_plane * own, part),
-            like(along_z(whole, block), wdown, planes, rows, width),
-            like(over_chips(whole, second), wo_line, planes, per_plane, own, width),
-            like(over_chips(whole, block), df, per_plane, rows, width),
-        ],
-        4,
-        planes,
-    )
-    wup_part, wdown_part = wup_part.reshape(width, part), wdown_part.reshape(part, width)
-    wo_all = wo_all.reshape(width, width)
-    df_plane = df_plane.reshape(per_plane * rows, width)
-
     token_shape = (per_plane, planes, rows, HEAD_DIM)
 
     def to_tokens(array):
         return like(over_plane(second, block), array.reshape(head_shape), *token_shape)
 
-    mixed, total = trade(
-        [to_tokens(mixed), like(over_plane(block, block), total, *total.shape)], "heads_out", 5
-    )
     traded_z, traded_plane = along_z(block, block), over_plane(block, block)
     down_bias_grad = jnp.sum(df.astype(full), axis=0)
     (
@@ -1431,7 +1698,7 @@
     ) = feed_stage(
         (
             mixed, total, x1, wo_all, gain_f[None], shift_f[None],
-            wup_part, bias_up[None], wdown_part, df_plane, g1,
+            wup_part, bias_up, wdown_part, df_plane, g1,
         ),
         6,
         planes,

time: 409 us -> 360 us (0.88)
  Pallas kernels: 345 us -> 317 us
  local copies, waits for them, and re-layouts: 28.8 us -> 18.5 us
  matrix products: 11.8 us -> 5.8 us
    pallas_call x6 -> x2, Pallas kernels: 151 us -> 58.9 us  [exchange(): pl.pallas_call(body, out_shape=[item[2] for item in items], in_specs=[pl....]
    pallas_call x1, Pallas kernels: 50.3 us -> 107 us  [open_stage(): pl.pallas_call(functools.partial(open_kernel, planes), out_shape=[o[0] fo...]
    unnamed x82 -> x56, local copies, waits for them, and re-layouts: 16.4 us -> 7.05 us
    pallas_call x1, Pallas kernels: 90.6 us -> 97.8 us  [feed_stage(): pl.pallas_call(functools.partial(feed_kernel, planes), out_shape=[o[0] fo...]
    dot_general x7 -> x5, matrix products: 11.8 us -> 5.8 us  [dot(): lax.dot_general(a, b, (contract, ((), ())), preferred_element_type=jnp.fl...]
where the time goes in v5:
time: 360 us
  Pallas kernels  317 us (88%)
  local copies, waits for them, and re-layouts  18.5 us (5%)
  other arithmetic  16.8 us (5%)
  matrix products  5.8 us (2%)
    pallas_call x1, Pallas kernels, open_stage(): pl.pallas_call(functools.partial(open_kernel, planes), out_shape=[o[0] fo...  107 us
    pallas_call x1, Pallas kernels, feed_stage(): pl.pallas_call(functools.partial(feed_kernel, planes), out_shape=[o[0] fo...  97.8 us
    pallas_call x2, Pallas kernels, exchange(): pl.pallas_call(body, out_shape=[item[2] for item in items], in_specs=[pl....  58.9 us
    pallas_call x1, Pallas kernels, attend_head_back(): pl.pallas_call(beside(kernel, 8, 2, len(scratch), items, planes), out_sha...  39.2 us
    pallas_call x1, Pallas kernels, sum_small(): pl.pallas_call(functools.partial(sum_small_kernel, planes, items), out_sh...  14.9 us

profile of v5, /device:TPU:0, one launch (start us, length us, event | category | flops | bytes accessed | tf_op | source)
XLA Modules:
  0.0 359.5 jit_solution(11168762837205370742)
XLA Ops:
  0.7 106.6 %open.1 = (s32[2,32,128]{2,1,0:T(8,128)}, f32[8,1024]{1,0:T(8,128)}, f32[1,512]{1,0:T(1,128)}, bf16[4,128,1024]{2,1,0:T(8,128)(2,1)}, bf16[4,8,32,256]{3,2,1,0:T...) custom-call(s32[4,128]{1,0:T(4,128)} %bitcast.150, ...), custom_call_target="tpu_custom_call" | custom-call | tf_op jit(solution)/shard_map/open/pallas_call | solution.py:1611
  107.2 1.5 fusion.8
  108.8 97.8 %feed.1 = (f32[128,1024]{1,0:T(8,128)}, f32[128,1024]{1,0:T(8,128)}, bf16[128,1024]{1,0:T(8,128)(2,1)}, bf16[4,128,256]{2,1,0:T(8,128)(2,1)}, bf16[4,8,128,128]{...) custom-call(bf16[8,4,128,128]{3,2,1,0:T(8,128)(2,1)} %get-tuple-elem, ...), custom_call_target="tpu_custom_call" | custom-call | tf_op jit(solution)/shard_map/feed/pallas_call | solution.py:1355
  206.8 0.5 copy-done.6
  207.3 0.9 copy-done
  208.2 0.6 copy-done.1
  208.8 1.2 copy-done.4
  210.0 0.9 copy-done.5
  211.0 39.2 %attend_back.1 = (bf16[4096,128]{1,0:T(8,128)(2,1)S(1)}, bf16[4096,128]{1,0:T(8,128)(2,1)S(1)}, bf16[8,128,1024]{2,1,0:T(8,128)(2,1)S(1)}, bf16[4,128,1024]{2,1,0:T(8,128)(2,1)S(1)}) custom-call(s32[4096]{0:T(1024)S(1)} %get-tuple-element.133.refs_0_, s32[4096]{0:T(1024)S(1)} %get-tuple-element.132.refs_1_, f32[32,128]{1,0:T(8,128)S(1)} %get-tuple-element.131.refs_2_, ...), custom_call_target="tpu_custom_call" | custom-call | tf_op jit(solution)/shard_map/attend_back/pallas_call | solution.py:1062
  250.2 1.0 copy-done.3
  251.3 1.3 fusion
  252.5 28.5 %grads_from_heads.1 = (bf16[8,4,128,128]{3,2,1,0:T(8,128)(2,1)}, bf16[8,4,128,128]{3,2,1,0:T(8,128)(2,1)}) custom-call(bf16[4,8,128,128]{3,2,1,0:T(8,128)(2,1)} %bitcast.100, bf16[4,8,128,128]{3,2,1,0:T(8,128)(2,1)} %bitcast.101), custom_call_target="tpu_custom_call" | custom-call | tf_op jit(solution)/shard_map/grads_from_heads/pallas_call | solution.py:650
  281.0 2.2 reduce.3
  283.2 1.1 copy.48
  284.3 1.3 convolution_convert_fusion
  285.6 2.2 reduce.2
  287.8 1.1 copy.47
  288.9 1.3 convolution_convert_fusion.1
  290.2 0.5 fusion.9
  290.7 1.5 add_convert_fusion
  292.2 1.0 convert_reduce_fusion.4
  293.1 30.5 %sum_second_grad.1 = (bf16[4,128,1024]{2,1,0:T(8,128)(2,1)}, bf16[8,4,32,256]{3,2,1,0:T(8,128)(2,1)}, bf16[8,4,32,256]{3,2,1,0:T(8,128)(2,1)}, bf16[8,32,1024]{2,1,0:T(8,128)(2,1)}, f32[8,32,512]{2,1,0:T(8,128)}) custom-call(bf16[4,128,1024]{2,1,0:T(8,128)(2,1)} %bitcast.107, bf16[4,8,32,256]{3,2,1,0:T(8,128)(2,1)} %bitcast.114, ...), custom_call_target="tpu_custom_call" | custom-call | tf_op jit(solution)/shard_map/sum_second_grad/pallas_call | solution.py:650
  323.6 2.1 convert_reduce_fusion.6
  325.7 1.7 convert_reduce_fusion.1
  327.6 0.2 multiply_reduce_fusion.2
  327.8 0.3 multiply_reduce_fusion
  328.6 0.5 broadcast.184
  329.1 0.7 reduce.10
  329.9 0.7 reduce.11
  330.8 1.1 convert_reduce_fusion.8
  332.2 0.6 pad.4.refs_0_
  332.8 14.9 %sum_small.1 = (f32[4,16,128]{2,1,0:T(8,128)}, f32[4,32,256]{2,1,0:T(8,128)}, f32[4,32,256]{2,1,0:T(8,128)}) custom-call(f32[8,16,128]{2,1,0:T(8,128)} %pad.4.refs_0_, f32[4,32,256]{2,1,0:T(8,128)} %get-tuple-element.142.refs_1_, f32[4,32,256]{2,1,0:T(8,128)} %get-tuple-element.141.refs_2_), custom_call_target="tpu_custom_call" | custom-call | tf_op jit(solution)/shard_map/sum_small/pallas_call | solution.py:1097
  347.8 0.8 reduce_sum.189
  348.6 0.5 broadcast_select_fusion.1
  349.1 1.0 copy.57
  350.1 0.7 broadcast_in_dim_reshape.10
  350.8 1.0 copy.56
  351.8 0.7 broadcast_in_dim_reshape.9
  352.6 0.5 slice_bitcast_fusion.2
  353.2 0.3 convert_reduce_fusion
  353.6 1.1 fusion.2
  354.8 0.2 reshape.301
  355.0 0.3 copy.58
  355.3 0.9 broadcast_in_dim_reshape.11
  356.2 0.7 convert_reduce_fusion.5
  356.9 1.0 convert_reduce_fusion.3
  357.9 0.8 copy.70
  358.7 0.8 copy.71
  (78 shorter events, 1.7 us)
Async XLA Ops:
  108.8 97.8 %copy-start.23 = (s32[2,32,128]{2,1,0:T(8,128)S(1)}, s32[2,32,128]{2,1,0:T(8,128)}, u32[]{:S(2)}) copy-start(s32[2,32,128]{2,1,0:T(8,128)} %get-tuple-element.65) | copy-start | bytes 98308
  108.8 97.8 %copy-start.15 = (bf16[4160,128]{1,0:T(8,128)(2,1)S(1)}, bf16[4160,128]{1,0:T(8,128)(2,1)}, u32[]{:S(2)}) copy-start(bf16[4160,128]{1,0:T(8,128)(2,1)} %get-tuple-element.66) | copy-start | bytes 3194884
  108.8 97.9 %copy-start.14 = (bf16[4160,128]{1,0:T(8,128)(2,1)S(1)}, bf16[4160,128]{1,0:T(8,128)(2,1)}, u32[]{:S(2)}) copy-start(bf16[4160,128]{1,0:T(8,128)(2,1)} %get-tuple-element.67) | copy-start | bytes 3194884
  206.6 0.8 copy-start.6
  206.6 1.6 copy-start
  206.6 2.2 copy-start.1
  208.8 1.2 copy-start.4
  210.0 0.9 copy-start.5
  211.0 40.3 %copy-start.22 = (bf16[4,128,256]{2,1,0:T(8,128)(2,1)S(1)}, bf16[4,128,256]{2,1,0:T(8,128)(2,1)}, u32[]{:S(2)}) copy-start(bf16[4,128,256]{2,1,0:T(8,128)(2,1)} %get-tuple-element.82) | copy-start | bytes 786436
  250.2 1.0 copy-start.3
  251.3 1.3 copy-start.2
  252.5 31.8 %copy-start.9 = (bf16[4,128,1024]{2,1,0:T(8,128)(2,1)S(1)}, bf16[4,128,1024]{2,1,0:T(8,128)(2,1)}, u32[]{:S(2)}) copy-start(bf16[4,128,1024]{2,1,0:T(8,128)(2,1)} %get-tuple-element.81) | copy-start | bytes 3145732
  284.3 3.5 copy-start.10
  288.8 1.3 copy-start.21
  288.9 1.8 copy-start.11
  288.9 1.8 copy-start.16
  290.7 1.5 copy-start.13
  323.6 3.9 %copy-start.7 = (f32[1,128,1024]{2,1,0:T(8,128)S(1)}, f32[1,128,1024]{2,1,0:T(8,128)}, u32[]{:S(2)}) copy-start(f32[1,128,1024]{2,1,0:T(8,128)} %param.18) | copy-start | bytes 1572868
  325.7 2.8 copy-start.26
  325.7 3.4 copy-start.25
  325.7 4.2 %copy-start.24 = (f32[1,1024]{1,0:T(1,128)S(1)}, f32[1,1024]{1,0:T(1,128)}, u32[]{:S(2)}) copy-start(f32[1,1024]{1,0:T(1,128)} %get-tuple-element.87) | copy-start | bytes 12292
  352.6 1.0 copy-start.8
  353.5 1.3 copy-start.20
  354.8 1.4 copy-start.17
  354.8 2.2 copy-start.12
  355.0 2.9 copy-start.19
  355.3 3.4 copy-start.18

commit v6 on v5

--- a/solution.py
+++ b/solution.py
@@ -12,7 +12,6 @@
 BLOCK = 64
 LATER = -1000000000.0
 SELF = -100000.0
-OUTSIDE = -3e38
 
 
 def from_behind(block, axis, distance):
@@ -638,26 +637,6 @@
         transfers = left
 
 
-def exchange(items, name, collective_id, planes):
-    count = len(items)
-
-    def body(*refs):
-        links = Links(planes, *refs[2 * count :])
-        links.greet()
-        links.meet()
-        drive([item[0](links, refs[k], refs[count + k]) for k, item in enumerate(items)])
-
-    return pl.pallas_call(
-        body,
-        out_shape=[item[2] for item in items],
-        in_specs=[pl.BlockSpec(memory_space=pl.ANY)] * count,
-        out_specs=[pl.BlockSpec(memory_space=pl.ANY)] * count,
-        scratch_shapes=link_scratch(),
-        compiler_params=pltpu.CompilerParams(collective_id=collective_id, has_side_effects=True),
-        name=name,
-    )(*[item[1] for item in items])
-
-
 def whole(ref, index):
     return ref
 
@@ -668,22 +647,6 @@
 
 def second(ref, index):
     return ref.at[:, index]
-
-
-def like(kind, array, *shape):
-    return (kind, array, jax.ShapeDtypeStruct(shape, array.dtype))
-
-
-def pick_rows(table, index_ref, start, count):
-    return jnp.concatenate(
-        [table[pl.ds(index_ref[start + row], 1), :] for row in range(count)], axis=0
-    )
-
-
-def window_masks():
-    query = lax.broadcasted_iota(jnp.int32, (128, 128), 0) // BLOCK
-    key = lax.broadcasted_iota(jnp.int32, (128, 128), 1) // BLOCK
-    return (query == 0) & (key == 1), key <= query
 
 
 def rows_of(index):
@@ -897,217 +860,8 @@
     lax.fori_loop(0, tiles // 2, finish, 0)
 
 
-def old_across(column):
-    return jnp.broadcast_to(column, (128, 128)).T
-
-
-def old_scores(raw, scale, query_pos, key_pos, inside):
-    scores = jnp.where(
-        key_pos > query_pos, LATER, jnp.where(key_pos == query_pos, SELF, raw * scale)
-    )
-    return jnp.where(inside, scores, OUTSIDE)
-
-
-def old_sort_pair(order, table, first, second, tile):
-    for part in range(4):
-        start = pl.multiple_of(tile * 128 + part * 32, 32)
-        picked = pick_rows(table, order, start, 32)
-        first[pl.ds(start, 32), :] = picked[:, :128].astype(first.dtype)
-        second[pl.ds(start, 32), :] = picked[:, 128:].astype(second.dtype)
-
-
-def attend_back_kernel(
-    tiles, unroll, order, place, order_rows, shared_sorted, values_sorted, total_sorted, grad_mixed, grad_total,
-    grad_shared_home, grad_values_home, table, grad_sorted, grad_total_sorted, scales, scale_sums, sums,
-):
-    def load(tile, carry):
-        rows = rows_of(tile)
-        table[rows, :128] = grad_mixed[rows, :].astype(jnp.float32)
-        table[rows, 128:] = down(grad_total[lax.rem(tile, 8), pl.ds(tile // 8, 1), :])
-        return carry
-
-    lax.fori_loop(0, tiles, load, 0)
-    sums[rows_of(tiles - 1), :] = jnp.zeros((128, 256), jnp.float32)
-    sort = functools.partial(old_sort_pair, order, table, grad_sorted, grad_total_sorted)
-    for tile in range(unroll):
-        sort(tile)
-    inside_left, inside_here = window_masks()
-    scales[0] = old_across(key_scales(shared_sorted[(tiles - 1) * 128 :, :])[2])
-    scale_sums[...] = jnp.zeros_like(scale_sums)
-
-    def back_tiles(step, carry):
-        first = step * unroll
-        left = lax.rem(first + tiles - 1, tiles)
-        numbers = [left] + [first + k for k in range(unroll)]
-        keys = [shared_sorted[rows_of(t), :] for t in numbers]
-        vals = [values_sorted[rows_of(t), :] for t in numbers]
-        places = [order_rows[pl.ds(t, 1), :] for t in numbers]
-        grads = [grad_sorted[rows_of(t), :] for t in numbers[1:]]
-        grad_totals = [grad_total_sorted[rows_of(t), :] for t in numbers[1:]]
-        totals = [total_sorted[rows_of(t), :] for t in numbers[1:]]
-        scale = [scales[0]] + [old_across(key_scales(k)[2]) for k in keys[1:]]
-        scales[0] = scale[-1]
-        for k in range(unroll):
-            sort(lax.rem(first + unroll + k, tiles))
-        key_sums, value_sums, scale_parts = [0.0] * (unroll + 1), [0.0] * (unroll + 1), [0.0] * (unroll + 1)
-        for k in range(unroll):
-            here, before, grad = keys[k + 1], keys[k], grads[k]
-            query_pos = down(places[k + 1])
-            raw_left = dot(here, before, ((1,), (1,)))
-            raw_here = dot(here, here, ((1,), (1,)))
-            prob_left = jnp.exp(
-                old_scores(raw_left, scale[k], query_pos, places[k], inside_left) - totals[k]
-            )
-            prob_here = jnp.exp(
-                old_scores(raw_here, scale[k + 1], query_pos, places[k + 1], inside_here) - totals[k]
-            )
-            grad_prob_left = dot(grad, vals[k], ((1,), (1,)))
-            grad_prob_here = dot(grad, vals[k + 1], ((1,), (1,)))
-            inner = jnp.sum(
-                prob_left * grad_prob_left + prob_here * grad_prob_here, axis=-1, keepdims=True
-            )
-            shift = grad_totals[k] - inner
-            keep_left = inside_left & (places[k] < query_pos)
-            keep_here = inside_here & (places[k + 1] < query_pos)
-            grad_score_left = jnp.where(keep_left, prob_left * (grad_prob_left + shift), 0.0)
-            grad_score_here = jnp.where(keep_here, prob_here * (grad_prob_here + shift), 0.0)
-            scale_parts[k] += jnp.sum(grad_score_left * raw_left, axis=0, keepdims=True)
-            scale_parts[k + 1] += jnp.sum(grad_score_here * raw_here, axis=0, keepdims=True)
-            grad_raw_left = (grad_score_left * scale[k]).astype(jnp.bfloat16)
-            grad_raw_here = (grad_score_here * scale[k + 1]).astype(jnp.bfloat16)
-            key_sums[k + 1] += (
-                dot(grad_raw_left, before, ((1,), (0,)))
-                + dot(grad_raw_here, here, ((1,), (0,)))
-                + dot(grad_raw_here, here, ((0,), (0,)))
-            )
-            key_sums[k] += dot(grad_raw_left, here, ((0,), (0,)))
-            value_sums[k + 1] += dot(prob_here.astype(jnp.bfloat16), grad, ((0,), (0,)))
-            value_sums[k] += dot(prob_left.astype(jnp.bfloat16), grad, ((0,), (0,)))
-        for k, tile in enumerate(numbers[1:]):
-            sums[rows_of(tile), :128] = key_sums[k + 1]
-            sums[rows_of(tile), 128:] = value_sums[k + 1]
-            scale_sums[pl.ds(tile, 1), :] = scale_parts[k + 1]
-        extra = pl.ds(pl.multiple_of(jnp.where(step == 0, tiles, left) * 128, 128), 128)
-        extra_row = pl.ds(jnp.where(step == 0, tiles, left), 1)
-        sums[extra, :128] += key_sums[0]
-        sums[extra, 128:] += value_sums[0]
-        scale_sums[extra_row, :] += scale_parts[0]
-        return carry
-
-    sums[pl.ds(tiles * 128, 128), :] = jnp.zeros((128, 256), jnp.float32)
-    lax.fori_loop(0, tiles // unroll, back_tiles, 0)
-    last = rows_of(tiles - 1)
-    sums[last, :] += sums[pl.ds(tiles * 128, 128), :]
-    scale_sums[pl.ds(tiles - 1, 1), :] += scale_sums[pl.ds(tiles, 1), :]
-
-    def finish(step, carry):
-        for part in range(2):
-            tile = step * 2 + part
-            rows = rows_of(tile)
-            keys, mean_square, scale = key_scales(shared_sorted[rows, :])
-            factor = down(scale_sums[pl.ds(tile, 1), :]) * (scale / (mean_square * HEAD_DIM))
-            sums[rows, :128] -= factor * keys
-        return carry
-
-    lax.fori_loop(0, tiles // 2, finish, 0)
-
-    def unsort(tile, carry):
-        old_sort_pair(place, sums, grad_shared_home, grad_values_home, tile)
-        return carry
-
-    lax.fori_loop(0, tiles, unsort, 0)
-
-
 VMEM = pl.BlockSpec(memory_space=pltpu.VMEM)
-SMEM = pl.BlockSpec(memory_space=pltpu.SMEM)
 ANY = pl.BlockSpec(memory_space=pl.ANY)
-
-
-def beside(kernel, inputs, outputs, scratch, items, planes):
-    count = len(items)
-
-    def body(*refs):
-        refs = list(refs)
-        own, refs = refs[:inputs], refs[inputs:]
-        here, refs = refs[:count], refs[count:]
-        own, refs = own + refs[:outputs], refs[outputs:]
-        there, refs = refs[:count], refs[count:]
-        links = Links(planes, *refs[scratch:])
-        links.greet()
-        links.meet()
-        transfers = [item[0](links, here[k], there[k]) for k, item in enumerate(items)]
-        for transfer in transfers:
-            next(transfer)
-        kernel(*own, *refs[:scratch])
-        drive(transfers)
-
-    return body
-
-
-def attend_head_back(
-    order, place, order_rows, shared_sorted, values_sorted, total_sorted, grad, grad_total,
-    items, collective_id, planes, unroll=2,
-):
-    length = grad.shape[0]
-    rows = jax.ShapeDtypeStruct((length, HEAD_DIM), jnp.bfloat16)
-    scratch = [
-        pltpu.VMEM((length, 256), jnp.float32),
-        pltpu.VMEM((length, HEAD_DIM), jnp.bfloat16),
-        pltpu.VMEM((length, HEAD_DIM), jnp.float32),
-        pltpu.VMEM((1, 128, 128), jnp.float32),
-        pltpu.VMEM((length // 128 + 8, 128), jnp.float32),
-        pltpu.VMEM((length + 128, 256), jnp.float32),
-    ]
-    kernel = functools.partial(attend_back_kernel, length // 128, unroll)
-    return pl.pallas_call(
-        beside(kernel, 8, 2, len(scratch), items, planes),
-        out_shape=[rows, rows] + [item[2] for item in items],
-        in_specs=[SMEM, SMEM] + [VMEM] * 6 + [ANY] * len(items),
-        out_specs=[VMEM] * 2 + [ANY] * len(items),
-        scratch_shapes=scratch + link_scratch(),
-        compiler_params=pltpu.CompilerParams(
-            vmem_limit_bytes=40 << 20, collective_id=collective_id, has_side_effects=True
-        ),
-        name="attend_back",
-    )(
-        order, place, order_rows, shared_sorted, values_sorted, total_sorted, grad, grad_total,
-        *[item[1] for item in items],
-    )
-
-
-def sum_small_kernel(planes, items, *refs):
-    count = len(items)
-    tiles, here, refs = refs[0], refs[1 : 1 + count], refs[1 + count :]
-    result, there, refs = refs[0], refs[1 : 1 + count], refs[1 + count :]
-    arrived, summed, refs = refs[0], refs[1], refs[2:]
-    links = Links(planes, *refs)
-    links.greet()
-    links.meet()
-    transfers = [item[0](links, here[k], there[k]) for k, item in enumerate(items)]
-    small = over_plane(block, block)(links, tiles, arrived)
-    next(small)
-    for transfer in transfers:
-        next(transfer)
-    drive([small])
-    summed[...] = jnp.sum(arrived[...], axis=0)
-    drive([along_z(whole, block)(links, summed, result)] + transfers)
-
-
-def sum_small(tiles, items, collective_id, planes):
-    return pl.pallas_call(
-        functools.partial(sum_small_kernel, planes, items),
-        out_shape=[jax.ShapeDtypeStruct((planes,) + tiles.shape[1:], tiles.dtype)]
-        + [item[2] for item in items],
-        in_specs=[VMEM] + [ANY] * len(items),
-        out_specs=[VMEM] + [ANY] * len(items),
-        scratch_shapes=[
-            pltpu.VMEM(tiles.shape, tiles.dtype),
-            pltpu.VMEM(tiles.shape[1:], tiles.dtype),
-        ]
-        + link_scratch(),
-        compiler_params=pltpu.CompilerParams(collective_id=collective_id, has_side_effects=True),
-        name="sum_small",
-    )(tiles, *[item[1] for item in items])
 
 
 def normal_parts(rows):
@@ -1138,7 +892,7 @@
 
 def feed_kernel(
     planes,
-    mixed, total, x1, wo_in, gain, shift, wup_in, bias_up, wdown_in, df_in, g1,
+    mixed, total, x1, wo_in, gains, wup_in, bias_up, wdown_in, df_in, g1,
     y1_out, g1_out, dout_out, attended_out, dmixed_home, dtotal_home, y2_out, up_grad_out, down_grad_out,
     up_bias_out, gain_out, shift_out,
     wo, wup, wdown, df, weights, attended, arrived, h2, dact, act, dpre, kept, to_sibling, from_sibling,
@@ -1178,7 +932,7 @@
     y1_out[...] = y1
     unit, _ = normal_parts(y1)
     own_rows = pl.ds(pl.multiple_of(links.p * 128, 128), 128)
-    h2[own_rows, :] = (unit * gain[...] + shift[...]).astype(low)
+    h2[own_rows, :] = (unit * gains[2:3, :] + gains[3:4, :]).astype(low)
 
     sibling, _ = links.near(1)
     own_h2 = h2.at[own_rows, :]
@@ -1244,7 +998,7 @@
     grad = own_sum + (
         from_chip[0].astype(full) + from_chip[1].astype(full) + from_chip[2].astype(full)
     )
-    part, gain_grad, shift_grad = norm_back(grad, y1_out[...], gain[...])
+    part, gain_grad, shift_grad = norm_back(grad, y1_out[...], gains[2:3, :])
     gain_out[...] = gain_grad
     shift_out[...] = shift_grad
     g1_new = g1[...] + part
@@ -1308,7 +1062,7 @@
 
 def feed_stage(arguments, collective_id, planes):
     low, full = jnp.bfloat16, jnp.float32
-    (mixed, total, x1, wo, gain, shift, wup, bias_up, wdown, df, g1) = arguments
+    (mixed, total, x1, wo, gains, wup, bias_up, wdown, df, g1) = arguments
     rows, width = x1.shape
     part = wup.shape[1]
     shape = jax.ShapeDtypeStruct
@@ -1355,7 +1109,7 @@
     return pl.pallas_call(
         functools.partial(feed_kernel, planes),
         out_shape=[o[0] for o in outputs],
-        in_specs=[VMEM, VMEM, VMEM, ANY, VMEM, VMEM, ANY, VMEM, ANY, ANY, VMEM],
+        in_specs=[VMEM, VMEM, VMEM, ANY, VMEM, ANY, VMEM, ANY, ANY, VMEM],
         out_specs=[o[1] for o in outputs],
         scratch_shapes=[pltpu.VMEM(*s) for s in scratch] + link_scratch(),
         compiler_params=pltpu.CompilerParams(
@@ -1621,8 +1375,272 @@
     )(*arguments)
 
 
-def matmul(a, b, contract=((1,), (0,))):
-    return dot(a, b, contract)
+def close_kernel(
+    planes,
+    places, shared_in, values_in, total_in, dmixed_in, dtotal_in, y2_in, dout_in, attended_in, normed_in,
+    wqk_in, wv_in, gains, x2_in, g2_in, up_in, down_in, up_bias, feed_gain, feed_shift,
+    y2_out, g2_out, shared_grad_out, value_grad_out, out_grad_out, up_out, down_out, vectors_out,
+    order_rows, order_s, place_s, shared, values, total_sorted, dmixed, dtotal, table, grad_sorted,
+    grad_total_sorted, sums, scale_sums, last_scale, kept, from_sibling, to_chip, from_chip, y2_parts,
+    dout_line, attended, normed, wqk, wv, x2, g2, up_parts, down_parts, up_sum, up_arrived, dshared, dvalues,
+    de_out, de, out_sent, out_arrived, weight_sent, weight_arrived, weight_sum, weight_final,
+    tiles_sent, tiles_arrived, tile, tile_line, send, receive, local,
+):
+    low, full = jnp.bfloat16, jnp.float32
+    links = Links(planes, send, receive, local)
+    links.greet()
+    tiles = planes * 8
+    line = planes * 128
+    first_loads = [
+        links.keep(a, b)
+        for a, b in (
+            (places.at[0], order_s), (places.at[1], place_s), (places.at[0], order_rows),
+            (dmixed_in, dmixed), (dtotal_in, dtotal), (shared_in, shared), (values_in, values),
+            (total_in, total_sorted), (up_in, up_parts),
+        )
+    ]
+    links.meet()
+    share_dout = along_z(whole, block)(links, dout_in, dout_line)
+    next(share_dout)
+    share_y2 = over_plane(block, block)(links, y2_in, y2_parts)
+    next(share_y2)
+    loads = [
+        links.keep(a, b)
+        for a, b in (
+            (attended_in, attended), (normed_in, normed), (wqk_in, wqk), (wv_in, wv), (x2_in, x2),
+            (g2_in, g2), (down_in, down_parts),
+        )
+    ]
+    for copy in first_loads:
+        copy.wait()
+    up_sum[...] = sum(up_parts[z].astype(full) for z in range(planes)).reshape(up_sum.shape)
+    share_up = over_plane(block, block)(links, up_sum, up_arrived)
+    next(share_up)
+
+    def load(index, carry):
+        z, p = index // 8, lax.rem(index, 8)
+        table[rows_of(index), :128] = dmixed[z, p].astype(full)
+        table[rows_of(index), 128:] = down(dtotal[p, pl.ds(z, 1), :])
+        return carry
+
+    lax.fori_loop(0, tiles, load, 0)
+    attend_back_tiles(
+        tiles, 4, order_s, order_rows, table, shared, values, total_sorted,
+        grad_sorted, grad_total_sorted, sums, scale_sums, last_scale,
+    )
+    sibling, _ = links.near(1)
+
+    def unsort(slot, step):
+        chip = links.near(step)[1] // 2
+        for core, goal in ((0, 1 - links.core), (1, links.core)):
+
+            def rows(z, carry):
+                for part in range(4):
+                    picked = pick_tile(sums, place_s, z * 8 + chip * 2 + goal, part)
+                    kept[slot, core, z, part * 32 : part * 32 + 32, :] = picked.astype(low)
+                return carry
+
+            lax.fori_loop(0, planes, rows, 0)
+            if core == 0:
+                traded = links.push(kept.at[slot, 0], from_sibling.at[slot], sibling)
+        return traded
+
+    def chip_sum(slot, step, traded):
+        traded.wait_recv()
+        result = kept[slot, 1].astype(full) + from_sibling[slot].astype(full)
+        if step == 0:
+            return result
+        to_chip[slot] = result.astype(low)
+        return links.push(to_chip.at[slot], from_chip.at[slot], links.near(step)[0])
+
+    steps = (6, 4, 2, 0)
+    traded, sent = [], []
+    for slot, step in enumerate(steps):
+        traded.append(unsort(slot, step))
+        if slot:
+            sent.append(chip_sum(slot - 1, steps[slot - 1], traded[slot - 1]))
+    for copy in loads:
+        copy.wait()
+    drive([share_dout])
+    all_dout = dout_line[...].reshape(line, -1)
+    out_sent[...] = (
+        dot(attended[...].reshape(line, 256), all_dout, ((0,), (0,))).astype(low).reshape(out_sent.shape)
+    )
+    own_sum = chip_sum(3, 0, traded[3])
+    share_out = over_plane(block, block)(links, out_sent, out_arrived)
+    next(share_out)
+    own_columns = pl.ds(pl.multiple_of(links.x * 128, 128), 128)
+    far_columns = pl.ds(pl.multiple_of((1 - links.x) * 128, 128), 128)
+
+    def settle_sum(columns, result):
+        result = result.astype(low).reshape(line, 256)
+        dshared[:, columns] = result[:, :128]
+        dvalues[:, columns] = result[:, 128:]
+
+    sent[2].wait_recv()
+    settle_sum(own_columns, own_sum + from_chip[2].astype(full))
+    sent[1].wait_recv()
+    sent[0].wait_recv()
+    settle_sum(far_columns, from_chip[1].astype(full) + from_chip[0].astype(full))
+    all_wqk, all_wv = wqk[...].reshape(-1, 256), wv[...].reshape(-1, 256)
+
+    def input_grad(z, carry):
+        rows = rows_of(z)
+        de_out[z] = (
+            dot(dshared[rows, :], all_wqk, ((1,), (1,))) + dot(dvalues[rows, :], all_wv, ((1,), (1,)))
+        ).astype(low)
+        return carry
+
+    lax.fori_loop(0, planes, input_grad, 0)
+    share_de = along_z(block, block)(links, de_out, de)
+    next(share_de)
+    all_normed = normed[...].reshape(line, -1)
+    for index, grad in enumerate((dshared, dvalues)):
+        weight_sent[index] = (
+            dot(all_normed, grad[...], ((0,), (0,))).astype(low).reshape(weight_sent.shape[1:])
+        )
+
+    def of_pair(ref, p):
+        return ref.at[:, :, p]
+
+    share_weights = over_plane(of_pair, block)(links, weight_sent, weight_arrived)
+    next(share_weights)
+    drive([share_y2])
+    y2_out[...] = x2[...] + (
+        sum(y2_parts[p].astype(full) for p in range(8)) + gains[4:5, :]
+    )
+    drive([share_up])
+    for p in range(8):
+        for z in range(planes):
+            up_out[:, (z * 8 + p) * 128 : (z * 8 + p + 1) * 128] = up_arrived[
+                p, :, z * 128 : (z + 1) * 128
+            ]
+    down_out[...] = sum(down_parts[z].astype(full) for z in range(planes))
+    drive([share_out])
+    out_grad_out[...] = sum(out_arrived[p].astype(full) for p in range(8))
+    down_bias = jnp.sum(g2[...].astype(low).astype(full), axis=0, keepdims=True)
+    drive([share_weights])
+    weight_sum[...] = sum(weight_arrived[p].astype(full) for p in range(8)).astype(low)
+
+    def pair_columns(ref, z):
+        return ref.at[:, :, pl.ds(pl.multiple_of(z * 256, 256), 256)]
+
+    share_final = along_z(second, pair_columns)(links, weight_sum, weight_final)
+    next(share_final)
+    drive([share_de])
+    part, gain_grad, shift_grad = norm_back(
+        sum(de[z].astype(full) for z in range(planes)), x2[...], gains[0:1, :]
+    )
+    vectors = [gain_grad, shift_grad, feed_gain[...], feed_shift[...], down_bias]
+    for x in range(2):
+        for index, vector in enumerate(vectors):
+            for z in range(planes):
+                chunk = (z * 2 + x) * 128
+                row = index * planes + z
+                tiles_sent[x, row : row + 1, :] = vector[:, chunk : chunk + 128]
+        tiles_sent[x, 5 * planes :, :] = jnp.zeros((24 - 5 * planes, 128), full)
+
+    def of_x(ref, p):
+        return ref.at[p // 4]
+
+    share_tiles = over_plane(of_x, block)(links, tiles_sent, tiles_arrived)
+    next(share_tiles)
+    g2_out[...] = g2[...] + part
+    drive([share_tiles])
+    tile[...] = jnp.sum(tiles_arrived[...], axis=0)
+    for z in range(planes):
+        tile[5 * planes + z : 5 * planes + z + 1, :] = up_bias[:, z * 128 : (z + 1) * 128]
+    share_tile = along_z(whole, block)(links, tile, tile_line)
+    next(share_tile)
+    drive([share_final])
+    shared_grad_out[...] = weight_final[0].astype(full)
+    value_grad_out[...] = weight_final[1].astype(full)
+    drive([share_tile])
+    tile[...] = jnp.sum(tile_line[...], axis=0)
+    for index in range(6):
+        vectors_out[index : index + 1, :] = tile[pl.ds(index * planes + links.z, 1), :]
+    vectors_out[6:8, :] = jnp.zeros((2, 128), full)
+    for copy in traded + sent:
+        copy.wait_send()
+
+
+def close_stage(arguments, collective_id, planes):
+    low, full, whole_number = jnp.bfloat16, jnp.float32, jnp.int32
+    x2, normed = arguments[13], arguments[9]
+    own, part = arguments[10].shape[2], arguments[15].shape[2]
+    rows, width = x2.shape
+    tiles = planes * 8
+    tokens = tiles * rows
+    shape = jax.ShapeDtypeStruct
+    outputs = [
+        shape((rows, width), full),
+        shape((rows, width), full),
+        shape((own, width), full),
+        shape((own, width), full),
+        shape((own, width), full),
+        shape((own, 8 * part), full),
+        shape((rows, width), full),
+        shape((8, rows), full),
+    ]
+    vmem = pltpu.VMEM
+    chip_blocks = (planes, rows, 256)
+    scratch = [
+        vmem((tiles, rows), whole_number),
+        pltpu.SMEM((tiles, rows), whole_number),
+        pltpu.SMEM((tiles, rows), whole_number),
+        vmem((tokens + BLOCK, HEAD_DIM), low),
+        vmem((tokens + BLOCK, HEAD_DIM), low),
+        vmem((tokens, HEAD_DIM), full),
+        vmem((planes, 8, rows, HEAD_DIM), low),
+        vmem((8, 8, rows), full),
+        vmem((tokens, 256), full),
+        vmem((tokens, HEAD_DIM), low),
+        vmem((tokens, HEAD_DIM), full),
+        vmem((tokens + rows, 256), full),
+        vmem((tiles + 8, rows), full),
+        vmem((1, rows), full),
+        vmem((4, 2) + chip_blocks, low),
+        vmem((4,) + chip_blocks, low),
+        vmem((3,) + chip_blocks, low),
+        vmem((3,) + chip_blocks, low),
+        vmem((8, rows, width), low),
+        vmem((planes, rows, width), low),
+        vmem(chip_blocks, low),
+        vmem((planes, rows, width), low),
+        vmem((planes, 8, own, 256), low),
+        vmem((planes, 8, own, 256), low),
+        vmem((rows, width), full),
+        vmem((rows, width), full),
+        vmem((planes, 8 * own, part), low),
+        vmem((planes, rows, width), low),
+        vmem((8, own, part), full),
+        vmem((8, own, part), full),
+        vmem((planes * rows, 256), low),
+        vmem((planes * rows, 256), low),
+        vmem((planes, rows, width), low),
+        vmem((planes, rows, width), low),
+        vmem((8, own, width), low),
+        vmem((8, own, width), low),
+        vmem((2, planes, 8, own, 256), low),
+        vmem((8, 2, planes, own, 256), low),
+        vmem((2, planes, own, 256), low),
+        vmem((2, own, width), low),
+        vmem((2, 24, rows), full),
+        vmem((8, 24, rows), full),
+        vmem((24, rows), full),
+        vmem((planes, 24, rows), full),
+    ]
+    return pl.pallas_call(
+        functools.partial(close_kernel, planes),
+        out_shape=outputs,
+        in_specs=[ANY] * 12 + [VMEM] + [ANY] * 4 + [VMEM] * 3,
+        out_specs=[VMEM] * len(outputs),
+        scratch_shapes=scratch + link_scratch(),
+        compiler_params=pltpu.CompilerParams(
+            vmem_limit_bytes=56 << 20, collective_id=collective_id, has_side_effects=True
+        ),
+        name="close",
+    )(*arguments)
 
 
 def plane_plan(
@@ -1646,25 +1664,15 @@
     sort_order,
     sort_place,
 ):
-    low, full = jnp.bfloat16, jnp.float32
-    devices, planes, per_plane = n_seq * n_sub, n_seq // 2, 2 * n_sub
+    planes = n_seq // 2
     rows, width = first_half.shape[1:]
-    hidden = upper_projection_weight.shape[2]
-    tokens = devices * rows
-    line = planes * rows
-    part = hidden // per_plane
-    seq, sub = lax.axis_index("seq"), lax.axis_index("sub")
-    me_p, me_z = lax.rem(seq, 2) * n_sub + sub, seq // 2
-    trade = functools.partial(exchange, planes=planes)
+    own = width // (n_seq * n_sub)
     x1, x2, g1, g2 = (a[0] for a in (first_half, second_half, grad_first, grad_second))
     wqk, wv, wo = query_key_weight[0], value_projection_weight[0], output_projection_weight[0]
     wup, wdown = upper_projection_weight[0], lower_projection_weight[0]
-    own = width // devices
-    pair = 2 * HEAD_DIM
-
     (
         places, gains, bias_up, normed_line, wqk_pair, wv_pair, wo_all, wup_part, wdown_part, df_plane,
-        shared_sorted, values_sorted, total_sorted, mixed, total,
+        shared, values, total_sorted, mixed, total,
     ) = open_stage(
         (
             sort_order[0, :, 0], sort_place[0, :, 0], attend_gain, attend_shift, feed_gain, feed_shift,
@@ -1673,127 +1681,32 @@
         1,
         planes,
     )
-    gain_a, shift_a, gain_f, shift_f, bias_down = (gains[k] for k in range(5))
-    attend_pull = jax.vjp(layer_norm, x2, gain_a, shift_a)[1]
-    order, place = places[0].reshape(tokens), places[1].reshape(tokens)
-    order_rows = places[0].astype(full)
-    normed_line = normed_line.reshape(line, width)
-    wqk_pair, wv_pair = wqk_pair.reshape(width, pair), wv_pair.reshape(width, pair)
-    wo_all = wo_all.reshape(width, width)
-    wup_part, wdown_part = wup_part.reshape(width, part), wdown_part.reshape(part, width)
-    df_plane = df_plane.reshape(per_plane * rows, width)
-    shared_sorted, values_sorted = shared_sorted[BLOCK:], values_sorted[BLOCK:]
-    df = g2.astype(low)
-    head_shape = (planes, per_plane, rows, HEAD_DIM)
-    token_shape = (per_plane, planes, rows, HEAD_DIM)
-
-    def to_tokens(array):
-        return like(over_plane(second, block), array.reshape(head_shape), *token_shape)
-
-    traded_z, traded_plane = along_z(block, block), over_plane(block, block)
-    down_bias_grad = jnp.sum(df.astype(full), axis=0)
     (
         y1, g1, dout, attended, dmixed, dtotal, y2_parts, up_grad, down_grad,
         up_bias_grad, feed_gain_grad, feed_shift_grad,
     ) = feed_stage(
         (
-            mixed, total, x1, wo_all, gain_f[None], shift_f[None],
-            wup_part, bias_up, wdown_part, df_plane, g1,
+            mixed, total, x1, wo_all.reshape(width, width), gains, wup_part.reshape(width, -1),
+            bias_up, wdown_part.reshape(-1, width), df_plane.reshape(8 * rows, width), g1,
         ),
-        6,
+        2,
         planes,
     )
-    attended = attended.reshape(line, pair)
-    up_grad = jnp.sum(up_grad.astype(full), axis=0).reshape(per_plane, own, part)
-    dshared, dvalues, y2_parts, dout_line = attend_head_back(
-        order,
-        place,
-        order_rows,
-        shared_sorted,
-        values_sorted,
-        total_sorted,
-        dmixed.reshape(tokens, HEAD_DIM),
-        dtotal,
-        [
-            like(traded_plane, y2_parts, *y2_parts.shape),
-            like(along_z(whole, block), dout, planes, rows, width),
-        ],
-        11,
+    (
+        y2, g2, shared_grad, value_grad, out_grad, up_grad, down_grad, vectors
+    ) = close_stage(
+        (
+            places, shared, values, total_sorted, dmixed, dtotal, y2_parts, dout, attended, normed_line,
+            wqk_pair, wv_pair, gains, x2, g2, up_grad, down_grad, up_bias_grad, feed_gain_grad,
+            feed_shift_grad,
+        ),
+        3,
         planes,
     )
-    y2 = x2 + (jnp.sum(y2_parts.astype(full), axis=0) + bias_down)
-    out_grad = matmul(attended, dout_line.reshape(line, width), ((0,), (0,)))
-    out_grad = out_grad.astype(low).reshape(per_plane, own, width)
-    dshared, dvalues = trade([to_tokens(dshared), to_tokens(dvalues)], "grads_from_heads", 12)
-
-    def over_rounds(array):
-        array = jnp.sum(array.reshape(2, n_sub, line, HEAD_DIM).astype(full), axis=1)
-        return jnp.swapaxes(array, 0, 1).reshape(line, pair).astype(low)
-
-    dshared, dvalues = over_rounds(dshared), over_rounds(dvalues)
-    de_parts = matmul(dshared, wqk_pair, ((1,), (1,))) + matmul(dvalues, wv_pair, ((1,), (1,)))
-    de_parts = de_parts.astype(low).reshape(planes, rows, width)
-
-    def to_owners(grad):
-        grad = grad.astype(low).reshape(planes, per_plane, own, pair)
-        return like(over_plane(second, block), grad, per_plane, planes, own, pair)
-
-    de_parts, shared_grad, value_grad, out_grad, up_grad = trade(
-        [
-            like(traded_z, de_parts, *de_parts.shape),
-            to_owners(matmul(normed_line, dshared, ((0,), (0,)))),
-            to_owners(matmul(normed_line, dvalues, ((0,), (0,)))),
-            like(traded_plane, out_grad, *out_grad.shape),
-            like(traded_plane, up_grad, *up_grad.shape),
-        ],
-        "sum_second_grad",
-        13,
-    )
-    two_part, attend_gain_grad, attend_shift_grad = attend_pull(
-        jnp.sum(de_parts.astype(full), axis=0)
-    )
-    g2 = g2 + two_part
-    shared_grad = jnp.sum(shared_grad.astype(full), axis=0)
-    value_grad = jnp.sum(value_grad.astype(full), axis=0)
-
-    def by_owner(vector):
-        return jnp.swapaxes(vector.reshape(planes, per_plane, own), 0, 1).reshape(per_plane, 1, rows)
-
-    vectors = [attend_gain_grad, attend_shift_grad, feed_gain_grad, feed_shift_grad, down_bias_grad]
-    up_bias_grad = jnp.where(
-        jnp.arange(per_plane)[:, None, None] == me_p, up_bias_grad.reshape(1, planes, rows), 0.0
-    )
-    tiles = jnp.concatenate([by_owner(v) for v in vectors] + [up_bias_grad], axis=1)
-    tiles = jnp.pad(tiles, ((0, 0), (0, 16 - tiles.shape[1]), (0, 0)))
-    vectors, shared_grad, value_grad = sum_small(
-        tiles,
-        [like(traded_z, shared_grad, planes, own, pair), like(traded_z, value_grad, planes, own, pair)],
-        14,
-        planes,
-    )
-    vectors = jnp.sum(vectors, axis=0)
-    pieces = jnp.take(vectors[:5].reshape(5, planes, own), me_z, axis=1)
-    up_bias_grad = jnp.take(vectors[5 : 5 + planes], me_z, axis=0)
-    shared_grad, value_grad = (
-        jnp.swapaxes(a, 0, 1).reshape(own, width) for a in (shared_grad, value_grad)
-    )
-    up_grad = jnp.transpose(up_grad.reshape(per_plane, own, planes, rows), (1, 2, 0, 3))
+    pieces = lax.dynamic_slice(vectors, (0, lax.axis_index("sub") * own), (5, own))
     outputs = (
-        y1,
-        y2,
-        g1,
-        g2,
-        pieces[0],
-        pieces[1],
-        shared_grad,
-        value_grad,
-        jnp.sum(out_grad.astype(full), axis=0),
-        pieces[2],
-        pieces[3],
-        up_grad.reshape(own, hidden),
-        up_bias_grad,
-        jnp.sum(down_grad.astype(full), axis=0),
-        pieces[4],
+        y1, y2, g1, g2, pieces[0], pieces[1], shared_grad, value_grad, out_grad, pieces[2], pieces[3],
+        up_grad, vectors[5], down_grad, pieces[4],
     )
     return tuple((a[None] for a in outputs))
 

time: 360 us -> 302 us (0.84)
  Pallas kernels: 317 us -> 291 us
  other arithmetic: 16.8 us -> 0 us
  local copies, waits for them, and re-layouts: 18.5 us -> 10.5 us
  matrix products: 5.8 us -> 0 us
    pallas_call x4 -> x1, Pallas kernels: 113 us -> 86.8 us  [close_stage(): pl.pallas_call(functools.partial(close_kernel, planes), out_shape=outputs...]
    reduce_sum x13 -> x0, other arithmetic: 13.7 us -> none  [the longest x2 4.31 us: over_rounds(): jnp.sum(array.reshape(2, n_sub, line, HEAD_DIM).astype(full), axis=1)]
    dot_general x5 -> x0, matrix products: 5.8 us -> none  [dot(): lax.dot_general(a, b, (contract, ((), ())), preferred_element_type=jnp.fl...]
    unnamed x56 -> x25, local copies, waits for them, and re-layouts: 7.05 us -> 7.91 us
where the time goes in v6:
time: 302 us
  Pallas kernels  291 us (96%)
  local copies, waits for them, and re-layouts  10.5 us (3%)
    pallas_call x1, Pallas kernels, open_stage(): pl.pallas_call(functools.partial(open_kernel, planes), out_shape=[o[0] fo...  107 us
    pallas_call x1, Pallas kernels, feed_stage(): pl.pallas_call(functools.partial(feed_kernel, planes), out_shape=[o[0] fo...  97.6 us
    pallas_call x1, Pallas kernels, close_stage(): pl.pallas_call(functools.partial(close_kernel, planes), out_shape=outputs...  86.8 us
    unnamed x25, local copies, waits for them, and re-layouts  7.91 us

profile of v6, /device:TPU:0, one launch (start us, length us, event | category | flops | bytes accessed | tf_op | source)
XLA Modules:
  0.0 302.2 jit_solution(7568302062040880402)
XLA Ops:
  0.7 106.6 %open.1 = (s32[2,32,128]{2,1,0:T(8,128)}, f32[8,1024]{1,0:T(8,128)}, f32[1,512]{1,0:T(1,128)}, bf16[4,128,1024]{2,1,0:T(8,128)(2,1)}, bf16[4,8,32,256]{3,2,1,0:T...) custom-call(s32[4,128]{1,0:T(4,128)} %bitcast.48, ...), custom_call_target="tpu_custom_call" | custom-call | tf_op jit(solution)/shard_map/open/pallas_call | solution.py:1365
  107.2 97.6 %feed.1 = (f32[128,1024]{1,0:T(8,128)}, f32[128,1024]{1,0:T(8,128)}, bf16[128,1024]{1,0:T(8,128)(2,1)}, bf16[4,128,256]{2,1,0:T(8,128)(2,1)}, bf16[4,8,128,128]{...) custom-call(bf16[8,4,128,128]{3,2,1,0:T(8,128)(2,1)} %get-tuple-elem, ...), custom_call_target="tpu_custom_call" | custom-call | tf_op jit(solution)/shard_map/feed/pallas_call | solution.py:1109
  204.8 0.0 copy-start.1
  204.8 86.8 %close.1 = (f32[128,1024]{1,0:T(8,128)}, f32[128,1024]{1,0:T(8,128)}, f32[32,1024]{1,0:T(8,128)}, f32[32,1024]{1,0:T(8,128)}, f32[32,1024]{1,0:T(8,128)}, /*inde...) custom-call(s32[2,32,128]{2,1,0:T(8,128)} %get-tuple-element.59.places, ...), custom_call_target="tpu_custom_call" | custom-call | tf_op jit(solution)/shard_map/close/pallas_call | solution.py:1633
  291.7 0.0 copy-start
  291.7 0.0 copy-start.4
  291.7 0.8 constant_dynamic-slice_fusion
  292.6 0.5 fusion
  293.1 1.2 slice.22
  294.3 0.0 copy-done.1
  294.3 0.0 copy-start.7
  294.3 0.0 copy-start.6
  294.3 0.0 copy-start.5
  294.3 0.8 copy.41
  295.1 0.0 copy-start.3
  295.1 1.9 copy.42
  297.0 0.0 copy-done
  297.0 0.0 copy-start.2
  297.0 0.8 copy.43
  297.8 0.0 copy-done.4
  297.8 0.8 copy.44
  298.6 0.0 copy-done.7
  298.6 0.7 copy.45
  299.3 0.0 copy-done.6
  299.3 0.7 copy.46
  300.0 0.0 copy-done.5
  300.0 0.7 copy.47
  300.6 0.0 copy-done.3
  300.6 0.8 copy.48
  301.4 0.0 copy-done.2
  301.4 0.8 copy.49
Async XLA Ops:
  204.8 89.5 %copy-start.1 = (f32[128,1024]{1,0:T(8,128)S(1)}, f32[128,1024]{1,0:T(8,128)}, u32[]{:S(2)}) copy-start(f32[128,1024]{1,0:T(8,128)} %get-tuple-element.58) | copy-start | bytes 1572868
  291.7 5.3 %copy-start = (f32[128,1024]{1,0:T(8,128)S(1)}, f32[128,1024]{1,0:T(8,128)}, u32[]{:S(2)}) copy-start(f32[128,1024]{1,0:T(8,128)} %get-tuple-element.77) | copy-start | bytes 1572868
  291.7 6.1 %copy-start.4 = (f32[128,1024]{1,0:T(8,128)S(1)}, f32[128,1024]{1,0:T(8,128)}, u32[]{:S(2)}) copy-start(f32[128,1024]{1,0:T(8,128)} %get-tuple-element.78) | copy-start | bytes 1572868
  294.3 4.3 %copy-start.7 = (f32[32,1024]{1,0:T(8,128)S(1)}, f32[32,1024]{1,0:T(8,128)}, u32[]{:S(2)}) copy-start(f32[32,1024]{1,0:T(8,128)} %get-tuple-element.80) | copy-start | bytes 393220
  294.3 5.0 %copy-start.6 = (f32[32,1024]{1,0:T(8,128)S(1)}, f32[32,1024]{1,0:T(8,128)}, u32[]{:S(2)}) copy-start(f32[32,1024]{1,0:T(8,128)} %get-tuple-element.81) | copy-start | bytes 393220
  294.3 5.7 %copy-start.5 = (f32[32,1024]{1,0:T(8,128)S(1)}, f32[32,1024]{1,0:T(8,128)}, u32[]{:S(2)}) copy-start(f32[32,1024]{1,0:T(8,128)} %get-tuple-element.82) | copy-start | bytes 393220
  295.1 5.5 %copy-start.3 = (f32[32,4096]{1,0:T(8,128)S(1)}, f32[32,4096]{1,0:T(8,128)}, u32[]{:S(2)}) copy-start(f32[32,4096]{1,0:T(8,128)} %get-tuple-element.83) | copy-start | bytes 1572868
  297.0 4.4 %copy-start.2 = (f32[128,1024]{1,0:T(8,128)S(1)}, f32[128,1024]{1,0:T(8,128)}, u32[]{:S(2)}) copy-start(f32[128,1024]{1,0:T(8,128)} %get-tuple-element.84) | copy-start | bytes 1572868

commit v7 on v6

--- a/solution.py
+++ b/solution.py
@@ -541,6 +541,54 @@
         self.used_local += 1
         copy.start()
         return copy
+
+
+class Chain:
+    def __init__(self, links, ref):
+        self.links, self.ref, self.first, self.sent = links, ref, links.used, []
+        links.used += 5
+        self.hand_on(links.z, links.z < 3, links.z > 0, 2)
+
+    def hand_on(self, shard, rightward, leftward, ways):
+        links = self.links
+        steps = ((1, rightward), (-1, leftward)) if ways == 2 else ((None, rightward | leftward),)
+        for step, wanted in steps:
+            if step is None:
+                step = jnp.where(rightward, 1, -1)
+            to = jnp.clip(links.z + step, 0, 3)
+            middle = jnp.where(to == 1, jnp.where(shard == 0, 0, shard - 1), jnp.where(shard == 3, 0, 2 - shard))
+            arrival = jnp.where((to == 0) | (to == 3), jnp.abs(to - shard) - 1, middle)
+            arrival = jnp.clip(arrival, 0, 2)
+            copy = pltpu.make_async_remote_copy(
+                src_ref=self.ref.at[shard],
+                dst_ref=self.ref.at[shard],
+                send_sem=links.send.at[self.first + len(self.sent)],
+                recv_sem=links.receive.at[self.first + arrival],
+                device_id=(to * 2 + links.x, links.y * 2 + links.core),
+                device_id_type=pl.DeviceIdType.MESH,
+            )
+            self.sent.append((wanted, copy))
+            pl.when(wanted)(copy.start)
+
+    def arrive(self, index):
+        links, z = self.links, self.links.z
+        ends = jnp.where(z == 0, index + 1, 2 - index)
+        inner = jnp.where(z == 1, (0, 2, 3)[index], (3, 1, 0)[index])
+        shard = jnp.where((z == 0) | (z == 3), ends, inner)
+        pltpu.make_async_remote_copy(
+            src_ref=self.ref.at[shard],
+            dst_ref=self.ref.at[shard],
+            send_sem=links.send.at[self.first],
+            recv_sem=links.receive.at[self.first + index],
+            device_id=(z * 2 + links.x, links.y * 2 + links.core),
+            device_id_type=pl.DeviceIdType.MESH,
+        ).wait_recv()
+        self.hand_on(shard, (shard < z) & (z < 3), (shard > z) & (z > 0), 1)
+        return shard
+
+    def finish(self):
+        for wanted, copy in self.sent:
+            pl.when(wanted)(copy.wait_send)
 
 
 COPIES = 160
@@ -936,7 +984,7 @@
 
     sibling, _ = links.near(1)
     own_h2 = h2.at[own_rows, :]
-    direct = {step: links.push(own_h2, own_h2, links.near(step)[0]) for step in (6, 4, 2)}
+    direct = {step: links.push(own_h2, own_h2, links.near(step)[0]) for step in (2, 4)}
     handed = {0: links.push(own_h2, own_h2, sibling)}
     for load in loads[1:]:
         load.wait()
@@ -973,8 +1021,11 @@
         to_chip[slot - 1] = result.astype(low)
         return links.push(to_chip.at[slot - 1], from_chip.at[slot - 1], links.near(step)[0])
 
+    traded = [feed(0, 0)]
+    for step in (2, 4):
+        direct[step].wait_send()
+    direct[6] = links.push(own_h2, own_h2, links.near(6)[0])
     pass_on(2)
-    traded = [feed(0, 0)]
     pass_on(4)
     traded.append(feed(1, 2))
     sent = [chip_sum(1, 2, traded[1])]
@@ -1016,8 +1067,7 @@
         return carry
 
     lax.fori_loop(0, planes, lower_grad, 0)
-    share_down = along_z(block, block)(links, down_grad, down_grad_out)
-    next(share_down)
+    keep_down = links.keep(down_grad, down_grad_out)
     up_bias_out[...] = jnp.sum(dpre[...].astype(full), axis=0, keepdims=True)
     drive([share])
 
@@ -1051,12 +1101,12 @@
 
     lax.fori_loop(0, 8, lower, 0)
     keep_y2 = links.keep(y2, y2_out)
-    for copy in list(direct.values()) + traded + sent:
+    for copy in [direct[6]] + traded + sent:
         copy.wait_send()
     for copy in handed.values():
         copy.wait_send()
-    drive(shares + [share_up, share_down])
-    for copy in (keep_attended, keep_dout, keep_y2):
+    drive(shares + [share_up])
+    for copy in (keep_attended, keep_dout, keep_y2, keep_down):
         copy.wait()
 
 
@@ -1161,6 +1211,8 @@
     ]
     for transfer in pair_shares:
         next(transfer)
+    wo_share = along_z(whole, block)(links, wo, wo_line)
+    next(wo_share)
     unit, _ = normal_parts(x2[...])
     next(share_floats)
 
@@ -1185,10 +1237,7 @@
 
     gain, shift = vector_of(0), vector_of(1)
     normed[links.z] = (unit * gain + shift).astype(low)
-    normed_copies = []
-    for step in range(1, planes):
-        device, _, _ = links.along(step)
-        normed_copies.append(links.push(normed.at[links.z], normed.at[links.z], device))
+    normed_chain = Chain(links, normed)
     for transfer in pair_shares:
         drive([transfer])
     pair_shares = [
@@ -1216,8 +1265,6 @@
             order_rows[tile : tile + 1, :] = all_ints[z, p, pl.ds(sub, 1), :]
             place_rows[tile : tile + 1, :] = all_ints[z, p, pl.ds(sub + 4, 1), :]
     to_scalars = [links.keep(order_rows, order_s), links.keep(place_rows, place_s)]
-    shares = [over_chips(whole, block)(links, df, df_out)]
-    next(shares[0])
 
     def head_columns(z):
         def columns(ref, p):
@@ -1239,21 +1286,20 @@
         return transfer
 
     head_shares = [project(links.z)]
-    wo_share = along_z(whole, block)(links, wo, wo_line)
-    next(wo_share)
-    for step, copy in enumerate(normed_copies, 1):
-        copy.wait_recv()
-        head_shares.append(project(links.along(step)[2]))
+    for index in range(3):
+        head_shares.append(project(normed_chain.arrive(index)))
         next(head_shares[-2])
     for transfer in upper_shares:
         drive([transfer])
-    shares += [
+    shares = [
+        over_chips(whole, block)(links, df, df_out),
         along_z(whole, block)(links, wup_rows, wup_out),
         along_z(whole, block)(links, wdown, wdown_out),
     ]
     next(shares[1])
+    next(head_shares[-1])
+    next(shares[0])
     next(shares[2])
-    next(head_shares[-1])
     drive([wo_share])
     wo_share = over_chips(whole, second)(links, wo_line, wo_out)
     for copy in to_scalars:
@@ -1301,8 +1347,7 @@
                 sent.append(links.push(source, target, device))
             else:
                 kept.append(links.keep(source, target))
-    for copy in normed_copies:
-        copy.wait_send()
+    normed_chain.finish()
     drive(shares + [wo_share])
     for copy in kept + sent:
         copy.wait()
@@ -1404,11 +1449,13 @@
     next(share_dout)
     share_y2 = over_plane(block, block)(links, y2_in, y2_parts)
     next(share_y2)
+    share_down = along_z(block, block)(links, down_in, down_parts)
+    next(share_down)
     loads = [
         links.keep(a, b)
         for a, b in (
             (attended_in, attended), (normed_in, normed), (wqk_in, wqk), (wv_in, wv), (x2_in, x2),
-            (g2_in, g2), (down_in, down_parts),
+            (g2_in, g2),
         )
     ]
     for copy in first_loads:
@@ -1515,6 +1562,7 @@
             up_out[:, (z * 8 + p) * 128 : (z * 8 + p + 1) * 128] = up_arrived[
                 p, :, z * 128 : (z + 1) * 128
             ]
+    drive([share_down])
     down_out[...] = sum(down_parts[z].astype(full) for z in range(planes))
     drive([share_out])
     out_grad_out[...] = sum(out_arrived[p].astype(full) for p in range(8))
@@ -1643,6 +1691,53 @@
     )(*arguments)
 
 
+def finish_kernel(
+    y1, y2, g1, g2, shared_grad, value_grad, out_grad, up_grad, down_grad, vectors,
+    y1_out, y2_out, g1_out, g2_out, gain_a_out, shift_a_out, shared_out, value_out, out_out,
+    gain_f_out, shift_f_out, up_out, up_bias_out, down_out, down_bias_out, arrived,
+):
+    pairs = (
+        (y1, y1_out), (y2, y2_out), (g1, g1_out), (g2, g2_out), (shared_grad, shared_out),
+        (value_grad, value_out), (out_grad, out_out), (up_grad, up_out), (down_grad, down_out),
+    )
+    copies = [
+        pltpu.make_async_copy(source, target.at[0], arrived.at[index])
+        for index, (source, target) in enumerate(pairs)
+    ]
+    for copy in copies:
+        copy.start()
+    sub = lax.axis_index("sub")
+    rows = vectors[...]
+    own = sum(
+        jnp.where(sub == u, rows[:, u * 32 : u * 32 + 32], 0.0) for u in range(4)
+    )
+    for row, target in enumerate((gain_a_out, shift_a_out, gain_f_out, shift_f_out, down_bias_out)):
+        target[...] = own[row : row + 1, :]
+    up_bias_out[...] = rows[5:6, :]
+    for copy in copies:
+        copy.wait()
+
+
+def finish_stage(arguments):
+    full = jnp.float32
+    large = [(jax.ShapeDtypeStruct((1,) + a.shape, full), ANY) for a in arguments[:-1]]
+    y1, y2, g1, g2, shared_grad, value_grad, out_grad, up_grad, down_grad = large
+    small = (jax.ShapeDtypeStruct((1, arguments[4].shape[0]), full), VMEM)
+    up_bias = (jax.ShapeDtypeStruct((1, arguments[-1].shape[1]), full), VMEM)
+    outputs = [
+        y1, y2, g1, g2, small, small, shared_grad, value_grad, out_grad, small, small, up_grad,
+        up_bias, down_grad, small,
+    ]
+    return pl.pallas_call(
+        finish_kernel,
+        out_shape=[o[0] for o in outputs],
+        in_specs=[VMEM] * 10,
+        out_specs=[o[1] for o in outputs],
+        scratch_shapes=[pltpu.SemaphoreType.DMA((9,))],
+        name="finish",
+    )(*arguments)
+
+
 def plane_plan(
     n_seq,
     n_sub,
@@ -1666,7 +1761,6 @@
 ):
     planes = n_seq // 2
     rows, width = first_half.shape[1:]
-    own = width // (n_seq * n_sub)
     x1, x2, g1, g2 = (a[0] for a in (first_half, second_half, grad_first, grad_second))
     wqk, wv, wo = query_key_weight[0], value_projection_weight[0], output_projection_weight[0]
     wup, wdown = upper_projection_weight[0], lower_projection_weight[0]
@@ -1703,12 +1797,9 @@
         3,
         planes,
     )
-    pieces = lax.dynamic_slice(vectors, (0, lax.axis_index("sub") * own), (5, own))
-    outputs = (
-        y1, y2, g1, g2, pieces[0], pieces[1], shared_grad, value_grad, out_grad, pieces[2], pieces[3],
-        up_grad, vectors[5], down_grad, pieces[4],
-    )
-    return tuple((a[None] for a in outputs))
+    return finish_stage(
+        (y1, y2, g1, g2, shared_grad, value_grad, out_grad, up_grad, down_grad, vectors)
+    )
 
 
 def on_device(n_seq, n_sub, *arguments):

time: 302 us -> 281 us (0.930)
  Pallas kernels: 291 us -> 280 us
  local copies, waits for them, and re-layouts: 10.5 us -> 0 us
    pallas_call x1, Pallas kernels: 97.6 us -> 80.8 us  [feed_stage(): pl.pallas_call(functools.partial(feed_kernel, planes), out_shape=[o[0] fo...]
    unnamed x25 -> x0, local copies, waits for them, and re-layouts: 7.91 us -> none
    pallas_call x0 -> x1, Pallas kernels: none -> 4.37 us  [finish_stage(): pl.pallas_call(finish_kernel, out_shape=[o[0] for o in outputs], in_specs...]
where the time goes in v7:
time: 281 us
  Pallas kernels  280 us (100%)
    pallas_call x1, Pallas kernels, open_stage(): pl.pallas_call(functools.partial(open_kernel, planes), out_shape=[o[0] fo...  106 us
    pallas_call x1, Pallas kernels, close_stage(): pl.pallas_call(functools.partial(close_kernel, planes), out_shape=outputs...  88.9 us
    pallas_call x1, Pallas kernels, feed_stage(): pl.pallas_call(functools.partial(feed_kernel, planes), out_shape=[o[0] fo...  80.8 us

profile of v7, /device:TPU:0, one launch (start us, length us, event | category | flops | bytes accessed | tf_op | source)
XLA Modules:
  0.0 280.9 jit_solution(6563471871487270956)
XLA Ops:
  0.7 106.1 %open.1 = (s32[2,32,128]{2,1,0:T(8,128)}, f32[8,1024]{1,0:T(8,128)}, f32[1,512]{1,0:T(1,128)}, bf16[4,128,1024]{2,1,0:T(8,128)(2,1)}, bf16[4,8,32,256]{3,2,1,0:T...) custom-call(s32[4,128]{1,0:T(4,128)} %bitcast.30, ...), custom_call_target="tpu_custom_call" | custom-call | tf_op jit(solution)/shard_map/open/pallas_call | solution.py:1410
  106.7 80.8 %feed.1 = (f32[128,1024]{1,0:T(8,128)}, f32[128,1024]{1,0:T(8,128)}, bf16[128,1024]{1,0:T(8,128)(2,1)}, bf16[4,128,256]{2,1,0:T(8,128)(2,1)}, bf16[4,8,128,128]{...) custom-call(bf16[8,4,128,128]{3,2,1,0:T(8,128)(2,1)} %get-tuple-elem, ...), custom_call_target="tpu_custom_call" | custom-call | tf_op jit(solution)/shard_map/feed/pallas_call | solution.py:1159
  187.5 88.9 %close.1 = (f32[128,1024]{1,0:T(8,128)}, f32[128,1024]{1,0:T(8,128)}, f32[32,1024]{1,0:T(8,128)}, f32[32,1024]{1,0:T(8,128)}, f32[32,1024]{1,0:T(8,128)}, /*inde...) custom-call(s32[2,32,128]{2,1,0:T(8,128)} %get-tuple-element.59.places, ...), custom_call_target="tpu_custom_call" | custom-call | tf_op jit(solution)/shard_map/close/pallas_call | solution.py:1681
  276.4 4.4 %finish.1 = (f32[1,128,1024]{2,1,0:T(8,128)}, f32[1,128,1024]{2,1,0:T(8,128)}, f32[1,128,1024]{2,1,0:T(8,128)}, f32[1,128,1024]{2,1,0:T(8,128)}, f32[1,32]{1,0:T...) custom-call(f32[128,1024]{1,0:T(8,128)} %get-tuple-element.58.y1, ...), custom_call_target="tpu_custom_call" | custom-call | tf_op jit(solution)/shard_map/finish/pallas_call | solution.py:1731

commit v8 on v7

--- a/solution.py
+++ b/solution.py
@@ -591,14 +591,14 @@
             pl.when(wanted)(copy.wait_send)
 
 
-COPIES = 160
+COPIES = 320
 
 
 def link_scratch():
     return [
         pltpu.SemaphoreType.DMA((COPIES,)),
         pltpu.SemaphoreType.DMA((COPIES,)),
-        pltpu.SemaphoreType.DMA((48,)),
+        pltpu.SemaphoreType.DMA((64,)),
     ]
 
 
@@ -912,6 +912,10 @@
 ANY = pl.BlockSpec(memory_space=pl.ANY)
 
 
+def narrow(ref, index):
+    return ref.at[:, index, :, pl.ds(0, HEAD_DIM)]
+
+
 def normal_parts(rows):
     center = jnp.mean(rows, axis=-1, keepdims=True)
     offset = rows - center
@@ -938,250 +942,16 @@
     return rows * below, below + rows * bell
 
 
-def feed_kernel(
-    planes,
-    mixed, total, x1, wo_in, gains, wup_in, bias_up, wdown_in, df_in, g1,
-    y1_out, g1_out, dout_out, attended_out, dmixed_home, dtotal_home, y2_out, up_grad_out, down_grad_out,
-    up_bias_out, gain_out, shift_out,
-    wo, wup, wdown, df, weights, attended, arrived, h2, dact, act, dpre, kept, to_sibling, from_sibling,
-    to_chip, from_chip, up_grad, down_grad, y2, dout, datt_out, datt, dmixed, dtotal, send, receive, local,
+def open_part(
+    links, planes,
+    sort_order, sort_place, gain_a_in, shift_a_in, gain_f_in, shift_f_in, bias_up_in, bias_down_in,
+    x2, wqk, wv, wo, wup, wdown, g2,
+    ints, all_ints, floats, all_floats, gains, bias_up, order_rows, place_rows, order_s, place_s, normed, df,
+    wqk_line, wv_line, wo_line, wup_rows, wqk_pair, wv_pair, heads, head_table, table, sums,
+    shared, values, total_sorted, mixed_home, total_home, last_scale,
+    wo_all, wup_part, wdown_part, df_plane, mixed_in, total_in,
 ):
     low, full = jnp.bfloat16, jnp.float32
-    links = Links(planes, send, receive, local)
-    links.greet()
-    loads = [links.keep(a, b) for a, b in ((wo_in, wo), (df_in, df), (wdown_in, wdown), (wup_in, wup))]
-
-    def combine(z, carry):
-        for x in range(2):
-            totals = [down(total[x * 4 + u, pl.ds(z, 1), :]) for u in range(4)]
-            highest = jnp.maximum(
-                jnp.maximum(totals[0], totals[1]), jnp.maximum(totals[2], totals[3])
-            )
-            parts = [jnp.exp(t - highest) for t in totals]
-            inverse = 1.0 / (parts[0] + parts[1] + parts[2] + parts[3])
-            result = 0.0
-            for u in range(4):
-                weight = parts[u] * inverse
-                weights[x * 4 + u, z] = weight
-                result += weight * mixed[x * 4 + u, z].astype(full)
-            attended[z, :, x * 128 : (x + 1) * 128] = result.astype(low)
-        return carry
-
-    lax.fori_loop(0, planes, combine, 0)
-    links.meet()
-    share = along_z(block, block)(links, attended, arrived)
-    next(share)
-    keep_attended = links.keep(attended, attended_out)
-    loads[0].wait()
-    drive([share])
-    y1 = x1[...]
-    for z in range(planes):
-        y1 += dot(arrived[z], wo[z * 256 : (z + 1) * 256, :], ((1,), (0,)))
-    y1_out[...] = y1
-    unit, _ = normal_parts(y1)
-    own_rows = pl.ds(pl.multiple_of(links.p * 128, 128), 128)
-    h2[own_rows, :] = (unit * gains[2:3, :] + gains[3:4, :]).astype(low)
-
-    sibling, _ = links.near(1)
-    own_h2 = h2.at[own_rows, :]
-    direct = {step: links.push(own_h2, own_h2, links.near(step)[0]) for step in (2, 4)}
-    handed = {0: links.push(own_h2, own_h2, sibling)}
-    for load in loads[1:]:
-        load.wait()
-
-    def upper_back(part, carry):
-        rows = pl.ds(pl.multiple_of(part * 256, 256), 256)
-        dact[rows, :] = dot(df[rows, :], wdown[...], ((1,), (1,)))
-        return carry
-
-    lax.fori_loop(0, 4, upper_back, 0)
-
-    def pass_on(step):
-        direct[step].wait_recv()
-        block_rows = h2.at[rows_of(links.near(step)[1]), :]
-        handed[step] = links.push(block_rows, block_rows, sibling)
-
-    def feed(slot, step):
-        handed[step].wait_recv()
-        chip = links.near(step)[1] // 2
-        rows = pl.ds(pl.multiple_of(chip * 256, 256), 256)
-        before = dot(h2[rows, :], wup[...], ((1,), (0,))) + bias_up[...]
-        value, slope = gelu_parts(before)
-        act[rows, :] = value.astype(low)
-        grad = (dact[rows, :] * slope).astype(low)
-        dpre[rows, :] = grad
-        kept[slot] = dot(grad, wup[...], ((1,), (1,))).reshape(2, 128, -1).astype(low)
-        return links.push(kept.at[slot, 1 - links.core], from_sibling.at[slot], sibling)
-
-    def chip_sum(slot, step, traded):
-        traded.wait_recv()
-        result = kept[slot, links.core].astype(full) + from_sibling[slot].astype(full)
-        if slot == 0:
-            return result
-        to_chip[slot - 1] = result.astype(low)
-        return links.push(to_chip.at[slot - 1], from_chip.at[slot - 1], links.near(step)[0])
-
-    traded = [feed(0, 0)]
-    for step in (2, 4):
-        direct[step].wait_send()
-    direct[6] = links.push(own_h2, own_h2, links.near(6)[0])
-    pass_on(2)
-    pass_on(4)
-    traded.append(feed(1, 2))
-    sent = [chip_sum(1, 2, traded[1])]
-    pass_on(6)
-    traded.append(feed(2, 4))
-    sent.append(chip_sum(2, 4, traded[2]))
-    traded.append(feed(3, 6))
-    sent.append(chip_sum(3, 6, traded[3]))
-    own_sum = chip_sum(0, 0, traded[0])
-
-    def upper_grad(part, carry):
-        rows = pl.ds(pl.multiple_of(part * 256, 256), 256)
-        up_grad[part] = dot(h2[:, rows], dpre[...], ((0,), (0,))).astype(low)
-        return carry
-
-    lax.fori_loop(0, planes, upper_grad, 0)
-    share_up = along_z(block, block)(links, up_grad, up_grad_out)
-    next(share_up)
-    for copy in sent:
-        copy.wait_recv()
-    grad = own_sum + (
-        from_chip[0].astype(full) + from_chip[1].astype(full) + from_chip[2].astype(full)
-    )
-    part, gain_grad, shift_grad = norm_back(grad, y1_out[...], gains[2:3, :])
-    gain_out[...] = gain_grad
-    shift_out[...] = shift_grad
-    g1_new = g1[...] + part
-    g1_out[...] = g1_new
-    dout[...] = g1_new.astype(low)
-    keep_dout = links.keep(dout, dout_out)
-    for z in range(planes):
-        datt_out[z] = dot(dout[...], wo[z * 256 : (z + 1) * 256, :], ((1,), (1,))).astype(low)
-    share = along_z(block, block)(links, datt_out, datt)
-    next(share)
-
-    def lower_grad(part, carry):
-        rows = pl.ds(pl.multiple_of(part * 128, 128), 128)
-        down_grad[part] = dot(act[:, rows], df[...], ((0,), (0,))).astype(low)
-        return carry
-
-    lax.fori_loop(0, planes, lower_grad, 0)
-    keep_down = links.keep(down_grad, down_grad_out)
-    up_bias_out[...] = jnp.sum(dpre[...].astype(full), axis=0, keepdims=True)
-    drive([share])
-
-    def combine_back(z, carry):
-        for x in range(2):
-            grad = datt[z, :, x * 128 : (x + 1) * 128].astype(full)
-            chosen = [weights[x * 4 + u, z] for u in range(4)]
-            inner = [
-                jnp.sum(grad * mixed[x * 4 + u, z].astype(full), axis=-1, keepdims=True)
-                for u in range(4)
-            ]
-            mean = sum(chosen[u] * inner[u] for u in range(4))
-            for u in range(4):
-                dmixed[x * 4 + u, z] = (chosen[u] * grad).astype(low)
-                change = (chosen[u] * (inner[u] - mean)).astype(low).astype(full)
-                dtotal[x * 4 + u, pl.ds(z, 1), :] = change.T[:1, :]
-        return carry
-
-    lax.fori_loop(0, planes, combine_back, 0)
-    shares = [
-        over_plane(block, second)(links, dmixed, dmixed_home),
-        over_plane(block, block)(links, dtotal, dtotal_home),
-    ]
-    for transfer in shares:
-        next(transfer)
-
-    def lower(part, carry):
-        rows = pl.ds(pl.multiple_of(part * 128, 128), 128)
-        y2[part] = dot(act[rows, :], wdown[...], ((1,), (0,))).astype(low)
-        return carry
-
-    lax.fori_loop(0, 8, lower, 0)
-    keep_y2 = links.keep(y2, y2_out)
-    for copy in [direct[6]] + traded + sent:
-        copy.wait_send()
-    for copy in handed.values():
-        copy.wait_send()
-    drive(shares + [share_up])
-    for copy in (keep_attended, keep_dout, keep_y2, keep_down):
-        copy.wait()
-
-
-def feed_stage(arguments, collective_id, planes):
-    low, full = jnp.bfloat16, jnp.float32
-    (mixed, total, x1, wo, gains, wup, bias_up, wdown, df, g1) = arguments
-    rows, width = x1.shape
-    part = wup.shape[1]
-    shape = jax.ShapeDtypeStruct
-    outputs = [
-        (shape((rows, width), full), VMEM),
-        (shape((rows, width), full), VMEM),
-        (shape((rows, width), low), ANY),
-        (shape((planes, rows, 256), low), ANY),
-        (shape((planes, 8, rows, HEAD_DIM), low), ANY),
-        (shape((8, 8, rows), full), ANY),
-        (shape((8, rows, width), low), ANY),
-        (shape((planes, width // planes, part), low), ANY),
-        (shape((planes, rows, width), low), ANY),
-        (shape((1, part), full), VMEM),
-        (shape((1, width), full), VMEM),
-        (shape((1, width), full), VMEM),
-    ]
-    scratch = [
-        (wo.shape, low),
-        (wup.shape, low),
-        (wdown.shape, low),
-        (df.shape, low),
-        ((8, planes, rows, HEAD_DIM), full),
-        ((planes, rows, 256), low),
-        ((planes, rows, 256), low),
-        ((8 * rows, width), low),
-        ((8 * rows, part), full),
-        ((8 * rows, part), low),
-        ((8 * rows, part), low),
-        ((4, 2, rows, width), low),
-        ((4, rows, width), low),
-        ((4, rows, width), low),
-        ((3, rows, width), low),
-        ((3, rows, width), low),
-        ((planes, width // planes, part), low),
-        ((planes, rows, width), low),
-        ((8, rows, width), low),
-        ((rows, width), low),
-        ((planes, rows, 256), low),
-        ((planes, rows, 256), low),
-        ((8, planes, rows, HEAD_DIM), low),
-        ((8, 8, rows), full),
-    ]
-    return pl.pallas_call(
-        functools.partial(feed_kernel, planes),
-        out_shape=[o[0] for o in outputs],
-        in_specs=[VMEM, VMEM, VMEM, ANY, VMEM, ANY, VMEM, ANY, ANY, VMEM],
-        out_specs=[o[1] for o in outputs],
-        scratch_shapes=[pltpu.VMEM(*s) for s in scratch] + link_scratch(),
-        compiler_params=pltpu.CompilerParams(
-            vmem_limit_bytes=56 << 20, collective_id=collective_id, has_side_effects=True
-        ),
-        name="feed",
-    )(*arguments)
-
-
-def open_kernel(
-    planes,
-    sort_order, sort_place, gain_a_in, shift_a_in, gain_f_in, shift_f_in, bias_up_in, bias_down_in,
-    x2, wqk, wv, wo, wup, wdown, g2,
-    places_out, gains_out, bias_up_out, normed_out, wqk_out, wv_out, wo_out, wup_out, wdown_out, df_out,
-    shared_out, values_out, total_out, mixed_out, total_home_out,
-    ints, all_ints, floats, all_floats, order_rows, place_rows, order_s, place_s, normed, df,
-    wqk_line, wv_line, wo_line, wup_rows, wqk_pair, wv_pair, heads, head_table, table, mixed,
-    shared, values, total_sorted, mixed_home, total_home, last_scale, send, receive, local,
-):
-    low, full = jnp.bfloat16, jnp.float32
-    links = Links(planes, send, receive, local)
-    links.greet()
     sub = links.y * 2 + links.core
     tiles = planes * 8
     ints[...] = jnp.concatenate([sort_order[...], sort_place[...]], axis=0)
@@ -1213,6 +983,8 @@
         next(transfer)
     wo_share = along_z(whole, block)(links, wo, wo_line)
     next(wo_share)
+    df_share = over_chips(whole, block)(links, df, df_plane)
+    next(df_share)
     unit, _ = normal_parts(x2[...])
     next(share_floats)
 
@@ -1251,12 +1023,12 @@
         next(transfer)
     for transfer in pair_shares:
         next(transfer)
-    gains_out[0:1, :] = gain
-    gains_out[1:2, :] = shift
+    gains[0:1, :] = gain
+    gains[1:2, :] = shift
     for row in (2, 3, 4):
-        gains_out[row : row + 1, :] = vector_of(row)
+        gains[row : row + 1, :] = vector_of(row)
     for z in range(planes):
-        bias_up_out[:, z * 128 : (z + 1) * 128] = all_floats[z, links.p, 5:6, :]
+        bias_up[:, z * 128 : (z + 1) * 128] = all_floats[z, links.p, 5:6, :]
     drive(pair_shares)
     drive([share_ints])
     for z in range(planes):
@@ -1286,25 +1058,25 @@
         return transfer
 
     head_shares = [project(links.z)]
+    next(df_share)
     for index in range(3):
         head_shares.append(project(normed_chain.arrive(index)))
         next(head_shares[-2])
     for transfer in upper_shares:
         drive([transfer])
-    shares = [
-        over_chips(whole, block)(links, df, df_out),
-        along_z(whole, block)(links, wup_rows, wup_out),
-        along_z(whole, block)(links, wdown, wdown_out),
-    ]
-    next(shares[1])
     next(head_shares[-1])
-    next(shares[0])
-    next(shares[2])
     drive([wo_share])
-    wo_share = over_chips(whole, second)(links, wo_line, wo_out)
+    wo_share = over_chips(whole, second)(links, wo_line, wo_all)
     for copy in to_scalars:
         copy.wait()
     drive(head_shares)
+    shares = [
+        df_share,
+        along_z(whole, block)(links, wup_rows, wup_part),
+        along_z(whole, block)(links, wdown, wdown_part),
+    ]
+    next(shares[1])
+    next(shares[2])
     next(wo_share)
 
     def load(tile, carry):
@@ -1313,20 +1085,10 @@
 
     lax.fori_loop(0, tiles, load, 0)
     attend_tiles(
-        tiles, 2, order_s, order_rows, table, shared, values, mixed, total_sorted, last_scale
+        tiles, 2, order_s, order_rows, table, shared, values, sums, total_sorted, last_scale
     )
     next(wo_share)
-    next(shares[0])
-    kept = [
-        links.keep(normed, normed_out),
-        links.keep(wqk_pair, wqk_out),
-        links.keep(wv_pair, wv_out),
-        links.keep(shared, shared_out),
-        links.keep(values, values_out),
-        links.keep(total_sorted, total_out),
-        links.keep(order_rows, places_out.at[0]),
-        links.keep(place_rows, places_out.at[1]),
-    ]
+    kept = []
     sent = []
     for step in (6, 7, 4, 5, 2, 3, 1, 0):
         device, p = links.near(step)
@@ -1334,140 +1096,247 @@
         def unsort(z, carry):
             totals = []
             for part in range(4):
-                picked = pick_tile(mixed, place_s, z * 8 + p, part)
+                picked = pick_tile(sums, place_s, z * 8 + p, part)
                 mixed_home[p, z, part * 32 : part * 32 + 32, :] = picked[:, :128].astype(low)
                 totals.append(picked[:, 128:])
             total_home[p, pl.ds(z, 1), :] = jnp.concatenate(totals, axis=0).T[:1, :]
             return carry
 
         lax.fori_loop(0, planes, unsort, 0)
-        for here, there in ((mixed_home, mixed_out), (total_home, total_home_out)):
+        for here, there in ((mixed_home, mixed_in), (total_home, total_in)):
             source, target = here.at[p], there.at[links.p]
             if step:
                 sent.append(links.push(source, target, device))
             else:
                 kept.append(links.keep(source, target))
     normed_chain.finish()
-    drive(shares + [wo_share])
     for copy in kept + sent:
         copy.wait()
-
-
-def open_stage(arguments, collective_id, planes):
-    low, full, whole_number = jnp.bfloat16, jnp.float32, jnp.int32
-    x2, wqk, wup = arguments[8], arguments[9], arguments[12]
-    rows, width = x2.shape
-    own, hidden = wup.shape
-    part = hidden // 8
-    tiles = planes * 8
-    tokens = tiles * rows
-    shape = jax.ShapeDtypeStruct
-    outputs = [
-        (shape((2, tiles, rows), whole_number), ANY),
-        (shape((8, width), full), VMEM),
-        (shape((1, part), full), VMEM),
-        (shape((planes, rows, width), low), ANY),
-        (shape((planes, 8, own, 256), low), ANY),
-        (shape((planes, 8, own, 256), low), ANY),
-        (shape((planes, 8, own, width), low), ANY),
-        (shape((planes, 8, own, part), low), ANY),
-        (shape((planes, rows, width), low), ANY),
-        (shape((8, rows, width), low), ANY),
-        (shape((tokens + BLOCK, HEAD_DIM), low), ANY),
-        (shape((tokens + BLOCK, HEAD_DIM), low), ANY),
-        (shape((tokens, HEAD_DIM), full), ANY),
-        (shape((8, planes, rows, HEAD_DIM), low), ANY),
-        (shape((8, 8, rows), full), ANY),
-    ]
-    scratch = [
-        pltpu.VMEM((8, rows), whole_number),
-        pltpu.VMEM((planes, 8, 8, rows), whole_number),
-        pltpu.VMEM((8, rows), full),
-        pltpu.VMEM((planes, 8, 8, rows), full),
-        pltpu.VMEM((tiles, rows), whole_number),
-        pltpu.VMEM((tiles, rows), whole_number),
-        pltpu.SMEM((tiles, rows), whole_number),
-        pltpu.SMEM((tiles, rows), whole_number),
-        pltpu.VMEM((planes, rows, width), low),
-        pltpu.VMEM((rows, width), low),
-        pltpu.VMEM((planes, own, 256), low),
-        pltpu.VMEM((planes, own, 256), low),
-        pltpu.VMEM((planes, own, width), low),
-        pltpu.VMEM((8, own, part), low),
-        pltpu.VMEM((planes, 8, own, 256), low),
-        pltpu.VMEM((planes, 8, own, 256), low),
-        pltpu.VMEM((planes, rows, 512), low),
-        pltpu.VMEM((planes, 8, rows, 256), low),
-        pltpu.VMEM((tokens, 256), full),
-        pltpu.VMEM((tokens, 256), full),
-        pltpu.VMEM((tokens + BLOCK, HEAD_DIM), low),
-        pltpu.VMEM((tokens + BLOCK, HEAD_DIM), low),
-        pltpu.VMEM((tokens, HEAD_DIM), full),
-        pltpu.VMEM((8, planes, rows, HEAD_DIM), low),
-        pltpu.VMEM((8, 8, rows), full),
-        pltpu.VMEM((1, rows), full),
-    ]
-    return pl.pallas_call(
-        functools.partial(open_kernel, planes),
-        out_shape=[o[0] for o in outputs],
-        in_specs=[VMEM] * 15,
-        out_specs=[o[1] for o in outputs],
-        scratch_shapes=scratch + link_scratch(),
-        compiler_params=pltpu.CompilerParams(
-            vmem_limit_bytes=56 << 20, collective_id=collective_id, has_side_effects=True
-        ),
-        name="open",
-    )(*arguments)
-
-
-def close_kernel(
-    planes,
-    places, shared_in, values_in, total_in, dmixed_in, dtotal_in, y2_in, dout_in, attended_in, normed_in,
-    wqk_in, wv_in, gains, x2_in, g2_in, up_in, down_in, up_bias, feed_gain, feed_shift,
-    y2_out, g2_out, shared_grad_out, value_grad_out, out_grad_out, up_out, down_out, vectors_out,
-    order_rows, order_s, place_s, shared, values, total_sorted, dmixed, dtotal, table, grad_sorted,
-    grad_total_sorted, sums, scale_sums, last_scale, kept, from_sibling, to_chip, from_chip, y2_parts,
-    dout_line, attended, normed, wqk, wv, x2, g2, up_parts, down_parts, up_sum, up_arrived, dshared, dvalues,
-    de_out, de, out_sent, out_arrived, weight_sent, weight_arrived, weight_sum, weight_final,
-    tiles_sent, tiles_arrived, tile, tile_line, send, receive, local,
+    return wo_share, shares
+
+
+def feed_part(
+    links, planes, wo_share, weight_shares,
+    x1, g1, y1_out, g1_out, gains, bias_up, sums, table, head_table, mixed_home, total_home,
+    wo_all, wup_part, wdown_part, df_plane, mixed_in, total_in, dtotal_in, attended, arrived, h2, act, dpre,
+    kept, from_sibling, to_chip, from_chip, up_grad, up_parts, down_grad, down_parts, dout, datt_out, datt,
+    up_bias, feed_gain, feed_shift, y2_parts, out_sibling,
 ):
     low, full = jnp.bfloat16, jnp.float32
-    links = Links(planes, send, receive, local)
-    links.greet()
+
+    def weight_rows(head, z):
+        return pl.ds(pl.multiple_of((head * planes + z) * 128, 128), 128)
+
+    def wo_rows(z):
+        return wo_all[z].reshape(256, -1)
+
+    def combine(z, carry):
+        for x in range(2):
+            totals = [down(total_in[x * 4 + u, pl.ds(z, 1), :]) for u in range(4)]
+            highest = jnp.maximum(
+                jnp.maximum(totals[0], totals[1]), jnp.maximum(totals[2], totals[3])
+            )
+            parts = [jnp.exp(t - highest) for t in totals]
+            inverse = 1.0 / (parts[0] + parts[1] + parts[2] + parts[3])
+            result = 0.0
+            for u in range(4):
+                weight = parts[u] * inverse
+                sums[weight_rows(x * 4 + u, z), :128] = weight
+                result += weight * mixed_in[x * 4 + u, z].astype(full)
+            attended[z, :, x * 128 : (x + 1) * 128] = result.astype(low)
+        return carry
+
+    lax.fori_loop(0, planes, combine, 0)
+    share = along_z(block, block)(links, attended, arrived)
+    next(share)
+    drive([wo_share])
+    drive([share])
+    y1 = x1[...]
+    for z in range(planes):
+        y1 += dot(arrived[z], wo_rows(z), ((1,), (0,)))
+    y1_out[...] = y1
+    unit, _ = normal_parts(y1)
+    own_rows = pl.ds(pl.multiple_of(links.p * 128, 128), 128)
+    h2[own_rows, :] = (unit * gains[2:3, :] + gains[3:4, :]).astype(low)
+
+    sibling, _ = links.near(1)
+    own_h2 = h2.at[own_rows, :]
+    direct = {step: links.push(own_h2, own_h2, links.near(step)[0]) for step in (2, 4)}
+    handed = {0: links.push(own_h2, own_h2, sibling)}
+    drive(weight_shares)
+
+    half = wup_part.shape[3] // 2
+
+    def upper_back(part, carry):
+        rows = pl.ds(pl.multiple_of(part * 256, 256), 256)
+        grad = df_plane[pl.ds(part * 2, 2)].reshape(256, -1)
+        result = dot(grad, wdown_part[...].reshape(half * 2, -1), ((1,), (1,)))
+        table[rows, :] = result[:, :half]
+        table[pl.ds(pl.multiple_of(1024 + part * 256, 256), 256), :] = result[:, half:]
+        return carry
+
+    lax.fori_loop(0, 4, upper_back, 0)
+
+    def pass_on(step):
+        direct[step].wait_recv()
+        block_rows = h2.at[rows_of(links.near(step)[1]), :]
+        handed[step] = links.push(block_rows, block_rows, sibling)
+
+    def feed(slot, step):
+        handed[step].wait_recv()
+        chip = links.near(step)[1] // 2
+        rows = pl.ds(pl.multiple_of(chip * 256, 256), 256)
+        before = dot(h2[rows, :], wup_part[...].reshape(-1, 2 * half), ((1,), (0,))) + bias_up[...]
+        value, slope = gelu_parts(before)
+        act[rows, :] = value.astype(low)
+        grad = jnp.concatenate(
+            [table[rows, :], table[pl.ds(pl.multiple_of(1024 + chip * 256, 256), 256), :]], axis=1
+        )
+        grad = (grad * slope).astype(low)
+        dpre[rows, :] = grad
+        kept[slot] = dot(grad, wup_part[...].reshape(-1, 2 * half), ((1,), (1,))).reshape(2, 128, -1).astype(low)
+        return links.push(kept.at[slot, 1 - links.core], from_sibling.at[slot], sibling)
+
+    def chip_sum(slot, step, traded):
+        traded.wait_recv()
+        result = kept[slot, links.core].astype(full) + from_sibling[slot].astype(full)
+        if slot == 0:
+            return result
+        to_chip[slot - 1] = result.astype(low)
+        return links.push(to_chip.at[slot - 1], from_chip.at[slot - 1], links.near(step)[0])
+
+    traded = [feed(0, 0)]
+    for step in (2, 4):
+        direct[step].wait_send()
+    direct[6] = links.push(own_h2, own_h2, links.near(6)[0])
+    pass_on(2)
+    pass_on(4)
+    traded.append(feed(1, 2))
+    sent = [chip_sum(1, 2, traded[1])]
+    pass_on(6)
+    traded.append(feed(2, 4))
+    sent.append(chip_sum(2, 4, traded[2]))
+    traded.append(feed(3, 6))
+    sent.append(chip_sum(3, 6, traded[3]))
+    own_sum = chip_sum(0, 0, traded[0])
+
+    def upper_grad(part, carry):
+        rows = pl.ds(pl.multiple_of(part * 256, 256), 256)
+        up_grad[part] = dot(h2[:, rows], dpre[...], ((0,), (0,))).astype(low)
+        return carry
+
+    lax.fori_loop(0, planes, upper_grad, 0)
+
+    def lower_grad(part, carry):
+        rows = pl.ds(pl.multiple_of(part * 128, 128), 128)
+        down_grad[part] = dot(act[:, rows], df_plane[...].reshape(act.shape[0], -1), ((0,), (0,))).astype(low)
+        return carry
+
+    lax.fori_loop(0, planes, lower_grad, 0)
+
+    def lower(part, carry):
+        rows = pl.ds(pl.multiple_of(part * 128, 128), 128)
+        df_plane[part] = dot(
+            act[rows, :], wdown_part[...].reshape(2 * half, -1), ((1,), (0,))
+        ).astype(low)
+        return carry
+
+    lax.fori_loop(0, 8, lower, 0)
+    share_y2 = over_plane(block, block)(links, df_plane, y2_parts)
+    next(share_y2)
+    for copy in sent:
+        copy.wait_recv()
+    grad = own_sum + (
+        from_chip[0].astype(full) + from_chip[1].astype(full) + from_chip[2].astype(full)
+    )
+    part, gain_grad, shift_grad = norm_back(grad, y1_out[...], gains[2:3, :])
+    feed_gain[...] = gain_grad
+    feed_shift[...] = shift_grad
+    g1_new = g1[...] + part
+    g1_out[...] = g1_new
+    dout[...] = g1_new.astype(low)
+    for z in range(planes):
+        datt_out[z] = dot(dout[...], wo_rows(z), ((1,), (1,))).astype(low)
+    share = along_z(block, block)(links, datt_out, datt)
+    next(share)
+    for copy in [direct[6]] + list(handed.values()):
+        copy.wait_send()
+    for z in range(planes):
+        part = dot(arrived[z], dout[...], ((0,), (0,))).astype(low)
+        for p in range(8):
+            row = p * 128 + z * 32
+            h2[row : row + 32, :] = part[p * 32 : p * 32 + 32]
+    out_traded = [
+        links.push(
+            h2.at[rows_of(links.near(step)[1] // 2 * 2 + 1 - links.core), :],
+            out_sibling.at[slot],
+            sibling,
+        )
+        for slot, step in enumerate((6, 4, 2, 0))
+    ]
+    up_bias[...] = jnp.sum(dpre[...].astype(full), axis=0, keepdims=True)
+    drive([share])
+    share_up = along_z(block, block)(links, up_grad, up_parts)
+    next(share_up)
+    share_down = along_z(block, block)(links, down_grad, down_parts)
+    next(share_down)
+    def combine_back(z, carry):
+        for x in range(2):
+            grad = datt[z, :, x * 128 : (x + 1) * 128].astype(full)
+            chosen = [sums[weight_rows(x * 4 + u, z), :128] for u in range(4)]
+            inner = [
+                jnp.sum(grad * mixed_in[x * 4 + u, z].astype(full), axis=-1, keepdims=True)
+                for u in range(4)
+            ]
+            mean = sum(chosen[u] * inner[u] for u in range(4))
+            for u in range(4):
+                mixed_home[x * 4 + u, z] = (chosen[u] * grad).astype(low)
+                change = (chosen[u] * (inner[u] - mean)).astype(low).astype(full)
+                total_home[x * 4 + u, pl.ds(z, 1), :] = change.T[:1, :]
+        return carry
+
+    lax.fori_loop(0, planes, combine_back, 0)
+    shares = [
+        over_plane(block, narrow)(links, mixed_home, head_table),
+        over_plane(block, block)(links, total_home, dtotal_in),
+    ]
+    for transfer in shares:
+        next(transfer)
+    for copy in traded + sent:
+        copy.wait_send()
+    return shares, share_y2, share_up, share_down, out_traded
+
+
+def close_part(
+    links, planes, shares, share_y2, share_up, share_down, out_traded,
+    x2, g2, y2_out, g2_out, shared_grad_out, value_grad_out, out_grad_out, up_out, down_out, vectors_out,
+    gains, order_rows, order_s, place_s, normed, wqk_pair, wv_pair, shared, values, total_sorted, head_table,
+    table, sums, last_scale, dtotal_in, attended, df_plane, h2, wup_part, wdown_part, up_parts, down_grad,
+    down_parts, kept, from_sibling, to_chip, from_chip, up_bias, feed_gain, feed_shift, grad_sorted,
+    grad_total_sorted, scale_sums, up_sum, up_arrived, dshared, dvalues, de, out_sent, out_arrived,
+    weight_arrived, weight_sum, weight_final, tiles_sent, tiles_arrived, tile, tile_line, y2_parts,
+    out_sibling, out_chip,
+):
+    low, full = jnp.bfloat16, jnp.float32
     tiles = planes * 8
     line = planes * 128
-    first_loads = [
-        links.keep(a, b)
-        for a, b in (
-            (places.at[0], order_s), (places.at[1], place_s), (places.at[0], order_rows),
-            (dmixed_in, dmixed), (dtotal_in, dtotal), (shared_in, shared), (values_in, values),
-            (total_in, total_sorted), (up_in, up_parts),
-        )
+    out_sums = []
+    for slot, step in enumerate((6, 4, 2, 0)):
+        out_traded[slot].wait()
+        rows = rows_of(links.near(step)[1] // 2 * 2 + links.core)
+        total = h2[rows, :].astype(full) + out_sibling[slot].astype(full)
+        h2[rows, :] = total.astype(low)
+        out_sums.append(rows)
+    drive(shares)
+    out_pushed = [
+        links.push(h2.at[out_sums[slot], :], out_chip.at[slot], links.near(step)[0])
+        for slot, step in enumerate((6, 4, 2))
     ]
-    links.meet()
-    share_dout = along_z(whole, block)(links, dout_in, dout_line)
-    next(share_dout)
-    share_y2 = over_plane(block, block)(links, y2_in, y2_parts)
-    next(share_y2)
-    share_down = along_z(block, block)(links, down_in, down_parts)
-    next(share_down)
-    loads = [
-        links.keep(a, b)
-        for a, b in (
-            (attended_in, attended), (normed_in, normed), (wqk_in, wqk), (wv_in, wv), (x2_in, x2),
-            (g2_in, g2),
-        )
-    ]
-    for copy in first_loads:
-        copy.wait()
-    up_sum[...] = sum(up_parts[z].astype(full) for z in range(planes)).reshape(up_sum.shape)
-    share_up = over_plane(block, block)(links, up_sum, up_arrived)
-    next(share_up)
 
     def load(index, carry):
         z, p = index // 8, lax.rem(index, 8)
-        table[rows_of(index), :128] = dmixed[z, p].astype(full)
-        table[rows_of(index), 128:] = down(dtotal[p, pl.ds(z, 1), :])
+        table[rows_of(index), :128] = head_table[z, p, :, :HEAD_DIM].astype(full)
+        table[rows_of(index), 128:] = down(dtotal_in[p, pl.ds(z, 1), :])
         return carry
 
     lax.fori_loop(0, tiles, load, 0)
@@ -1482,9 +1351,10 @@
         for core, goal in ((0, 1 - links.core), (1, links.core)):
 
             def rows(z, carry):
+                columns = pl.ds(pl.multiple_of(z * 256, 256), 256)
                 for part in range(4):
                     picked = pick_tile(sums, place_s, z * 8 + chip * 2 + goal, part)
-                    kept[slot, core, z, part * 32 : part * 32 + 32, :] = picked.astype(low)
+                    kept[slot, core, part * 32 : part * 32 + 32, columns] = picked.astype(low)
                 return carry
 
             lax.fori_loop(0, planes, rows, 0)
@@ -1506,51 +1376,51 @@
         traded.append(unsort(slot, step))
         if slot:
             sent.append(chip_sum(slot - 1, steps[slot - 1], traded[slot - 1]))
-    for copy in loads:
+    total = h2[out_sums[3], :].astype(full)
+    for slot, copy in enumerate(out_pushed):
         copy.wait()
-    drive([share_dout])
-    all_dout = dout_line[...].reshape(line, -1)
-    out_sent[...] = (
-        dot(attended[...].reshape(line, 256), all_dout, ((0,), (0,))).astype(low).reshape(out_sent.shape)
-    )
+        total += out_chip[slot].astype(full)
+    out_sent[...] = total.astype(low).reshape(out_sent.shape)
     own_sum = chip_sum(3, 0, traded[3])
-    share_out = over_plane(block, block)(links, out_sent, out_arrived)
+    share_out = along_z(block, block)(links, out_sent, out_arrived)
     next(share_out)
     own_columns = pl.ds(pl.multiple_of(links.x * 128, 128), 128)
     far_columns = pl.ds(pl.multiple_of((1 - links.x) * 128, 128), 128)
 
     def settle_sum(columns, result):
-        result = result.astype(low).reshape(line, 256)
-        dshared[:, columns] = result[:, :128]
-        dvalues[:, columns] = result[:, 128:]
+        for z in range(planes):
+            part = result[:, z * 256 : z * 256 + 256].astype(low)
+            dshared[z * 128 : z * 128 + 128, columns] = part[:, :128]
+            dvalues[z * 128 : z * 128 + 128, columns] = part[:, 128:]
 
     sent[2].wait_recv()
     settle_sum(own_columns, own_sum + from_chip[2].astype(full))
     sent[1].wait_recv()
     sent[0].wait_recv()
     settle_sum(far_columns, from_chip[1].astype(full) + from_chip[0].astype(full))
-    all_wqk, all_wv = wqk[...].reshape(-1, 256), wv[...].reshape(-1, 256)
+    all_wqk, all_wv = wqk_pair[...].reshape(-1, 256), wv_pair[...].reshape(-1, 256)
+    drive([share_down])
 
     def input_grad(z, carry):
         rows = rows_of(z)
-        de_out[z] = (
+        down_grad[z] = (
             dot(dshared[rows, :], all_wqk, ((1,), (1,))) + dot(dvalues[rows, :], all_wv, ((1,), (1,)))
         ).astype(low)
         return carry
 
     lax.fori_loop(0, planes, input_grad, 0)
-    share_de = along_z(block, block)(links, de_out, de)
+    share_de = along_z(block, block)(links, down_grad, de)
     next(share_de)
+    drive([share_up])
+    up_sum[...] = sum(up_parts[z].astype(full) for z in range(planes)).reshape(up_sum.shape)
+    share_up = over_plane(block, block)(links, up_sum, up_arrived)
+    next(share_up)
     all_normed = normed[...].reshape(line, -1)
     for index, grad in enumerate((dshared, dvalues)):
-        weight_sent[index] = (
-            dot(all_normed, grad[...], ((0,), (0,))).astype(low).reshape(weight_sent.shape[1:])
+        wup_part[:, :, :, index * 256 : index * 256 + 256] = (
+            dot(all_normed, grad[...], ((0,), (0,))).astype(low).reshape(wup_part.shape[:3] + (256,))
         )
-
-    def of_pair(ref, p):
-        return ref.at[:, :, p]
-
-    share_weights = over_plane(of_pair, block)(links, weight_sent, weight_arrived)
+    share_weights = over_plane(second, block)(links, wup_part, weight_arrived)
     next(share_weights)
     drive([share_y2])
     y2_out[...] = x2[...] + (
@@ -1562,18 +1432,14 @@
             up_out[:, (z * 8 + p) * 128 : (z * 8 + p + 1) * 128] = up_arrived[
                 p, :, z * 128 : (z + 1) * 128
             ]
-    drive([share_down])
     down_out[...] = sum(down_parts[z].astype(full) for z in range(planes))
     drive([share_out])
-    out_grad_out[...] = sum(out_arrived[p].astype(full) for p in range(8))
+    out_grad_out[...] = sum(out_arrived[z].astype(full) for z in range(planes))
     down_bias = jnp.sum(g2[...].astype(low).astype(full), axis=0, keepdims=True)
     drive([share_weights])
     weight_sum[...] = sum(weight_arrived[p].astype(full) for p in range(8)).astype(low)
 
-    def pair_columns(ref, z):
-        return ref.at[:, :, pl.ds(pl.multiple_of(z * 256, 256), 256)]
-
-    share_final = along_z(second, pair_columns)(links, weight_sum, weight_final)
+    share_final = along_z(block, block)(links, weight_sum, weight_final)
     next(share_final)
     drive([share_de])
     part, gain_grad, shift_grad = norm_back(
@@ -1601,8 +1467,10 @@
     share_tile = along_z(whole, block)(links, tile, tile_line)
     next(share_tile)
     drive([share_final])
-    shared_grad_out[...] = weight_final[0].astype(full)
-    value_grad_out[...] = weight_final[1].astype(full)
+    for z in range(planes):
+        columns = slice(z * 256, z * 256 + 256)
+        shared_grad_out[:, columns] = weight_final[z, :, :256].astype(full)
+        value_grad_out[:, columns] = weight_final[z, :, 256:].astype(full)
     drive([share_tile])
     tile[...] = jnp.sum(tile_line[...], axis=0)
     for index in range(6):
@@ -1612,82 +1480,153 @@
         copy.wait_send()
 
 
-def close_stage(arguments, collective_id, planes):
+LAYER_INPUTS = (
+    "sort_order", "sort_place", "gain_a_in", "shift_a_in", "gain_f_in", "shift_f_in", "bias_up_in",
+    "bias_down_in", "x2", "wqk", "wv", "wo", "wup", "wdown", "g2", "x1", "g1",
+)
+LAYER_OUTPUTS = (
+    "y1_out", "y2_out", "g1_out", "g2_out", "shared_grad_out", "value_grad_out", "out_grad_out",
+    "up_out", "down_out", "vectors_out",
+)
+OPEN_REFS = (
+    "sort_order", "sort_place", "gain_a_in", "shift_a_in", "gain_f_in", "shift_f_in", "bias_up_in",
+    "bias_down_in", "x2", "wqk", "wv", "wo", "wup", "wdown", "g2", "ints", "all_ints", "floats",
+    "all_floats", "gains", "bias_up", "order_rows", "place_rows", "order_s", "place_s", "normed",
+    "df", "wqk_line", "wv_line", "wo_line", "wup_rows", "wqk_pair", "wv_pair", "heads",
+    "head_table", "table", "sums", "shared", "values", "total_sorted", "mixed_home", "total_home",
+    "last_scale", "wo_all", "wup_part", "wdown_part", "df_plane", "mixed_in", "total_in",
+)
+FEED_REFS = (
+    "x1", "g1", "y1_out", "g1_out", "gains", "bias_up", "sums", "table", "head_table", "mixed_home",
+    "total_home", "wo_all", "wup_part", "wdown_part", "df_plane", "mixed_in", "total_in",
+    "dtotal_in", "attended", "arrived", "h2", "act", "dpre", "kept", "from_sibling", "to_chip",
+    "from_chip", "up_grad", "up_parts", "down_grad", "down_parts", "dout", "datt_out", "datt",
+    "up_bias", "feed_gain", "feed_shift", "y2_parts", "out_sibling",
+)
+CLOSE_REFS = (
+    "x2", "g2", "y2_out", "g2_out", "shared_grad_out", "value_grad_out", "out_grad_out", "up_out",
+    "down_out", "vectors_out", "gains", "order_rows", "order_s", "place_s", "normed", "wqk_pair",
+    "wv_pair", "shared", "values", "total_sorted", "head_table", "table", "sums", "last_scale",
+    "dtotal_in", "attended", "df_plane", "h2", "wup_part", "wdown_part", "up_parts", "down_grad",
+    "down_parts", "kept", "from_sibling", "to_chip", "from_chip", "up_bias", "feed_gain",
+    "feed_shift", "grad_sorted", "grad_total_sorted", "scale_sums", "up_sum", "up_arrived",
+    "dshared", "dvalues", "de", "out_sent", "out_arrived", "weight_arrived", "weight_sum",
+    "weight_final", "tiles_sent", "tiles_arrived", "tile", "tile_line",
+    "y2_parts", "out_sibling", "out_chip",
+)
+
+
+def layer_scratch(planes, rows, width, own, part):
     low, full, whole_number = jnp.bfloat16, jnp.float32, jnp.int32
-    x2, normed = arguments[13], arguments[9]
-    own, part = arguments[10].shape[2], arguments[15].shape[2]
-    rows, width = x2.shape
     tiles = planes * 8
     tokens = tiles * rows
+    return {
+        "ints": pltpu.VMEM((8, rows), whole_number),
+        "all_ints": pltpu.VMEM((planes, 8, 8, rows), whole_number),
+        "floats": pltpu.VMEM((8, rows), full),
+        "all_floats": pltpu.VMEM((planes, 8, 8, rows), full),
+        "gains": pltpu.VMEM((8, width), full),
+        "bias_up": pltpu.VMEM((1, part), full),
+        "order_rows": pltpu.VMEM((tiles, rows), whole_number),
+        "place_rows": pltpu.VMEM((tiles, rows), whole_number),
+        "order_s": pltpu.SMEM((tiles, rows), whole_number),
+        "place_s": pltpu.SMEM((tiles, rows), whole_number),
+        "normed": pltpu.VMEM((planes, rows, width), low),
+        "df": pltpu.VMEM((rows, width), low),
+        "wqk_line": pltpu.VMEM((planes, own, 256), low),
+        "wv_line": pltpu.VMEM((planes, own, 256), low),
+        "wo_line": pltpu.VMEM((planes, own, width), low),
+        "wup_rows": pltpu.VMEM((8, own, part), low),
+        "wqk_pair": pltpu.VMEM((planes, 8, own, 256), low),
+        "wv_pair": pltpu.VMEM((planes, 8, own, 256), low),
+        "heads": pltpu.VMEM((planes, rows, 512), low),
+        "head_table": pltpu.VMEM((planes, 8, rows, 256), low),
+        "table": pltpu.VMEM((tokens, 256), full),
+        "sums": pltpu.VMEM((tokens + rows, 256), full),
+        "shared": pltpu.VMEM((tokens + BLOCK, HEAD_DIM), low),
+        "values": pltpu.VMEM((tokens + BLOCK, HEAD_DIM), low),
+        "total_sorted": pltpu.VMEM((tokens, HEAD_DIM), full),
+        "mixed_home": pltpu.VMEM((8, planes, rows, HEAD_DIM), low),
+        "total_home": pltpu.VMEM((8, 8, rows), full),
+        "last_scale": pltpu.VMEM((1, rows), full),
+        "wo_all": pltpu.VMEM((planes, 8, own, width), low),
+        "wup_part": pltpu.VMEM((planes, 8, own, part), low),
+        "wdown_part": pltpu.VMEM((planes, rows, width), low),
+        "df_plane": pltpu.VMEM((8, rows, width), low),
+        "mixed_in": pltpu.VMEM((8, planes, rows, HEAD_DIM), low),
+        "total_in": pltpu.VMEM((8, 8, rows), full),
+        "dtotal_in": pltpu.VMEM((8, 8, rows), full),
+        "attended": pltpu.VMEM((planes, rows, 256), low),
+        "arrived": pltpu.VMEM((planes, rows, 256), low),
+        "h2": pltpu.VMEM((8 * rows, width), low),
+        "act": pltpu.VMEM((8 * rows, part), low),
+        "dpre": pltpu.VMEM((8 * rows, part), low),
+        "kept": pltpu.VMEM((4, 2, rows, width), low),
+        "from_sibling": pltpu.VMEM((4, rows, width), low),
+        "to_chip": pltpu.VMEM((3, rows, width), low),
+        "from_chip": pltpu.VMEM((3, rows, width), low),
+        "up_grad": pltpu.VMEM((planes, width // planes, part), low),
+        "up_parts": pltpu.VMEM((planes, width // planes, part), low),
+        "down_grad": pltpu.VMEM((planes, rows, width), low),
+        "down_parts": pltpu.VMEM((planes, rows, width), low),
+        "dout": pltpu.VMEM((rows, width), low),
+        "datt_out": pltpu.VMEM((planes, rows, 256), low),
+        "datt": pltpu.VMEM((planes, rows, 256), low),
+        "up_bias": pltpu.VMEM((1, part), full),
+        "feed_gain": pltpu.VMEM((1, width), full),
+        "feed_shift": pltpu.VMEM((1, width), full),
+        "grad_sorted": pltpu.VMEM((tokens, HEAD_DIM), low),
+        "grad_total_sorted": pltpu.VMEM((tokens, HEAD_DIM), full),
+        "scale_sums": pltpu.VMEM((tiles + 8, rows), full),
+        "up_sum": pltpu.VMEM((8, own, part), full),
+        "up_arrived": pltpu.VMEM((8, own, part), full),
+        "dshared": pltpu.VMEM((planes * rows, 256), low),
+        "dvalues": pltpu.VMEM((planes * rows, 256), low),
+        "de": pltpu.VMEM((planes, rows, width), low),
+        "out_sent": pltpu.VMEM((planes, own, width), low),
+        "out_arrived": pltpu.VMEM((planes, own, width), low),
+        "y2_parts": pltpu.VMEM((8, rows, width), low),
+        "out_sibling": pltpu.VMEM((4, rows, width), low),
+        "out_chip": pltpu.VMEM((3, rows, width), low),
+        "weight_arrived": pltpu.VMEM((8, planes, own, 512), low),
+        "weight_sum": pltpu.VMEM((planes, own, 512), low),
+        "weight_final": pltpu.VMEM((planes, own, 512), low),
+        "tiles_sent": pltpu.VMEM((2, 24, rows), full),
+        "tiles_arrived": pltpu.VMEM((8, 24, rows), full),
+        "tile": pltpu.VMEM((24, rows), full),
+        "tile_line": pltpu.VMEM((planes, 24, rows), full),
+    }
+
+
+def layer_kernel(planes, names, *refs):
+    links = Links(planes, *refs[len(names) :])
+    held = dict(zip(names, refs))
+    links.greet()
+    shares = open_part(links, planes, *[held[name] for name in OPEN_REFS])
+    shares = feed_part(links, planes, *shares, *[held[name] for name in FEED_REFS])
+    close_part(links, planes, *shares, *[held[name] for name in CLOSE_REFS])
+
+
+def layer_stage(arguments, collective_id, planes):
+    rows, width = arguments[LAYER_INPUTS.index("x2")].shape
+    own, hidden = arguments[LAYER_INPUTS.index("wup")].shape
     shape = jax.ShapeDtypeStruct
-    outputs = [
-        shape((rows, width), full),
-        shape((rows, width), full),
-        shape((own, width), full),
-        shape((own, width), full),
-        shape((own, width), full),
-        shape((own, 8 * part), full),
-        shape((rows, width), full),
-        shape((8, rows), full),
+    token, weight = shape((rows, width), jnp.float32), shape((own, width), jnp.float32)
+    outputs = [token] * 4 + [weight] * 3 + [
+        shape((own, hidden), jnp.float32), token, shape((8, rows), jnp.float32)
     ]
-    vmem = pltpu.VMEM
-    chip_blocks = (planes, rows, 256)
-    scratch = [
-        vmem((tiles, rows), whole_number),
-        pltpu.SMEM((tiles, rows), whole_number),
-        pltpu.SMEM((tiles, rows), whole_number),
-        vmem((tokens + BLOCK, HEAD_DIM), low),
-        vmem((tokens + BLOCK, HEAD_DIM), low),
-        vmem((tokens, HEAD_DIM), full),
-        vmem((planes, 8, rows, HEAD_DIM), low),
-        vmem((8, 8, rows), full),
-        vmem((tokens, 256), full),
-        vmem((tokens, HEAD_DIM), low),
-        vmem((tokens, HEAD_DIM), full),
-        vmem((tokens + rows, 256), full),
-        vmem((tiles + 8, rows), full),
-        vmem((1, rows), full),
-        vmem((4, 2) + chip_blocks, low),
-        vmem((4,) + chip_blocks, low),
-        vmem((3,) + chip_blocks, low),
-        vmem((3,) + chip_blocks, low),
-        vmem((8, rows, width), low),
-        vmem((planes, rows, width), low),
-        vmem(chip_blocks, low),
-        vmem((planes, rows, width), low),
-        vmem((planes, 8, own, 256), low),
-        vmem((planes, 8, own, 256), low),
-        vmem((rows, width), full),
-        vmem((rows, width), full),
-        vmem((planes, 8 * own, part), low),
-        vmem((planes, rows, width), low),
-        vmem((8, own, part), full),
-        vmem((8, own, part), full),
-        vmem((planes * rows, 256), low),
-        vmem((planes * rows, 256), low),
-        vmem((planes, rows, width), low),
-        vmem((planes, rows, width), low),
-        vmem((8, own, width), low),
-        vmem((8, own, width), low),
-        vmem((2, planes, 8, own, 256), low),
-        vmem((8, 2, planes, own, 256), low),
-        vmem((2, planes, own, 256), low),
-        vmem((2, own, width), low),
-        vmem((2, 24, rows), full),
-        vmem((8, 24, rows), full),
-        vmem((24, rows), full),
-        vmem((planes, 24, rows), full),
-    ]
+    scratch = layer_scratch(planes, rows, width, own, hidden // 8)
+    names = LAYER_INPUTS + LAYER_OUTPUTS + tuple(scratch)
     return pl.pallas_call(
-        functools.partial(close_kernel, planes),
+        functools.partial(layer_kernel, planes, names),
         out_shape=outputs,
-        in_specs=[ANY] * 12 + [VMEM] + [ANY] * 4 + [VMEM] * 3,
+        in_specs=[VMEM] * len(arguments),
         out_specs=[VMEM] * len(outputs),
-        scratch_shapes=scratch + link_scratch(),
+        scratch_shapes=list(scratch.values()) + link_scratch(),
         compiler_params=pltpu.CompilerParams(
-            vmem_limit_bytes=56 << 20, collective_id=collective_id, has_side_effects=True
+            vmem_limit_bytes=60 << 20, collective_id=collective_id, has_side_effects=True
         ),
-        name="close",
+        name="layer",
     )(*arguments)
 
 
@@ -1760,46 +1699,18 @@
     sort_place,
 ):
     planes = n_seq // 2
-    rows, width = first_half.shape[1:]
     x1, x2, g1, g2 = (a[0] for a in (first_half, second_half, grad_first, grad_second))
     wqk, wv, wo = query_key_weight[0], value_projection_weight[0], output_projection_weight[0]
     wup, wdown = upper_projection_weight[0], lower_projection_weight[0]
-    (
-        places, gains, bias_up, normed_line, wqk_pair, wv_pair, wo_all, wup_part, wdown_part, df_plane,
-        shared, values, total_sorted, mixed, total,
-    ) = open_stage(
+    results = layer_stage(
         (
             sort_order[0, :, 0], sort_place[0, :, 0], attend_gain, attend_shift, feed_gain, feed_shift,
-            upper_projection_bias, lower_projection_bias, x2, wqk, wv, wo, wup, wdown, g2,
+            upper_projection_bias, lower_projection_bias, x2, wqk, wv, wo, wup, wdown, g2, x1, g1,
         ),
         1,
         planes,
     )
-    (
-        y1, g1, dout, attended, dmixed, dtotal, y2_parts, up_grad, down_grad,
-        up_bias_grad, feed_gain_grad, feed_shift_grad,
-    ) = feed_stage(
-        (
-            mixed, total, x1, wo_all.reshape(width, width), gains, wup_part.reshape(width, -1),
-            bias_up, wdown_part.reshape(-1, width), df_plane.reshape(8 * rows, width), g1,
-        ),
-        2,
-        planes,
-    )
-    (
-        y2, g2, shared_grad, value_grad, out_grad, up_grad, down_grad, vectors
-    ) = close_stage(
-        (
-            places, shared, values, total_sorted, dmixed, dtotal, y2_parts, dout, attended, normed_line,
-            wqk_pair, wv_pair, gains, x2, g2, up_grad, down_grad, up_bias_grad, feed_gain_grad,
-            feed_shift_grad,
-        ),
-        3,
-        planes,
-    )
-    return finish_stage(
-        (y1, y2, g1, g2, shared_grad, value_grad, out_grad, up_grad, down_grad, vectors)
-    )
+    return finish_stage(results)
 
 
 def on_device(n_seq, n_sub, *arguments):

time: 281 us -> 251 us (0.89)
  Pallas kernels: 280 us -> 250 us
    pallas_call x3 -> x1, Pallas kernels: 276 us -> 246 us  [layer_stage(): pl.pallas_call(functools.partial(layer_kernel, planes, names), out_shape=...]
where the time goes in v8:
time: 251 us
  Pallas kernels  250 us (100%)
    pallas_call x1, Pallas kernels, layer_stage(): pl.pallas_call(functools.partial(layer_kernel, planes, names), out_shape=...  246 us

profile of v8, /device:TPU:0, one launch (start us, length us, event | category | flops | bytes accessed | tf_op | source)
XLA Modules:
  0.0 250.8 jit_solution(11195584884487798626)
XLA Ops:
  0.7 245.6 %layer.1 = (f32[128,1024]{1,0:T(8,128)}, f32[128,1024]{1,0:T(8,128)}, f32[128,1024]{1,0:T(8,128)}, f32[128,1024]{1,0:T(8,128)}, f32[32,1024]{1,0:T(8,128)}, /*in...) custom-call(s32[4,128]{1,0:T(4,128)} %bitcast.20, ...), custom_call_target="tpu_custom_call" | custom-call | tf_op jit(solution)/shard_map/layer/pallas_call | solution.py:1620
  246.3 4.4 %finish.1 = (f32[1,128,1024]{2,1,0:T(8,128)}, f32[1,128,1024]{2,1,0:T(8,128)}, f32[1,128,1024]{2,1,0:T(8,128)}, f32[1,128,1024]{2,1,0:T(8,128)}, f32[1,32]{1,0:T...) custom-call(f32[128,1024]{1,0:T(8,128)} %get-tuple-element.25.y1, ...), custom_call_target="tpu_custom_call" | custom-call | tf_op jit(solution)/shard_map/finish/pallas_call | solution.py:1670

commit v9 on v8

--- a/solution.py
+++ b/solution.py
@@ -523,7 +523,7 @@
     def meet(self):
         pl.semaphore_wait(pltpu.get_barrier_semaphore(), self.greeted)
 
-    def push(self, source, target, device):
+    def push(self, source, target, device, start=True):
         copy = pltpu.make_async_remote_copy(
             src_ref=source,
             dst_ref=target,
@@ -533,7 +533,8 @@
             device_id_type=pl.DeviceIdType.MESH,
         )
         self.used += 1
-        copy.start()
+        if start:
+            copy.start()
         return copy
 
     def keep(self, source, target):
@@ -609,6 +610,27 @@
         for step in range(1, links.planes):
             device, to, _ = links.along(step)
             copies.append(links.push(source(here, to), target(there, links.z), device))
+        yield
+        own.wait()
+        for copy in copies:
+            copy.wait()
+
+    return transfer
+
+
+def along_z_in_turn(source, target):
+    def transfer(links, here, there):
+        own = links.keep(source(here, links.z), target(there, links.z))
+        copies = []
+        for step in range(1, links.planes):
+            device, to, _ = links.along(step)
+            copies.append(links.push(source(here, to), target(there, links.z), device, start=False))
+        outer = (links.z == 0) | (links.z == links.planes - 1)
+        for copy in copies:
+            pl.when(outer)(copy.start)
+        yield
+        for copy in copies:
+            pl.when(jnp.logical_not(outer))(copy.start)
         yield
         own.wait()
         for copy in copies:
@@ -1064,19 +1086,26 @@
         next(head_shares[-2])
     for transfer in upper_shares:
         drive([transfer])
+    up_share = along_z_in_turn(whole, block)(links, wup_rows, wup_part)
+    next(up_share)
+
+    def first_rows(ref, z):
+        return ref.at[pl.ds(0, 64), :]
+
+    def first_landing(ref, z):
+        return ref.at[z, pl.ds(0, 64), :]
+
+    down_share = along_z_in_turn(first_rows, first_landing)(links, wdown, wdown_part)
+    next(down_share)
     next(head_shares[-1])
     drive([wo_share])
     wo_share = over_chips(whole, second)(links, wo_line, wo_all)
     for copy in to_scalars:
         copy.wait()
     drive(head_shares)
-    shares = [
-        df_share,
-        along_z(whole, block)(links, wup_rows, wup_part),
-        along_z(whole, block)(links, wdown, wdown_part),
-    ]
-    next(shares[1])
-    next(shares[2])
+    shares = [df_share, up_share, down_share]
+    next(up_share)
+    next(down_share)
     next(wo_share)
 
     def load(tile, carry):
@@ -1120,7 +1149,7 @@
     x1, g1, y1_out, g1_out, gains, bias_up, sums, table, head_table, mixed_home, total_home,
     wo_all, wup_part, wdown_part, df_plane, mixed_in, total_in, dtotal_in, attended, arrived, h2, act, dpre,
     kept, from_sibling, to_chip, from_chip, up_grad, up_parts, down_grad, down_parts, dout, datt_out, datt,
-    up_bias, feed_gain, feed_shift, y2_parts, out_sibling,
+    up_bias, feed_gain, feed_shift, y2_sibling, y2_chip, out_sibling, wdown,
 ):
     low, full = jnp.bfloat16, jnp.float32
 
@@ -1149,6 +1178,15 @@
     lax.fori_loop(0, planes, combine, 0)
     share = along_z(block, block)(links, attended, arrived)
     next(share)
+
+    def last_rows(ref, z):
+        return ref.at[pl.ds(64, 64), :]
+
+    def last_landing(ref, z):
+        return ref.at[z, pl.ds(64, 64), :]
+
+    down_share = along_z(last_rows, last_landing)(links, wdown, wdown_part)
+    next(down_share)
     drive([wo_share])
     drive([share])
     y1 = x1[...]
@@ -1163,7 +1201,7 @@
     own_h2 = h2.at[own_rows, :]
     direct = {step: links.push(own_h2, own_h2, links.near(step)[0]) for step in (2, 4)}
     handed = {0: links.push(own_h2, own_h2, sibling)}
-    drive(weight_shares)
+    drive(weight_shares + [down_share])
 
     half = wup_part.shape[3] // 2
 
@@ -1242,8 +1280,14 @@
         return carry
 
     lax.fori_loop(0, 8, lower, 0)
-    share_y2 = over_plane(block, block)(links, df_plane, y2_parts)
-    next(share_y2)
+
+    def of_chip(step, core):
+        return links.near(step)[1] // 2 * 2 + core
+
+    y2_traded = [
+        links.push(df_plane.at[of_chip(step, 1 - links.core)], y2_sibling.at[slot], sibling)
+        for slot, step in enumerate((6, 4, 2, 0))
+    ]
     for copy in sent:
         copy.wait_recv()
     grad = own_sum + (
@@ -1259,6 +1303,17 @@
         datt_out[z] = dot(dout[...], wo_rows(z), ((1,), (1,))).astype(low)
     share = along_z(block, block)(links, datt_out, datt)
     next(share)
+    y2_pushed = []
+    for slot, step in enumerate((6, 4, 2, 0)):
+        y2_traded[slot].wait()
+        mine = of_chip(step, links.core)
+        df_plane[mine] = (
+            df_plane[mine].astype(full) + y2_sibling[slot].astype(full)
+        ).astype(low)
+        if step:
+            y2_pushed.append(
+                links.push(df_plane.at[mine], y2_chip.at[slot], links.near(step)[0])
+            )
     for copy in [direct[6]] + list(handed.values()):
         copy.wait_send()
     for z in range(planes):
@@ -1304,17 +1359,17 @@
         next(transfer)
     for copy in traded + sent:
         copy.wait_send()
-    return shares, share_y2, share_up, share_down, out_traded
+    return shares, y2_pushed, share_up, share_down, out_traded
 
 
 def close_part(
-    links, planes, shares, share_y2, share_up, share_down, out_traded,
+    links, planes, shares, y2_pushed, share_up, share_down, out_traded,
     x2, g2, y2_out, g2_out, shared_grad_out, value_grad_out, out_grad_out, up_out, down_out, vectors_out,
     gains, order_rows, order_s, place_s, normed, wqk_pair, wv_pair, shared, values, total_sorted, head_table,
     table, sums, last_scale, dtotal_in, attended, df_plane, h2, wup_part, wdown_part, up_parts, down_grad,
     down_parts, kept, from_sibling, to_chip, from_chip, up_bias, feed_gain, feed_shift, grad_sorted,
     grad_total_sorted, scale_sums, up_sum, up_arrived, dshared, dvalues, de, out_sent, out_arrived,
-    weight_arrived, weight_sum, weight_final, tiles_sent, tiles_arrived, tile, tile_line, y2_parts,
+    weight_arrived, weight_sum, weight_final, tiles_sent, tiles_arrived, tile, tile_line, y2_chip,
     out_sibling, out_chip,
 ):
     low, full = jnp.bfloat16, jnp.float32
@@ -1422,9 +1477,12 @@
         )
     share_weights = over_plane(second, block)(links, wup_part, weight_arrived)
     next(share_weights)
-    drive([share_y2])
+    for copy in y2_pushed:
+        copy.wait()
     y2_out[...] = x2[...] + (
-        sum(y2_parts[p].astype(full) for p in range(8)) + gains[4:5, :]
+        df_plane[links.p].astype(full)
+        + sum(y2_chip[slot].astype(full) for slot in range(3))
+        + gains[4:5, :]
     )
     drive([share_up])
     for p in range(8):
@@ -1501,7 +1559,7 @@
     "total_home", "wo_all", "wup_part", "wdown_part", "df_plane", "mixed_in", "total_in",
     "dtotal_in", "attended", "arrived", "h2", "act", "dpre", "kept", "from_sibling", "to_chip",
     "from_chip", "up_grad", "up_parts", "down_grad", "down_parts", "dout", "datt_out", "datt",
-    "up_bias", "feed_gain", "feed_shift", "y2_parts", "out_sibling",
+    "up_bias", "feed_gain", "feed_shift", "y2_sibling", "y2_chip", "out_sibling", "wdown",
 )
 CLOSE_REFS = (
     "x2", "g2", "y2_out", "g2_out", "shared_grad_out", "value_grad_out", "out_grad_out", "up_out",
@@ -1512,7 +1570,7 @@
     "feed_shift", "grad_sorted", "grad_total_sorted", "scale_sums", "up_sum", "up_arrived",
     "dshared", "dvalues", "de", "out_sent", "out_arrived", "weight_arrived", "weight_sum",
     "weight_final", "tiles_sent", "tiles_arrived", "tile", "tile_line",
-    "y2_parts", "out_sibling", "out_chip",
+    "y2_chip", "out_sibling", "out_chip",
 )
 
 
@@ -1585,7 +1643,8 @@
         "de": pltpu.VMEM((planes, rows, width), low),
         "out_sent": pltpu.VMEM((planes, own, width), low),
         "out_arrived": pltpu.VMEM((planes, own, width), low),
-        "y2_parts": pltpu.VMEM((8, rows, width), low),
+        "y2_sibling": pltpu.VMEM((4, rows, width), low),
+        "y2_chip": pltpu.VMEM((3, rows, width), low),
         "out_sibling": pltpu.VMEM((4, rows, width), low),
         "out_chip": pltpu.VMEM((3, rows, width), low),
         "weight_arrived": pltpu.VMEM((8, planes, own, 512), low),

time: 251 us -> 244 us (0.972)
  Pallas kernels: 250 us -> 243 us
    pallas_call x1, Pallas kernels: 246 us -> 239 us  [layer_stage(): pl.pallas_call(functools.partial(layer_kernel, planes, names), out_shape=...]
where the time goes in v9:
time: 244 us
  Pallas kernels  243 us (100%)
    pallas_call x1, Pallas kernels, layer_stage(): pl.pallas_call(functools.partial(layer_kernel, planes, names), out_shape=...  239 us

profile of v9, /device:TPU:0, one launch (start us, length us, event | category | flops | bytes accessed | tf_op | source)
XLA Modules:
  0.0 244.2 jit_solution(10432701695203163992)
XLA Ops:
  0.7 239.0 %layer.1 = (f32[128,1024]{1,0:T(8,128)}, f32[128,1024]{1,0:T(8,128)}, f32[128,1024]{1,0:T(8,128)}, f32[128,1024]{1,0:T(8,128)}, f32[32,1024]{1,0:T(8,128)}, /*in...) custom-call(s32[4,128]{1,0:T(4,128)} %bitcast.20, ...), custom_call_target="tpu_custom_call" | custom-call | tf_op jit(solution)/shard_map/layer/pallas_call | solution.py:1679
  239.7 4.4 %finish.1 = (f32[1,128,1024]{2,1,0:T(8,128)}, f32[1,128,1024]{2,1,0:T(8,128)}, f32[1,128,1024]{2,1,0:T(8,128)}, f32[1,128,1024]{2,1,0:T(8,128)}, f32[1,32]{1,0:T...) custom-call(f32[128,1024]{1,0:T(8,128)} %get-tuple-element.25.y1, ...), custom_call_target="tpu_custom_call" | custom-call | tf_op jit(solution)/shard_map/finish/pallas_call | solution.py:1729

commit v10 on v9

--- a/solution.py
+++ b/solution.py
@@ -634,6 +634,27 @@
         yield
         own.wait()
         for copy in copies:
+            copy.wait()
+
+    return transfer
+
+
+def along_z_outer_first(source, target):
+    def transfer(links, here, there):
+        copies = []
+        for step in range(1, links.planes):
+            device, to, _ = links.along(step)
+            copy = links.push(source(here, to), target(there, links.z), device, start=False)
+            copies.append(((to == 0) | (to == links.planes - 1), copy))
+        for outer, copy in copies:
+            pl.when(outer)(copy.start)
+        yield
+        for outer, copy in copies:
+            pl.when(jnp.logical_not(outer))(copy.start)
+        own = links.keep(source(here, links.z), target(there, links.z))
+        yield
+        own.wait()
+        for _, copy in copies:
             copy.wait()
 
     return transfer
@@ -1369,7 +1390,7 @@
     table, sums, last_scale, dtotal_in, attended, df_plane, h2, wup_part, wdown_part, up_parts, down_grad,
     down_parts, kept, from_sibling, to_chip, from_chip, up_bias, feed_gain, feed_shift, grad_sorted,
     grad_total_sorted, scale_sums, up_sum, up_arrived, dshared, dvalues, de, out_sent, out_arrived,
-    weight_arrived, weight_sum, weight_final, tiles_sent, tiles_arrived, tile, tile_line, y2_chip,
+    weight_arrived, weight_sum, weight_final, tiles_sent, tiles_arrived, tile, tile_line, y2_sibling, y2_chip,
     out_sibling, out_chip,
 ):
     low, full = jnp.bfloat16, jnp.float32
@@ -1399,73 +1420,81 @@
         tiles, 4, order_s, order_rows, table, shared, values, total_sorted,
         grad_sorted, grad_total_sorted, sums, scale_sums, last_scale,
     )
-    sibling, _ = links.near(1)
-
-    def unsort(slot, step):
-        chip = links.near(step)[1] // 2
-        for core, goal in ((0, 1 - links.core), (1, links.core)):
-
-            def rows(z, carry):
-                columns = pl.ds(pl.multiple_of(z * 256, 256), 256)
-                for part in range(4):
-                    picked = pick_tile(sums, place_s, z * 8 + chip * 2 + goal, part)
-                    kept[slot, core, part * 32 : part * 32 + 32, columns] = picked.astype(low)
-                return carry
-
-            lax.fori_loop(0, planes, rows, 0)
-            if core == 0:
-                traded = links.push(kept.at[slot, 0], from_sibling.at[slot], sibling)
-        return traded
-
-    def chip_sum(slot, step, traded):
-        traded.wait_recv()
-        result = kept[slot, 1].astype(full) + from_sibling[slot].astype(full)
-        if step == 0:
-            return result
-        to_chip[slot] = result.astype(low)
-        return links.push(to_chip.at[slot], from_chip.at[slot], links.near(step)[0])
-
-    steps = (6, 4, 2, 0)
-    traded, sent = [], []
-    for slot, step in enumerate(steps):
-        traded.append(unsort(slot, step))
-        if slot:
-            sent.append(chip_sum(slot - 1, steps[slot - 1], traded[slot - 1]))
     total = h2[out_sums[3], :].astype(full)
     for slot, copy in enumerate(out_pushed):
         copy.wait()
         total += out_chip[slot].astype(full)
     out_sent[...] = total.astype(low).reshape(out_sent.shape)
-    own_sum = chip_sum(3, 0, traded[3])
     share_out = along_z(block, block)(links, out_sent, out_arrived)
     next(share_out)
+    sibling, _ = links.near(1)
+    steps = (6, 4, 2, 0)
+    halves = ((0, 3), (1, 2))
+
+    def unsort(half, slot, step):
+        chip = links.near(step)[1] // 2
+        columns = pl.ds(half * 512, 512)
+        for core, goal in ((0, 1 - links.core), (1, links.core)):
+
+            def rows(index, carry):
+                z = index * 3 if half == 0 else index + 1
+                place = pl.ds(pl.multiple_of(half * 512 + index * 256, 256), 256)
+                for part in range(4):
+                    picked = pick_tile(sums, place_s, z * 8 + chip * 2 + goal, part)
+                    kept[slot, core, part * 32 : part * 32 + 32, place] = picked.astype(low)
+                return carry
+
+            lax.fori_loop(0, 2, rows, 0)
+            if core == 0:
+                traded = links.push(
+                    kept.at[slot, 0, :, columns], from_sibling.at[slot, :, columns], sibling
+                )
+        return traded
+
+    def chip_sum(half, slot, traded):
+        traded.wait_recv()
+        columns = slice(half * 512, half * 512 + 512)
+        result = kept[slot, 1, :, columns].astype(full) + from_sibling[slot, :, columns].astype(full)
+        if steps[slot] == 0:
+            return result
+        to_chip[slot, :, columns] = result.astype(low)
+        columns = pl.ds(half * 512, 512)
+        return links.push(
+            to_chip.at[slot, :, columns], from_chip.at[slot, :, columns], links.near(steps[slot])[0]
+        )
+
+    traded, sent = [[], []], [[], []]
+    for half in range(2):
+        for slot, step in enumerate(steps):
+            traded[half].append(unsort(half, slot, step))
+            if slot:
+                sent[half].append(chip_sum(half, slot - 1, traded[half][slot - 1]))
     own_columns = pl.ds(pl.multiple_of(links.x * 128, 128), 128)
     far_columns = pl.ds(pl.multiple_of((1 - links.x) * 128, 128), 128)
-
-    def settle_sum(columns, result):
-        for z in range(planes):
-            part = result[:, z * 256 : z * 256 + 256].astype(low)
+    all_wqk, all_wv = wqk_pair[...].reshape(-1, 256), wv_pair[...].reshape(-1, 256)
+
+    def settle_sum(half, columns, result):
+        for index, z in enumerate(halves[half]):
+            part = result[:, index * 256 : index * 256 + 256].astype(low)
             dshared[z * 128 : z * 128 + 128, columns] = part[:, :128]
             dvalues[z * 128 : z * 128 + 128, columns] = part[:, 128:]
 
-    sent[2].wait_recv()
-    settle_sum(own_columns, own_sum + from_chip[2].astype(full))
-    sent[1].wait_recv()
-    sent[0].wait_recv()
-    settle_sum(far_columns, from_chip[1].astype(full) + from_chip[0].astype(full))
-    all_wqk, all_wv = wqk_pair[...].reshape(-1, 256), wv_pair[...].reshape(-1, 256)
-    drive([share_down])
-
-    def input_grad(z, carry):
-        rows = rows_of(z)
-        down_grad[z] = (
-            dot(dshared[rows, :], all_wqk, ((1,), (1,))) + dot(dvalues[rows, :], all_wv, ((1,), (1,)))
-        ).astype(low)
-        return carry
-
-    lax.fori_loop(0, planes, input_grad, 0)
-    share_de = along_z(block, block)(links, down_grad, de)
-    next(share_de)
+    share_de = along_z_outer_first(block, block)(links, y2_sibling, de)
+    for half in range(2):
+        own_sum = chip_sum(half, 3, traded[half][3])
+        columns = slice(half * 512, half * 512 + 512)
+        for copy in sent[half]:
+            copy.wait_recv()
+        settle_sum(half, own_columns, own_sum + from_chip[2, :, columns].astype(full))
+        settle_sum(
+            half, far_columns, from_chip[1, :, columns].astype(full) + from_chip[0, :, columns].astype(full)
+        )
+        for z in halves[half]:
+            rows = slice(z * 128, z * 128 + 128)
+            y2_sibling[z] = (
+                dot(dshared[rows, :], all_wqk, ((1,), (1,))) + dot(dvalues[rows, :], all_wv, ((1,), (1,)))
+            ).astype(low)
+        next(share_de)
     drive([share_up])
     up_sum[...] = sum(up_parts[z].astype(full) for z in range(planes)).reshape(up_sum.shape)
     share_up = over_plane(block, block)(links, up_sum, up_arrived)
@@ -1490,6 +1519,7 @@
             up_out[:, (z * 8 + p) * 128 : (z * 8 + p + 1) * 128] = up_arrived[
                 p, :, z * 128 : (z + 1) * 128
             ]
+    drive([share_down])
     down_out[...] = sum(down_parts[z].astype(full) for z in range(planes))
     drive([share_out])
     out_grad_out[...] = sum(out_arrived[z].astype(full) for z in range(planes))
@@ -1534,7 +1564,7 @@
     for index in range(6):
         vectors_out[index : index + 1, :] = tile[pl.ds(index * planes + links.z, 1), :]
     vectors_out[6:8, :] = jnp.zeros((2, 128), full)
-    for copy in traded + sent:
+    for copy in traded[0] + traded[1] + sent[0] + sent[1]:
         copy.wait_send()
 
 
@@ -1570,7 +1600,7 @@
     "feed_shift", "grad_sorted", "grad_total_sorted", "scale_sums", "up_sum", "up_arrived",
     "dshared", "dvalues", "de", "out_sent", "out_arrived", "weight_arrived", "weight_sum",
     "weight_final", "tiles_sent", "tiles_arrived", "tile", "tile_line",
-    "y2_chip", "out_sibling", "out_chip",
+    "y2_sibling", "y2_chip", "out_sibling", "out_chip",
 )
 
 

time: 244 us -> 238 us (0.975)
  Pallas kernels: 243 us -> 237 us
    pallas_call x1, Pallas kernels: 239 us -> 233 us  [layer_stage(): pl.pallas_call(functools.partial(layer_kernel, planes, names), out_shape=...]
where the time goes in v10:
time: 238 us
  Pallas kernels  237 us (100%)
    pallas_call x1, Pallas kernels, layer_stage(): pl.pallas_call(functools.partial(layer_kernel, planes, names), out_shape=...  233 us

profile of v10, /device:TPU:0, one launch (start us, length us, event | category | flops | bytes accessed | tf_op | source)
XLA Modules:
  0.0 238.2 jit_solution(12907999873557547312)
XLA Ops:
  0.7 233.0 %layer.1 = (f32[128,1024]{1,0:T(8,128)}, f32[128,1024]{1,0:T(8,128)}, f32[128,1024]{1,0:T(8,128)}, f32[128,1024]{1,0:T(8,128)}, f32[32,1024]{1,0:T(8,128)}, /*in...) custom-call(s32[4,128]{1,0:T(4,128)} %bitcast.20, ...), custom_call_target="tpu_custom_call" | custom-call | tf_op jit(solution)/shard_map/layer/pallas_call | solution.py:1709
  233.6 4.4 %finish.1 = (f32[1,128,1024]{2,1,0:T(8,128)}, f32[1,128,1024]{2,1,0:T(8,128)}, f32[1,128,1024]{2,1,0:T(8,128)}, f32[1,128,1024]{2,1,0:T(8,128)}, f32[1,32]{1,0:T...) custom-call(f32[128,1024]{1,0:T(8,128)} %get-tuple-element.25.y1, ...), custom_call_target="tpu_custom_call" | custom-call | tf_op jit(solution)/shard_map/finish/pallas_call | solution.py:1759

commit v11 on v10

--- a/solution.py
+++ b/solution.py
@@ -1109,14 +1109,7 @@
         drive([transfer])
     up_share = along_z_in_turn(whole, block)(links, wup_rows, wup_part)
     next(up_share)
-
-    def first_rows(ref, z):
-        return ref.at[pl.ds(0, 64), :]
-
-    def first_landing(ref, z):
-        return ref.at[z, pl.ds(0, 64), :]
-
-    down_share = along_z_in_turn(first_rows, first_landing)(links, wdown, wdown_part)
+    down_share = along_z_in_turn(whole, block)(links, wdown, wdown_part)
     next(down_share)
     next(head_shares[-1])
     drive([wo_share])
@@ -1170,7 +1163,7 @@
     x1, g1, y1_out, g1_out, gains, bias_up, sums, table, head_table, mixed_home, total_home,
     wo_all, wup_part, wdown_part, df_plane, mixed_in, total_in, dtotal_in, attended, arrived, h2, act, dpre,
     kept, from_sibling, to_chip, from_chip, up_grad, up_parts, down_grad, down_parts, dout, datt_out, datt,
-    up_bias, feed_gain, feed_shift, y2_sibling, y2_chip, out_sibling, wdown,
+    up_bias, feed_gain, feed_shift, y2_sibling, y2_chip, out_sibling,
 ):
     low, full = jnp.bfloat16, jnp.float32
 
@@ -1199,15 +1192,6 @@
     lax.fori_loop(0, planes, combine, 0)
     share = along_z(block, block)(links, attended, arrived)
     next(share)
-
-    def last_rows(ref, z):
-        return ref.at[pl.ds(64, 64), :]
-
-    def last_landing(ref, z):
-        return ref.at[z, pl.ds(64, 64), :]
-
-    down_share = along_z(last_rows, last_landing)(links, wdown, wdown_part)
-    next(down_share)
     drive([wo_share])
     drive([share])
     y1 = x1[...]
@@ -1222,7 +1206,7 @@
     own_h2 = h2.at[own_rows, :]
     direct = {step: links.push(own_h2, own_h2, links.near(step)[0]) for step in (2, 4)}
     handed = {0: links.push(own_h2, own_h2, sibling)}
-    drive(weight_shares + [down_share])
+    drive(weight_shares)
 
     half = wup_part.shape[3] // 2
 
@@ -1589,7 +1573,7 @@
     "total_home", "wo_all", "wup_part", "wdown_part", "df_plane", "mixed_in", "total_in",
     "dtotal_in", "attended", "arrived", "h2", "act", "dpre", "kept", "from_sibling", "to_chip",
     "from_chip", "up_grad", "up_parts", "down_grad", "down_parts", "dout", "datt_out", "datt",
-    "up_bias", "feed_gain", "feed_shift", "y2_sibling", "y2_chip", "out_sibling", "wdown",
+    "up_bias", "feed_gain", "feed_shift", "y2_sibling", "y2_chip", "out_sibling",
 )
 CLOSE_REFS = (
     "x2", "g2", "y2_out", "g2_out", "shared_grad_out", "value_grad_out", "out_grad_out", "up_out",

time: 238 us -> 233 us (0.979)
  Pallas kernels: 237 us -> 232 us
    pallas_call x1, Pallas kernels: 233 us -> 227 us  [layer_stage(): pl.pallas_call(functools.partial(layer_kernel, planes, names), out_shape=...]
where the time goes in v11:
time: 233 us
  Pallas kernels  232 us (100%)
    pallas_call x1, Pallas kernels, layer_stage(): pl.pallas_call(functools.partial(layer_kernel, planes, names), out_shape=...  227 us

profile of v11, /device:TPU:0, one launch (start us, length us, event | category | flops | bytes accessed | tf_op | source)
XLA Modules:
  0.0 232.6 jit_solution(757134747789501729)
XLA Ops:
  0.7 227.4 %layer.1 = (f32[128,1024]{1,0:T(8,128)}, f32[128,1024]{1,0:T(8,128)}, f32[128,1024]{1,0:T(8,128)}, f32[128,1024]{1,0:T(8,128)}, f32[32,1024]{1,0:T(8,128)}, /*in...) custom-call(s32[4,128]{1,0:T(4,128)} %bitcast.20, ...), custom_call_target="tpu_custom_call" | custom-call | tf_op jit(solution)/shard_map/layer/pallas_call | solution.py:1693
  228.1 4.4 %finish.1 = (f32[1,128,1024]{2,1,0:T(8,128)}, f32[1,128,1024]{2,1,0:T(8,128)}, f32[1,128,1024]{2,1,0:T(8,128)}, f32[1,128,1024]{2,1,0:T(8,128)}, f32[1,32]{1,0:T...) custom-call(f32[128,1024]{1,0:T(8,128)} %get-tuple-element.25.y1, ...), custom_call_target="tpu_custom_call" | custom-call | tf_op jit(solution)/shard_map/finish/pallas_call | solution.py:1743
